TPU v7x, 32 devices: a whole 2x2x4 slice. The times are simulated.
32 devices in a mesh: row: 8 (over y, x, core), col: 4 (over z).
Axes of the slice: x: 2, y: 2, z: 4, core: 2. Of those that a mesh axis runs over, the one named last changes fastest.
Arguments:
- cached_inverse: float32 [4, 8, 128, 8, 4, 128], P(None, 'row', None, None, 'col'), may hold values from -6 to 6
- parent_panel: float32 [256, 24, 128], P('col', 'row'), may hold values from -0.09375 to 0.09375
- parent_blocks: int32 [24], P('row'), may hold values from -1 to 31, as said below
- parent_sizes: int32 [24], P('row'), may hold values from 0 to 128, as said below
- parent_diagonal: float32 [256, 256], P('col'), may hold values from -6 to 6
- child_panel: float32 [256, 24, 128], P('col', 'row'), may hold values from -0.09375 to 0.09375
- child_top: float32 [256, 256], P('col'), may hold values from -0.375 to 0.375
- child_blocks: int32 [24], P('row'), may hold values from -1 to 31, as said below
- child_sizes: int32 [24], P('row'), may hold values from 0 to 128, as said below
- child_diagonal: float32 [256, 256], P('col'), may hold values from -6 to 6
Outputs:
- parent_rows: float32 [4, 8, 128, 256], P(None, 'row', 'col')
- parent_diag: float32 [256, 256], P('col')
- child_rows: float32 [4, 8, 128, 256], P(None, 'row', 'col')
- child_upper: float32 [256, 256], P('col')
- child_diag: float32 [256, 256], P('col')
Inputs may be any that keep to these rules, and one draw needn't show every extreme that they name: `parent_blocks`: slots p*3 to p*3 + 2 belong to index p of row; their live slots come first, name distinct block numbers congruent to p modulo the size of row, and the rest hold -1. Some index of row has 3 live slots. `parent_sizes`: 0 exactly for the slots that hold -1 in parent_blocks. `child_blocks`: slot k holds either parent_blocks[k] (a live parent slot) or -1. `child_sizes`: 0 exactly for the slots that hold -1 in child_blocks, else at most parent_sizes of the same slot.
All inputs are finite; a program needn't handle non-finite values.
Results may differ from a plain program's by a relative error of at most 0.000096.
Values sent between devices are 32-bit elements; how exact they have to be, the bound alone decides.
No kernel may reach another device: no remote copies, remote signals or barrier semaphores. Data moves between devices by JAX's collectives and lax.ppermute only.
A program may use at most 64 MiB of HBM per device.

v0:
```python
import jax
import jax.numpy as jnp
from jax import lax
from jax.sharding import PartitionSpec as P

highest = lax.Precision.HIGHEST


def from_root(value, axis, source):
    kept = jnp.where(lax.axis_index(axis) == source, value, 0).astype(value.dtype)
    return lax.psum(kept, axis)


def live_rows(sizes, block_rows):
    return (jnp.arange(block_rows, dtype=jnp.int32)[None, :] < sizes[:, None]).astype(jnp.float32)


def own_share(widened, blocks, row_live, row_index, row_total, col_index, row_share, local_rows):
    wanted = jnp.arange(local_rows, dtype=jnp.int32) * row_total + row_index
    onehot = (blocks[None, :] == wanted[:, None]).astype(jnp.float32)
    sliced = lax.dynamic_slice_in_dim(widened, col_index * row_share, row_share, 2)
    own_rows = jnp.einsum("rk,wkb->rbw", onehot, sliced, precision=highest)
    live_part = lax.dynamic_slice_in_dim(row_live, col_index * row_share, row_share, 1)
    row_alive = jnp.einsum("rk,kb->rb", onehot, live_part, precision=highest)
    return (own_rows, row_alive)


def add_columns(column_dense, widened, blocks, col_index, col_total):
    wanted = jnp.arange(column_dense.shape[0], dtype=jnp.int32) * col_total + col_index
    onehot = (blocks[None, :] == wanted[:, None]).astype(jnp.float32)
    return column_dense + jnp.einsum("ck,wky->cwy", onehot, widened, precision=highest)


def column_panel(widened, blocks, col_index, col_total, row_total, col_blocks):
    column_dense = jnp.zeros((col_blocks, widened.shape[0], widened.shape[2]), jnp.float32)
    for repeat in range(row_total // col_total):
        sender = col_index + repeat * col_total
        heard_panel, heard_blocks = (
            from_root(widened, "row", sender),
            from_root(blocks, "row", sender),
        )
        column_dense = add_columns(column_dense, heard_panel, heard_blocks, col_index, col_total)
    return column_dense


def child_panels(
    child_panel, child_top, child_live, child_blocks, col_index, col_total, row_total, col_blocks
):
    wide_child, top_full = (
        lax.all_gather(child_panel, "col", axis=0, tiled=True),
        lax.all_gather(child_top, "col", axis=0, tiled=True),
    )
    child_full = wide_child * child_live[None, :, :]
    child_dense = column_panel(
        child_full, child_blocks, col_index, col_total, row_total, col_blocks
    )
    return (child_full, child_dense, top_full)


def apply_inverse(cached, column_dense):
    summed = lax.psum_scatter(
        jnp.einsum(
            "rxcy,cwy->xrw",
            cached,
            column_dense,
            precision=highest,
            preferred_element_type=jnp.float32,
        ),
        "col",
        scatter_dimension=0,
        tiled=True,
    )
    return jnp.transpose(summed, (1, 0, 2))


def diagonal_sum(partial_rows, panel_width, col_share, col_index):
    entire = lax.psum(partial_rows(0, panel_width), ("row", "col"))
    return lax.dynamic_slice_in_dim(entire, col_index * col_share, col_share, 0)


def body(
    cached_inverse,
    parent_panel,
    parent_blocks,
    parent_sizes,
    parent_diagonal,
    child_panel,
    child_top,
    child_blocks,
    child_sizes,
    child_diagonal,
):
    row_total = lax.axis_size("row")
    col_total = lax.axis_size("col")
    row_index = lax.axis_index("row")
    col_index = lax.axis_index("col")
    local_rows = cached_inverse.shape[0]
    block_rows = cached_inverse.shape[2]
    col_blocks = cached_inverse.shape[3]
    cached = cached_inverse.reshape(local_rows, block_rows, col_blocks, block_rows)
    panel_width = parent_diagonal.shape[1]
    row_share = block_rows // col_total
    col_share = panel_width // col_total
    parent_live = live_rows(parent_sizes, block_rows)
    child_live = live_rows(child_sizes, block_rows)
    wide_parent = lax.all_gather(parent_panel, "col", axis=0, tiled=True)
    parent_full = wide_parent * parent_live[None, :, :]
    parent_dense = column_panel(
        parent_full, parent_blocks, col_index, col_total, row_total, col_blocks
    )
    child_full, child_dense, top_full = child_panels(
        child_panel,
        child_top,
        child_live,
        child_blocks,
        col_index,
        col_total,
        row_total,
        col_blocks,
    )
    parent_own, parent_alive = own_share(
        parent_full,
        parent_blocks,
        parent_live,
        row_index,
        row_total,
        col_index,
        row_share,
        local_rows,
    )
    both_local = apply_inverse(cached, jnp.concatenate([parent_dense, child_dense], axis=1))
    parent_local = -both_local[:, :, :panel_width] * parent_alive[:, :, None]
    child_own, child_alive = own_share(
        child_full, child_blocks, child_live, row_index, row_total, col_index, row_share, local_rows
    )
    carried = jnp.einsum("rbw,wv->rbv", parent_local, top_full, precision=highest)
    child_local = -(both_local[:, :, panel_width:] + carried) * child_alive[:, :, None]

    def stacked_terms(offset, amount):
        first_part = jnp.einsum("rbw,rbv->wv", parent_own, parent_local, precision=highest)
        second_part = jnp.einsum("rbw,rbv->wv", parent_local, child_own, precision=highest)
        third_part = jnp.einsum("rbc,rbv->cv", child_own, child_local, precision=highest)
        return jnp.concatenate([first_part, second_part, third_part], axis=1)

    stacked_sum = diagonal_sum(stacked_terms, panel_width, col_share, col_index)
    parent_diag = parent_diagonal - stacked_sum[:, :panel_width]
    child_upper = -(
        jnp.dot(parent_diag, top_full, precision=highest, preferred_element_type=jnp.float32)
        + stacked_sum[:, panel_width : 2 * panel_width]
    )
    upper_whole = lax.all_gather(child_upper, "col", axis=0, tiled=True)
    top_columns = lax.dynamic_slice_in_dim(top_full, col_index * col_share, col_share, 1)
    child_diag = (
        child_diagonal
        - jnp.dot(top_columns.T, upper_whole, precision=highest, preferred_element_type=jnp.float32)
        - stacked_sum[:, 2 * panel_width :]
    )
    return (
        parent_local[:, None, :, :],
        parent_diag,
        child_local[:, None, :, :],
        child_upper,
        child_diag,
    )


def solution(mesh):
    in_specs = (
        P(None, "row", None, None, "col", None),
        P("col", "row", None),
        P("row"),
        P("row"),
        P("col", None),
        P("col", "row", None),
        P("col", None),
        P("row"),
        P("row"),
        P("col", None),
    )
    out_specs = (
        P(None, "row", "col", None),
        P("col", None),
        P(None, "row", "col", None),
        P("col", None),
        P("col", None),
    )
    return jax.shard_map(body, mesh=mesh, in_specs=in_specs, out_specs=out_specs, check_vma=False)
```

profile of v0, /device:TPU:0, one launch (start us, length us, event | category | flops | bytes accessed | tf_op | source)
XLA Modules:
  0.0 341.0 jit_solution(10888981561500528218)
XLA Ops:
  7.2 1.4 fusion.64
  8.7 1.3 iota_compare_fusion
  10.0 16.4 %all_gather.12 = f32[256,3,128]{2,0,1:T(8,128)S(1)} all-gather(f32[64,3,128]{2,0,1:T(8,128)} %param.11), channel_id=1, replica_groups=mesh['row'=8,'col'=4] {'col'}, dimensions={0}, use_global_device_ids=true | all-gather | bytes 491520 | tf_op jit(solution)/shard_map/all_gather | solution.py:106
  26.4 0.2 copy.34
  26.7 15.7 %all_gather.13 = f32[256,3,128]{2,0,1:T(8,128)S(1)} all-gather(f32[64,3,128]{2,0,1:T(8,128)} %param.15), channel_id=1, replica_groups=mesh['row'=8,'col'=4] {'col'}, dimensions={0}, use_global_device_ids=true | all-gather | bytes 491520 | tf_op jit(solution)/shard_map/all_gather | solution.py:50
  42.4 0.2 copy.35
  42.6 1.9 broadcast_select_fusion.1
  44.5 1.9 broadcast_select_fusion.3
  46.5 1.2 broadcast_select_fusion
  47.8 8.0 %all-reduce.1 = (s32[3]{0:T(128)S(1)}, s32[3]{0:T(128)S(1)}, s32[3]{0:T(128)S(1)}, s32[3]{0:T(128)S(1)}) all-reduce(s32[3]{0:T(128)S(1)} %get-tuple-element.32, s32[3]{0:T(128)S(1)} %get-tuple-element.31, s32[3]{0:T(128)S(1)} %get-tuple-element.35, s32[3]{0:T(128)S(1)} %get-tuple-element.36), channel_id=1, replica_groups=mesh['row'=8,'col'=4] {'row'}, use_global_device_ids=true, to_apply=%region_6.7 | all-reduce | flops 12 | bytes 96 | tf_op jit(solution)/shard_map/psum | solution.py:11
  55.9 54.6 %all-reduce.11.cloned.1.call-done = (f32[256,3,128]{0,1,2:T(4,128)}, f32[256,3,128]{0,1,2:T(4,128)}, f32[256,3,128]{0,1,2:T(4,128)}, f32[256,3,128]{0,1,2:T(4,128)}) async-done(((f32[256,3,128]{0,1,2:T(4,128)}, f32[256,3,128]{0,1,2:T(4,128)}, f32[256,3,128]{0,1,2:T(4,128)}, f32[256,3,128]{0,1,2:T(4,128)}), (f32[256,3,128]{0,1,2:T(4,128)}, f32[256,3,128]{0,1,2:T(4,128)}, f32[256,3,128]{0,1,2:T(4,128)}, ...) | async-done | bytes 1572880 | tf_op jit(solution)/shard_map/psum | solution.py:11
  110.4 2.1 copy.57
  112.5 2.0 copy.55
  114.6 0.3 copy.53
  114.9 1.3 copy.51
  116.1 1.7 fusion.29
  117.8 1.7 fusion.31
  119.5 0.3 copy_add_fusion
  119.8 0.6 fusion.33
  120.5 0.6 fusion.35
  121.1 0.3 copy_add_fusion.1
  121.5 3.7 %fusion.4 = f32[128,4,512]{0,2,1:T(8,128)S(1)} fusion(f32[4,128,8,128]{3,2,1,0:T(8,128)S(1)} %bitcast.62, f32[8,256,128]{2,1,0:T(8,128)S(1)} %copy_add_fusion, f32[8,256,128]{2,1,0:T(8,128)S(1)} %copy_add_fusion.1), kind=kOutput, calls=%fused_computation.5 | convolution fusion | flops 3221749760 | bytes 5242880 | tf_op jit(solution)/shard_map/rxcy,cwy->xrw/dot_general | solution.py:62
  125.2 1.4 copy.37
  126.7 15.9 %all_gather.14 = f32[256,256]{1,0:T(8,128)S(1)} all-gather(f32[64,256]{1,0:T(8,128)S(1)} %copy-done.6), channel_id=1, replica_groups=mesh['row'=8,'col'=4] {'col'}, dimensions={0}, use_global_device_ids=true | all-gather | bytes 327680 | tf_op jit(solution)/shard_map/all_gather | solution.py:51
  142.5 0.6 dynamic-slice
  143.8 0.2 fusion.27
  144.0 0.9 fusion.25
  144.8 1.2 convolution_bitcast_fusion.3
  146.1 1.2 fusion.17
  147.3 32.9 %all-reduce.9.cloned.1.call-done = f32[128,4,512]{2,1,0:T(4,128)} async-done(((f32[128,4,512]{2,1,0:T(4,128)}), f32[128,4,512]{2,1,0:T(4,128)}) %all-reduce.9.cloned.1.call-update) | async-done | bytes 1048592
  180.1 1.0 constant_dynamic-slice_fusion
  181.1 0.1 copy.80
  181.2 0.5 convolution_bitcast_fusion.2
  181.7 0.5 convolution_bitcast_fusion.1
  182.2 0.3 fusion.10
  182.5 0.4 convolution_bitcast_fusion
  182.9 1.0 pad_maximum_fusion
  183.9 0.1 copy.41
  184.0 0.1 copy.44
  184.1 0.7 fusion.24
  184.9 129.7 %all-reduce.7.cloned.1.call-done = f32[256,768]{0,1:T(8,128)} async-done(((f32[256,768]{0,1:T(8,128)}), f32[256,768]{0,1:T(8,128)}) %all-reduce.7.cloned.1.call-update) | async-done | bytes 786448 | tf_op jit(solution)/shard_map/psum | solution.py:77
  314.6 1.0 dynamic-slice_subtract_fusion
  315.6 0.7 copy.47
  316.3 1.5 fusion.8
  317.8 0.1 copy.49
  317.9 14.3 %all_gather.15 = f32[256,256]{1,0:T(8,128)S(1)} all-gather(f32[64,256]{1,0:T(8,128)S(1)} %copy.49), channel_id=1, replica_groups=mesh['row'=8,'col'=4] {'col'}, dimensions={0}, use_global_device_ids=true | all-gather | bytes 327680 | tf_op jit(solution)/shard_map/all_gather | solution.py:151
  332.2 1.6 fusion.7
  333.8 0.7 copy.50
  (33 shorter events, 0.3 us)
Async XLA Ops:
  7.2 114.3 %copy-start = (f32[4,1,128,8,1,128]{5,4,3,2,1,0:T(1,128)S(1)}, f32[4,1,128,8,1,128]{5,4,3,2,1,0:T(1,128)}, u32[]{:S(2)}) copy-start(f32[4,1,128,8,1,128]{5,4,3,2,1,0:T(1,128)} %param.10) | copy-start | bytes 6291460
  7.2 103.2 %all-reduce.11.cloned.1.call-start = ((), (), s32[]{:S(2)}) async-start(), calls=%async_computation.2 | async-start | bytes 4194304 | tf_op jit(solution)/shard_map/psum | solution.py:11
  44.5 1.9 copy-start.1
  46.4 1.3 copy-start.2
  46.4 1.3 copy-start.9
  46.4 1.3 copy-start.10
  47.7 132.4 %all-reduce.9.cloned.1.call-start = ((), (), s32[]{:S(2)}) async-start(), calls=%async_computation.1 | async-start | bytes 2097152
  110.4 4.2 %copy-start.3 = (f32[256,3,128]{0,1,2:T(4,128)S(1)}, f32[256,3,128]{0,1,2:T(4,128)}, u32[]{:S(2)}) copy-start(f32[256,3,128]{0,1,2:T(4,128)} %get-tuple-element.21) | copy-start | bytes 1179652
  125.2 1.5 copy-start.6
  125.2 17.4 %copy-start.11 = (u32[32]{0:T(128)S(1)}, u32[32]{0:T(128)}, u32[]{:S(2)}) copy-start(u32[32]{0:T(128)} %constant.35) | copy-start | bytes 388
  126.6 188.0 %all-reduce.7.cloned.1.call-start = ((), (), s32[]{:S(2)}) async-start(), calls=%async_computation | async-start | bytes 1572864 | tf_op jit(solution)/shard_map/psum | solution.py:77
  181.7 2.2 copy-start.7
  181.7 2.3 copy-start.8
  182.5 135.3 %copy-start.4 = (f32[4,32,256]{2,1,0:T(8,128)}, f32[4,32,256]{2,1,0:T(8,128)S(1)}, u32[]{:S(2)}) copy-start(f32[4,32,256]{2,1,0:T(8,128)S(1)} %fusion.10) | copy-start | bytes 393220
  317.9 16.6 %copy-start.5 = (f32[64,256]{1,0:T(8,128)}, f32[64,256]{1,0:T(8,128)S(1)}, u32[]{:S(2)}) copy-start(f32[64,256]{1,0:T(8,128)S(1)} %copy.49) | copy-start | bytes 196612
Sparse Core Ops, SparseCore 0:
  47.8 62.5 all-reduce.10
  126.7 53.3 all-reduce.8
  186.2 128.3 all-reduce.6
where the time goes:
time: 342 us; the launch traced here: 341 us
  waiting for transfers between devices  217 us (63%)
  blocking collectives  70.4 us (21%)
  matrix products  16.5 us (5%)
  between operations  14.7 us (4%)
  other arithmetic  11.2 us (3%)
  local copies, waits for them, and re-layouts  10.9 us (3%)
    psum x1, waiting for transfers between devices, diagonal_sum(): entire = lax.psum(partial_rows(0, panel_width), ('row', 'col'))  130 us
    psum x1, waiting for transfers between devices, from_root(): return lax.psum(kept, axis)  54.6 us
    unnamed x4, waiting for transfers between devices  32.9 us
    all_gather x1, blocking collectives, body(): wide_parent = lax.all_gather(parent_panel, 'col', axis=0, tiled=True)  16.4 us
    all_gather x1, blocking collectives, child_panels(): lax.all_gather(child_top, 'col', axis=0, tiled=True)  15.9 us
    all_gather x1, blocking collectives, child_panels(): lax.all_gather(child_panel, 'col', axis=0, tiled=True)  15.7 us
    all_gather x1, blocking collectives, body(): upper_whole = lax.all_gather(child_upper, 'col', axis=0, tiled=True)  14.3 us
    psum x1, blocking collectives, from_root(): return lax.psum(kept, axis)  8.04 us
  transfers between devices with their start and end apart: 3, of which 3 were waited for; matrix products, arithmetic and copies ran while one was open for 1% of the time, Pallas kernels for 0%

commit v1 on v0

--- a/solution.py
+++ b/solution.py
@@ -1,7 +1,371 @@
+import functools
+
 import jax
 import jax.numpy as jnp
 from jax import lax
+from jax.experimental import pallas as pl
+from jax.experimental.pallas import tpu as pltpu
 from jax.sharding import PartitionSpec as P
+
+f32 = jnp.float32
+bf16 = jnp.bfloat16
+
+NN = (((1,), (0,)), ((), ()))
+NT = (((1,), (1,)), ((), ()))
+TN = (((0,), (0,)), ((), ()))
+
+
+def split(value):
+    high = value.astype(bf16)
+    return high, (value - high.astype(f32)).astype(bf16)
+
+
+def dot3(left, right, dims):
+    (lh, ll), (rh, rl) = left, right
+    dot = functools.partial(lax.dot_general, dimension_numbers=dims, preferred_element_type=f32)
+    return dot(lh, rh) + (dot(lh, rl) + dot(ll, rh))
+
+
+def vmem(count):
+    return [pl.BlockSpec(memory_space=pltpu.VMEM)] * count
+
+
+def smem(count):
+    return [pl.BlockSpec(memory_space=pltpu.SMEM)] * count
+
+
+def call(kernel, scalars, arrays, outs, scratch=(), flops=0):
+    nbytes = sum(a.size * 4 for a in arrays) + sum(4 * o[0] * o[1] for o in outs)
+    return pl.pallas_call(
+        kernel,
+        out_shape=[jax.ShapeDtypeStruct(o, f32) for o in outs],
+        in_specs=smem(len(scalars)) + vmem(len(arrays)),
+        out_specs=vmem(len(outs)),
+        scratch_shapes=list(scratch),
+        compiler_params=pltpu.CompilerParams(vmem_limit_bytes=48 * 1024 * 1024),
+        cost_estimate=pl.CostEstimate(flops=flops, bytes_accessed=nbytes, transcendentals=0),
+    )(*scalars, *arrays)
+
+
+def exchange(value, mask, row_total):
+    return lax.ppermute(value, "row", [(i, i ^ mask) for i in range(row_total)])
+
+
+def shift(value, step, col_total):
+    return lax.ppermute(value, "col", [(i, (i + step) % col_total) for i in range(col_total)])
+
+
+class Shape:
+    def __init__(self, rows, cols, panel, cached, width):
+        self.R, self.C = rows, cols
+        self.ws, self.slots, self.B = panel.shape
+        self.W = width
+        self.RC = cached.shape[0]
+        self.CC = cached.shape[3]
+        self.Q = rows // cols
+        self.payload = self.slots * 2 * self.ws
+        self.piece = self.payload // cols
+        self.chunk = self.ws // 2
+        self.share = self.B // cols
+        self.chips = rows // 2
+        self.eight = self.ws // rows
+
+
+def pack(s, blocks, psize, csize, parent, child, top, *outs):
+    sends, payload = outs[: s.C], outs[s.C]
+    col = lax.axis_index("col")
+    lane = lax.broadcasted_iota(jnp.int32, (s.ws, s.B), 1)
+    for slot in range(s.slots):
+        base = slot * 2 * s.ws
+        for which, panel, sizes in ((0, parent, psize), (1, child, csize)):
+            live = jnp.where(lane < sizes[slot], panel[:, slot, :], 0.0)
+            payload[base + which * s.ws : base + (which + 1) * s.ws, :] = live
+    half = s.W // s.B
+    for part in range(half):
+        start = s.payload + part * s.ws
+        payload[start : start + s.ws, :] = top[:, part * s.B : (part + 1) * s.B]
+    row8 = lax.broadcasted_iota(jnp.int32, (8, s.B), 0)
+    ids = jnp.zeros((8, s.B), f32)
+    for slot in range(s.slots):
+        ids = jnp.where(row8 == slot, blocks[slot].astype(f32), ids)
+    for turn in range(s.C):
+        start = pl.multiple_of(lax.rem(turn - col + s.C, s.C) * s.piece, s.piece)
+        sends[turn][: s.piece, :] = payload[pl.ds(start, s.piece), :]
+        sends[turn][s.piece :, :] = ids
+
+
+def join(s, *refs):
+    pieces, out = refs[: s.C], refs[s.C]
+    part = lax.rem(lax.axis_index("row"), s.C)
+    for turn in range(s.C):
+        start = pl.multiple_of(lax.rem(turn - part + s.C, s.C) * s.piece, s.piece)
+        out[pl.ds(start, s.piece), :] = pieces[turn][: s.piece, :]
+    out[s.payload :, :] = pieces[0][s.piece :, :]
+
+
+def main(s, blocks, cached, pd, *refs):
+    panels, refs = refs[: s.R], refs[s.R :]
+    owned, refs = refs[: s.C], refs[s.C :]
+    shares, refs = refs[: s.C], refs[s.C :]
+    keep, send, base, top, refs = refs[0], refs[1], refs[2], refs[3], refs[4:]
+    xh, xl, ph, plo, sh, sl, total, both = refs
+    row, col = lax.axis_index("row"), lax.axis_index("col")
+    per = s.piece // s.chunk
+    for mask in range(s.R):
+        part = lax.rem(jnp.bitwise_xor(row, mask), s.C)
+        for i in range(per):
+            at = part * per + i
+            group, off = lax.div(at, 2), lax.rem(at, 2) * s.chunk
+            slot, which = lax.div(group, 2), lax.rem(group, 2)
+            for source in range(s.C):
+                start = source * s.piece + i * s.chunk
+                high, low = split(panels[mask][start : start + s.chunk, :])
+                dest = pl.multiple_of(which * s.W + source * s.ws + off, s.chunk)
+                lead = (mask // s.C) * s.slots + slot
+                xh[lead, pl.ds(dest, s.chunk), :] = high
+                xl[lead, pl.ds(dest, s.chunk), :] = low
+    for step in range(s.C):
+        source = lax.rem(col - step + s.C, s.C)
+        for slot in range(s.slots):
+            for which in range(2):
+                start = (slot * 2 + which) * s.ws
+                high, low = split(owned[step][start : start + s.ws, :])
+                dest = pl.multiple_of(which * s.W + source * s.ws, s.ws)
+                ph[slot, pl.ds(dest, s.ws), :] = high
+                plo[slot, pl.ds(dest, s.ws), :] = low
+        for part in range(s.W // s.B):
+            start = s.payload + part * s.ws
+            dest = pl.multiple_of(source * s.ws, s.ws)
+            top[pl.ds(dest, s.ws), part * s.B : (part + 1) * s.B] = owned[step][
+                start : start + s.ws, :
+            ]
+    for slot in range(s.slots):
+        p = lax.div(jnp.maximum(blocks[slot], 0), s.R)
+        for other in range(s.Q):
+            for k in range(s.slots):
+                at = s.payload + k
+                number = jnp.max(panels[other * s.C][at : at + 1, :]).astype(jnp.int32)
+                m = lax.div(jnp.maximum(number, 0), s.C)
+                start = p * (s.B * s.CC) + m
+                high, low = split(cached[pl.ds(start, s.B, stride=s.CC), :])
+                lead = (other * s.slots + k) * s.B
+                sh[slot * s.B : (slot + 1) * s.B, lead : lead + s.B] = high
+                sl[slot * s.B : (slot + 1) * s.B, lead : lead + s.B] = low
+    wide = s.Q * s.slots
+    right = tuple(jnp.concatenate([x[i] for i in range(wide)], axis=1) for x in (xh, xl))
+    total[...] = dot3((sh[...], sl[...]), right, NT)
+    for step in range(s.C):
+        target = lax.rem(col + step, s.C)
+        for slot in range(s.slots):
+            start = pl.multiple_of(slot * s.B + target * s.share, s.share)
+            shares[step][slot * s.share : (slot + 1) * s.share, :] = total[pl.ds(start, s.share), :]
+    left = tuple(jnp.concatenate([x[i] for i in range(s.slots)], axis=1) for x in (ph, plo))
+    lower = tuple(x[s.W :, :] for x in left)
+    ab = dot3(left, split(total[:, : s.W]), NN)
+    a, b = ab[: s.W], ab[s.W :]
+    d = dot3(lower, split(total[:, s.W :]), NN)
+    top_full = split(top[...])
+    u = b.T - dot3(split(a), top_full, NN)
+    parts = [owned[0][s.payload + i * s.ws : s.payload + (i + 1) * s.ws, :] for i in range(s.W // s.B)]
+    top_own = split(jnp.concatenate(parts, axis=1))
+    lead = dot3(split(pd[...]), top_full, NN)
+    base[...] = -lead
+    cd = d - dot3(split(b), top_full, NN) - dot3(top_full, split(u), TN)
+    cd = cd + dot3(top_own, split(lead * (1.0 / s.R)), TN)
+    both[0 : s.W, :] = a
+    both[s.W : 2 * s.W, :] = u
+    both[2 * s.W :, :] = cd
+    core = lax.rem(row, 2)
+    n = s.eight
+    for out, flip in ((keep, 0), (send, 1)):
+        offset = jnp.bitwise_xor(core, flip) * (s.ws // 2)
+        for chip in range(s.chips):
+            for source in range(s.C):
+                for kind in range(3):
+                    at = pl.multiple_of(kind * s.W + source * s.ws + chip * n + offset, n)
+                    to = ((chip * s.C + source) * 3 + kind) * n
+                    out[to : to + n, :] = both[pl.ds(at, n), :]
+
+
+def add_chips(s, kept, got, *outs):
+    size = s.C * 3 * s.eight
+    chip = lax.div(lax.axis_index("row"), 2)
+    for mask in range(s.chips):
+        rows = pl.ds(pl.multiple_of(jnp.bitwise_xor(chip, mask) * size, size), size)
+        outs[mask][...] = kept[rows, :] + got[rows, :]
+
+
+def add_cols(s, *refs):
+    terms, outs, total = refs[: s.chips], refs[s.chips : -1], refs[-1]
+    size = 3 * s.eight
+    col = lax.axis_index("col")
+    value = terms[0][...]
+    for term in terms[1:]:
+        value = value + term[...]
+    total[...] = value
+    for step in range(s.C):
+        rows = pl.ds(pl.multiple_of(lax.rem(col + step, s.C) * size, size), size)
+        outs[step][...] = total[rows, :]
+
+
+def add_all(s, *refs):
+    value = refs[0][...]
+    for term in refs[1:-1]:
+        value = value + term[...]
+    refs[-1][...] = value
+
+
+def finish(s, pd, cd, base, *refs):
+    parts, outs = refs[: s.R], refs[s.R :]
+    row = lax.axis_index("row")
+    n = s.eight
+    starts = (pd, base, cd)
+    for mask in range(s.R):
+        source = jnp.bitwise_xor(row, mask)
+        at = lax.rem(source, 2) * (s.ws // 2) + lax.div(source, 2) * n
+        rows = pl.ds(pl.multiple_of(at, n), n)
+        for kind in range(3):
+            outs[kind][rows, :] = starts[kind][rows, :] + parts[mask][kind * n : (kind + 1) * n, :]
+
+
+def rows_out(s, blocks, psize, csize, top, *refs):
+    terms, (parent, child) = refs[: s.C], refs[s.C :]
+    first = lax.axis_index("col") * s.share
+    value = terms[0][...]
+    for term in terms[1:]:
+        value = value + term[...]
+    index = lax.broadcasted_iota(jnp.int32, (s.share, s.W), 0) + first
+    plive = jnp.concatenate([index < psize[k] for k in range(s.slots)], axis=0)
+    clive = jnp.concatenate([index < csize[k] for k in range(s.slots)], axis=0)
+    y = jnp.where(plive, -value[:, : s.W], 0.0)
+    carried = dot3(split(y), split(top[...]), NN)
+    z = jnp.where(clive, -(value[:, s.W :] + carried), 0.0)
+    parent[...] = jnp.zeros_like(parent)
+    child[...] = jnp.zeros_like(child)
+    for slot in range(s.slots):
+        @pl.when(blocks[slot] >= 0)
+        def _():
+            at = lax.div(blocks[slot], s.R) * s.share
+            rows = pl.ds(pl.multiple_of(at, s.share), s.share)
+            parent[rows, :] = y[slot * s.share : (slot + 1) * s.share, :]
+            child[rows, :] = z[slot * s.share : (slot + 1) * s.share, :]
+
+
+def scatter_perm(s, turn):
+    return [
+        ((q * s.C + a) * s.C + c, (q * s.C + (turn - c) % s.C) * s.C + a)
+        for q in range(s.Q)
+        for a in range(s.C)
+        for c in range(s.C)
+    ]
+
+
+def fast_body(
+    cached_inverse,
+    parent_panel,
+    parent_blocks,
+    parent_sizes,
+    parent_diagonal,
+    child_panel,
+    child_top,
+    child_blocks,
+    child_sizes,
+    child_diagonal,
+):
+    R, C = lax.axis_size("row"), lax.axis_size("col")
+    B = cached_inverse.shape[2]
+    s = Shape(R, C, parent_panel, cached_inverse, parent_diagonal.shape[1])
+    cached = cached_inverse.reshape(-1, B)
+    bind = lambda kernel: functools.partial(kernel, s)
+    sent = (s.piece + 8, B)
+    whole = (s.payload + (s.W // B) * s.ws, B)
+    with jax.named_scope("pack"):
+        *sends, payload = call(
+            bind(pack),
+            (parent_blocks, parent_sizes, child_sizes),
+            (parent_panel, child_panel, child_top),
+            [sent] * C + [whole],
+        )
+    with jax.named_scope("scatter"):
+        pieces = [
+            lax.ppermute(sends[t], ("row", "col"), scatter_perm(s, t)) for t in range(C)
+        ]
+    with jax.named_scope("join"):
+        (own,) = call(bind(join), (), pieces, [(s.payload + 8, B)])
+    with jax.named_scope("panels"):
+        panels = {0: own}
+        for mask in range(2, R, 2):
+            panels[mask] = exchange(own, mask, R)
+        for mask in range(0, R, 2):
+            panels[mask + 1] = exchange(panels[mask], 1, R)
+    with jax.named_scope("owned"):
+        owned = [payload] + [shift(payload, k, C) for k in range(1, C)]
+    W, ws = s.W, s.ws
+    D = 3 * W
+    wide = s.Q * s.slots
+    live = s.slots * B
+    scratch = [
+        pltpu.VMEM((wide, 2 * W, B), bf16),
+        pltpu.VMEM((wide, 2 * W, B), bf16),
+        pltpu.VMEM((s.slots, 2 * W, B), bf16),
+        pltpu.VMEM((s.slots, 2 * W, B), bf16),
+        pltpu.VMEM((live, wide * B), bf16),
+        pltpu.VMEM((live, wide * B), bf16),
+        pltpu.VMEM((live, 2 * W), f32),
+        pltpu.VMEM((D, W), f32),
+    ]
+    outs = [(s.slots * s.share, 2 * W)] * C + [(D // 2, W), (D // 2, W), (ws, W), (W, W)]
+    with jax.named_scope("products"):
+        out = call(
+            bind(main),
+            (parent_blocks,),
+            (cached, parent_diagonal, *[panels[m] for m in range(R)], *owned),
+            outs,
+            scratch,
+            flops=2 * live * wide * B * 2 * W * 3,
+        )
+    shares, (keep, send, base, top) = out[:C], out[C:]
+    with jax.named_scope("sum_core"):
+        got = exchange(send, 1, R)
+    with jax.named_scope("sum_shares"):
+        rows = [shares[0]] + [shift(shares[k], k, C) for k in range(1, C)]
+    with jax.named_scope("sum_chips"):
+        mine = call(bind(add_chips), (), (keep, got), [(C * 3 * s.eight, W)] * s.chips)
+        mine = [mine[0]] + [exchange(mine[m], 2 * m, R) for m in range(1, s.chips)]
+    with jax.named_scope("sum_cols"):
+        scr = [pltpu.VMEM((C * 3 * s.eight, W), f32)]
+        cols = call(bind(add_cols), (), mine, [(3 * s.eight, W)] * C, scr)
+        cols = [cols[0]] + [shift(cols[k], k, C) for k in range(1, C)]
+    with jax.named_scope("spread"):
+        (done,) = call(bind(add_all), (), cols, [(3 * s.eight, W)])
+        parts = {0: done}
+        for mask in range(2, R, 2):
+            parts[mask] = exchange(done, mask, R)
+        for mask in range(0, R, 2):
+            parts[mask + 1] = exchange(parts[mask], 1, R)
+    with jax.named_scope("rows_out"):
+        parent_rows, child_rows = call(
+            bind(rows_out),
+            (parent_blocks, parent_sizes, child_sizes),
+            (top, *rows),
+            [(s.RC * s.share, W)] * 2,
+        )
+    with jax.named_scope("finish"):
+        parent_diag, child_upper, child_diag = call(
+            bind(finish),
+            (),
+            (parent_diagonal, child_diagonal, base, *[parts[m] for m in range(R)]),
+            [(ws, W)] * 3,
+        )
+    shape = (s.RC, 1, s.share, W)
+    return (
+        parent_rows.reshape(shape),
+        parent_diag,
+        child_rows.reshape(shape),
+        child_upper,
+        child_diag,
+    )
+
 
 highest = lax.Precision.HIGHEST
 
@@ -164,6 +528,27 @@
     )
 
 
+def fits(rows, cols, panel, cached, width):
+    s = Shape(rows, cols, panel, cached, width)
+    return (
+        rows & (rows - 1) == 0
+        and rows % cols == 0
+        and s.payload % cols == 0
+        and s.chunk % 16 == 0
+        and s.piece % s.chunk == 0
+        and s.share % 16 == 0
+        and s.ws % rows == 0
+        and s.eight % 8 == 0
+        and width % s.B == 0
+    )
+
+
+def chosen(*args):
+    sizes = lax.axis_size("row"), lax.axis_size("col")
+    ok = fits(*sizes, args[1], args[0], args[4].shape[1])
+    return (fast_body if ok else body)(*args)
+
+
 def solution(mesh):
     in_specs = (
         P(None, "row", None, None, "col", None),
@@ -184,4 +569,4 @@
         P("col", None),
         P("col", None),
     )
-    return jax.shard_map(body, mesh=mesh, in_specs=in_specs, out_specs=out_specs, check_vma=False)
+    return jax.shard_map(chosen, mesh=mesh, in_specs=in_specs, out_specs=out_specs, check_vma=False)

time: 342 us -> 92.8 us (0.27)
  waiting for transfers between devices: 217 us -> 43.7 us
  blocking collectives: 70.4 us -> 0 us
  starting transfers between devices: 0.12 us -> 32.4 us
  matrix products: 16.5 us -> 0 us
  between operations: 14.7 us -> 0.83 us
  other arithmetic: 11.2 us -> 0 us
  Pallas kernels: 0 us -> 8.35 us
  local copies, waits for them, and re-layouts: 10.9 us -> 6.24 us
    psum x2 -> x0, waiting for transfers between devices: 184 us -> none  [the longest x1 130 us: diagonal_sum(): entire = lax.psum(partial_rows(0, panel_width), ('row', 'col'))]
    all_gather x4 -> x0, blocking collectives: 62.4 us -> none  [the longest x1 16.4 us: body(): wide_parent = lax.all_gather(parent_panel, 'col', axis=0, tiled=True)]
    ppermute x0 -> x31, waiting for transfers between devices: none -> 43.7 us  [the longest x9 24.7 us: shift(): lax.ppermute(value, 'col', [(i, (i + step) % col_total) for i in range(co...]
    unnamed x4 -> x0, waiting for transfers between devices: 32.9 us -> none
    ppermute x0 -> x31, starting transfers between devices: none -> 32.4 us  [the longest x9 11.6 us: shift(): lax.ppermute(value, 'col', [(i, (i + step) % col_total) for i in range(co...]
    dot_general x15 -> x0, matrix products: 16.5 us -> none  [the longest x4 4.6 us: add_columns(): jnp.einsum('ck,wky->cwy', onehot, widened, precision=highest)]
    pallas_call x0 -> x8, Pallas kernels: none -> 8.35 us  [call(): pl.pallas_call(kernel, out_shape=[jax.ShapeDtypeStruct(o, f32) for o in o...]
    psum x1 -> x0, blocking collectives: 8.04 us -> none  [from_root(): return lax.psum(kept, axis)]
  transfers between devices with their start and end apart: 3 -> 31, of which waited for: 3 -> 14; matrix products, arithmetic and copies ran while one was open for 1% -> 0% of each run, Pallas kernels for 0% -> 2%
where the time goes in v1:
time: 92.8 us; the launch traced here: 91.5 us
  waiting for transfers between devices  43.7 us (47%)
  starting transfers between devices  32.4 us (35%)
  Pallas kernels  8.35 us (9%)
  local copies, waits for them, and re-layouts  6.24 us (7%)
    ppermute x9, waiting for transfers between devices, shift(): lax.ppermute(value, 'col', [(i, (i + step) % col_total) for i in range(co...  24.7 us
    ppermute x18, waiting for transfers between devices, exchange(): return lax.ppermute(value, 'row', [(i, i ^ mask) for i in range(row_total)])  12.4 us
    ppermute x9, starting transfers between devices, shift(): lax.ppermute(value, 'col', [(i, (i + step) % col_total) for i in range(co...  11.6 us
    ppermute x4, starting transfers between devices, fast_body(): lax.ppermute(sends[t], ('row', 'col'), scatter_perm(s, t))  10.5 us
    ppermute x18, starting transfers between devices, exchange(): return lax.ppermute(value, 'row', [(i, i ^ mask) for i in range(row_total)])  10.3 us
    pallas_call x8, Pallas kernels, call(): pl.pallas_call(kernel, out_shape=[jax.ShapeDtypeStruct(o, f32) for o in o...  8.35 us
    ppermute x4, waiting for transfers between devices, fast_body(): lax.ppermute(sends[t], ('row', 'col'), scatter_perm(s, t))  6.56 us
    unnamed x24, local copies, waits for them, and re-layouts  6.24 us
  transfers between devices with their start and end apart: 31, of which 14 were waited for; matrix products, arithmetic and copies ran while one was open for 0% of the time, Pallas kernels for 2%

profile of v1, /device:TPU:0, one launch (start us, length us, event | category | flops | bytes accessed | tf_op | source)
XLA Modules:
  0.0 91.5 jit_solution(5420982520295384265)
XLA Ops:
  0.6 1.0 %copy.14.parent = f32[64,3,128]{2,1,0:T(4,128)S(1)} copy(f32[64,3,128]{2,0,1:T(8,128)} %param.11) | data formatting | bytes 196608 | tf_op args[1]
  1.6 1.0 %copy.15.child = f32[64,3,128]{2,1,0:T(4,128)S(1)} copy(f32[64,3,128]{2,0,1:T(8,128)} %param.15) | data formatting | bytes 196608 | tf_op args[5]
  2.6 0.8 copy-done.2
  3.4 0.7 copy-done.4
  4.1 0.7 copy-done.7
  4.7 0.7 copy-done.9
  5.4 0.7 pack.1
  6.1 0.7 collective-permute-start
  6.7 4.4 %collective-permute-start.1 = (f32[104,128]{1,0:T(8,128)S(1)}, f32[104,128]{1,0:T(8,128)S(1)}, u32[]{:S(2)}, u32[]{:S(2)}) collective-permute-start(f32[104,128]{1,0:T(8,128)S(1)} %get-tuple-element.32), channel_id=1, source_target_pairs={{0,4},{1,0},{2,12},{3,8},{4,5},{5,1},{6,13},{7,9},{8,6},{9,2},{10,... | collective-permute-start | bytes 159752 | tf_op jit(solution)/shard_map/scatter/ppermute | solution.py:291
  11.2 5.4 %collective-permute-start.2 = (f32[104,128]{1,0:T(8,128)S(1)}, f32[104,128]{1,0:T(8,128)S(1)}, u32[]{:S(2)}, u32[]{:S(2)}) collective-permute-start(f32[104,128]{1,0:T(8,128)S(1)} %get-tuple-element.33), channel_id=1, source_target_pairs={{0,8},{1,4},{2,0},{3,12},{4,9},{5,5},{6,1},{7,13},{8,10},{9,6},{10... | collective-permute-start | bytes 159752 | tf_op jit(solution)/shard_map/scatter/ppermute | solution.py:291
  16.6 6.6 %collective-permute-done.2.refs_2_ = f32[104,128]{1,0:T(8,128)S(1)} collective-permute-done((f32[104,128]{1,0:T(8,128)S(1)}, f32[104,128]{1,0:T(8,128)S(1)}, u32[]{:S(2)}, u32[]{:S(2)}) %collective-permute-start.2) | collective-permute-done | bytes 53280 | tf_op jit(solution)/shard_map/scatter/ppermute | solution.py:291
  23.2 0.2 collective-permute-start.9
  23.5 1.4 %collective-permute-start.7 = (f32[392,128]{1,0:T(8,128)S(1)}, f32[392,128]{1,0:T(8,128)S(1)}, u32[]{:S(2)}, u32[]{:S(2)}) collective-permute-start(f32[392,128]{1,0:T(8,128)S(1)} %join.1.refs_0_), channel_id=1, source_target_pairs={{0,16},{4,20},{8,24},{12,28},{16,0},{20,4},{24,8},{28,12},{1,17},{... | collective-permute-start | bytes 602120 | tf_op jit(solution)/shard_map/panels/ppermute | solution.py:51
  24.9 2.1 %collective-permute-start.13 = (f32[512,128]{1,0:T(8,128)S(1)}, f32[512,128]{1,0:T(8,128)S(1)}, u32[]{:S(2)}, u32[]{:S(2)}) collective-permute-start(f32[512,128]{1,0:T(8,128)S(1)} %get-tuple-element.35.refs_8_), channel_id=1, source_target_pairs={{0,3},{1,0},{2,1},{3,2},{4,7},{5,4},{6,5},{7,6},{8,11},{9,8},{10,9... | collective-permute-start | bytes 786440 | tf_op jit(solution)/shard_map/owned/ppermute | solution.py:55
  27.1 1.3 %collective-permute-start.5 = (f32[392,128]{1,0:T(8,128)S(1)}, f32[392,128]{1,0:T(8,128)S(1)}, u32[]{:S(2)}, u32[]{:S(2)}) collective-permute-start(f32[392,128]{1,0:T(8,128)S(1)} %join.1.refs_0_), channel_id=1, source_target_pairs={{0,8},{4,12},{8,0},{12,4},{16,24},{20,28},{24,16},{28,20},{1,9},{5... | collective-permute-start | bytes 602120 | tf_op jit(solution)/shard_map/panels/ppermute | solution.py:51
  28.4 3.7 %collective-permute-done.9.refs_6_ = f32[392,128]{1,0:T(8,128)S(1)} collective-permute-done((f32[392,128]{1,0:T(8,128)S(1)}, f32[392,128]{1,0:T(8,128)S(1)}, u32[]{:S(2)}, u32[]{:S(2)}) %collective-permute-start.9) | collective-permute-done | bytes 200736 | tf_op jit(solution)/shard_map/panels/ppermute | solution.py:51
  32.1 0.8 collective-permute-start.12
  32.9 2.1 %collective-permute-done.7.refs_4_ = f32[392,128]{1,0:T(8,128)S(1)} collective-permute-done((f32[392,128]{1,0:T(8,128)S(1)}, f32[392,128]{1,0:T(8,128)S(1)}, u32[]{:S(2)}, u32[]{:S(2)}) %collective-permute-start.7) | collective-permute-done | bytes 200736 | tf_op jit(solution)/shard_map/panels/ppermute | solution.py:51
  35.0 0.9 collective-permute-done.5.refs_2_
  35.9 0.5 collective-permute-start.8
  36.5 14.3 %collective-permute-done.12.refs_10_ = f32[512,128]{1,0:T(8,128)S(1)} collective-permute-done((f32[512,128]{1,0:T(8,128)S(1)}, f32[512,128]{1,0:T(8,128)S(1)}, u32[]{:S(2)}, u32[]{:S(2)}) %collective-permute-start.12) | collective-permute-done | bytes 262176 | tf_op jit(solution)/shard_map/owned/ppermute | solution.py:55
  50.8 0.8 copy-done
  51.6 0.7 copy-done.5
  52.3 5.3 %products.1 = (f32[96,512]{1,0:T(8,128)S(1)}, f32[96,512]{1,0:T(8,128)S(1)}, f32[96,512]{1,0:T(8,128)S(1)}, f32[96,512]{1,0:T(8,128)S(1)}, f32[384,256]{1,0:T(8,...) custom-call(s32[3]{0:T(128)S(1)} %copy-done.5, f32[4096,128]{1,0:T(8,128)} %bitcast.7, ...), custom_call_target="tpu_custom_call" | custom-call | flops 905969664 | bytes 6717440 | tf_op jit(solution)/shard_map/products/pallas_call | solution.py:39
  57.6 0.1 collective-permute-start.17
  57.7 1.7 %collective-permute-done.17.got = f32[384,256]{1,0:T(8,128)S(1)} collective-permute-done((f32[384,256]{1,0:T(8,128)S(1)}, f32[384,256]{1,0:T(8,128)S(1)}, u32[]{:S(2)}, u32[]{:S(2)}) %collective-permute-start.17) | collective-permute-done | bytes 393248 | tf_op jit(solution)/shard_map/sum_core/ppermute | solution.py:51
  59.5 0.9 collective-permute-start.18
  60.4 0.3 collective-permute-start.14
  60.6 1.9 %collective-permute-start.15 = (f32[96,512]{1,0:T(8,128)S(1)}, f32[96,512]{1,0:T(8,128)S(1)}, u32[]{:S(2)}, u32[]{:S(2)}) collective-permute-start(f32[96,512]{1,0:T(8,128)S(1)} %get-tuple-element.39), channel_id=1, source_target_pairs={{0,2},{1,3},{2,0},{3,1},{4,6},{5,7},{6,4},{7,5},{8,10},{9,11},{10,... | collective-permute-start | bytes 589832 | tf_op jit(solution)/shard_map/sum_shares/ppermute | solution.py:55
  62.6 1.5 %collective-permute-start.19 = (f32[96,256]{1,0:T(8,128)S(1)}, f32[96,256]{1,0:T(8,128)S(1)}, u32[]{:S(2)}, u32[]{:S(2)}) collective-permute-start(f32[96,256]{1,0:T(8,128)S(1)} %get-tuple-element.47), channel_id=1, source_target_pairs={{0,16},{4,20},{8,24},{12,28},{16,0},{20,4},{24,8},{28,12},{1,17},{... | collective-permute-start | bytes 294920 | tf_op jit(solution)/shard_map/sum_chips/ppermute | solution.py:51
  64.1 0.4 collective-permute-start.20
  64.4 2.9 %collective-permute-start.16 = (f32[96,512]{1,0:T(8,128)S(1)}, f32[96,512]{1,0:T(8,128)S(1)}, u32[]{:S(2)}, u32[]{:S(2)}) collective-permute-start(f32[96,512]{1,0:T(8,128)S(1)} %get-tuple-element.40), channel_id=1, source_target_pairs={{0,3},{1,0},{2,1},{3,2},{4,7},{5,4},{6,5},{7,6},{8,11},{9,8},{10,9... | collective-permute-start | bytes 589832 | tf_op jit(solution)/shard_map/sum_shares/ppermute | solution.py:55
  67.4 0.9 collective-permute-done.19.refs_2_
  68.2 1.4 %collective-permute-done.20.refs_3_ = f32[96,256]{1,0:T(8,128)S(1)} collective-permute-done((f32[96,256]{1,0:T(8,128)S(1)}, f32[96,256]{1,0:T(8,128)S(1)}, u32[]{:S(2)}, u32[]{:S(2)}) %collective-permute-start.20) | collective-permute-done | bytes 98336 | tf_op jit(solution)/shard_map/sum_chips/ppermute | solution.py:51
  69.6 1.9 %collective-permute-start.21 = (f32[24,256]{1,0:T(8,128)S(1)}, f32[24,256]{1,0:T(8,128)S(1)}, u32[]{:S(2)}, u32[]{:S(2)}) collective-permute-start(f32[24,256]{1,0:T(8,128)S(1)} %get-tuple-element.50), channel_id=1, source_target_pairs={{0,1},{1,2},{2,3},{3,0},{4,5},{5,6},{6,7},{7,4},{8,9},{9,10},{10,1... | collective-permute-start | bytes 73736 | tf_op jit(solution)/shard_map/sum_cols/ppermute | solution.py:55
  71.5 1.7 %collective-permute-start.22 = (f32[24,256]{1,0:T(8,128)S(1)}, f32[24,256]{1,0:T(8,128)S(1)}, u32[]{:S(2)}, u32[]{:S(2)}) collective-permute-start(f32[24,256]{1,0:T(8,128)S(1)} %get-tuple-element.51), channel_id=1, source_target_pairs={{0,2},{1,3},{2,0},{3,1},{4,6},{5,7},{6,4},{7,5},{8,10},{9,11},{10,... | collective-permute-start | bytes 73736 | tf_op jit(solution)/shard_map/sum_cols/ppermute | solution.py:55
  73.2 5.0 %collective-permute-done.21.refs_1_ = f32[24,256]{1,0:T(8,128)S(1)} collective-permute-done((f32[24,256]{1,0:T(8,128)S(1)}, f32[24,256]{1,0:T(8,128)S(1)}, u32[]{:S(2)}, u32[]{:S(2)}) %collective-permute-start.21) | collective-permute-done | bytes 24608 | tf_op jit(solution)/shard_map/sum_cols/ppermute | solution.py:55
  78.2 4.0 %collective-permute-done.22.refs_2_ = f32[24,256]{1,0:T(8,128)S(1)} collective-permute-done((f32[24,256]{1,0:T(8,128)S(1)}, f32[24,256]{1,0:T(8,128)S(1)}, u32[]{:S(2)}, u32[]{:S(2)}) %collective-permute-start.22) | collective-permute-done | bytes 24608 | tf_op jit(solution)/shard_map/sum_cols/ppermute | solution.py:55
  82.2 1.4 %collective-permute-done.23.refs_3_ = f32[24,256]{1,0:T(8,128)S(1)} collective-permute-done((f32[24,256]{1,0:T(8,128)S(1)}, f32[24,256]{1,0:T(8,128)S(1)}, u32[]{:S(2)}, u32[]{:S(2)}) %collective-permute-start.23) | collective-permute-done | bytes 24608 | tf_op jit(solution)/shard_map/sum_cols/ppermute | solution.py:55
  83.6 1.1 %collective-permute-start.29 = (f32[24,256]{1,0:T(8,128)S(1)}, f32[24,256]{1,0:T(8,128)S(1)}, u32[]{:S(2)}, u32[]{:S(2)}) collective-permute-start(f32[24,256]{1,0:T(8,128)S(1)} %spread.1.refs_0_), channel_id=1, source_target_pairs={{0,24},{4,28},{8,16},{12,20},{16,8},{20,12},{24,0},{28,4},{1,25},{... | collective-permute-start | bytes 73736 | tf_op jit(solution)/shard_map/spread/ppermute | solution.py:51
  84.7 0.6 collective-permute-start.27
  85.3 1.8 %collective-permute-start.25 = (f32[24,256]{1,0:T(8,128)S(1)}, f32[24,256]{1,0:T(8,128)S(1)}, u32[]{:S(2)}, u32[]{:S(2)}) collective-permute-start(f32[24,256]{1,0:T(8,128)S(1)} %spread.1.refs_0_), channel_id=1, source_target_pairs={{0,8},{4,12},{8,0},{12,4},{16,24},{20,28},{24,16},{28,20},{1,9},{5... | collective-permute-start | bytes 73736 | tf_op jit(solution)/shard_map/spread/ppermute | solution.py:51
  87.2 1.2 %collective-permute-done.29.refs_6_ = f32[24,256]{1,0:T(8,128)S(1)} collective-permute-done((f32[24,256]{1,0:T(8,128)S(1)}, f32[24,256]{1,0:T(8,128)S(1)}, u32[]{:S(2)}, u32[]{:S(2)}) %collective-permute-start.29) | collective-permute-done | bytes 24608 | tf_op jit(solution)/shard_map/spread/ppermute | solution.py:51
  88.4 0.3 collective-permute-done.27.refs_4_
  88.7 0.3 collective-permute-start.28
  88.9 0.2 collective-permute-done.25.refs_2_
  89.2 1.5 %rows_out.1 = (f32[128,256]{1,0:T(8,128)}, f32[128,256]{1,0:T(8,128)}) custom-call(s32[3]{0:T(128)S(1)} %copy-done.6, s32[3]{0:T(128)S(1)} %copy-done.8, s32[3]{0:T(128)S(1)} %copy-done.10, f32[256,256]{1,0:T(8,128)S(1)} %get-tuple-element.36.top, f32[96,512]{1,0:T(8,128)S(1)} %get-tuple-element.37.refs_0_, f32[96,512]{1,0:T(8,128)S(1)} %collective-permute-done.14.refs_1_, ...), custom_call_target="tpu_custom_call" | custom-call | bytes 1310720 | tf_op jit(solution)/shard_map/rows_out/pallas_call | solution.py:39
  90.8 0.7 finish.1
  (46 shorter events, 0.4 us)
Async XLA Ops:
  2.6 0.8 copy-start.2
  3.4 0.7 copy-start.4
  4.1 0.7 copy-start.7
  4.7 0.7 copy-start.9
  6.1 10.6 %collective-permute-start = (f32[104,128]{1,0:T(8,128)S(1)}, f32[104,128]{1,0:T(8,128)S(1)}, u32[]{:S(2)}, u32[]{:S(2)}) collective-permute-start(f32[104,128]{1,0:T(8,128)S(1)} %get-tuple-element.31), channel_id=1, source_target_pairs={{0,0},{1,12},{2,8},{3,4},{4,1},{5,13},{6,9},{7,5},{8,2},{9,14},{10... | collective-permute-start | bytes 159752 | tf_op jit(solution)/shard_map/scatter/ppermute | solution.py:291
  6.7 9.9 %collective-permute-start.1 = (f32[104,128]{1,0:T(8,128)S(1)}, f32[104,128]{1,0:T(8,128)S(1)}, u32[]{:S(2)}, u32[]{:S(2)}) collective-permute-start(f32[104,128]{1,0:T(8,128)S(1)} %get-tuple-element.32), channel_id=1, source_target_pairs={{0,4},{1,0},{2,12},{3,8},{4,5},{5,1},{6,13},{7,9},{8,6},{9,2},{10,... | collective-permute-start | bytes 159752 | tf_op jit(solution)/shard_map/scatter/ppermute | solution.py:291
  11.2 12.0 %collective-permute-start.2 = (f32[104,128]{1,0:T(8,128)S(1)}, f32[104,128]{1,0:T(8,128)S(1)}, u32[]{:S(2)}, u32[]{:S(2)}) collective-permute-start(f32[104,128]{1,0:T(8,128)S(1)} %get-tuple-element.33), channel_id=1, source_target_pairs={{0,8},{1,4},{2,0},{3,12},{4,9},{5,5},{6,1},{7,13},{8,10},{9,6},{10... | collective-permute-start | bytes 159752 | tf_op jit(solution)/shard_map/scatter/ppermute | solution.py:291
  16.5 6.7 %collective-permute-start.3 = (f32[104,128]{1,0:T(8,128)S(1)}, f32[104,128]{1,0:T(8,128)S(1)}, u32[]{:S(2)}, u32[]{:S(2)}) collective-permute-start(f32[104,128]{1,0:T(8,128)S(1)} %get-tuple-element.34), channel_id=1, source_target_pairs={{0,12},{1,8},{2,4},{3,0},{4,13},{5,9},{6,5},{7,1},{8,14},{9,10},{1... | collective-permute-start | bytes 159752 | tf_op jit(solution)/shard_map/scatter/ppermute | solution.py:291
  23.2 8.8 %collective-permute-start.9 = (f32[392,128]{1,0:T(8,128)S(1)}, f32[392,128]{1,0:T(8,128)S(1)}, u32[]{:S(2)}, u32[]{:S(2)}) collective-permute-start(f32[392,128]{1,0:T(8,128)S(1)} %join.1.refs_0_), channel_id=1, source_target_pairs={{0,24},{4,28},{8,16},{12,20},{16,8},{20,12},{24,0},{28,4},{1,25},{... | collective-permute-start | bytes 602120 | tf_op jit(solution)/shard_map/panels/ppermute | solution.py:51
  23.5 11.5 %collective-permute-start.7 = (f32[392,128]{1,0:T(8,128)S(1)}, f32[392,128]{1,0:T(8,128)S(1)}, u32[]{:S(2)}, u32[]{:S(2)}) collective-permute-start(f32[392,128]{1,0:T(8,128)S(1)} %join.1.refs_0_), channel_id=1, source_target_pairs={{0,16},{4,20},{8,24},{12,28},{16,0},{20,4},{24,8},{28,12},{1,17},{... | collective-permute-start | bytes 602120 | tf_op jit(solution)/shard_map/panels/ppermute | solution.py:51
  24.9 11.5 %collective-permute-start.13 = (f32[512,128]{1,0:T(8,128)S(1)}, f32[512,128]{1,0:T(8,128)S(1)}, u32[]{:S(2)}, u32[]{:S(2)}) collective-permute-start(f32[512,128]{1,0:T(8,128)S(1)} %get-tuple-element.35.refs_8_), channel_id=1, source_target_pairs={{0,3},{1,0},{2,1},{3,2},{4,7},{5,4},{6,5},{7,6},{8,11},{9,8},{10,9... | collective-permute-start | bytes 786440 | tf_op jit(solution)/shard_map/owned/ppermute | solution.py:55
  27.1 8.8 %collective-permute-start.5 = (f32[392,128]{1,0:T(8,128)S(1)}, f32[392,128]{1,0:T(8,128)S(1)}, u32[]{:S(2)}, u32[]{:S(2)}) collective-permute-start(f32[392,128]{1,0:T(8,128)S(1)} %join.1.refs_0_), channel_id=1, source_target_pairs={{0,8},{4,12},{8,0},{12,4},{16,24},{20,28},{24,16},{28,20},{1,9},{5... | collective-permute-start | bytes 602120 | tf_op jit(solution)/shard_map/panels/ppermute | solution.py:51
  28.4 7.5 %collective-permute-start.4 = (f32[392,128]{1,0:T(8,128)S(1)}, f32[392,128]{1,0:T(8,128)S(1)}, u32[]{:S(2)}, u32[]{:S(2)}) collective-permute-start(f32[392,128]{1,0:T(8,128)S(1)} %join.1.refs_0_), channel_id=1, source_target_pairs={{0,4},{4,0},{8,12},{12,8},{16,20},{20,16},{24,28},{28,24},{1,5},{5... | collective-permute-start | bytes 602120 | tf_op jit(solution)/shard_map/panels/ppermute | solution.py:51
  32.1 18.7 %collective-permute-start.12 = (f32[512,128]{1,0:T(8,128)S(1)}, f32[512,128]{1,0:T(8,128)S(1)}, u32[]{:S(2)}, u32[]{:S(2)}) collective-permute-start(f32[512,128]{1,0:T(8,128)S(1)} %get-tuple-element.35.refs_8_), channel_id=1, source_target_pairs={{0,2},{1,3},{2,0},{3,1},{4,6},{5,7},{6,4},{7,5},{8,10},{9,11},{10,... | collective-permute-start | bytes 786440 | tf_op jit(solution)/shard_map/owned/ppermute | solution.py:55
  35.0 15.8 %collective-permute-start.11 = (f32[512,128]{1,0:T(8,128)S(1)}, f32[512,128]{1,0:T(8,128)S(1)}, u32[]{:S(2)}, u32[]{:S(2)}) collective-permute-start(f32[512,128]{1,0:T(8,128)S(1)} %get-tuple-element.35.refs_8_), channel_id=1, source_target_pairs={{0,1},{1,2},{2,3},{3,0},{4,5},{5,6},{6,7},{7,4},{8,9},{9,10},{10,1... | collective-permute-start | bytes 786440 | tf_op jit(solution)/shard_map/owned/ppermute | solution.py:55
  35.9 14.9 %collective-permute-start.10 = (f32[392,128]{1,0:T(8,128)S(1)}, f32[392,128]{1,0:T(8,128)S(1)}, u32[]{:S(2)}, u32[]{:S(2)}) collective-permute-start(f32[392,128]{1,0:T(8,128)S(1)} %collective-permute-done.9.refs_6_), channel_id=1, source_target_pairs={{0,4},{4,0},{8,12},{12,8},{16,20},{20,16},{24,28},{28,24},{1,5},{5... | collective-permute-start | bytes 602120 | tf_op jit(solution)/shard_map/panels/ppermute | solution.py:51
  35.9 14.9 %collective-permute-start.8 = (f32[392,128]{1,0:T(8,128)S(1)}, f32[392,128]{1,0:T(8,128)S(1)}, u32[]{:S(2)}, u32[]{:S(2)}) collective-permute-start(f32[392,128]{1,0:T(8,128)S(1)} %collective-permute-done.7.refs_4_), channel_id=1, source_target_pairs={{0,4},{4,0},{8,12},{12,8},{16,20},{20,16},{24,28},{28,24},{1,5},{5... | collective-permute-start | bytes 602120 | tf_op jit(solution)/shard_map/panels/ppermute | solution.py:51
  36.4 14.4 %collective-permute-start.6 = (f32[392,128]{1,0:T(8,128)S(1)}, f32[392,128]{1,0:T(8,128)S(1)}, u32[]{:S(2)}, u32[]{:S(2)}) collective-permute-start(f32[392,128]{1,0:T(8,128)S(1)} %collective-permute-done.5.refs_2_), channel_id=1, source_target_pairs={{0,4},{4,0},{8,12},{12,8},{16,20},{20,16},{24,28},{28,24},{1,5},{5... | collective-permute-start | bytes 602120 | tf_op jit(solution)/shard_map/panels/ppermute | solution.py:51
  50.8 0.8 copy-start
  51.6 0.7 copy-start.5
  52.3 36.9 %copy-start.6 = (s32[3]{0:T(128)S(1)}, s32[3]{0:T(128)}, u32[]{:S(2)}) copy-start(s32[3]{0:T(128)} %blocks.5) | copy-start | bytes 40
  52.3 36.9 %copy-start.8 = (s32[3]{0:T(128)S(1)}, s32[3]{0:T(128)}, u32[]{:S(2)}) copy-start(s32[3]{0:T(128)} %psize.3) | copy-start | bytes 40
  52.3 36.9 %copy-start.10 = (s32[3]{0:T(128)S(1)}, s32[3]{0:T(128)}, u32[]{:S(2)}) copy-start(s32[3]{0:T(128)} %csize.3) | copy-start | bytes 40
  57.6 33.1 %copy-start.1 = (f32[64,256]{1,0:T(8,128)S(1)}, f32[64,256]{1,0:T(8,128)}, u32[]{:S(2)}) copy-start(f32[64,256]{1,0:T(8,128)} %pd.3) | copy-start | bytes 196612
  57.6 33.1 %copy-start.3 = (f32[64,256]{1,0:T(8,128)S(1)}, f32[64,256]{1,0:T(8,128)}, u32[]{:S(2)}) copy-start(f32[64,256]{1,0:T(8,128)} %cd.1) | copy-start | bytes 196612
  57.6 1.8 %collective-permute-start.17 = (f32[384,256]{1,0:T(8,128)S(1)}, f32[384,256]{1,0:T(8,128)S(1)}, u32[]{:S(2)}, u32[]{:S(2)}) collective-permute-start(f32[384,256]{1,0:T(8,128)S(1)} %get-tuple-element.44), channel_id=1, source_target_pairs={{0,4},{4,0},{8,12},{12,8},{16,20},{20,16},{24,28},{28,24},{1,5},{5... | collective-permute-start | bytes 1179656 | tf_op jit(solution)/shard_map/sum_core/ppermute | solution.py:51
  59.5 5.0 %collective-permute-start.18 = (f32[96,256]{1,0:T(8,128)S(1)}, f32[96,256]{1,0:T(8,128)S(1)}, u32[]{:S(2)}, u32[]{:S(2)}) collective-permute-start(f32[96,256]{1,0:T(8,128)S(1)} %get-tuple-element.46), channel_id=1, source_target_pairs={{0,8},{4,12},{8,0},{12,4},{16,24},{20,28},{24,16},{28,20},{1,9},{5... | collective-permute-start | bytes 294920 | tf_op jit(solution)/shard_map/sum_chips/ppermute | solution.py:51
  60.4 24.9 %collective-permute-start.14 = (f32[96,512]{1,0:T(8,128)S(1)}, f32[96,512]{1,0:T(8,128)S(1)}, u32[]{:S(2)}, u32[]{:S(2)}) collective-permute-start(f32[96,512]{1,0:T(8,128)S(1)} %get-tuple-element.38), channel_id=1, source_target_pairs={{0,1},{1,2},{2,3},{3,0},{4,5},{5,6},{6,7},{7,4},{8,9},{9,10},{10,1... | collective-permute-start | bytes 589832 | tf_op jit(solution)/shard_map/sum_shares/ppermute | solution.py:55
  60.6 26.5 %collective-permute-start.15 = (f32[96,512]{1,0:T(8,128)S(1)}, f32[96,512]{1,0:T(8,128)S(1)}, u32[]{:S(2)}, u32[]{:S(2)}) collective-permute-start(f32[96,512]{1,0:T(8,128)S(1)} %get-tuple-element.39), channel_id=1, source_target_pairs={{0,2},{1,3},{2,0},{3,1},{4,6},{5,7},{6,4},{7,5},{8,10},{9,11},{10,... | collective-permute-start | bytes 589832 | tf_op jit(solution)/shard_map/sum_shares/ppermute | solution.py:55
  62.6 5.7 %collective-permute-start.19 = (f32[96,256]{1,0:T(8,128)S(1)}, f32[96,256]{1,0:T(8,128)S(1)}, u32[]{:S(2)}, u32[]{:S(2)}) collective-permute-start(f32[96,256]{1,0:T(8,128)S(1)} %get-tuple-element.47), channel_id=1, source_target_pairs={{0,16},{4,20},{8,24},{12,28},{16,0},{20,4},{24,8},{28,12},{1,17},{... | collective-permute-start | bytes 294920 | tf_op jit(solution)/shard_map/sum_chips/ppermute | solution.py:51
  64.1 5.5 %collective-permute-start.20 = (f32[96,256]{1,0:T(8,128)S(1)}, f32[96,256]{1,0:T(8,128)S(1)}, u32[]{:S(2)}, u32[]{:S(2)}) collective-permute-start(f32[96,256]{1,0:T(8,128)S(1)} %get-tuple-element.48), channel_id=1, source_target_pairs={{0,24},{4,28},{8,16},{12,20},{16,8},{20,12},{24,0},{28,4},{1,25},{... | collective-permute-start | bytes 294920 | tf_op jit(solution)/shard_map/sum_chips/ppermute | solution.py:51
  64.4 24.7 %collective-permute-start.16 = (f32[96,512]{1,0:T(8,128)S(1)}, f32[96,512]{1,0:T(8,128)S(1)}, u32[]{:S(2)}, u32[]{:S(2)}) collective-permute-start(f32[96,512]{1,0:T(8,128)S(1)} %get-tuple-element.40), channel_id=1, source_target_pairs={{0,3},{1,0},{2,1},{3,2},{4,7},{5,4},{6,5},{7,6},{8,11},{9,8},{10,9... | collective-permute-start | bytes 589832 | tf_op jit(solution)/shard_map/sum_shares/ppermute | solution.py:55
  69.6 8.6 %collective-permute-start.21 = (f32[24,256]{1,0:T(8,128)S(1)}, f32[24,256]{1,0:T(8,128)S(1)}, u32[]{:S(2)}, u32[]{:S(2)}) collective-permute-start(f32[24,256]{1,0:T(8,128)S(1)} %get-tuple-element.50), channel_id=1, source_target_pairs={{0,1},{1,2},{2,3},{3,0},{4,5},{5,6},{6,7},{7,4},{8,9},{9,10},{10,1... | collective-permute-start | bytes 73736 | tf_op jit(solution)/shard_map/sum_cols/ppermute | solution.py:55
  71.5 10.6 %collective-permute-start.22 = (f32[24,256]{1,0:T(8,128)S(1)}, f32[24,256]{1,0:T(8,128)S(1)}, u32[]{:S(2)}, u32[]{:S(2)}) collective-permute-start(f32[24,256]{1,0:T(8,128)S(1)} %get-tuple-element.51), channel_id=1, source_target_pairs={{0,2},{1,3},{2,0},{3,1},{4,6},{5,7},{6,4},{7,5},{8,10},{9,11},{10,... | collective-permute-start | bytes 73736 | tf_op jit(solution)/shard_map/sum_cols/ppermute | solution.py:55
  78.2 5.4 %collective-permute-start.23 = (f32[24,256]{1,0:T(8,128)S(1)}, f32[24,256]{1,0:T(8,128)S(1)}, u32[]{:S(2)}, u32[]{:S(2)}) collective-permute-start(f32[24,256]{1,0:T(8,128)S(1)} %get-tuple-element.52), channel_id=1, source_target_pairs={{0,3},{1,0},{2,1},{3,2},{4,7},{5,4},{6,5},{7,6},{8,11},{9,8},{10,9... | collective-permute-start | bytes 73736 | tf_op jit(solution)/shard_map/sum_cols/ppermute | solution.py:55
  83.6 4.8 %collective-permute-start.29 = (f32[24,256]{1,0:T(8,128)S(1)}, f32[24,256]{1,0:T(8,128)S(1)}, u32[]{:S(2)}, u32[]{:S(2)}) collective-permute-start(f32[24,256]{1,0:T(8,128)S(1)} %spread.1.refs_0_), channel_id=1, source_target_pairs={{0,24},{4,28},{8,16},{12,20},{16,8},{20,12},{24,0},{28,4},{1,25},{... | collective-permute-start | bytes 73736 | tf_op jit(solution)/shard_map/spread/ppermute | solution.py:51
  84.7 3.9 %collective-permute-start.27 = (f32[24,256]{1,0:T(8,128)S(1)}, f32[24,256]{1,0:T(8,128)S(1)}, u32[]{:S(2)}, u32[]{:S(2)}) collective-permute-start(f32[24,256]{1,0:T(8,128)S(1)} %spread.1.refs_0_), channel_id=1, source_target_pairs={{0,16},{4,20},{8,24},{12,28},{16,0},{20,4},{24,8},{28,12},{1,17},{... | collective-permute-start | bytes 73736 | tf_op jit(solution)/shard_map/spread/ppermute | solution.py:51
  85.3 3.8 %collective-permute-start.25 = (f32[24,256]{1,0:T(8,128)S(1)}, f32[24,256]{1,0:T(8,128)S(1)}, u32[]{:S(2)}, u32[]{:S(2)}) collective-permute-start(f32[24,256]{1,0:T(8,128)S(1)} %spread.1.refs_0_), channel_id=1, source_target_pairs={{0,8},{4,12},{8,0},{12,4},{16,24},{20,28},{24,16},{28,20},{1,9},{5... | collective-permute-start | bytes 73736 | tf_op jit(solution)/shard_map/spread/ppermute | solution.py:51
  87.2 3.5 %collective-permute-start.24 = (f32[24,256]{1,0:T(8,128)S(1)}, f32[24,256]{1,0:T(8,128)S(1)}, u32[]{:S(2)}, u32[]{:S(2)}) collective-permute-start(f32[24,256]{1,0:T(8,128)S(1)} %spread.1.refs_0_), channel_id=1, source_target_pairs={{0,4},{4,0},{8,12},{12,8},{16,20},{20,16},{24,28},{28,24},{1,5},{5... | collective-permute-start | bytes 73736 | tf_op jit(solution)/shard_map/spread/ppermute | solution.py:51
  88.4 2.3 %collective-permute-start.30 = (f32[24,256]{1,0:T(8,128)S(1)}, f32[24,256]{1,0:T(8,128)S(1)}, u32[]{:S(2)}, u32[]{:S(2)}) collective-permute-start(f32[24,256]{1,0:T(8,128)S(1)} %collective-permute-done.29.refs_6_), channel_id=1, source_target_pairs={{0,4},{4,0},{8,12},{12,8},{16,20},{20,16},{24,28},{28,24},{1,5},{5... | collective-permute-start | bytes 73736 | tf_op jit(solution)/shard_map/spread/ppermute | solution.py:51
  88.7 2.1 %collective-permute-start.28 = (f32[24,256]{1,0:T(8,128)S(1)}, f32[24,256]{1,0:T(8,128)S(1)}, u32[]{:S(2)}, u32[]{:S(2)}) collective-permute-start(f32[24,256]{1,0:T(8,128)S(1)} %collective-permute-done.27.refs_4_), channel_id=1, source_target_pairs={{0,4},{4,0},{8,12},{12,8},{16,20},{20,16},{24,28},{28,24},{1,5},{5... | collective-permute-start | bytes 73736 | tf_op jit(solution)/shard_map/spread/ppermute | solution.py:51
  89.2 1.6 %collective-permute-start.26 = (f32[24,256]{1,0:T(8,128)S(1)}, f32[24,256]{1,0:T(8,128)S(1)}, u32[]{:S(2)}, u32[]{:S(2)}) collective-permute-start(f32[24,256]{1,0:T(8,128)S(1)} %collective-permute-done.25.refs_2_), channel_id=1, source_target_pairs={{0,4},{4,0},{8,12},{12,8},{16,20},{20,16},{24,28},{28,24},{1,5},{5... | collective-permute-start | bytes 73736 | tf_op jit(solution)/shard_map/spread/ppermute | solution.py:51

commit v2 on v1

--- a/solution.py
+++ b/solution.py
@@ -22,37 +22,58 @@
 
 def dot3(left, right, dims):
     (lh, ll), (rh, rl) = left, right
-    dot = functools.partial(lax.dot_general, dimension_numbers=dims, preferred_element_type=f32)
-    return dot(lh, rh) + (dot(lh, rl) + dot(ll, rh))
-
-
-def vmem(count):
-    return [pl.BlockSpec(memory_space=pltpu.VMEM)] * count
-
-
-def smem(count):
-    return [pl.BlockSpec(memory_space=pltpu.SMEM)] * count
-
-
-def call(kernel, scalars, arrays, outs, scratch=(), flops=0):
-    nbytes = sum(a.size * 4 for a in arrays) + sum(4 * o[0] * o[1] for o in outs)
+    on_left, on_right = dims[0][0][0], dims[0][1][0]
+    return lax.dot_general(
+        jnp.concatenate([lh, lh, ll], axis=on_left),
+        jnp.concatenate([rh, rl, rh], axis=on_right),
+        dims,
+        preferred_element_type=f32,
+    )
+
+
+def call(kernel, inputs, outs, scratch=(), flops=0, limit=40, alias=None):
+    arrays = [a for _, a in inputs]
+    shapes = [jax.ShapeDtypeStruct(*(o if isinstance(o[0], tuple) else (o, f32))) for o in outs]
+    nbytes = sum(a.size * a.dtype.itemsize for a in arrays + shapes)
     return pl.pallas_call(
         kernel,
-        out_shape=[jax.ShapeDtypeStruct(o, f32) for o in outs],
-        in_specs=smem(len(scalars)) + vmem(len(arrays)),
-        out_specs=vmem(len(outs)),
+        out_shape=shapes,
+        in_specs=[pl.BlockSpec(memory_space=space) for space, _ in inputs],
+        out_specs=[pl.BlockSpec(memory_space=pltpu.VMEM)] * len(outs),
         scratch_shapes=list(scratch),
-        compiler_params=pltpu.CompilerParams(vmem_limit_bytes=48 * 1024 * 1024),
+        input_output_aliases=alias or {},
+        compiler_params=pltpu.CompilerParams(vmem_limit_bytes=limit and limit * 1024 * 1024),
         cost_estimate=pl.CostEstimate(flops=flops, bytes_accessed=nbytes, transcendentals=0),
-    )(*scalars, *arrays)
+    )(*arrays)
+
+
+def vmem(*arrays):
+    return [(pltpu.VMEM, a) for a in arrays]
+
+
+def smem(*arrays):
+    return [(pltpu.SMEM, a) for a in arrays]
+
+
+def hbm(*arrays):
+    return [(pltpu.HBM, a) for a in arrays]
+
+
+def fetch(sources, targets, sems):
+    copies = [
+        pltpu.make_async_copy(a, b, sems.at[i]) for i, (a, b) in enumerate(zip(sources, targets))
+    ]
+    for copy in copies:
+        copy.start()
+    return copies
 
 
 def exchange(value, mask, row_total):
     return lax.ppermute(value, "row", [(i, i ^ mask) for i in range(row_total)])
 
 
-def shift(value, step, col_total):
-    return lax.ppermute(value, "col", [(i, (i + step) % col_total) for i in range(col_total)])
+def flip(value, mask, col_total):
+    return lax.ppermute(value, "col", [(i, i ^ mask) for i in range(col_total)])
 
 
 class Shape:
@@ -69,21 +90,28 @@
         self.share = self.B // cols
         self.chips = rows // 2
         self.eight = self.ws // rows
-
-
-def pack(s, blocks, psize, csize, parent, child, top, *outs):
-    sends, payload = outs[: s.C], outs[s.C]
+        self.live = self.slots * self.B
+        self.parts = self.W // self.B
+        self.block = self.payload + 8
+
+
+def pack(s, *refs):
+    sources, refs = refs[:6], refs[6:]
+    sends, payload, refs = refs[: s.C], refs[s.C], refs[s.C + 1 :]
+    targets, sems = refs[:6], refs[6]
+    for copy in fetch(sources, targets, sems):
+        copy.wait()
+    blocks, psize, csize, parent, child, top = targets
     col = lax.axis_index("col")
     lane = lax.broadcasted_iota(jnp.int32, (s.ws, s.B), 1)
     for slot in range(s.slots):
         base = slot * 2 * s.ws
         for which, panel, sizes in ((0, parent, psize), (1, child, csize)):
-            live = jnp.where(lane < sizes[slot], panel[:, slot, :], 0.0)
+            live = jnp.where(lane < sizes[slot], panel[slot], 0.0)
             payload[base + which * s.ws : base + (which + 1) * s.ws, :] = live
-    half = s.W // s.B
-    for part in range(half):
-        start = s.payload + part * s.ws
-        payload[start : start + s.ws, :] = top[:, part * s.B : (part + 1) * s.B]
+    wide = s.W // 2
+    mine = lax.rem(lax.axis_index("row"), 2) * wide
+    payload[s.payload :, :] = top[:, pl.ds(pl.multiple_of(mine, wide), wide)]
     row8 = lax.broadcasted_iota(jnp.int32, (8, s.B), 0)
     ids = jnp.zeros((8, s.B), f32)
     for slot in range(s.slots):
@@ -94,8 +122,29 @@
         sends[turn][s.piece :, :] = ids
 
 
+def split_live(s, cached, blocks, high, low, held, numbers, sems):
+    copy = pltpu.make_async_copy(blocks, numbers, sems.at[0])
+    copy.start()
+    copy.wait()
+    size = s.B * s.CC
+    copies = []
+    for slot in range(s.slots):
+        p = lax.div(jnp.maximum(numbers[slot], 0), s.R)
+        source = cached.at[pl.ds(pl.multiple_of(p * size, size), size), :]
+        copy = pltpu.make_async_copy(source, held.at[pl.ds(slot * size, size), :], sems.at[1 + slot])
+        copy.start()
+        copies.append(copy)
+    for slot in range(s.slots):
+        copies[slot].wait()
+        rows = slice(slot * s.B, (slot + 1) * s.B)
+        for m in range(s.CC):
+            h, l = split(held[pl.ds(slot * size + m, s.B, stride=s.CC), :])
+            high[rows, m * s.B : (m + 1) * s.B] = h
+            low[rows, m * s.B : (m + 1) * s.B] = l
+
+
 def join(s, *refs):
-    pieces, out = refs[: s.C], refs[s.C]
+    pieces, out = refs[: s.C], refs[s.C + 2]
     part = lax.rem(lax.axis_index("row"), s.C)
     for turn in range(s.C):
         start = pl.multiple_of(lax.rem(turn - part + s.C, s.C) * s.piece, s.piece)
@@ -103,86 +152,101 @@
     out[s.payload :, :] = pieces[0][s.piece :, :]
 
 
-def main(s, blocks, cached, pd, *refs):
-    panels, refs = refs[: s.R], refs[s.R :]
-    owned, refs = refs[: s.C], refs[s.C :]
-    shares, refs = refs[: s.C], refs[s.C :]
-    keep, send, base, top, refs = refs[0], refs[1], refs[2], refs[3], refs[4:]
-    xh, xl, ph, plo, sh, sl, total, both = refs
+def collect(s, *refs):
+    owned, (lh, ll, half, panel) = refs[: s.C], refs[s.C :]
+    col = lax.axis_index("col")
+    for mask in range(s.C):
+        source = jnp.bitwise_xor(col, mask)
+        for slot in range(s.slots):
+            for which in range(2):
+                start = (slot * 2 + which) * s.ws
+                dest = pl.multiple_of(which * s.W + source * s.ws, s.ws)
+                panel[pl.ds(dest, s.ws), slot * s.B : (slot + 1) * s.B] = owned[mask][
+                    start : start + s.ws, :
+                ]
+        dest = pl.multiple_of(source * s.ws, s.ws)
+        half[pl.ds(dest, s.ws), :] = owned[mask][s.payload :, :]
+    lh[...], ll[...] = split(panel[...])
+
+
+def own_panels(s, pd, lh, ll, mine, theirs, vh, vl, th, tl, base, extra, top):
     row, col = lax.axis_index("row"), lax.axis_index("col")
+    wide = s.W // 2
+    core = lax.rem(row, 2)
+    top[:, pl.ds(pl.multiple_of(core * wide, wide), wide)] = mine[...]
+    top[:, pl.ds(pl.multiple_of((1 - core) * wide, wide), wide)] = theirs[...]
+    th[...], tl[...] = split(top[...])
+    full = (th[...], tl[...])
+    vh[...], vl[...] = split(dot3(split(top[...].T), (lh[: s.W, :], ll[: s.W, :]), NN))
+    lead = dot3(split(pd[...]), full, NN)
+    base[...] = -lead
+    own = top[pl.ds(pl.multiple_of(col * s.ws, s.ws), s.ws), :]
+    extra[...] = dot3(split(own), split(lead * (1.0 / s.R)), TN)
+
+
+def products(s, sh, sl, lh, ll, vh, vl, th, tl, extra, *refs):
+    panels, (stay, leave, keep, send, xh, xl, total, both) = refs[: s.R], refs[s.R :]
+    row = lax.axis_index("row")
+    core = lax.rem(row, 2)
+    places = []
+    for owner in range(s.Q):
+        for slot in range(s.slots):
+            at = s.payload + slot
+            number = jnp.max(panels[owner * s.C][at : at + 1, :]).astype(jnp.int32)
+            places.append(jnp.where(number < 0, s.CC, lax.div(jnp.maximum(number, 0), s.C)))
+    for m in range(s.CC):
+        taken = places[0] == m
+        for place in places[1:]:
+            taken = jnp.logical_or(taken, place == m)
+
+        @pl.when(jnp.logical_not(taken))
+        def _():
+            xh[m] = jnp.zeros((2 * s.W, s.B), bf16)
+            xl[m] = jnp.zeros((2 * s.W, s.B), bf16)
+
     per = s.piece // s.chunk
     for mask in range(s.R):
+        owner = mask // s.C
         part = lax.rem(jnp.bitwise_xor(row, mask), s.C)
         for i in range(per):
             at = part * per + i
             group, off = lax.div(at, 2), lax.rem(at, 2) * s.chunk
             slot, which = lax.div(group, 2), lax.rem(group, 2)
+            place = places[owner * s.slots]
+            for k in range(1, s.slots):
+                place = jnp.where(slot == k, places[owner * s.slots + k], place)
             for source in range(s.C):
                 start = source * s.piece + i * s.chunk
                 high, low = split(panels[mask][start : start + s.chunk, :])
                 dest = pl.multiple_of(which * s.W + source * s.ws + off, s.chunk)
-                lead = (mask // s.C) * s.slots + slot
-                xh[lead, pl.ds(dest, s.chunk), :] = high
-                xl[lead, pl.ds(dest, s.chunk), :] = low
-    for step in range(s.C):
-        source = lax.rem(col - step + s.C, s.C)
-        for slot in range(s.slots):
-            for which in range(2):
-                start = (slot * 2 + which) * s.ws
-                high, low = split(owned[step][start : start + s.ws, :])
-                dest = pl.multiple_of(which * s.W + source * s.ws, s.ws)
-                ph[slot, pl.ds(dest, s.ws), :] = high
-                plo[slot, pl.ds(dest, s.ws), :] = low
-        for part in range(s.W // s.B):
-            start = s.payload + part * s.ws
-            dest = pl.multiple_of(source * s.ws, s.ws)
-            top[pl.ds(dest, s.ws), part * s.B : (part + 1) * s.B] = owned[step][
-                start : start + s.ws, :
-            ]
-    for slot in range(s.slots):
-        p = lax.div(jnp.maximum(blocks[slot], 0), s.R)
-        for other in range(s.Q):
-            for k in range(s.slots):
-                at = s.payload + k
-                number = jnp.max(panels[other * s.C][at : at + 1, :]).astype(jnp.int32)
-                m = lax.div(jnp.maximum(number, 0), s.C)
-                start = p * (s.B * s.CC) + m
-                high, low = split(cached[pl.ds(start, s.B, stride=s.CC), :])
-                lead = (other * s.slots + k) * s.B
-                sh[slot * s.B : (slot + 1) * s.B, lead : lead + s.B] = high
-                sl[slot * s.B : (slot + 1) * s.B, lead : lead + s.B] = low
-    wide = s.Q * s.slots
-    right = tuple(jnp.concatenate([x[i] for i in range(wide)], axis=1) for x in (xh, xl))
+                xh[place, pl.ds(dest, s.chunk), :] = high
+                xl[place, pl.ds(dest, s.chunk), :] = low
+    right = tuple(jnp.concatenate([x[i] for i in range(s.CC)], axis=1) for x in (xh, xl))
     total[...] = dot3((sh[...], sl[...]), right, NT)
-    for step in range(s.C):
-        target = lax.rem(col + step, s.C)
+    col = lax.axis_index("col")
+    for mask in range(s.C):
+        out = leave if mask % 2 else stay
+        target = jnp.bitwise_xor(col, mask)
         for slot in range(s.slots):
             start = pl.multiple_of(slot * s.B + target * s.share, s.share)
-            shares[step][slot * s.share : (slot + 1) * s.share, :] = total[pl.ds(start, s.share), :]
-    left = tuple(jnp.concatenate([x[i] for i in range(s.slots)], axis=1) for x in (ph, plo))
-    lower = tuple(x[s.W :, :] for x in left)
-    ab = dot3(left, split(total[:, : s.W]), NN)
-    a, b = ab[: s.W], ab[s.W :]
-    d = dot3(lower, split(total[:, s.W :]), NN)
-    top_full = split(top[...])
-    u = b.T - dot3(split(a), top_full, NN)
-    parts = [owned[0][s.payload + i * s.ws : s.payload + (i + 1) * s.ws, :] for i in range(s.W // s.B)]
-    top_own = split(jnp.concatenate(parts, axis=1))
-    lead = dot3(split(pd[...]), top_full, NN)
-    base[...] = -lead
-    cd = d - dot3(split(b), top_full, NN) - dot3(top_full, split(u), TN)
-    cd = cd + dot3(top_own, split(lead * (1.0 / s.R)), TN)
-    both[0 : s.W, :] = a
-    both[s.W : 2 * s.W, :] = u
-    both[2 * s.W :, :] = cd
-    core = lax.rem(row, 2)
+            to = (mask // 2 * s.slots + slot) * s.share
+            out[to : to + s.share, :] = total[pl.ds(start, s.share), :]
+    W = s.W
+    left = tuple(jnp.concatenate([x[...], y[...]], axis=0) for x, y in ((lh, vh), (ll, vl)))
+    first = dot3(left, split(total[:, :W]), NN)
+    d = dot3((lh[W:, :], ll[W:, :]), split(total[:, W:]), NN)
+    second = dot3(split(first), (th[...], tl[...]), NN)
+    both[0:W, :] = first[:W]
+    both[W : 2 * W, :] = first[W : 2 * W].T - second[:W]
+    cross = second[W : 2 * W]
+    both[2 * W :, :] = d - cross - cross.T + second[2 * W :] + extra[...]
     n = s.eight
-    for out, flip in ((keep, 0), (send, 1)):
-        offset = jnp.bitwise_xor(core, flip) * (s.ws // 2)
+    for out, swap in ((keep, 0), (send, 1)):
+        offset = jnp.bitwise_xor(core, swap) * (s.ws // 2)
         for chip in range(s.chips):
             for source in range(s.C):
                 for kind in range(3):
-                    at = pl.multiple_of(kind * s.W + source * s.ws + chip * n + offset, n)
+                    at = pl.multiple_of(kind * W + source * s.ws + chip * n + offset, n)
                     to = ((chip * s.C + source) * 3 + kind) * n
                     out[to : to + n, :] = both[pl.ds(at, n), :]
 
@@ -196,16 +260,26 @@
 
 
 def add_cols(s, *refs):
-    terms, outs, total = refs[: s.chips], refs[s.chips : -1], refs[-1]
+    terms, (kept, got), refs = refs[: s.chips], refs[s.chips : s.chips + 2], refs[s.chips + 2 :]
+    outs, (stay, leave, total) = refs[: s.C], refs[s.C :]
     size = 3 * s.eight
     col = lax.axis_index("col")
     value = terms[0][...]
     for term in terms[1:]:
         value = value + term[...]
     total[...] = value
-    for step in range(s.C):
-        rows = pl.ds(pl.multiple_of(lax.rem(col + step, s.C) * size, size), size)
-        outs[step][...] = total[rows, :]
+    for mask in range(s.C):
+        rows = pl.ds(pl.multiple_of(jnp.bitwise_xor(col, mask) * size, size), size)
+        outs[mask][...] = total[rows, :]
+    halve(s, kept, got, stay, leave)
+
+
+def halve(s, kept, got, stay, leave):
+    size = s.slots * s.share
+    for i in range(kept.shape[0] // size):
+        out, at = (leave if i % 2 else stay), i // 2 * size
+        rows = slice(i * size, (i + 1) * size)
+        out[at : at + size, :] = kept[rows, :] + got[rows, :]
 
 
 def add_all(s, *refs):
@@ -228,21 +302,19 @@
             outs[kind][rows, :] = starts[kind][rows, :] + parts[mask][kind * n : (kind + 1) * n, :]
 
 
-def rows_out(s, blocks, psize, csize, top, *refs):
-    terms, (parent, child) = refs[: s.C], refs[s.C :]
+def rows_out(s, blocks, psize, csize, th, tl, kept, got, parent, child):
+    value = kept[...] + got[...]
     first = lax.axis_index("col") * s.share
-    value = terms[0][...]
-    for term in terms[1:]:
-        value = value + term[...]
     index = lax.broadcasted_iota(jnp.int32, (s.share, s.W), 0) + first
     plive = jnp.concatenate([index < psize[k] for k in range(s.slots)], axis=0)
     clive = jnp.concatenate([index < csize[k] for k in range(s.slots)], axis=0)
     y = jnp.where(plive, -value[:, : s.W], 0.0)
-    carried = dot3(split(y), split(top[...]), NN)
+    carried = dot3(split(y), (th[...], tl[...]), NN)
     z = jnp.where(clive, -(value[:, s.W :] + carried), 0.0)
     parent[...] = jnp.zeros_like(parent)
     child[...] = jnp.zeros_like(child)
     for slot in range(s.slots):
+
         @pl.when(blocks[slot] >= 0)
         def _():
             at = lax.div(blocks[slot], s.R) * s.share
@@ -275,69 +347,108 @@
     R, C = lax.axis_size("row"), lax.axis_size("col")
     B = cached_inverse.shape[2]
     s = Shape(R, C, parent_panel, cached_inverse, parent_diagonal.shape[1])
+    W, ws, live = s.W, s.ws, s.live
     cached = cached_inverse.reshape(-1, B)
     bind = lambda kernel: functools.partial(kernel, s)
-    sent = (s.piece + 8, B)
-    whole = (s.payload + (s.W // B) * s.ws, B)
+    numbers = pltpu.SMEM((s.slots,), jnp.int32)
+    by_slot = (s.slots, ws, B)
     with jax.named_scope("pack"):
         *sends, payload = call(
             bind(pack),
-            (parent_blocks, parent_sizes, child_sizes),
-            (parent_panel, child_panel, child_top),
-            [sent] * C + [whole],
+            hbm(
+                parent_blocks,
+                parent_sizes,
+                child_sizes,
+                jnp.transpose(parent_panel, (1, 0, 2)),
+                jnp.transpose(child_panel, (1, 0, 2)),
+                child_top,
+            ),
+            [(s.piece + 8, B)] * C + [(s.payload + ws, B)],
+            [numbers] * 3
+            + [pltpu.VMEM(by_slot, f32)] * 2
+            + [pltpu.VMEM((ws, W), f32), pltpu.SemaphoreType.DMA((6,))],
+            limit=None,
         )
     with jax.named_scope("scatter"):
-        pieces = [
-            lax.ppermute(sends[t], ("row", "col"), scatter_perm(s, t)) for t in range(C)
-        ]
+        pieces = [lax.ppermute(sends[t], ("row", "col"), scatter_perm(s, t)) for t in range(C)]
+    with jax.named_scope("owned"):
+        owned = {0: payload}
+        mask = C // 2
+        while mask:
+            owned.update({m ^ mask: flip(owned[m], mask, C) for m in list(owned)})
+            mask //= 2
+    with jax.named_scope("split_live"):
+        sh, sl = call(
+            bind(split_live),
+            hbm(cached, parent_blocks),
+            [((live, s.CC * B), bf16)] * 2,
+            [pltpu.VMEM((s.slots * B * s.CC, B), f32), numbers]
+            + [pltpu.SemaphoreType.DMA((1 + s.slots,))],
+        )
     with jax.named_scope("join"):
-        (own,) = call(bind(join), (), pieces, [(s.payload + 8, B)])
+        own, sh, sl = call(
+            bind(join),
+            vmem(*pieces, sh, sl),
+            [(s.block, B), (sh.shape, bf16), (sl.shape, bf16)],
+            alias={C: 1, C + 1: 2},
+        )
     with jax.named_scope("panels"):
         panels = {0: own}
         for mask in range(2, R, 2):
             panels[mask] = exchange(own, mask, R)
         for mask in range(0, R, 2):
             panels[mask + 1] = exchange(panels[mask], 1, R)
-    with jax.named_scope("owned"):
-        owned = [payload] + [shift(payload, k, C) for k in range(1, C)]
-    W, ws = s.W, s.ws
-    D = 3 * W
-    wide = s.Q * s.slots
-    live = s.slots * B
-    scratch = [
-        pltpu.VMEM((wide, 2 * W, B), bf16),
-        pltpu.VMEM((wide, 2 * W, B), bf16),
-        pltpu.VMEM((s.slots, 2 * W, B), bf16),
-        pltpu.VMEM((s.slots, 2 * W, B), bf16),
-        pltpu.VMEM((live, wide * B), bf16),
-        pltpu.VMEM((live, wide * B), bf16),
-        pltpu.VMEM((live, 2 * W), f32),
-        pltpu.VMEM((D, W), f32),
-    ]
-    outs = [(s.slots * s.share, 2 * W)] * C + [(D // 2, W), (D // 2, W), (ws, W), (W, W)]
+    with jax.named_scope("collect"):
+        lh, ll, half = call(
+            bind(collect),
+            vmem(*[owned[m] for m in range(C)]),
+            [((2 * W, live), bf16)] * 2 + [(W, W // 2)],
+            [pltpu.VMEM((2 * W, live), f32)],
+        )
+        theirs = exchange(half, 1, R)
+    with jax.named_scope("own_panels"):
+        vh, vl, th, tl, base, extra = call(
+            bind(own_panels),
+            vmem(parent_diagonal, lh, ll, half, theirs),
+            [((W, live), bf16)] * 2 + [((W, W), bf16)] * 2 + [(ws, W), (W, W)],
+            [pltpu.VMEM((W, W), f32)],
+        )
     with jax.named_scope("products"):
-        out = call(
-            bind(main),
-            (parent_blocks,),
-            (cached, parent_diagonal, *[panels[m] for m in range(R)], *owned),
-            outs,
-            scratch,
-            flops=2 * live * wide * B * 2 * W * 3,
-        )
-    shares, (keep, send, base, top) = out[:C], out[C:]
+        half = C // 2 * s.slots * s.share
+        stay, leave, keep, send = call(
+            bind(products),
+            vmem(sh, sl, lh, ll, vh, vl, th, tl, extra, *[panels[m] for m in range(R)]),
+            [(half, 2 * W), (half, 2 * W), (3 * W // 2, W), (3 * W // 2, W)],
+            [pltpu.VMEM((s.CC + 1, 2 * W, B), bf16)] * 2
+            + [pltpu.VMEM((live, 2 * W), f32), pltpu.VMEM((3 * W, W), f32)],
+            flops=2 * live * s.CC * B * 2 * W * 3,
+        )
     with jax.named_scope("sum_core"):
         got = exchange(send, 1, R)
     with jax.named_scope("sum_shares"):
-        rows = [shares[0]] + [shift(shares[k], k, C) for k in range(1, C)]
+        got_rows = flip(leave, 1, C)
     with jax.named_scope("sum_chips"):
-        mine = call(bind(add_chips), (), (keep, got), [(C * 3 * s.eight, W)] * s.chips)
+        mine = call(bind(add_chips), vmem(keep, got), [(C * 3 * s.eight, W)] * s.chips)
         mine = [mine[0]] + [exchange(mine[m], 2 * m, R) for m in range(1, s.chips)]
     with jax.named_scope("sum_cols"):
         scr = [pltpu.VMEM((C * 3 * s.eight, W), f32)]
-        cols = call(bind(add_cols), (), mine, [(3 * s.eight, W)] * C, scr)
-        cols = [cols[0]] + [shift(cols[k], k, C) for k in range(1, C)]
+        half //= 2
+        *cols, stay, leave = call(
+            bind(add_cols),
+            vmem(*mine, stay, got_rows),
+            [(3 * s.eight, W)] * C + [(half, 2 * W)] * 2,
+            scr,
+        )
+        cols = [cols[0]] + [flip(cols[m], m, C) for m in range(1, C)]
+        got_rows = flip(leave, 2, C)
+        mask = 4
+        while mask < C:
+            half //= 2
+            stay, leave = call(bind(halve), vmem(stay, got_rows), [(half, 2 * W)] * 2)
+            got_rows = flip(leave, mask, C)
+            mask *= 2
     with jax.named_scope("spread"):
-        (done,) = call(bind(add_all), (), cols, [(3 * s.eight, W)])
+        (done,) = call(bind(add_all), vmem(*cols), [(3 * s.eight, W)])
         parts = {0: done}
         for mask in range(2, R, 2):
             parts[mask] = exchange(done, mask, R)
@@ -346,15 +457,13 @@
     with jax.named_scope("rows_out"):
         parent_rows, child_rows = call(
             bind(rows_out),
-            (parent_blocks, parent_sizes, child_sizes),
-            (top, *rows),
+            smem(parent_blocks, parent_sizes, child_sizes) + vmem(th, tl, stay, got_rows),
             [(s.RC * s.share, W)] * 2,
         )
     with jax.named_scope("finish"):
         parent_diag, child_upper, child_diag = call(
             bind(finish),
-            (),
-            (parent_diagonal, child_diagonal, base, *[parts[m] for m in range(R)]),
+            vmem(parent_diagonal, child_diagonal, base, *[parts[m] for m in range(R)]),
             [(ws, W)] * 3,
         )
     shape = (s.RC, 1, s.share, W)
@@ -532,7 +641,10 @@
     s = Shape(rows, cols, panel, cached, width)
     return (
         rows & (rows - 1) == 0
+        and cols & (cols - 1) == 0
         and rows % cols == 0
+        and cols > 2
+        and width == 2 * s.B
         and s.payload % cols == 0
         and s.chunk % 16 == 0
         and s.piece % s.chunk == 0

time: 92.8 us -> 81.8 us (0.88); the launches traced: 91.5 us -> 81.6 us
  waiting for transfers between devices: 43.7 us -> 31 us
  starting transfers between devices: 32.4 us -> 37.1 us
  local copies, waits for them, and re-layouts: 6.24 us -> 2.28 us
  Pallas kernels: 8.35 us -> 10.4 us
    ppermute x9 -> x8, waiting for transfers between devices: 24.7 us -> 12.5 us  [flip(): return lax.ppermute(value, 'col', [(i, i ^ mask) for i in range(col_total)])]
    unnamed x24 -> x16, local copies, waits for them, and re-layouts: 6.24 us -> 2.28 us
    ppermute x9 -> x8, starting transfers between devices: 11.6 us -> 15.2 us  [flip(): return lax.ppermute(value, 'col', [(i, i ^ mask) for i in range(col_total)])]
    ppermute x18 -> x19, starting transfers between devices: 10.3 us -> 12.8 us  [exchange(): return lax.ppermute(value, 'row', [(i, i ^ mask) for i in range(row_total)])]
    pallas_call x8 -> x11, Pallas kernels: 8.35 us -> 10.4 us  [call(): pl.pallas_call(kernel, out_shape=shapes, in_specs=[pl.BlockSpec(memory_sp...]
    ppermute x4, starting transfers between devices: 10.5 us -> 9.07 us  [fast_body(): lax.ppermute(sends[t], ('row', 'col'), scatter_perm(s, t))]
    ppermute x4, waiting for transfers between devices: 6.56 us -> 5.42 us  [fast_body(): lax.ppermute(sends[t], ('row', 'col'), scatter_perm(s, t))]
    ppermute x18 -> x19, waiting for transfers between devices: 12.4 us -> 13.1 us  [exchange(): return lax.ppermute(value, 'row', [(i, i ^ mask) for i in range(row_total)])]
  transfers between devices with their start and end apart: 31 -> 31, of which waited for: 14 -> 13; matrix products, arithmetic and copies ran while one was open for 0% -> 0% of each run, Pallas kernels for 2% -> 4%
where the time goes in v2:
time: 81.8 us; the launch traced here: 81.6 us
  starting transfers between devices  37.1 us (45%)
  waiting for transfers between devices  31 us (38%)
  Pallas kernels  10.4 us (13%)
  local copies, waits for them, and re-layouts  2.28 us (3%)
  between operations  0.84 us (1%)
    ppermute x8, starting transfers between devices, flip(): return lax.ppermute(value, 'col', [(i, i ^ mask) for i in range(col_total)])  15.2 us
    ppermute x19, waiting for transfers between devices, exchange(): return lax.ppermute(value, 'row', [(i, i ^ mask) for i in range(row_total)])  13.1 us
    ppermute x19, starting transfers between devices, exchange(): return lax.ppermute(value, 'row', [(i, i ^ mask) for i in range(row_total)])  12.8 us
    ppermute x8, waiting for transfers between devices, flip(): return lax.ppermute(value, 'col', [(i, i ^ mask) for i in range(col_total)])  12.5 us
    pallas_call x11, Pallas kernels, call(): pl.pallas_call(kernel, out_shape=shapes, in_specs=[pl.BlockSpec(memory_sp...  10.4 us
    ppermute x4, starting transfers between devices, fast_body(): lax.ppermute(sends[t], ('row', 'col'), scatter_perm(s, t))  9.07 us
    ppermute x4, waiting for transfers between devices, fast_body(): lax.ppermute(sends[t], ('row', 'col'), scatter_perm(s, t))  5.42 us
    unnamed x16, local copies, waits for them, and re-layouts  2.28 us
  transfers between devices with their start and end apart: 31, of which 13 were waited for; matrix products, arithmetic and copies ran while one was open for 0% of the time, Pallas kernels for 4%

profile of v2, /device:TPU:0, one launch (start us, length us, event | category | flops | bytes accessed | tf_op | source)
XLA Modules:
  0.0 81.6 jit_solution(6874104712415483271)
XLA Ops:
  0.6 1.8 %pack.1 = (f32[104,128]{1,0:T(8,128)}, f32[104,128]{1,0:T(8,128)}, f32[104,128]{1,0:T(8,128)}, f32[104,128]{1,0:T(8,128)}, f32[448,128]{1,0:T(8,128)}) custom-call(s32[3]{0:T(128)} %blocks.3, s32[3]{0:T(128)} %psize.1, s32[3]{0:T(128)} %csize.1, f32[3,64,128]{2,1,0:T(8,128)} %bitcast.10, f32[3,64,128]{2,1,0:T(8,128)} %bitcast.11, f32[64,256]{1,0:T(8,128)} %refs_5_.1), custom_call_target="tpu_custom_call" | custom-call | bytes 704548 | tf_op jit(solution)/shard_map/pack/pallas_call | solution.py:38
  2.4 4.1 %collective-permute-start.1 = (f32[448,128]{1,0:T(8,128)}, f32[448,128]{1,0:T(8,128)S(1)}, u32[]{:S(2)}, u32[]{:S(2)}) collective-permute-start(f32[448,128]{1,0:T(8,128)} %get-tuple-element.43.refs_0_), channel_id=1, source_target_pairs={{0,2},{1,3},{2,0},{3,1},{4,6},{5,7},{6,4},{7,5},{8,10},{9,11},{10,... | collective-permute-start | bytes 688136 | tf_op jit(solution)/shard_map/owned/ppermute | solution.py:76
  6.5 1.5 %collective-permute-start.4 = (f32[104,128]{1,0:T(8,128)}, f32[104,128]{1,0:T(8,128)S(1)}, u32[]{:S(2)}, u32[]{:S(2)}) collective-permute-start(f32[104,128]{1,0:T(8,128)} %get-tuple-element.49), channel_id=1, source_target_pairs={{0,0},{1,12},{2,8},{3,4},{4,1},{5,13},{6,9},{7,5},{8,2},{9,14},{10... | collective-permute-start | bytes 159752 | tf_op jit(solution)/shard_map/scatter/ppermute | solution.py:373
  8.0 2.2 %collective-permute-start.5 = (f32[104,128]{1,0:T(8,128)}, f32[104,128]{1,0:T(8,128)S(1)}, u32[]{:S(2)}, u32[]{:S(2)}) collective-permute-start(f32[104,128]{1,0:T(8,128)} %get-tuple-element.50), channel_id=1, source_target_pairs={{0,4},{1,0},{2,12},{3,8},{4,5},{5,1},{6,13},{7,9},{8,6},{9,2},{10,... | collective-permute-start | bytes 159752 | tf_op jit(solution)/shard_map/scatter/ppermute | solution.py:373
  10.2 5.4 %collective-permute-start.6 = (f32[104,128]{1,0:T(8,128)}, f32[104,128]{1,0:T(8,128)S(1)}, u32[]{:S(2)}, u32[]{:S(2)}) collective-permute-start(f32[104,128]{1,0:T(8,128)} %get-tuple-element.51), channel_id=1, source_target_pairs={{0,8},{1,4},{2,0},{3,12},{4,9},{5,5},{6,1},{7,13},{8,10},{9,6},{10... | collective-permute-start | bytes 159752 | tf_op jit(solution)/shard_map/scatter/ppermute | solution.py:373
  15.5 0.1 collective-permute-start.7
  15.6 1.5 %collective-permute-start = (f32[448,128]{1,0:T(8,128)}, f32[448,128]{1,0:T(8,128)S(1)}, u32[]{:S(2)}, u32[]{:S(2)}) collective-permute-start(f32[448,128]{1,0:T(8,128)} %get-tuple-element.43.refs_0_), channel_id=1, source_target_pairs={{0,1},{1,0},{2,3},{3,2},{4,5},{5,4},{6,7},{7,6},{8,9},{9,8},{10,11... | collective-permute-start | bytes 688136 | tf_op jit(solution)/shard_map/owned/ppermute | solution.py:76
  17.1 1.6 %copy-done = f32[4,1,128,8,1,128]{5,4,3,2,1,0:T(1,128)S(1)} copy-done((f32[4,1,128,8,1,128]{5,4,3,2,1,0:T(1,128)S(1)}, f32[4,1,128,8,1,128]{5,4,3,2,1,0:T(1,128)}, u32[]{:S(2)}) %copy-start) | copy-done | bytes 2097176
  18.7 0.7 copy-done.4
  19.3 1.2 %split_live.1 = (bf16[384,1024]{1,0:T(8,128)(2,1)S(1)}, bf16[384,1024]{1,0:T(8,128)(2,1)S(1)}) custom-call(f32[4096,128]{1,0:T(8,128)S(1)} %bitcast.9, s32[3]{0:T(128)S(1)} %copy-done.4), custom_call_target="tpu_custom_call" | custom-call | bytes 3670028 | tf_op jit(solution)/shard_map/split_live/pallas_call | solution.py:38
  20.5 5.4 %collective-permute-done.6.refs_2_ = f32[104,128]{1,0:T(8,128)S(1)} collective-permute-done((f32[104,128]{1,0:T(8,128)}, f32[104,128]{1,0:T(8,128)S(1)}, u32[]{:S(2)}, u32[]{:S(2)}) %collective-permute-start.6) | collective-permute-done | bytes 53280 | tf_op jit(solution)/shard_map/scatter/ppermute | solution.py:373
  26.0 4.2 %collective-permute-start.13 = (f32[392,128]{1,0:T(8,128)S(1)}, f32[392,128]{1,0:T(8,128)S(1)}, u32[]{:S(2)}, u32[]{:S(2)}) collective-permute-start(f32[392,128]{1,0:T(8,128)S(1)} %get-tuple-element.60.refs_0_), channel_id=1, source_target_pairs={{0,24},{4,28},{8,16},{12,20},{16,8},{20,12},{24,0},{28,4},{1,25},{... | collective-permute-start | bytes 602120 | tf_op jit(solution)/shard_map/panels/ppermute | solution.py:72
  30.2 0.3 collective-permute-start.11
  30.5 0.3 collective-permute-start.9
  30.8 2.0 %collective-permute-start.2 = (f32[448,128]{1,0:T(8,128)S(1)}, f32[448,128]{1,0:T(8,128)S(1)}, u32[]{:S(2)}, u32[]{:S(2)}) collective-permute-start(f32[448,128]{1,0:T(8,128)S(1)} %collective-permute-done.1.refs_2_), channel_id=1, source_target_pairs={{0,1},{1,0},{2,3},{3,2},{4,5},{5,4},{6,7},{7,6},{8,9},{9,8},{10,11... | collective-permute-start | bytes 688136 | tf_op jit(solution)/shard_map/owned/ppermute | solution.py:76
  32.8 3.2 %collective-permute-done.13.refs_6_ = f32[392,128]{1,0:T(8,128)S(1)} collective-permute-done((f32[392,128]{1,0:T(8,128)S(1)}, f32[392,128]{1,0:T(8,128)S(1)}, u32[]{:S(2)}, u32[]{:S(2)}) %collective-permute-start.13) | collective-permute-done | bytes 200736 | tf_op jit(solution)/shard_map/panels/ppermute | solution.py:72
  36.1 3.0 %collective-permute-done.11.refs_4_ = f32[392,128]{1,0:T(8,128)S(1)} collective-permute-done((f32[392,128]{1,0:T(8,128)S(1)}, f32[392,128]{1,0:T(8,128)S(1)}, u32[]{:S(2)}, u32[]{:S(2)}) %collective-permute-start.11) | collective-permute-done | bytes 200736 | tf_op jit(solution)/shard_map/panels/ppermute | solution.py:72
  39.1 0.5 collective-permute-start.10
  39.6 0.3 collect.1
  39.9 0.1 collective-permute-start.3
  39.9 1.3 %collective-permute-done.3.theirs = f32[256,128]{1,0:T(8,128)S(1)} collective-permute-done((f32[256,128]{1,0:T(8,128)S(1)}, f32[256,128]{1,0:T(8,128)S(1)}, u32[]{:S(2)}, u32[]{:S(2)}) %collective-permute-start.3) | collective-permute-done | bytes 131104 | tf_op jit(solution)/shard_map/collect/ppermute | solution.py:72
  41.3 0.8 own_panels.1
  42.1 4.1 %products.1 = (f32[192,512]{1,0:T(8,128)S(1)}, f32[192,512]{1,0:T(8,128)S(1)}, f32[384,256]{1,0:T(8,128)S(1)}, f32[384,256]{1,0:T(8,128)S(1)}) custom-call(bf16[384,1024]{1,0:T(8,128)(2,1)S(1)} %get-tuple-element.55.sh, bf16[384,1024]{1,0:T(8,128)(2,1)S(1)} %get-tuple-element.56.sl, bf16[512,384]{1,0:T(8,128)(2,1)S(1)} %get-tuple-element.44.lh, ...), custom_call_target="tpu_custom_call" | custom-call | flops 1207959552 | bytes 6455296 | tf_op jit(solution)/shard_map/products/pallas_call | solution.py:38
  46.1 0.0 copy-start.3
  46.2 0.2 collective-permute-start.15
  46.4 0.4 collective-permute-start.19
  46.8 1.2 %collective-permute-done.15.got = f32[384,256]{1,0:T(8,128)S(1)} collective-permute-done((f32[384,256]{1,0:T(8,128)S(1)}, f32[384,256]{1,0:T(8,128)S(1)}, u32[]{:S(2)}, u32[]{:S(2)}) %collective-permute-start.15) | collective-permute-done | bytes 393248 | tf_op jit(solution)/shard_map/sum_core/ppermute | solution.py:72
  48.0 1.5 %collective-permute-start.16 = (f32[96,256]{1,0:T(8,128)S(1)}, f32[96,256]{1,0:T(8,128)S(1)}, u32[]{:S(2)}, u32[]{:S(2)}) collective-permute-start(f32[96,256]{1,0:T(8,128)S(1)} %get-tuple-element.64), channel_id=1, source_target_pairs={{0,8},{4,12},{8,0},{12,4},{16,24},{20,28},{24,16},{28,20},{1,9},{5... | collective-permute-start | bytes 294920 | tf_op jit(solution)/shard_map/sum_chips/ppermute | solution.py:72
  49.5 0.9 %collective-permute-start.17 = (f32[96,256]{1,0:T(8,128)S(1)}, f32[96,256]{1,0:T(8,128)S(1)}, u32[]{:S(2)}, u32[]{:S(2)}) collective-permute-start(f32[96,256]{1,0:T(8,128)S(1)} %get-tuple-element.65), channel_id=1, source_target_pairs={{0,16},{4,20},{8,24},{12,28},{16,0},{20,4},{24,8},{28,12},{1,17},{... | collective-permute-start | bytes 294920 | tf_op jit(solution)/shard_map/sum_chips/ppermute | solution.py:72
  50.5 1.1 %collective-permute-start.18 = (f32[96,256]{1,0:T(8,128)S(1)}, f32[96,256]{1,0:T(8,128)S(1)}, u32[]{:S(2)}, u32[]{:S(2)}) collective-permute-start(f32[96,256]{1,0:T(8,128)S(1)} %get-tuple-element.66), channel_id=1, source_target_pairs={{0,24},{4,28},{8,16},{12,20},{16,8},{20,12},{24,0},{28,4},{1,25},{... | collective-permute-start | bytes 294920 | tf_op jit(solution)/shard_map/sum_chips/ppermute | solution.py:72
  51.6 6.2 %collective-permute-done.19.refs_5_ = f32[192,512]{1,0:T(8,128)S(1)} collective-permute-done((f32[192,512]{1,0:T(8,128)S(1)}, f32[192,512]{1,0:T(8,128)S(1)}, u32[]{:S(2)}, u32[]{:S(2)}) %collective-permute-start.19) | collective-permute-done | bytes 393248 | tf_op jit(solution)/shard_map/sum_shares/ppermute | solution.py:76
  57.8 0.1 sum_cols.1
  57.9 2.9 %collective-permute-start.20 = (f32[96,512]{1,0:T(8,128)S(1)}, f32[96,512]{1,0:T(8,128)S(1)}, u32[]{:S(2)}, u32[]{:S(2)}) collective-permute-start(f32[96,512]{1,0:T(8,128)S(1)} %get-tuple-element.70), channel_id=1, source_target_pairs={{0,2},{1,3},{2,0},{3,1},{4,6},{5,7},{6,4},{7,5},{8,10},{9,11},{10,... | collective-permute-start | bytes 589832 | tf_op jit(solution)/shard_map/sum_cols/ppermute | solution.py:76
  60.7 0.9 %collective-permute-start.21 = (f32[24,256]{1,0:T(8,128)S(1)}, f32[24,256]{1,0:T(8,128)S(1)}, u32[]{:S(2)}, u32[]{:S(2)}) collective-permute-start(f32[24,256]{1,0:T(8,128)S(1)} %get-tuple-element.74), channel_id=1, source_target_pairs={{0,1},{1,0},{2,3},{3,2},{4,5},{5,4},{6,7},{7,6},{8,9},{9,8},{10,11... | collective-permute-start | bytes 73736 | tf_op jit(solution)/shard_map/sum_cols/ppermute | solution.py:76
  61.6 0.1 collective-permute-start.22
  61.7 3.4 %collective-permute-start.23 = (f32[24,256]{1,0:T(8,128)S(1)}, f32[24,256]{1,0:T(8,128)S(1)}, u32[]{:S(2)}, u32[]{:S(2)}) collective-permute-start(f32[24,256]{1,0:T(8,128)S(1)} %get-tuple-element.76), channel_id=1, source_target_pairs={{0,3},{1,2},{2,1},{3,0},{4,7},{5,6},{6,5},{7,4},{8,11},{9,10},{10,... | collective-permute-start | bytes 73736 | tf_op jit(solution)/shard_map/sum_cols/ppermute | solution.py:76
  65.1 0.6 collective-permute-done.21.refs_1_
  65.7 5.7 %collective-permute-done.22.refs_2_ = f32[24,256]{1,0:T(8,128)S(1)} collective-permute-done((f32[24,256]{1,0:T(8,128)S(1)}, f32[24,256]{1,0:T(8,128)S(1)}, u32[]{:S(2)}, u32[]{:S(2)}) %collective-permute-start.22) | collective-permute-done | bytes 24608 | tf_op jit(solution)/shard_map/sum_cols/ppermute | solution.py:76
  71.4 2.1 %collective-permute-start.29 = (f32[24,256]{1,0:T(8,128)S(1)}, f32[24,256]{1,0:T(8,128)S(1)}, u32[]{:S(2)}, u32[]{:S(2)}) collective-permute-start(f32[24,256]{1,0:T(8,128)S(1)} %spread.1.refs_0_), channel_id=1, source_target_pairs={{0,24},{4,28},{8,16},{12,20},{16,8},{20,12},{24,0},{28,4},{1,25},{... | collective-permute-start | bytes 73736 | tf_op jit(solution)/shard_map/spread/ppermute | solution.py:72
  73.5 0.8 %collective-permute-start.27 = (f32[24,256]{1,0:T(8,128)S(1)}, f32[24,256]{1,0:T(8,128)S(1)}, u32[]{:S(2)}, u32[]{:S(2)}) collective-permute-start(f32[24,256]{1,0:T(8,128)S(1)} %spread.1.refs_0_), channel_id=1, source_target_pairs={{0,16},{4,20},{8,24},{12,28},{16,0},{20,4},{24,8},{28,12},{1,17},{... | collective-permute-start | bytes 73736 | tf_op jit(solution)/shard_map/spread/ppermute | solution.py:72
  74.3 0.6 collective-permute-start.25
  75.0 1.2 %collective-permute-done.29.refs_6_ = f32[24,256]{1,0:T(8,128)S(1)} collective-permute-done((f32[24,256]{1,0:T(8,128)S(1)}, f32[24,256]{1,0:T(8,128)S(1)}, u32[]{:S(2)}, u32[]{:S(2)}) %collective-permute-start.29) | collective-permute-done | bytes 24608 | tf_op jit(solution)/shard_map/spread/ppermute | solution.py:72
  76.2 1.1 %collective-permute-done.27.refs_4_ = f32[24,256]{1,0:T(8,128)S(1)} collective-permute-done((f32[24,256]{1,0:T(8,128)S(1)}, f32[24,256]{1,0:T(8,128)S(1)}, u32[]{:S(2)}, u32[]{:S(2)}) %collective-permute-start.27) | collective-permute-done | bytes 24608 | tf_op jit(solution)/shard_map/spread/ppermute | solution.py:72
  77.3 0.8 %collective-permute-done.25.refs_2_ = f32[24,256]{1,0:T(8,128)S(1)} collective-permute-done((f32[24,256]{1,0:T(8,128)S(1)}, f32[24,256]{1,0:T(8,128)S(1)}, u32[]{:S(2)}, u32[]{:S(2)}) %collective-permute-start.25) | collective-permute-done | bytes 24608 | tf_op jit(solution)/shard_map/spread/ppermute | solution.py:72
  78.1 0.4 collective-permute-done.28.refs_5_
  78.5 0.8 %collective-permute-done.26.refs_3_ = f32[24,256]{1,0:T(8,128)S(1)} collective-permute-done((f32[24,256]{1,0:T(8,128)S(1)}, f32[24,256]{1,0:T(8,128)S(1)}, u32[]{:S(2)}, u32[]{:S(2)}) %collective-permute-start.26) | collective-permute-done | bytes 24608 | tf_op jit(solution)/shard_map/spread/ppermute | solution.py:72
  79.3 0.7 finish.1
  80.1 1.5 %rows_out.1 = (f32[128,256]{1,0:T(8,128)}, f32[128,256]{1,0:T(8,128)}) custom-call(s32[3]{0:T(128)S(1)} %copy-done.5, s32[3]{0:T(128)S(1)} %copy-done.6, s32[3]{0:T(128)S(1)} %copy-done.7, bf16[256,256]{1,0:T(8,128)(2,1)S(1)} %get-tuple-element.47.th, bf16[256,256]{1,0:T(8,128)(2,1)S(1)} %get-tuple-element.48.tl, f32[96,512]{1,0:T(8,128)S(1)} %get-tuple-element.69.kept, ...), custom_call_target="tpu_custom_call" | custom-call | bytes 917540 | tf_op jit(solution)/shard_map/rows_out/pallas_call | solution.py:38
  (41 shorter events, 0.2 us)
Async XLA Ops:
  2.4 28.4 %collective-permute-start.1 = (f32[448,128]{1,0:T(8,128)}, f32[448,128]{1,0:T(8,128)S(1)}, u32[]{:S(2)}, u32[]{:S(2)}) collective-permute-start(f32[448,128]{1,0:T(8,128)} %get-tuple-element.43.refs_0_), channel_id=1, source_target_pairs={{0,2},{1,3},{2,0},{3,1},{4,6},{5,7},{6,4},{7,5},{8,10},{9,11},{10,... | collective-permute-start | bytes 688136 | tf_op jit(solution)/shard_map/owned/ppermute | solution.py:76
  6.5 9.1 %collective-permute-start.4 = (f32[104,128]{1,0:T(8,128)}, f32[104,128]{1,0:T(8,128)S(1)}, u32[]{:S(2)}, u32[]{:S(2)}) collective-permute-start(f32[104,128]{1,0:T(8,128)} %get-tuple-element.49), channel_id=1, source_target_pairs={{0,0},{1,12},{2,8},{3,4},{4,1},{5,13},{6,9},{7,5},{8,2},{9,14},{10... | collective-permute-start | bytes 159752 | tf_op jit(solution)/shard_map/scatter/ppermute | solution.py:373
  8.0 12.5 %collective-permute-start.5 = (f32[104,128]{1,0:T(8,128)}, f32[104,128]{1,0:T(8,128)S(1)}, u32[]{:S(2)}, u32[]{:S(2)}) collective-permute-start(f32[104,128]{1,0:T(8,128)} %get-tuple-element.50), channel_id=1, source_target_pairs={{0,4},{1,0},{2,12},{3,8},{4,5},{5,1},{6,13},{7,9},{8,6},{9,2},{10,... | collective-permute-start | bytes 159752 | tf_op jit(solution)/shard_map/scatter/ppermute | solution.py:373
  10.2 15.7 %collective-permute-start.6 = (f32[104,128]{1,0:T(8,128)}, f32[104,128]{1,0:T(8,128)S(1)}, u32[]{:S(2)}, u32[]{:S(2)}) collective-permute-start(f32[104,128]{1,0:T(8,128)} %get-tuple-element.51), channel_id=1, source_target_pairs={{0,8},{1,4},{2,0},{3,12},{4,9},{5,5},{6,1},{7,13},{8,10},{9,6},{10... | collective-permute-start | bytes 159752 | tf_op jit(solution)/shard_map/scatter/ppermute | solution.py:373
  15.5 10.4 %collective-permute-start.7 = (f32[104,128]{1,0:T(8,128)}, f32[104,128]{1,0:T(8,128)S(1)}, u32[]{:S(2)}, u32[]{:S(2)}) collective-permute-start(f32[104,128]{1,0:T(8,128)} %get-tuple-element.52), channel_id=1, source_target_pairs={{0,12},{1,8},{2,4},{3,0},{4,13},{5,9},{6,5},{7,1},{8,14},{9,10},{1... | collective-permute-start | bytes 159752 | tf_op jit(solution)/shard_map/scatter/ppermute | solution.py:373
  15.6 17.2 %collective-permute-start = (f32[448,128]{1,0:T(8,128)}, f32[448,128]{1,0:T(8,128)S(1)}, u32[]{:S(2)}, u32[]{:S(2)}) collective-permute-start(f32[448,128]{1,0:T(8,128)} %get-tuple-element.43.refs_0_), channel_id=1, source_target_pairs={{0,1},{1,0},{2,3},{3,2},{4,5},{5,4},{6,7},{7,6},{8,9},{9,8},{10,11... | collective-permute-start | bytes 688136 | tf_op jit(solution)/shard_map/owned/ppermute | solution.py:76
  17.1 1.6 %copy-start = (f32[4,1,128,8,1,128]{5,4,3,2,1,0:T(1,128)S(1)}, f32[4,1,128,8,1,128]{5,4,3,2,1,0:T(1,128)}, u32[]{:S(2)}) copy-start(f32[4,1,128,8,1,128]{5,4,3,2,1,0:T(1,128)} %param.10) | copy-start | bytes 6291460
  18.7 0.7 copy-start.4
  19.3 20.3 %copy-start.2 = (f32[448,128]{1,0:T(8,128)S(1)}, f32[448,128]{1,0:T(8,128)}, u32[]{:S(2)}) copy-start(f32[448,128]{1,0:T(8,128)} %get-tuple-element.43.refs_0_) | copy-start | bytes 688132
  19.3 21.9 %copy-start.1 = (f32[64,256]{1,0:T(8,128)S(1)}, f32[64,256]{1,0:T(8,128)}, u32[]{:S(2)}) copy-start(f32[64,256]{1,0:T(8,128)} %pd.3) | copy-start | bytes 196612
  26.0 10.1 %collective-permute-start.13 = (f32[392,128]{1,0:T(8,128)S(1)}, f32[392,128]{1,0:T(8,128)S(1)}, u32[]{:S(2)}, u32[]{:S(2)}) collective-permute-start(f32[392,128]{1,0:T(8,128)S(1)} %get-tuple-element.60.refs_0_), channel_id=1, source_target_pairs={{0,24},{4,28},{8,16},{12,20},{16,8},{20,12},{24,0},{28,4},{1,25},{... | collective-permute-start | bytes 602120 | tf_op jit(solution)/shard_map/panels/ppermute | solution.py:72
  30.2 8.9 %collective-permute-start.11 = (f32[392,128]{1,0:T(8,128)S(1)}, f32[392,128]{1,0:T(8,128)S(1)}, u32[]{:S(2)}, u32[]{:S(2)}) collective-permute-start(f32[392,128]{1,0:T(8,128)S(1)} %get-tuple-element.60.refs_0_), channel_id=1, source_target_pairs={{0,16},{4,20},{8,24},{12,28},{16,0},{20,4},{24,8},{28,12},{1,17},{... | collective-permute-start | bytes 602120 | tf_op jit(solution)/shard_map/panels/ppermute | solution.py:72
  30.5 8.6 %collective-permute-start.9 = (f32[392,128]{1,0:T(8,128)S(1)}, f32[392,128]{1,0:T(8,128)S(1)}, u32[]{:S(2)}, u32[]{:S(2)}) collective-permute-start(f32[392,128]{1,0:T(8,128)S(1)} %get-tuple-element.60.refs_0_), channel_id=1, source_target_pairs={{0,8},{4,12},{8,0},{12,4},{16,24},{20,28},{24,16},{28,20},{1,9},{5... | collective-permute-start | bytes 602120 | tf_op jit(solution)/shard_map/panels/ppermute | solution.py:72
  30.8 8.8 %collective-permute-start.2 = (f32[448,128]{1,0:T(8,128)S(1)}, f32[448,128]{1,0:T(8,128)S(1)}, u32[]{:S(2)}, u32[]{:S(2)}) collective-permute-start(f32[448,128]{1,0:T(8,128)S(1)} %collective-permute-done.1.refs_2_), channel_id=1, source_target_pairs={{0,1},{1,0},{2,3},{3,2},{4,5},{5,4},{6,7},{7,6},{8,9},{9,8},{10,11... | collective-permute-start | bytes 688136 | tf_op jit(solution)/shard_map/owned/ppermute | solution.py:76
  32.8 9.2 %collective-permute-start.8 = (f32[392,128]{1,0:T(8,128)S(1)}, f32[392,128]{1,0:T(8,128)S(1)}, u32[]{:S(2)}, u32[]{:S(2)}) collective-permute-start(f32[392,128]{1,0:T(8,128)S(1)} %get-tuple-element.60.refs_0_), channel_id=1, source_target_pairs={{0,4},{4,0},{8,12},{12,8},{16,20},{20,16},{24,28},{28,24},{1,5},{5... | collective-permute-start | bytes 602120 | tf_op jit(solution)/shard_map/panels/ppermute | solution.py:72
  36.1 6.0 %collective-permute-start.14 = (f32[392,128]{1,0:T(8,128)S(1)}, f32[392,128]{1,0:T(8,128)S(1)}, u32[]{:S(2)}, u32[]{:S(2)}) collective-permute-start(f32[392,128]{1,0:T(8,128)S(1)} %collective-permute-done.13.refs_6_), channel_id=1, source_target_pairs={{0,4},{4,0},{8,12},{12,8},{16,20},{20,16},{24,28},{28,24},{1,5},{5... | collective-permute-start | bytes 602120 | tf_op jit(solution)/shard_map/panels/ppermute | solution.py:72
  39.1 3.0 %collective-permute-start.12 = (f32[392,128]{1,0:T(8,128)S(1)}, f32[392,128]{1,0:T(8,128)S(1)}, u32[]{:S(2)}, u32[]{:S(2)}) collective-permute-start(f32[392,128]{1,0:T(8,128)S(1)} %collective-permute-done.11.refs_4_), channel_id=1, source_target_pairs={{0,4},{4,0},{8,12},{12,8},{16,20},{20,16},{24,28},{28,24},{1,5},{5... | collective-permute-start | bytes 602120 | tf_op jit(solution)/shard_map/panels/ppermute | solution.py:72
  39.1 3.0 %collective-permute-start.10 = (f32[392,128]{1,0:T(8,128)S(1)}, f32[392,128]{1,0:T(8,128)S(1)}, u32[]{:S(2)}, u32[]{:S(2)}) collective-permute-start(f32[392,128]{1,0:T(8,128)S(1)} %collective-permute-done.9.refs_2_), channel_id=1, source_target_pairs={{0,4},{4,0},{8,12},{12,8},{16,20},{20,16},{24,28},{28,24},{1,5},{5... | collective-permute-start | bytes 602120 | tf_op jit(solution)/shard_map/panels/ppermute | solution.py:72
  39.9 1.4 %collective-permute-start.3 = (f32[256,128]{1,0:T(8,128)S(1)}, f32[256,128]{1,0:T(8,128)S(1)}, u32[]{:S(2)}, u32[]{:S(2)}) collective-permute-start(f32[256,128]{1,0:T(8,128)S(1)} %get-tuple-element.46.mine), channel_id=1, source_target_pairs={{0,4},{4,0},{8,12},{12,8},{16,20},{20,16},{24,28},{28,24},{1,5},{5... | collective-permute-start | bytes 393224 | tf_op jit(solution)/shard_map/collect/ppermute | solution.py:72
  46.1 33.2 %copy-start.3 = (f32[64,256]{1,0:T(8,128)S(1)}, f32[64,256]{1,0:T(8,128)}, u32[]{:S(2)}) copy-start(f32[64,256]{1,0:T(8,128)} %cd.1) | copy-start | bytes 196612
  46.1 33.9 %copy-start.5 = (s32[3]{0:T(128)S(1)}, s32[3]{0:T(128)}, u32[]{:S(2)}) copy-start(s32[3]{0:T(128)} %blocks.3) | copy-start | bytes 40
  46.2 33.9 %copy-start.6 = (s32[3]{0:T(128)S(1)}, s32[3]{0:T(128)}, u32[]{:S(2)}) copy-start(s32[3]{0:T(128)} %psize.1) | copy-start | bytes 40
  46.2 33.9 %copy-start.7 = (s32[3]{0:T(128)S(1)}, s32[3]{0:T(128)}, u32[]{:S(2)}) copy-start(s32[3]{0:T(128)} %csize.1) | copy-start | bytes 40
  46.2 1.8 %collective-permute-start.15 = (f32[384,256]{1,0:T(8,128)S(1)}, f32[384,256]{1,0:T(8,128)S(1)}, u32[]{:S(2)}, u32[]{:S(2)}) collective-permute-start(f32[384,256]{1,0:T(8,128)S(1)} %get-tuple-element.62), channel_id=1, source_target_pairs={{0,4},{4,0},{8,12},{12,8},{16,20},{20,16},{24,28},{28,24},{1,5},{5... | collective-permute-start | bytes 1179656 | tf_op jit(solution)/shard_map/sum_core/ppermute | solution.py:72
  46.4 11.4 %collective-permute-start.19 = (f32[192,512]{1,0:T(8,128)S(1)}, f32[192,512]{1,0:T(8,128)S(1)}, u32[]{:S(2)}, u32[]{:S(2)}) collective-permute-start(f32[192,512]{1,0:T(8,128)S(1)} %get-tuple-element.68), channel_id=1, source_target_pairs={{0,1},{1,0},{2,3},{3,2},{4,5},{5,4},{6,7},{7,6},{8,9},{9,8},{10,11... | collective-permute-start | bytes 1179656 | tf_op jit(solution)/shard_map/sum_shares/ppermute | solution.py:76
  48.0 9.8 %collective-permute-start.16 = (f32[96,256]{1,0:T(8,128)S(1)}, f32[96,256]{1,0:T(8,128)S(1)}, u32[]{:S(2)}, u32[]{:S(2)}) collective-permute-start(f32[96,256]{1,0:T(8,128)S(1)} %get-tuple-element.64), channel_id=1, source_target_pairs={{0,8},{4,12},{8,0},{12,4},{16,24},{20,28},{24,16},{28,20},{1,9},{5... | collective-permute-start | bytes 294920 | tf_op jit(solution)/shard_map/sum_chips/ppermute | solution.py:72
  49.5 8.3 %collective-permute-start.17 = (f32[96,256]{1,0:T(8,128)S(1)}, f32[96,256]{1,0:T(8,128)S(1)}, u32[]{:S(2)}, u32[]{:S(2)}) collective-permute-start(f32[96,256]{1,0:T(8,128)S(1)} %get-tuple-element.65), channel_id=1, source_target_pairs={{0,16},{4,20},{8,24},{12,28},{16,0},{20,4},{24,8},{28,12},{1,17},{... | collective-permute-start | bytes 294920 | tf_op jit(solution)/shard_map/sum_chips/ppermute | solution.py:72
  50.5 7.3 %collective-permute-start.18 = (f32[96,256]{1,0:T(8,128)S(1)}, f32[96,256]{1,0:T(8,128)S(1)}, u32[]{:S(2)}, u32[]{:S(2)}) collective-permute-start(f32[96,256]{1,0:T(8,128)S(1)} %get-tuple-element.66), channel_id=1, source_target_pairs={{0,24},{4,28},{8,16},{12,20},{16,8},{20,12},{24,0},{28,4},{1,25},{... | collective-permute-start | bytes 294920 | tf_op jit(solution)/shard_map/sum_chips/ppermute | solution.py:72
  57.9 22.2 %collective-permute-start.20 = (f32[96,512]{1,0:T(8,128)S(1)}, f32[96,512]{1,0:T(8,128)S(1)}, u32[]{:S(2)}, u32[]{:S(2)}) collective-permute-start(f32[96,512]{1,0:T(8,128)S(1)} %get-tuple-element.70), channel_id=1, source_target_pairs={{0,2},{1,3},{2,0},{3,1},{4,6},{5,7},{6,4},{7,5},{8,10},{9,11},{10,... | collective-permute-start | bytes 589832 | tf_op jit(solution)/shard_map/sum_cols/ppermute | solution.py:76
  60.7 5.0 %collective-permute-start.21 = (f32[24,256]{1,0:T(8,128)S(1)}, f32[24,256]{1,0:T(8,128)S(1)}, u32[]{:S(2)}, u32[]{:S(2)}) collective-permute-start(f32[24,256]{1,0:T(8,128)S(1)} %get-tuple-element.74), channel_id=1, source_target_pairs={{0,1},{1,0},{2,3},{3,2},{4,5},{5,4},{6,7},{7,6},{8,9},{9,8},{10,11... | collective-permute-start | bytes 73736 | tf_op jit(solution)/shard_map/sum_cols/ppermute | solution.py:76
  61.6 9.7 %collective-permute-start.22 = (f32[24,256]{1,0:T(8,128)S(1)}, f32[24,256]{1,0:T(8,128)S(1)}, u32[]{:S(2)}, u32[]{:S(2)}) collective-permute-start(f32[24,256]{1,0:T(8,128)S(1)} %get-tuple-element.75), channel_id=1, source_target_pairs={{0,2},{1,3},{2,0},{3,1},{4,6},{5,7},{6,4},{7,5},{8,10},{9,11},{10,... | collective-permute-start | bytes 73736 | tf_op jit(solution)/shard_map/sum_cols/ppermute | solution.py:76
  61.7 9.7 %collective-permute-start.23 = (f32[24,256]{1,0:T(8,128)S(1)}, f32[24,256]{1,0:T(8,128)S(1)}, u32[]{:S(2)}, u32[]{:S(2)}) collective-permute-start(f32[24,256]{1,0:T(8,128)S(1)} %get-tuple-element.76), channel_id=1, source_target_pairs={{0,3},{1,2},{2,1},{3,0},{4,7},{5,6},{6,5},{7,4},{8,11},{9,10},{10,... | collective-permute-start | bytes 73736 | tf_op jit(solution)/shard_map/sum_cols/ppermute | solution.py:76
  71.4 4.8 %collective-permute-start.29 = (f32[24,256]{1,0:T(8,128)S(1)}, f32[24,256]{1,0:T(8,128)S(1)}, u32[]{:S(2)}, u32[]{:S(2)}) collective-permute-start(f32[24,256]{1,0:T(8,128)S(1)} %spread.1.refs_0_), channel_id=1, source_target_pairs={{0,24},{4,28},{8,16},{12,20},{16,8},{20,12},{24,0},{28,4},{1,25},{... | collective-permute-start | bytes 73736 | tf_op jit(solution)/shard_map/spread/ppermute | solution.py:72
  73.5 3.8 %collective-permute-start.27 = (f32[24,256]{1,0:T(8,128)S(1)}, f32[24,256]{1,0:T(8,128)S(1)}, u32[]{:S(2)}, u32[]{:S(2)}) collective-permute-start(f32[24,256]{1,0:T(8,128)S(1)} %spread.1.refs_0_), channel_id=1, source_target_pairs={{0,16},{4,20},{8,24},{12,28},{16,0},{20,4},{24,8},{28,12},{1,17},{... | collective-permute-start | bytes 73736 | tf_op jit(solution)/shard_map/spread/ppermute | solution.py:72
  74.3 3.8 %collective-permute-start.25 = (f32[24,256]{1,0:T(8,128)S(1)}, f32[24,256]{1,0:T(8,128)S(1)}, u32[]{:S(2)}, u32[]{:S(2)}) collective-permute-start(f32[24,256]{1,0:T(8,128)S(1)} %spread.1.refs_0_), channel_id=1, source_target_pairs={{0,8},{4,12},{8,0},{12,4},{16,24},{20,28},{24,16},{28,20},{1,9},{5... | collective-permute-start | bytes 73736 | tf_op jit(solution)/shard_map/spread/ppermute | solution.py:72
  75.0 3.2 %collective-permute-start.24 = (f32[24,256]{1,0:T(8,128)S(1)}, f32[24,256]{1,0:T(8,128)S(1)}, u32[]{:S(2)}, u32[]{:S(2)}) collective-permute-start(f32[24,256]{1,0:T(8,128)S(1)} %spread.1.refs_0_), channel_id=1, source_target_pairs={{0,4},{4,0},{8,12},{12,8},{16,20},{20,16},{24,28},{28,24},{1,5},{5... | collective-permute-start | bytes 73736 | tf_op jit(solution)/shard_map/spread/ppermute | solution.py:72
  76.2 2.0 %collective-permute-start.30 = (f32[24,256]{1,0:T(8,128)S(1)}, f32[24,256]{1,0:T(8,128)S(1)}, u32[]{:S(2)}, u32[]{:S(2)}) collective-permute-start(f32[24,256]{1,0:T(8,128)S(1)} %collective-permute-done.29.refs_6_), channel_id=1, source_target_pairs={{0,4},{4,0},{8,12},{12,8},{16,20},{20,16},{24,28},{28,24},{1,5},{5... | collective-permute-start | bytes 73736 | tf_op jit(solution)/shard_map/spread/ppermute | solution.py:72
  77.3 1.2 %collective-permute-start.28 = (f32[24,256]{1,0:T(8,128)S(1)}, f32[24,256]{1,0:T(8,128)S(1)}, u32[]{:S(2)}, u32[]{:S(2)}) collective-permute-start(f32[24,256]{1,0:T(8,128)S(1)} %collective-permute-done.27.refs_4_), channel_id=1, source_target_pairs={{0,4},{4,0},{8,12},{12,8},{16,20},{20,16},{24,28},{28,24},{1,5},{5... | collective-permute-start | bytes 73736 | tf_op jit(solution)/shard_map/spread/ppermute | solution.py:72
  78.1 1.2 %collective-permute-start.26 = (f32[24,256]{1,0:T(8,128)S(1)}, f32[24,256]{1,0:T(8,128)S(1)}, u32[]{:S(2)}, u32[]{:S(2)}) collective-permute-start(f32[24,256]{1,0:T(8,128)S(1)} %collective-permute-done.25.refs_2_), channel_id=1, source_target_pairs={{0,4},{4,0},{8,12},{12,8},{16,20},{20,16},{24,28},{28,24},{1,5},{5... | collective-permute-start | bytes 73736 | tf_op jit(solution)/shard_map/spread/ppermute | solution.py:72

commit v3 on v2

--- a/solution.py
+++ b/solution.py
@@ -31,7 +31,11 @@
     )
 
 
-def call(kernel, inputs, outs, scratch=(), flops=0, limit=40, alias=None):
+def call(kernel, inputs, outs, scratch=(), flops=0, limit=40, passed=()):
+    alias = {len(inputs) + i: len(outs) + i for i in range(len(passed))}
+    spaces = [pltpu.VMEM] * len(outs) + [pl.ANY] * len(passed)
+    inputs = list(inputs) + [(pl.ANY, a) for a in passed]
+    outs = list(outs) + [(a.shape, a.dtype) for a in passed]
     arrays = [a for _, a in inputs]
     shapes = [jax.ShapeDtypeStruct(*(o if isinstance(o[0], tuple) else (o, f32))) for o in outs]
     nbytes = sum(a.size * a.dtype.itemsize for a in arrays + shapes)
@@ -39,9 +43,9 @@
         kernel,
         out_shape=shapes,
         in_specs=[pl.BlockSpec(memory_space=space) for space, _ in inputs],
-        out_specs=[pl.BlockSpec(memory_space=pltpu.VMEM)] * len(outs),
+        out_specs=[pl.BlockSpec(memory_space=space) for space in spaces],
         scratch_shapes=list(scratch),
-        input_output_aliases=alias or {},
+        input_output_aliases=alias,
         compiler_params=pltpu.CompilerParams(vmem_limit_bytes=limit and limit * 1024 * 1024),
         cost_estimate=pl.CostEstimate(flops=flops, bytes_accessed=nbytes, transcendentals=0),
     )(*arrays)
@@ -260,8 +264,7 @@
 
 
 def add_cols(s, *refs):
-    terms, (kept, got), refs = refs[: s.chips], refs[s.chips : s.chips + 2], refs[s.chips + 2 :]
-    outs, (stay, leave, total) = refs[: s.C], refs[s.C :]
+    terms, outs, total = refs[: s.chips], refs[s.chips : -1], refs[-1]
     size = 3 * s.eight
     col = lax.axis_index("col")
     value = terms[0][...]
@@ -271,7 +274,6 @@
     for mask in range(s.C):
         rows = pl.ds(pl.multiple_of(jnp.bitwise_xor(col, mask) * size, size), size)
         outs[mask][...] = total[rows, :]
-    halve(s, kept, got, stay, leave)
 
 
 def halve(s, kept, got, stay, leave):
@@ -283,14 +285,16 @@
 
 
 def add_all(s, *refs):
-    value = refs[0][...]
-    for term in refs[1:-1]:
+    terms, (kept, got, out, stay, leave) = refs[: s.C], refs[s.C :]
+    value = terms[0][...]
+    for term in terms[1:]:
         value = value + term[...]
-    refs[-1][...] = value
+    out[...] = value
+    halve(s, kept, got, stay, leave)
 
 
 def finish(s, pd, cd, base, *refs):
-    parts, outs = refs[: s.R], refs[s.R :]
+    parts, outs = refs[: s.R], refs[s.R + 2 : s.R + 5]
     row = lax.axis_index("row")
     n = s.eight
     starts = (pd, base, cd)
@@ -388,9 +392,9 @@
     with jax.named_scope("join"):
         own, sh, sl = call(
             bind(join),
-            vmem(*pieces, sh, sl),
-            [(s.block, B), (sh.shape, bf16), (sl.shape, bf16)],
-            alias={C: 1, C + 1: 2},
+            vmem(*pieces),
+            [(s.block, B)],
+            passed=(sh, sl),
         )
     with jax.named_scope("panels"):
         panels = {0: own}
@@ -432,14 +436,15 @@
         mine = [mine[0]] + [exchange(mine[m], 2 * m, R) for m in range(1, s.chips)]
     with jax.named_scope("sum_cols"):
         scr = [pltpu.VMEM((C * 3 * s.eight, W), f32)]
+        cols = call(bind(add_cols), vmem(*mine), [(3 * s.eight, W)] * C, scr)
+        cols = [cols[0]] + [flip(cols[m], m, C) for m in range(1, C)]
+    with jax.named_scope("spread"):
         half //= 2
-        *cols, stay, leave = call(
-            bind(add_cols),
-            vmem(*mine, stay, got_rows),
-            [(3 * s.eight, W)] * C + [(half, 2 * W)] * 2,
-            scr,
-        )
-        cols = [cols[0]] + [flip(cols[m], m, C) for m in range(1, C)]
+        done, stay, leave = call(
+            bind(add_all),
+            vmem(*cols, stay, got_rows),
+            [(3 * s.eight, W)] + [(half, 2 * W)] * 2,
+        )
         got_rows = flip(leave, 2, C)
         mask = 4
         while mask < C:
@@ -447,8 +452,6 @@
             stay, leave = call(bind(halve), vmem(stay, got_rows), [(half, 2 * W)] * 2)
             got_rows = flip(leave, mask, C)
             mask *= 2
-    with jax.named_scope("spread"):
-        (done,) = call(bind(add_all), vmem(*cols), [(3 * s.eight, W)])
         parts = {0: done}
         for mask in range(2, R, 2):
             parts[mask] = exchange(done, mask, R)
@@ -461,10 +464,11 @@
             [(s.RC * s.share, W)] * 2,
         )
     with jax.named_scope("finish"):
-        parent_diag, child_upper, child_diag = call(
+        parent_diag, child_upper, child_diag, parent_rows, child_rows = call(
             bind(finish),
             vmem(parent_diagonal, child_diagonal, base, *[parts[m] for m in range(R)]),
             [(ws, W)] * 3,
+            passed=(parent_rows, child_rows),
         )
     shape = (s.RC, 1, s.share, W)
     return (

time: 81.8 us -> 76.2 us (0.932)
  waiting for transfers between devices: 31 us -> 27.7 us
  starting transfers between devices: 37.1 us -> 34.7 us
    ppermute x8, waiting for transfers between devices: 12.5 us -> 6.92 us  [flip(): return lax.ppermute(value, 'col', [(i, i ^ mask) for i in range(col_total)])]
    ppermute x8, starting transfers between devices: 15.2 us -> 12.5 us  [flip(): return lax.ppermute(value, 'col', [(i, i ^ mask) for i in range(col_total)])]
    ppermute x19, waiting for transfers between devices: 13.1 us -> 15.4 us  [exchange(): return lax.ppermute(value, 'row', [(i, i ^ mask) for i in range(row_total)])]
  transfers between devices with their start and end apart: 31 -> 31, of which waited for: 13 -> 13; matrix products, arithmetic and copies ran while one was open for 0% -> 0% of each run, Pallas kernels for 4% -> 5%
where the time goes in v3:
time: 76.2 us; the launch traced here: 75.9 us
  starting transfers between devices  34.7 us (46%)
  waiting for transfers between devices  27.7 us (36%)
  Pallas kernels  10.4 us (14%)
  local copies, waits for them, and re-layouts  2.28 us (3%)
  between operations  0.84 us (1%)
    ppermute x19, waiting for transfers between devices, exchange(): return lax.ppermute(value, 'row', [(i, i ^ mask) for i in range(row_total)])  15.4 us
    ppermute x19, starting transfers between devices, exchange(): return lax.ppermute(value, 'row', [(i, i ^ mask) for i in range(row_total)])  13 us
    ppermute x8, starting transfers between devices, flip(): return lax.ppermute(value, 'col', [(i, i ^ mask) for i in range(col_total)])  12.5 us
    pallas_call x11, Pallas kernels, call(): pl.pallas_call(kernel, out_shape=shapes, in_specs=[pl.BlockSpec(memory_sp...  10.4 us
    ppermute x4, starting transfers between devices, fast_body(): lax.ppermute(sends[t], ('row', 'col'), scatter_perm(s, t))  9.07 us
    ppermute x8, waiting for transfers between devices, flip(): return lax.ppermute(value, 'col', [(i, i ^ mask) for i in range(col_total)])  6.92 us
    ppermute x4, waiting for transfers between devices, fast_body(): lax.ppermute(sends[t], ('row', 'col'), scatter_perm(s, t))  5.42 us
    unnamed x16, local copies, waits for them, and re-layouts  2.28 us
  transfers between devices with their start and end apart: 31, of which 13 were waited for; matrix products, arithmetic and copies ran while one was open for 0% of the time, Pallas kernels for 5%

profile of v3, /device:TPU:0, one launch (start us, length us, event | category | flops | bytes accessed | tf_op | source)
XLA Modules:
  0.0 75.9 jit_solution(17721887569520431443)
XLA Ops:
  0.6 1.8 %pack.1 = (f32[104,128]{1,0:T(8,128)}, f32[104,128]{1,0:T(8,128)}, f32[104,128]{1,0:T(8,128)}, f32[104,128]{1,0:T(8,128)}, f32[448,128]{1,0:T(8,128)}) custom-call(s32[3]{0:T(128)} %blocks.3, s32[3]{0:T(128)} %psize.1, s32[3]{0:T(128)} %csize.1, f32[3,64,128]{2,1,0:T(8,128)} %bitcast.12, f32[3,64,128]{2,1,0:T(8,128)} %bitcast.13, f32[64,256]{1,0:T(8,128)} %refs_5_.1), custom_call_target="tpu_custom_call" | custom-call | bytes 704548 | tf_op jit(solution)/shard_map/pack/pallas_call | solution.py:42
  2.4 4.1 %collective-permute-start.1 = (f32[448,128]{1,0:T(8,128)}, f32[448,128]{1,0:T(8,128)S(1)}, u32[]{:S(2)}, u32[]{:S(2)}) collective-permute-start(f32[448,128]{1,0:T(8,128)} %get-tuple-element.46.refs_0_), channel_id=1, source_target_pairs={{0,2},{1,3},{2,0},{3,1},{4,6},{5,7},{6,4},{7,5},{8,10},{9,11},{10,... | collective-permute-start | bytes 688136 | tf_op jit(solution)/shard_map/owned/ppermute | solution.py:80
  6.5 1.5 %collective-permute-start.4 = (f32[104,128]{1,0:T(8,128)}, f32[104,128]{1,0:T(8,128)S(1)}, u32[]{:S(2)}, u32[]{:S(2)}) collective-permute-start(f32[104,128]{1,0:T(8,128)} %get-tuple-element.51), channel_id=1, source_target_pairs={{0,0},{1,12},{2,8},{3,4},{4,1},{5,13},{6,9},{7,5},{8,2},{9,14},{10... | collective-permute-start | bytes 159752 | tf_op jit(solution)/shard_map/scatter/ppermute | solution.py:377
  8.0 2.2 %collective-permute-start.5 = (f32[104,128]{1,0:T(8,128)}, f32[104,128]{1,0:T(8,128)S(1)}, u32[]{:S(2)}, u32[]{:S(2)}) collective-permute-start(f32[104,128]{1,0:T(8,128)} %get-tuple-element.52), channel_id=1, source_target_pairs={{0,4},{1,0},{2,12},{3,8},{4,5},{5,1},{6,13},{7,9},{8,6},{9,2},{10,... | collective-permute-start | bytes 159752 | tf_op jit(solution)/shard_map/scatter/ppermute | solution.py:377
  10.2 5.4 %collective-permute-start.6 = (f32[104,128]{1,0:T(8,128)}, f32[104,128]{1,0:T(8,128)S(1)}, u32[]{:S(2)}, u32[]{:S(2)}) collective-permute-start(f32[104,128]{1,0:T(8,128)} %get-tuple-element.53), channel_id=1, source_target_pairs={{0,8},{1,4},{2,0},{3,12},{4,9},{5,5},{6,1},{7,13},{8,10},{9,6},{10... | collective-permute-start | bytes 159752 | tf_op jit(solution)/shard_map/scatter/ppermute | solution.py:377
  15.5 0.1 collective-permute-start.7
  15.6 1.5 %collective-permute-start = (f32[448,128]{1,0:T(8,128)}, f32[448,128]{1,0:T(8,128)S(1)}, u32[]{:S(2)}, u32[]{:S(2)}) collective-permute-start(f32[448,128]{1,0:T(8,128)} %get-tuple-element.46.refs_0_), channel_id=1, source_target_pairs={{0,1},{1,0},{2,3},{3,2},{4,5},{5,4},{6,7},{7,6},{8,9},{9,8},{10,11... | collective-permute-start | bytes 688136 | tf_op jit(solution)/shard_map/owned/ppermute | solution.py:80
  17.1 1.6 %copy-done = f32[4,1,128,8,1,128]{5,4,3,2,1,0:T(1,128)S(1)} copy-done((f32[4,1,128,8,1,128]{5,4,3,2,1,0:T(1,128)S(1)}, f32[4,1,128,8,1,128]{5,4,3,2,1,0:T(1,128)}, u32[]{:S(2)}) %copy-start) | copy-done | bytes 2097176
  18.7 0.7 copy-done.4
  19.3 1.2 %split_live.1 = (bf16[384,1024]{1,0:T(8,128)(2,1)S(1)}, bf16[384,1024]{1,0:T(8,128)(2,1)S(1)}) custom-call(f32[4096,128]{1,0:T(8,128)S(1)} %bitcast.9, s32[3]{0:T(128)S(1)} %copy-done.4), custom_call_target="tpu_custom_call" | custom-call | bytes 3670028 | tf_op jit(solution)/shard_map/split_live/pallas_call | solution.py:42
  20.5 5.4 %collective-permute-done.6.refs_2_ = f32[104,128]{1,0:T(8,128)S(1)} collective-permute-done((f32[104,128]{1,0:T(8,128)}, f32[104,128]{1,0:T(8,128)S(1)}, u32[]{:S(2)}, u32[]{:S(2)}) %collective-permute-start.6) | collective-permute-done | bytes 53280 | tf_op jit(solution)/shard_map/scatter/ppermute | solution.py:377
  26.0 4.2 %collective-permute-start.13 = (f32[392,128]{1,0:T(8,128)S(1)}, f32[392,128]{1,0:T(8,128)S(1)}, u32[]{:S(2)}, u32[]{:S(2)}) collective-permute-start(f32[392,128]{1,0:T(8,128)S(1)} %get-tuple-element.64.refs_0_), channel_id=1, source_target_pairs={{0,24},{4,28},{8,16},{12,20},{16,8},{20,12},{24,0},{28,4},{1,25},{... | collective-permute-start | bytes 602120 | tf_op jit(solution)/shard_map/panels/ppermute | solution.py:76
  30.2 0.3 collective-permute-start.11
  30.5 0.3 collective-permute-start.9
  30.8 2.0 %collective-permute-start.2 = (f32[448,128]{1,0:T(8,128)S(1)}, f32[448,128]{1,0:T(8,128)S(1)}, u32[]{:S(2)}, u32[]{:S(2)}) collective-permute-start(f32[448,128]{1,0:T(8,128)S(1)} %collective-permute-done.1.refs_2_), channel_id=1, source_target_pairs={{0,1},{1,0},{2,3},{3,2},{4,5},{5,4},{6,7},{7,6},{8,9},{9,8},{10,11... | collective-permute-start | bytes 688136 | tf_op jit(solution)/shard_map/owned/ppermute | solution.py:80
  32.8 3.2 %collective-permute-done.13.refs_6_ = f32[392,128]{1,0:T(8,128)S(1)} collective-permute-done((f32[392,128]{1,0:T(8,128)S(1)}, f32[392,128]{1,0:T(8,128)S(1)}, u32[]{:S(2)}, u32[]{:S(2)}) %collective-permute-start.13) | collective-permute-done | bytes 200736 | tf_op jit(solution)/shard_map/panels/ppermute | solution.py:76
  36.0 3.0 %collective-permute-done.11.refs_4_ = f32[392,128]{1,0:T(8,128)S(1)} collective-permute-done((f32[392,128]{1,0:T(8,128)S(1)}, f32[392,128]{1,0:T(8,128)S(1)}, u32[]{:S(2)}, u32[]{:S(2)}) %collective-permute-start.11) | collective-permute-done | bytes 200736 | tf_op jit(solution)/shard_map/panels/ppermute | solution.py:76
  39.1 0.5 collective-permute-start.10
  39.6 0.3 collect.1
  39.8 0.1 collective-permute-start.3
  39.9 1.3 %collective-permute-done.3.theirs = f32[256,128]{1,0:T(8,128)S(1)} collective-permute-done((f32[256,128]{1,0:T(8,128)S(1)}, f32[256,128]{1,0:T(8,128)S(1)}, u32[]{:S(2)}, u32[]{:S(2)}) %collective-permute-start.3) | collective-permute-done | bytes 131104 | tf_op jit(solution)/shard_map/collect/ppermute | solution.py:76
  41.3 0.8 own_panels.1
  42.1 4.1 %products.1 = (f32[192,512]{1,0:T(8,128)S(1)}, f32[192,512]{1,0:T(8,128)S(1)}, f32[384,256]{1,0:T(8,128)S(1)}, f32[384,256]{1,0:T(8,128)S(1)}) custom-call(bf16[384,1024]{1,0:T(8,128)(2,1)S(1)} %get-tuple-element.57.sh, bf16[384,1024]{1,0:T(8,128)(2,1)S(1)} %get-tuple-element.58.sl, bf16[512,384]{1,0:T(8,128)(2,1)S(1)} %get-tuple-element.47.lh, ...), custom_call_target="tpu_custom_call" | custom-call | flops 1207959552 | bytes 6455296 | tf_op jit(solution)/shard_map/products/pallas_call | solution.py:42
  46.2 0.2 collective-permute-start.15
  46.4 0.4 collective-permute-start.22
  46.8 1.2 %collective-permute-done.15.got = f32[384,256]{1,0:T(8,128)S(1)} collective-permute-done((f32[384,256]{1,0:T(8,128)S(1)}, f32[384,256]{1,0:T(8,128)S(1)}, u32[]{:S(2)}, u32[]{:S(2)}) %collective-permute-start.15) | collective-permute-done | bytes 393248 | tf_op jit(solution)/shard_map/sum_core/ppermute | solution.py:76
  48.0 1.5 %collective-permute-start.16 = (f32[96,256]{1,0:T(8,128)S(1)}, f32[96,256]{1,0:T(8,128)S(1)}, u32[]{:S(2)}, u32[]{:S(2)}) collective-permute-start(f32[96,256]{1,0:T(8,128)S(1)} %get-tuple-element.68), channel_id=1, source_target_pairs={{0,8},{4,12},{8,0},{12,4},{16,24},{20,28},{24,16},{28,20},{1,9},{5... | collective-permute-start | bytes 294920 | tf_op jit(solution)/shard_map/sum_chips/ppermute | solution.py:76
  49.5 0.9 %collective-permute-start.17 = (f32[96,256]{1,0:T(8,128)S(1)}, f32[96,256]{1,0:T(8,128)S(1)}, u32[]{:S(2)}, u32[]{:S(2)}) collective-permute-start(f32[96,256]{1,0:T(8,128)S(1)} %get-tuple-element.69), channel_id=1, source_target_pairs={{0,16},{4,20},{8,24},{12,28},{16,0},{20,4},{24,8},{28,12},{1,17},{... | collective-permute-start | bytes 294920 | tf_op jit(solution)/shard_map/sum_chips/ppermute | solution.py:76
  50.5 1.1 %collective-permute-start.18 = (f32[96,256]{1,0:T(8,128)S(1)}, f32[96,256]{1,0:T(8,128)S(1)}, u32[]{:S(2)}, u32[]{:S(2)}) collective-permute-start(f32[96,256]{1,0:T(8,128)S(1)} %get-tuple-element.70), channel_id=1, source_target_pairs={{0,24},{4,28},{8,16},{12,20},{16,8},{20,12},{24,0},{28,4},{1,25},{... | collective-permute-start | bytes 294920 | tf_op jit(solution)/shard_map/sum_chips/ppermute | solution.py:76
  51.6 1.4 %collective-permute-done.16.refs_1_ = f32[96,256]{1,0:T(8,128)S(1)} collective-permute-done((f32[96,256]{1,0:T(8,128)S(1)}, f32[96,256]{1,0:T(8,128)S(1)}, u32[]{:S(2)}, u32[]{:S(2)}) %collective-permute-start.16) | collective-permute-done | bytes 98336 | tf_op jit(solution)/shard_map/sum_chips/ppermute | solution.py:76
  52.9 3.5 %collective-permute-done.17.refs_2_ = f32[96,256]{1,0:T(8,128)S(1)} collective-permute-done((f32[96,256]{1,0:T(8,128)S(1)}, f32[96,256]{1,0:T(8,128)S(1)}, u32[]{:S(2)}, u32[]{:S(2)}) %collective-permute-start.17) | collective-permute-done | bytes 98336 | tf_op jit(solution)/shard_map/sum_chips/ppermute | solution.py:76
  56.4 0.6 collective-permute-start.19
  57.0 3.3 %collective-permute-start.20 = (f32[24,256]{1,0:T(8,128)S(1)}, f32[24,256]{1,0:T(8,128)S(1)}, u32[]{:S(2)}, u32[]{:S(2)}) collective-permute-start(f32[24,256]{1,0:T(8,128)S(1)} %get-tuple-element.73), channel_id=1, source_target_pairs={{0,2},{1,3},{2,0},{3,1},{4,6},{5,7},{6,4},{7,5},{8,10},{9,11},{10,... | collective-permute-start | bytes 73736 | tf_op jit(solution)/shard_map/sum_cols/ppermute | solution.py:80
  60.3 0.7 collective-permute-start.21
  61.0 1.1 %collective-permute-done.20.refs_2_ = f32[24,256]{1,0:T(8,128)S(1)} collective-permute-done((f32[24,256]{1,0:T(8,128)S(1)}, f32[24,256]{1,0:T(8,128)S(1)}, u32[]{:S(2)}, u32[]{:S(2)}) %collective-permute-start.20) | collective-permute-done | bytes 24608 | tf_op jit(solution)/shard_map/sum_cols/ppermute | solution.py:80
  62.1 4.1 %collective-permute-done.21.refs_3_ = f32[24,256]{1,0:T(8,128)S(1)} collective-permute-done((f32[24,256]{1,0:T(8,128)S(1)}, f32[24,256]{1,0:T(8,128)S(1)}, u32[]{:S(2)}, u32[]{:S(2)}) %collective-permute-start.21) | collective-permute-done | bytes 24608 | tf_op jit(solution)/shard_map/sum_cols/ppermute | solution.py:80
  66.2 0.1 spread.1
  66.2 0.1 collective-permute-start.30
  66.3 1.0 %collective-permute-start.28 = (f32[24,256]{1,0:T(8,128)S(1)}, f32[24,256]{1,0:T(8,128)S(1)}, u32[]{:S(2)}, u32[]{:S(2)}) collective-permute-start(f32[24,256]{1,0:T(8,128)S(1)} %get-tuple-element.77.refs_0_), channel_id=1, source_target_pairs={{0,24},{4,28},{8,16},{12,20},{16,8},{20,12},{24,0},{28,4},{1,25},{... | collective-permute-start | bytes 73736 | tf_op jit(solution)/shard_map/spread/ppermute | solution.py:76
  67.3 0.7 collective-permute-start.26
  68.0 1.8 %collective-permute-start.24 = (f32[24,256]{1,0:T(8,128)S(1)}, f32[24,256]{1,0:T(8,128)S(1)}, u32[]{:S(2)}, u32[]{:S(2)}) collective-permute-start(f32[24,256]{1,0:T(8,128)S(1)} %get-tuple-element.77.refs_0_), channel_id=1, source_target_pairs={{0,8},{4,12},{8,0},{12,4},{16,24},{20,28},{24,16},{28,20},{1,9},{5... | collective-permute-start | bytes 73736 | tf_op jit(solution)/shard_map/spread/ppermute | solution.py:76
  69.9 1.3 %collective-permute-done.28.refs_6_ = f32[24,256]{1,0:T(8,128)S(1)} collective-permute-done((f32[24,256]{1,0:T(8,128)S(1)}, f32[24,256]{1,0:T(8,128)S(1)}, u32[]{:S(2)}, u32[]{:S(2)}) %collective-permute-start.28) | collective-permute-done | bytes 24608 | tf_op jit(solution)/shard_map/spread/ppermute | solution.py:76
  71.1 0.2 collective-permute-done.26.refs_4_
  71.4 0.3 collective-permute-start.27
  71.6 0.2 collective-permute-done.24.refs_2_
  71.9 1.7 %collective-permute-done.30.got = f32[96,512]{1,0:T(8,128)S(1)} collective-permute-done((f32[96,512]{1,0:T(8,128)S(1)}, f32[96,512]{1,0:T(8,128)S(1)}, u32[]{:S(2)}, u32[]{:S(2)}) %collective-permute-start.30) | collective-permute-done | bytes 196640 | tf_op jit(solution)/shard_map/spread/ppermute | solution.py:80
  73.6 1.5 %rows_out.1 = (f32[128,256]{1,0:T(8,128)}, f32[128,256]{1,0:T(8,128)}) custom-call(s32[3]{0:T(128)S(1)} %copy-done.5, s32[3]{0:T(128)S(1)} %copy-done.6, s32[3]{0:T(128)S(1)} %copy-done.7, bf16[256,256]{1,0:T(8,128)(2,1)S(1)} %get-tuple-element.61.th, bf16[256,256]{1,0:T(8,128)(2,1)S(1)} %get-tuple-element.62.tl, f32[96,512]{1,0:T(8,128)S(1)} %get-tuple-element.78.kept, ...), custom_call_target="tpu_custom_call" | custom-call | bytes 917540 | tf_op jit(solution)/shard_map/rows_out/pallas_call | solution.py:42
  75.1 0.7 finish.1
  (41 shorter events, 0.2 us)
Async XLA Ops:
  2.4 28.4 %collective-permute-start.1 = (f32[448,128]{1,0:T(8,128)}, f32[448,128]{1,0:T(8,128)S(1)}, u32[]{:S(2)}, u32[]{:S(2)}) collective-permute-start(f32[448,128]{1,0:T(8,128)} %get-tuple-element.46.refs_0_), channel_id=1, source_target_pairs={{0,2},{1,3},{2,0},{3,1},{4,6},{5,7},{6,4},{7,5},{8,10},{9,11},{10,... | collective-permute-start | bytes 688136 | tf_op jit(solution)/shard_map/owned/ppermute | solution.py:80
  6.5 9.1 %collective-permute-start.4 = (f32[104,128]{1,0:T(8,128)}, f32[104,128]{1,0:T(8,128)S(1)}, u32[]{:S(2)}, u32[]{:S(2)}) collective-permute-start(f32[104,128]{1,0:T(8,128)} %get-tuple-element.51), channel_id=1, source_target_pairs={{0,0},{1,12},{2,8},{3,4},{4,1},{5,13},{6,9},{7,5},{8,2},{9,14},{10... | collective-permute-start | bytes 159752 | tf_op jit(solution)/shard_map/scatter/ppermute | solution.py:377
  8.0 12.5 %collective-permute-start.5 = (f32[104,128]{1,0:T(8,128)}, f32[104,128]{1,0:T(8,128)S(1)}, u32[]{:S(2)}, u32[]{:S(2)}) collective-permute-start(f32[104,128]{1,0:T(8,128)} %get-tuple-element.52), channel_id=1, source_target_pairs={{0,4},{1,0},{2,12},{3,8},{4,5},{5,1},{6,13},{7,9},{8,6},{9,2},{10,... | collective-permute-start | bytes 159752 | tf_op jit(solution)/shard_map/scatter/ppermute | solution.py:377
  10.2 15.7 %collective-permute-start.6 = (f32[104,128]{1,0:T(8,128)}, f32[104,128]{1,0:T(8,128)S(1)}, u32[]{:S(2)}, u32[]{:S(2)}) collective-permute-start(f32[104,128]{1,0:T(8,128)} %get-tuple-element.53), channel_id=1, source_target_pairs={{0,8},{1,4},{2,0},{3,12},{4,9},{5,5},{6,1},{7,13},{8,10},{9,6},{10... | collective-permute-start | bytes 159752 | tf_op jit(solution)/shard_map/scatter/ppermute | solution.py:377
  15.5 10.4 %collective-permute-start.7 = (f32[104,128]{1,0:T(8,128)}, f32[104,128]{1,0:T(8,128)S(1)}, u32[]{:S(2)}, u32[]{:S(2)}) collective-permute-start(f32[104,128]{1,0:T(8,128)} %get-tuple-element.54), channel_id=1, source_target_pairs={{0,12},{1,8},{2,4},{3,0},{4,13},{5,9},{6,5},{7,1},{8,14},{9,10},{1... | collective-permute-start | bytes 159752 | tf_op jit(solution)/shard_map/scatter/ppermute | solution.py:377
  15.6 17.2 %collective-permute-start = (f32[448,128]{1,0:T(8,128)}, f32[448,128]{1,0:T(8,128)S(1)}, u32[]{:S(2)}, u32[]{:S(2)}) collective-permute-start(f32[448,128]{1,0:T(8,128)} %get-tuple-element.46.refs_0_), channel_id=1, source_target_pairs={{0,1},{1,0},{2,3},{3,2},{4,5},{5,4},{6,7},{7,6},{8,9},{9,8},{10,11... | collective-permute-start | bytes 688136 | tf_op jit(solution)/shard_map/owned/ppermute | solution.py:80
  17.1 1.6 %copy-start = (f32[4,1,128,8,1,128]{5,4,3,2,1,0:T(1,128)S(1)}, f32[4,1,128,8,1,128]{5,4,3,2,1,0:T(1,128)}, u32[]{:S(2)}) copy-start(f32[4,1,128,8,1,128]{5,4,3,2,1,0:T(1,128)} %param.10) | copy-start | bytes 6291460
  18.7 0.7 copy-start.4
  19.3 20.3 %copy-start.2 = (f32[448,128]{1,0:T(8,128)S(1)}, f32[448,128]{1,0:T(8,128)}, u32[]{:S(2)}) copy-start(f32[448,128]{1,0:T(8,128)} %get-tuple-element.46.refs_0_) | copy-start | bytes 688132
  19.3 21.9 %copy-start.1 = (f32[64,256]{1,0:T(8,128)S(1)}, f32[64,256]{1,0:T(8,128)}, u32[]{:S(2)}) copy-start(f32[64,256]{1,0:T(8,128)} %pd.3) | copy-start | bytes 196612
  26.0 10.1 %collective-permute-start.13 = (f32[392,128]{1,0:T(8,128)S(1)}, f32[392,128]{1,0:T(8,128)S(1)}, u32[]{:S(2)}, u32[]{:S(2)}) collective-permute-start(f32[392,128]{1,0:T(8,128)S(1)} %get-tuple-element.64.refs_0_), channel_id=1, source_target_pairs={{0,24},{4,28},{8,16},{12,20},{16,8},{20,12},{24,0},{28,4},{1,25},{... | collective-permute-start | bytes 602120 | tf_op jit(solution)/shard_map/panels/ppermute | solution.py:76
  30.2 8.9 %collective-permute-start.11 = (f32[392,128]{1,0:T(8,128)S(1)}, f32[392,128]{1,0:T(8,128)S(1)}, u32[]{:S(2)}, u32[]{:S(2)}) collective-permute-start(f32[392,128]{1,0:T(8,128)S(1)} %get-tuple-element.64.refs_0_), channel_id=1, source_target_pairs={{0,16},{4,20},{8,24},{12,28},{16,0},{20,4},{24,8},{28,12},{1,17},{... | collective-permute-start | bytes 602120 | tf_op jit(solution)/shard_map/panels/ppermute | solution.py:76
  30.5 8.6 %collective-permute-start.9 = (f32[392,128]{1,0:T(8,128)S(1)}, f32[392,128]{1,0:T(8,128)S(1)}, u32[]{:S(2)}, u32[]{:S(2)}) collective-permute-start(f32[392,128]{1,0:T(8,128)S(1)} %get-tuple-element.64.refs_0_), channel_id=1, source_target_pairs={{0,8},{4,12},{8,0},{12,4},{16,24},{20,28},{24,16},{28,20},{1,9},{5... | collective-permute-start | bytes 602120 | tf_op jit(solution)/shard_map/panels/ppermute | solution.py:76
  30.8 8.8 %collective-permute-start.2 = (f32[448,128]{1,0:T(8,128)S(1)}, f32[448,128]{1,0:T(8,128)S(1)}, u32[]{:S(2)}, u32[]{:S(2)}) collective-permute-start(f32[448,128]{1,0:T(8,128)S(1)} %collective-permute-done.1.refs_2_), channel_id=1, source_target_pairs={{0,1},{1,0},{2,3},{3,2},{4,5},{5,4},{6,7},{7,6},{8,9},{9,8},{10,11... | collective-permute-start | bytes 688136 | tf_op jit(solution)/shard_map/owned/ppermute | solution.py:80
  32.8 9.2 %collective-permute-start.8 = (f32[392,128]{1,0:T(8,128)S(1)}, f32[392,128]{1,0:T(8,128)S(1)}, u32[]{:S(2)}, u32[]{:S(2)}) collective-permute-start(f32[392,128]{1,0:T(8,128)S(1)} %get-tuple-element.64.refs_0_), channel_id=1, source_target_pairs={{0,4},{4,0},{8,12},{12,8},{16,20},{20,16},{24,28},{28,24},{1,5},{5... | collective-permute-start | bytes 602120 | tf_op jit(solution)/shard_map/panels/ppermute | solution.py:76
  36.0 6.0 %collective-permute-start.14 = (f32[392,128]{1,0:T(8,128)S(1)}, f32[392,128]{1,0:T(8,128)S(1)}, u32[]{:S(2)}, u32[]{:S(2)}) collective-permute-start(f32[392,128]{1,0:T(8,128)S(1)} %collective-permute-done.13.refs_6_), channel_id=1, source_target_pairs={{0,4},{4,0},{8,12},{12,8},{16,20},{20,16},{24,28},{28,24},{1,5},{5... | collective-permute-start | bytes 602120 | tf_op jit(solution)/shard_map/panels/ppermute | solution.py:76
  39.1 3.0 %collective-permute-start.12 = (f32[392,128]{1,0:T(8,128)S(1)}, f32[392,128]{1,0:T(8,128)S(1)}, u32[]{:S(2)}, u32[]{:S(2)}) collective-permute-start(f32[392,128]{1,0:T(8,128)S(1)} %collective-permute-done.11.refs_4_), channel_id=1, source_target_pairs={{0,4},{4,0},{8,12},{12,8},{16,20},{20,16},{24,28},{28,24},{1,5},{5... | collective-permute-start | bytes 602120 | tf_op jit(solution)/shard_map/panels/ppermute | solution.py:76
  39.1 3.0 %collective-permute-start.10 = (f32[392,128]{1,0:T(8,128)S(1)}, f32[392,128]{1,0:T(8,128)S(1)}, u32[]{:S(2)}, u32[]{:S(2)}) collective-permute-start(f32[392,128]{1,0:T(8,128)S(1)} %collective-permute-done.9.refs_2_), channel_id=1, source_target_pairs={{0,4},{4,0},{8,12},{12,8},{16,20},{20,16},{24,28},{28,24},{1,5},{5... | collective-permute-start | bytes 602120 | tf_op jit(solution)/shard_map/panels/ppermute | solution.py:76
  39.8 1.4 %collective-permute-start.3 = (f32[256,128]{1,0:T(8,128)S(1)}, f32[256,128]{1,0:T(8,128)S(1)}, u32[]{:S(2)}, u32[]{:S(2)}) collective-permute-start(f32[256,128]{1,0:T(8,128)S(1)} %get-tuple-element.49.mine), channel_id=1, source_target_pairs={{0,4},{4,0},{8,12},{12,8},{16,20},{20,16},{24,28},{28,24},{1,5},{5... | collective-permute-start | bytes 393224 | tf_op jit(solution)/shard_map/collect/ppermute | solution.py:76
  42.1 31.5 %copy-start.5 = (s32[3]{0:T(128)S(1)}, s32[3]{0:T(128)}, u32[]{:S(2)}) copy-start(s32[3]{0:T(128)} %blocks.3) | copy-start | bytes 40
  42.1 31.5 %copy-start.6 = (s32[3]{0:T(128)S(1)}, s32[3]{0:T(128)}, u32[]{:S(2)}) copy-start(s32[3]{0:T(128)} %psize.1) | copy-start | bytes 40
  42.1 31.5 %copy-start.7 = (s32[3]{0:T(128)S(1)}, s32[3]{0:T(128)}, u32[]{:S(2)}) copy-start(s32[3]{0:T(128)} %csize.1) | copy-start | bytes 40
  46.2 29.0 %copy-start.3 = (f32[64,256]{1,0:T(8,128)S(1)}, f32[64,256]{1,0:T(8,128)}, u32[]{:S(2)}) copy-start(f32[64,256]{1,0:T(8,128)} %cd.1) | copy-start | bytes 196612
  46.2 1.8 %collective-permute-start.15 = (f32[384,256]{1,0:T(8,128)S(1)}, f32[384,256]{1,0:T(8,128)S(1)}, u32[]{:S(2)}, u32[]{:S(2)}) collective-permute-start(f32[384,256]{1,0:T(8,128)S(1)} %get-tuple-element.66), channel_id=1, source_target_pairs={{0,4},{4,0},{8,12},{12,8},{16,20},{20,16},{24,28},{28,24},{1,5},{5... | collective-permute-start | bytes 1179656 | tf_op jit(solution)/shard_map/sum_core/ppermute | solution.py:76
  46.4 14.6 %collective-permute-start.22 = (f32[192,512]{1,0:T(8,128)S(1)}, f32[192,512]{1,0:T(8,128)S(1)}, u32[]{:S(2)}, u32[]{:S(2)}) collective-permute-start(f32[192,512]{1,0:T(8,128)S(1)} %get-tuple-element.76), channel_id=1, source_target_pairs={{0,1},{1,0},{2,3},{3,2},{4,5},{5,4},{6,7},{7,6},{8,9},{9,8},{10,11... | collective-permute-start | bytes 1179656 | tf_op jit(solution)/shard_map/sum_shares/ppermute | solution.py:80
  48.0 4.9 %collective-permute-start.16 = (f32[96,256]{1,0:T(8,128)S(1)}, f32[96,256]{1,0:T(8,128)S(1)}, u32[]{:S(2)}, u32[]{:S(2)}) collective-permute-start(f32[96,256]{1,0:T(8,128)S(1)} %get-tuple-element.68), channel_id=1, source_target_pairs={{0,8},{4,12},{8,0},{12,4},{16,24},{20,28},{24,16},{28,20},{1,9},{5... | collective-permute-start | bytes 294920 | tf_op jit(solution)/shard_map/sum_chips/ppermute | solution.py:76
  49.5 6.9 %collective-permute-start.17 = (f32[96,256]{1,0:T(8,128)S(1)}, f32[96,256]{1,0:T(8,128)S(1)}, u32[]{:S(2)}, u32[]{:S(2)}) collective-permute-start(f32[96,256]{1,0:T(8,128)S(1)} %get-tuple-element.69), channel_id=1, source_target_pairs={{0,16},{4,20},{8,24},{12,28},{16,0},{20,4},{24,8},{28,12},{1,17},{... | collective-permute-start | bytes 294920 | tf_op jit(solution)/shard_map/sum_chips/ppermute | solution.py:76
  50.5 5.9 %collective-permute-start.18 = (f32[96,256]{1,0:T(8,128)S(1)}, f32[96,256]{1,0:T(8,128)S(1)}, u32[]{:S(2)}, u32[]{:S(2)}) collective-permute-start(f32[96,256]{1,0:T(8,128)S(1)} %get-tuple-element.70), channel_id=1, source_target_pairs={{0,24},{4,28},{8,16},{12,20},{16,8},{20,12},{24,0},{28,4},{1,25},{... | collective-permute-start | bytes 294920 | tf_op jit(solution)/shard_map/sum_chips/ppermute | solution.py:76
  56.4 4.5 %collective-permute-start.19 = (f32[24,256]{1,0:T(8,128)S(1)}, f32[24,256]{1,0:T(8,128)S(1)}, u32[]{:S(2)}, u32[]{:S(2)}) collective-permute-start(f32[24,256]{1,0:T(8,128)S(1)} %get-tuple-element.72), channel_id=1, source_target_pairs={{0,1},{1,0},{2,3},{3,2},{4,5},{5,4},{6,7},{7,6},{8,9},{9,8},{10,11... | collective-permute-start | bytes 73736 | tf_op jit(solution)/shard_map/sum_cols/ppermute | solution.py:80
  57.0 5.1 %collective-permute-start.20 = (f32[24,256]{1,0:T(8,128)S(1)}, f32[24,256]{1,0:T(8,128)S(1)}, u32[]{:S(2)}, u32[]{:S(2)}) collective-permute-start(f32[24,256]{1,0:T(8,128)S(1)} %get-tuple-element.73), channel_id=1, source_target_pairs={{0,2},{1,3},{2,0},{3,1},{4,6},{5,7},{6,4},{7,5},{8,10},{9,11},{10,... | collective-permute-start | bytes 73736 | tf_op jit(solution)/shard_map/sum_cols/ppermute | solution.py:80
  60.3 5.9 %collective-permute-start.21 = (f32[24,256]{1,0:T(8,128)S(1)}, f32[24,256]{1,0:T(8,128)S(1)}, u32[]{:S(2)}, u32[]{:S(2)}) collective-permute-start(f32[24,256]{1,0:T(8,128)S(1)} %get-tuple-element.74), channel_id=1, source_target_pairs={{0,3},{1,2},{2,1},{3,0},{4,7},{5,6},{6,5},{7,4},{8,11},{9,10},{10,... | collective-permute-start | bytes 73736 | tf_op jit(solution)/shard_map/sum_cols/ppermute | solution.py:80
  66.2 7.4 %collective-permute-start.30 = (f32[96,512]{1,0:T(8,128)S(1)}, f32[96,512]{1,0:T(8,128)S(1)}, u32[]{:S(2)}, u32[]{:S(2)}) collective-permute-start(f32[96,512]{1,0:T(8,128)S(1)} %get-tuple-element.79), channel_id=1, source_target_pairs={{0,2},{1,3},{2,0},{3,1},{4,6},{5,7},{6,4},{7,5},{8,10},{9,11},{10,... | collective-permute-start | bytes 589832 | tf_op jit(solution)/shard_map/spread/ppermute | solution.py:80
  66.3 4.8 %collective-permute-start.28 = (f32[24,256]{1,0:T(8,128)S(1)}, f32[24,256]{1,0:T(8,128)S(1)}, u32[]{:S(2)}, u32[]{:S(2)}) collective-permute-start(f32[24,256]{1,0:T(8,128)S(1)} %get-tuple-element.77.refs_0_), channel_id=1, source_target_pairs={{0,24},{4,28},{8,16},{12,20},{16,8},{20,12},{24,0},{28,4},{1,25},{... | collective-permute-start | bytes 73736 | tf_op jit(solution)/shard_map/spread/ppermute | solution.py:76
  67.3 4.1 %collective-permute-start.26 = (f32[24,256]{1,0:T(8,128)S(1)}, f32[24,256]{1,0:T(8,128)S(1)}, u32[]{:S(2)}, u32[]{:S(2)}) collective-permute-start(f32[24,256]{1,0:T(8,128)S(1)} %get-tuple-element.77.refs_0_), channel_id=1, source_target_pairs={{0,16},{4,20},{8,24},{12,28},{16,0},{20,4},{24,8},{28,12},{1,17},{... | collective-permute-start | bytes 73736 | tf_op jit(solution)/shard_map/spread/ppermute | solution.py:76
  68.0 3.8 %collective-permute-start.24 = (f32[24,256]{1,0:T(8,128)S(1)}, f32[24,256]{1,0:T(8,128)S(1)}, u32[]{:S(2)}, u32[]{:S(2)}) collective-permute-start(f32[24,256]{1,0:T(8,128)S(1)} %get-tuple-element.77.refs_0_), channel_id=1, source_target_pairs={{0,8},{4,12},{8,0},{12,4},{16,24},{20,28},{24,16},{28,20},{1,9},{5... | collective-permute-start | bytes 73736 | tf_op jit(solution)/shard_map/spread/ppermute | solution.py:76
  69.9 5.3 %collective-permute-start.23 = (f32[24,256]{1,0:T(8,128)S(1)}, f32[24,256]{1,0:T(8,128)S(1)}, u32[]{:S(2)}, u32[]{:S(2)}) collective-permute-start(f32[24,256]{1,0:T(8,128)S(1)} %get-tuple-element.77.refs_0_), channel_id=1, source_target_pairs={{0,4},{4,0},{8,12},{12,8},{16,20},{20,16},{24,28},{28,24},{1,5},{5... | collective-permute-start | bytes 73736 | tf_op jit(solution)/shard_map/spread/ppermute | solution.py:76
  71.1 4.0 %collective-permute-start.29 = (f32[24,256]{1,0:T(8,128)S(1)}, f32[24,256]{1,0:T(8,128)S(1)}, u32[]{:S(2)}, u32[]{:S(2)}) collective-permute-start(f32[24,256]{1,0:T(8,128)S(1)} %collective-permute-done.28.refs_6_), channel_id=1, source_target_pairs={{0,4},{4,0},{8,12},{12,8},{16,20},{20,16},{24,28},{28,24},{1,5},{5... | collective-permute-start | bytes 73736 | tf_op jit(solution)/shard_map/spread/ppermute | solution.py:76
  71.4 3.8 %collective-permute-start.27 = (f32[24,256]{1,0:T(8,128)S(1)}, f32[24,256]{1,0:T(8,128)S(1)}, u32[]{:S(2)}, u32[]{:S(2)}) collective-permute-start(f32[24,256]{1,0:T(8,128)S(1)} %collective-permute-done.26.refs_4_), channel_id=1, source_target_pairs={{0,4},{4,0},{8,12},{12,8},{16,20},{20,16},{24,28},{28,24},{1,5},{5... | collective-permute-start | bytes 73736 | tf_op jit(solution)/shard_map/spread/ppermute | solution.py:76
  71.9 3.3 %collective-permute-start.25 = (f32[24,256]{1,0:T(8,128)S(1)}, f32[24,256]{1,0:T(8,128)S(1)}, u32[]{:S(2)}, u32[]{:S(2)}) collective-permute-start(f32[24,256]{1,0:T(8,128)S(1)} %collective-permute-done.24.refs_2_), channel_id=1, source_target_pairs={{0,4},{4,0},{8,12},{12,8},{16,20},{20,16},{24,28},{28,24},{1,5},{5... | collective-permute-start | bytes 73736 | tf_op jit(solution)/shard_map/spread/ppermute | solution.py:76

commit v4 on v3

--- a/solution.py
+++ b/solution.py
@@ -31,7 +31,7 @@
     )
 
 
-def call(kernel, inputs, outs, scratch=(), flops=0, limit=40, passed=()):
+def call(kernel, inputs, outs, scratch=(), ahead=0, limit=40, passed=()):
     alias = {len(inputs) + i: len(outs) + i for i in range(len(passed))}
     spaces = [pltpu.VMEM] * len(outs) + [pl.ANY] * len(passed)
     inputs = list(inputs) + [(pl.ANY, a) for a in passed]
@@ -47,7 +47,7 @@
         scratch_shapes=list(scratch),
         input_output_aliases=alias,
         compiler_params=pltpu.CompilerParams(vmem_limit_bytes=limit and limit * 1024 * 1024),
-        cost_estimate=pl.CostEstimate(flops=flops, bytes_accessed=nbytes, transcendentals=0),
+        cost_estimate=pl.CostEstimate(flops=int(ahead), bytes_accessed=nbytes, transcendentals=0),
     )(*arrays)
 
 
@@ -89,41 +89,38 @@
         self.CC = cached.shape[3]
         self.Q = rows // cols
         self.payload = self.slots * 2 * self.ws
-        self.piece = self.payload // cols
-        self.chunk = self.ws // 2
         self.share = self.B // cols
         self.chips = rows // 2
         self.eight = self.ws // rows
         self.live = self.slots * self.B
         self.parts = self.W // self.B
-        self.block = self.payload + 8
+        self.block = self.payload + self.ws + 8
 
 
 def pack(s, *refs):
-    sources, refs = refs[:6], refs[6:]
-    sends, payload, refs = refs[: s.C], refs[s.C], refs[s.C + 1 :]
-    targets, sems = refs[:6], refs[6]
+    sources, (sent, mine, *targets, sems) = refs[:6], refs[6:]
     for copy in fetch(sources, targets, sems):
         copy.wait()
     blocks, psize, csize, parent, child, top = targets
-    col = lax.axis_index("col")
     lane = lax.broadcasted_iota(jnp.int32, (s.ws, s.B), 1)
     for slot in range(s.slots):
         base = slot * 2 * s.ws
         for which, panel, sizes in ((0, parent, psize), (1, child, csize)):
             live = jnp.where(lane < sizes[slot], panel[slot], 0.0)
-            payload[base + which * s.ws : base + (which + 1) * s.ws, :] = live
-    wide = s.W // 2
-    mine = lax.rem(lax.axis_index("row"), 2) * wide
-    payload[s.payload :, :] = top[:, pl.ds(pl.multiple_of(mine, wide), wide)]
+            rows = slice(base + which * s.ws, base + (which + 1) * s.ws)
+            mine[rows, :] = live
+            sent[rows, :] = live
+    half = lax.div(lax.axis_index("row"), s.C) * s.B
+    sent[s.payload : s.payload + s.ws, :] = top[:, pl.ds(pl.multiple_of(half, s.B), s.B)]
     row8 = lax.broadcasted_iota(jnp.int32, (8, s.B), 0)
     ids = jnp.zeros((8, s.B), f32)
     for slot in range(s.slots):
         ids = jnp.where(row8 == slot, blocks[slot].astype(f32), ids)
-    for turn in range(s.C):
-        start = pl.multiple_of(lax.rem(turn - col + s.C, s.C) * s.piece, s.piece)
-        sends[turn][: s.piece, :] = payload[pl.ds(start, s.piece), :]
-        sends[turn][s.piece :, :] = ids
+    sent[s.payload + s.ws :, :] = ids
+
+
+def order(s, *refs):
+    pass
 
 
 def split_live(s, cached, blocks, high, low, held, numbers, sems):
@@ -147,103 +144,81 @@
             low[rows, m * s.B : (m + 1) * s.B] = l
 
 
-def join(s, *refs):
-    pieces, out = refs[: s.C], refs[s.C + 2]
-    part = lax.rem(lax.axis_index("row"), s.C)
-    for turn in range(s.C):
-        start = pl.multiple_of(lax.rem(turn - part + s.C, s.C) * s.piece, s.piece)
-        out[pl.ds(start, s.piece), :] = pieces[turn][: s.piece, :]
-    out[s.payload :, :] = pieces[0][s.piece :, :]
+def shares_of(s, pd, sh, sl, *refs):
+    panels, refs = refs[: s.R], refs[s.R :]
+    shares, refs = refs[: s.C], refs[s.C :]
+    gh, gl, th, tl, ih, il, base, extra, xh, xl, total, top = refs
+    row, col = lax.axis_index("row"), lax.axis_index("col")
+    places = []
+    for owner in range(s.Q):
+        for slot in range(s.slots):
+            at = s.payload + s.ws + slot
+            number = jnp.max(panels[owner * s.C][at : at + 1, :]).astype(jnp.int32)
+            places.append(jnp.where(number < 0, s.CC, lax.div(jnp.maximum(number, 0), s.C)))
+    for m in range(s.CC):
+        taken = places[0] == m
+        for place in places[1:]:
+            taken = jnp.logical_or(taken, place == m)
+
+        @pl.when(jnp.logical_not(taken))
+        def _():
+            xh[m] = jnp.zeros((2 * s.W, s.B), bf16)
+            xl[m] = jnp.zeros((2 * s.W, s.B), bf16)
+
+    for mask in range(s.R):
+        sender = jnp.bitwise_xor(row, mask)
+        first = pl.multiple_of(lax.rem(sender, s.C) * s.ws, s.ws)
+        for slot in range(s.slots):
+            place = places[mask // s.C * s.slots + slot]
+            for which in range(2):
+                start = (slot * 2 + which) * s.ws
+                high, low = split(panels[mask][start : start + s.ws, :])
+                rows = pl.ds(pl.multiple_of(which * s.W + first, s.ws), s.ws)
+                xh[place, rows, :] = high
+                xl[place, rows, :] = low
+        half = pl.multiple_of(lax.div(sender, s.C) * s.B, s.B)
+        top[pl.ds(first, s.ws), pl.ds(half, s.B)] = panels[mask][s.payload : s.payload + s.ws, :]
+    right = tuple(jnp.concatenate([x[i] for i in range(s.CC)], axis=1) for x in (xh, xl))
+    total[...] = dot3((sh[...], sl[...]), right, NT)
+    gh[...], gl[...] = split(total[...])
+    for mask in range(s.C):
+        target = jnp.bitwise_xor(col, mask)
+        for slot in range(s.slots):
+            start = pl.multiple_of(slot * s.B + target * s.share, s.share)
+            rows = slice(slot * s.share, (slot + 1) * s.share)
+            shares[mask][rows, :] = total[pl.ds(start, s.share), :]
+    th[...], tl[...] = split(top[...])
+    ih[...], il[...] = split(top[...].T)
+    lead = dot3(split(pd[...]), (th[...], tl[...]), NN)
+    base[...] = -lead
+    own = top[pl.ds(pl.multiple_of(col * s.ws, s.ws), s.ws), :]
+    extra[...] = dot3(split(own), split(lead * (1.0 / s.R)), TN)
 
 
 def collect(s, *refs):
-    owned, (lh, ll, half, panel) = refs[: s.C], refs[s.C :]
+    owned, (lh, ll) = refs[: s.C], refs[s.C + 2 : s.C + 4]
     col = lax.axis_index("col")
     for mask in range(s.C):
         source = jnp.bitwise_xor(col, mask)
         for slot in range(s.slots):
             for which in range(2):
                 start = (slot * 2 + which) * s.ws
-                dest = pl.multiple_of(which * s.W + source * s.ws, s.ws)
-                panel[pl.ds(dest, s.ws), slot * s.B : (slot + 1) * s.B] = owned[mask][
-                    start : start + s.ws, :
-                ]
-        dest = pl.multiple_of(source * s.ws, s.ws)
-        half[pl.ds(dest, s.ws), :] = owned[mask][s.payload :, :]
-    lh[...], ll[...] = split(panel[...])
-
-
-def own_panels(s, pd, lh, ll, mine, theirs, vh, vl, th, tl, base, extra, top):
-    row, col = lax.axis_index("row"), lax.axis_index("col")
-    wide = s.W // 2
-    core = lax.rem(row, 2)
-    top[:, pl.ds(pl.multiple_of(core * wide, wide), wide)] = mine[...]
-    top[:, pl.ds(pl.multiple_of((1 - core) * wide, wide), wide)] = theirs[...]
-    th[...], tl[...] = split(top[...])
-    full = (th[...], tl[...])
-    vh[...], vl[...] = split(dot3(split(top[...].T), (lh[: s.W, :], ll[: s.W, :]), NN))
-    lead = dot3(split(pd[...]), full, NN)
-    base[...] = -lead
-    own = top[pl.ds(pl.multiple_of(col * s.ws, s.ws), s.ws), :]
-    extra[...] = dot3(split(own), split(lead * (1.0 / s.R)), TN)
-
-
-def products(s, sh, sl, lh, ll, vh, vl, th, tl, extra, *refs):
-    panels, (stay, leave, keep, send, xh, xl, total, both) = refs[: s.R], refs[s.R :]
-    row = lax.axis_index("row")
-    core = lax.rem(row, 2)
-    places = []
-    for owner in range(s.Q):
-        for slot in range(s.slots):
-            at = s.payload + slot
-            number = jnp.max(panels[owner * s.C][at : at + 1, :]).astype(jnp.int32)
-            places.append(jnp.where(number < 0, s.CC, lax.div(jnp.maximum(number, 0), s.C)))
-    for m in range(s.CC):
-        taken = places[0] == m
-        for place in places[1:]:
-            taken = jnp.logical_or(taken, place == m)
-
-        @pl.when(jnp.logical_not(taken))
-        def _():
-            xh[m] = jnp.zeros((2 * s.W, s.B), bf16)
-            xl[m] = jnp.zeros((2 * s.W, s.B), bf16)
-
-    per = s.piece // s.chunk
-    for mask in range(s.R):
-        owner = mask // s.C
-        part = lax.rem(jnp.bitwise_xor(row, mask), s.C)
-        for i in range(per):
-            at = part * per + i
-            group, off = lax.div(at, 2), lax.rem(at, 2) * s.chunk
-            slot, which = lax.div(group, 2), lax.rem(group, 2)
-            place = places[owner * s.slots]
-            for k in range(1, s.slots):
-                place = jnp.where(slot == k, places[owner * s.slots + k], place)
-            for source in range(s.C):
-                start = source * s.piece + i * s.chunk
-                high, low = split(panels[mask][start : start + s.chunk, :])
-                dest = pl.multiple_of(which * s.W + source * s.ws + off, s.chunk)
-                xh[place, pl.ds(dest, s.chunk), :] = high
-                xl[place, pl.ds(dest, s.chunk), :] = low
-    right = tuple(jnp.concatenate([x[i] for i in range(s.CC)], axis=1) for x in (xh, xl))
-    total[...] = dot3((sh[...], sl[...]), right, NT)
-    col = lax.axis_index("col")
-    for mask in range(s.C):
-        out = leave if mask % 2 else stay
-        target = jnp.bitwise_xor(col, mask)
-        for slot in range(s.slots):
-            start = pl.multiple_of(slot * s.B + target * s.share, s.share)
-            to = (mask // 2 * s.slots + slot) * s.share
-            out[to : to + s.share, :] = total[pl.ds(start, s.share), :]
+                rows = pl.ds(pl.multiple_of(which * s.W + source * s.ws, s.ws), s.ws)
+                lanes = slice(slot * s.B, (slot + 1) * s.B)
+                lh[rows, lanes], ll[rows, lanes] = split(owned[mask][start : start + s.ws, :])
+
+
+def products(s, gh, gl, th, tl, ih, il, extra, lh, ll, keep, send, both):
+    core = lax.rem(lax.axis_index("row"), 2)
     W = s.W
-    left = tuple(jnp.concatenate([x[...], y[...]], axis=0) for x, y in ((lh, vh), (ll, vl)))
-    first = dot3(left, split(total[:, :W]), NN)
-    d = dot3((lh[W:, :], ll[W:, :]), split(total[:, W:]), NN)
+    first = dot3((lh[...], ll[...]), (gh[:, :W], gl[:, :W]), NN)
+    d = dot3((lh[W:, :], ll[W:, :]), (gh[:, W:], gl[:, W:]), NN)
     second = dot3(split(first), (th[...], tl[...]), NN)
+    third = dot3((ih[...], il[...]), split(second[:W]), NN)
     both[0:W, :] = first[:W]
-    both[W : 2 * W, :] = first[W : 2 * W].T - second[:W]
-    cross = second[W : 2 * W]
-    both[2 * W :, :] = d - cross - cross.T + second[2 * W :] + extra[...]
+    both[W : 2 * W, :] = first[W:].T - second[:W]
+    cross = second[W:]
+    both[2 * W :, :] = d - cross - cross.T + third + extra[...]
     n = s.eight
     for out, swap in ((keep, 0), (send, 1)):
         offset = jnp.bitwise_xor(core, swap) * (s.ws // 2)
@@ -255,7 +230,8 @@
                     out[to : to + n, :] = both[pl.ds(at, n), :]
 
 
-def add_chips(s, kept, got, *outs):
+def add_chips(s, kept, got, share, *outs):
+    outs = outs[: s.chips]
     size = s.C * 3 * s.eight
     chip = lax.div(lax.axis_index("row"), 2)
     for mask in range(s.chips):
@@ -276,25 +252,22 @@
         outs[mask][...] = total[rows, :]
 
 
-def halve(s, kept, got, stay, leave):
-    size = s.slots * s.share
-    for i in range(kept.shape[0] // size):
-        out, at = (leave if i % 2 else stay), i // 2 * size
-        rows = slice(i * size, (i + 1) * size)
-        out[at : at + size, :] = kept[rows, :] + got[rows, :]
+def plus(s, *refs):
+    count = len(refs) // 3
+    for one, two, out in zip(refs[:count], refs[count : 2 * count], refs[2 * count :]):
+        out[...] = one[...] + two[...]
 
 
 def add_all(s, *refs):
-    terms, (kept, got, out, stay, leave) = refs[: s.C], refs[s.C :]
+    terms, out = refs[: s.C], refs[s.C + 2]
     value = terms[0][...]
     for term in terms[1:]:
         value = value + term[...]
     out[...] = value
-    halve(s, kept, got, stay, leave)
 
 
 def finish(s, pd, cd, base, *refs):
-    parts, outs = refs[: s.R], refs[s.R + 2 : s.R + 5]
+    parts, outs = refs[: s.R], refs[s.R :]
     row = lax.axis_index("row")
     n = s.eight
     starts = (pd, base, cd)
@@ -306,8 +279,11 @@
             outs[kind][rows, :] = starts[kind][rows, :] + parts[mask][kind * n : (kind + 1) * n, :]
 
 
-def rows_out(s, blocks, psize, csize, th, tl, kept, got, parent, child):
-    value = kept[...] + got[...]
+def rows_out(s, blocks, psize, csize, th, tl, *refs):
+    terms, (parent, child) = refs[:-2], refs[-2:]
+    value = terms[0][...]
+    for term in terms[1:]:
+        value = value + term[...]
     first = lax.axis_index("col") * s.share
     index = lax.broadcasted_iota(jnp.int32, (s.share, s.W), 0) + first
     plive = jnp.concatenate([index < psize[k] for k in range(s.slots)], axis=0)
@@ -327,9 +303,9 @@
             child[rows, :] = z[slot * s.share : (slot + 1) * s.share, :]
 
 
-def scatter_perm(s, turn):
+def swap_perm(s):
     return [
-        ((q * s.C + a) * s.C + c, (q * s.C + (turn - c) % s.C) * s.C + a)
+        ((q * s.C + a) * s.C + c, (q * s.C + c) * s.C + a)
         for q in range(s.Q)
         for a in range(s.C)
         for c in range(s.C)
@@ -357,7 +333,7 @@
     numbers = pltpu.SMEM((s.slots,), jnp.int32)
     by_slot = (s.slots, ws, B)
     with jax.named_scope("pack"):
-        *sends, payload = call(
+        sent, mine = call(
             bind(pack),
             hbm(
                 parent_blocks,
@@ -367,20 +343,14 @@
                 jnp.transpose(child_panel, (1, 0, 2)),
                 child_top,
             ),
-            [(s.piece + 8, B)] * C + [(s.payload + ws, B)],
+            [(s.block, B), (s.payload, B)],
             [numbers] * 3
             + [pltpu.VMEM(by_slot, f32)] * 2
             + [pltpu.VMEM((ws, W), f32), pltpu.SemaphoreType.DMA((6,))],
             limit=None,
         )
-    with jax.named_scope("scatter"):
-        pieces = [lax.ppermute(sends[t], ("row", "col"), scatter_perm(s, t)) for t in range(C)]
-    with jax.named_scope("owned"):
-        owned = {0: payload}
-        mask = C // 2
-        while mask:
-            owned.update({m ^ mask: flip(owned[m], mask, C) for m in list(owned)})
-            mask //= 2
+    with jax.named_scope("swap"):
+        own = lax.ppermute(sent, ("row", "col"), swap_perm(s))
     with jax.named_scope("split_live"):
         sh, sl = call(
             bind(split_live),
@@ -389,86 +359,103 @@
             [pltpu.VMEM((s.slots * B * s.CC, B), f32), numbers]
             + [pltpu.SemaphoreType.DMA((1 + s.slots,))],
         )
-    with jax.named_scope("join"):
-        own, sh, sl = call(
-            bind(join),
-            vmem(*pieces),
-            [(s.block, B)],
-            passed=(sh, sl),
-        )
+    with jax.named_scope("owned"):
+        owned = {0: mine, 1: flip(mine, 1, C)}
+        mask = C // 2
+        while mask > 1:
+            owned.update({m ^ mask: flip(owned[m], mask, C) for m in owned if m != 1})
+            mask //= 2
+        owned.update({m ^ 1: flip(owned[m], 1, C) for m in list(owned) if m > 1})
+    with jax.named_scope("order"):
+        own, owned[1], sh, sl = call(bind(order), (), (), passed=(own, owned[1], sh, sl))
     with jax.named_scope("panels"):
         panels = {0: own}
         for mask in range(2, R, 2):
             panels[mask] = exchange(own, mask, R)
         for mask in range(0, R, 2):
             panels[mask + 1] = exchange(panels[mask], 1, R)
-    with jax.named_scope("collect"):
-        lh, ll, half = call(
+    with jax.named_scope("shares_of"):
+        pair = lambda rows, cols: [((rows, cols), bf16)] * 2
+        *shares, gh, gl, th, tl, ih, il, base, extra = call(
+            bind(shares_of),
+            vmem(parent_diagonal, sh, sl, *[panels[m] for m in range(R)]),
+            [(s.slots * s.share, 2 * W)] * C
+            + pair(live, 2 * W)
+            + pair(W, W)
+            + pair(W, W)
+            + [(ws, W), (W, W)],
+            [pltpu.VMEM((s.CC + 1, 2 * W, B), bf16)] * 2
+            + [pltpu.VMEM((live, 2 * W), f32), pltpu.VMEM((W, W), f32)],
+        )
+    with jax.named_scope("products"):
+        lh, ll, gh, gl = call(
             bind(collect),
             vmem(*[owned[m] for m in range(C)]),
-            [((2 * W, live), bf16)] * 2 + [(W, W // 2)],
-            [pltpu.VMEM((2 * W, live), f32)],
-        )
-        theirs = exchange(half, 1, R)
-    with jax.named_scope("own_panels"):
-        vh, vl, th, tl, base, extra = call(
-            bind(own_panels),
-            vmem(parent_diagonal, lh, ll, half, theirs),
-            [((W, live), bf16)] * 2 + [((W, W), bf16)] * 2 + [(ws, W), (W, W)],
-            [pltpu.VMEM((W, W), f32)],
-        )
-    with jax.named_scope("products"):
-        half = C // 2 * s.slots * s.share
-        stay, leave, keep, send = call(
+            pair(2 * W, live),
+            ahead=3e9,
+            passed=(gh, gl),
+        )
+        keep, send = call(
             bind(products),
-            vmem(sh, sl, lh, ll, vh, vl, th, tl, extra, *[panels[m] for m in range(R)]),
-            [(half, 2 * W), (half, 2 * W), (3 * W // 2, W), (3 * W // 2, W)],
-            [pltpu.VMEM((s.CC + 1, 2 * W, B), bf16)] * 2
-            + [pltpu.VMEM((live, 2 * W), f32), pltpu.VMEM((3 * W, W), f32)],
-            flops=2 * live * s.CC * B * 2 * W * 3,
+            vmem(gh, gl, th, tl, ih, il, extra, lh, ll),
+            [(3 * W // 2, W)] * 2,
+            [pltpu.VMEM((3 * W, W), f32)],
         )
     with jax.named_scope("sum_core"):
         got = exchange(send, 1, R)
     with jax.named_scope("sum_shares"):
-        got_rows = flip(leave, 1, C)
+        arrived, mask = [shares[0]], 1
+        while mask < C:
+            far = list(range(3 * mask, C, 2 * mask))
+            if far:
+                come = [flip(shares[m], mask, C) for m in far]
+                to = [m ^ mask for m in far]
+                added = call(
+                    bind(plus),
+                    vmem(*[shares[m] for m in to], *come),
+                    [shares[0].shape] * len(far),
+                    ahead=6e9,
+                )
+                for m, value in zip(to, added):
+                    shares[m] = value
+            mask *= 2
     with jax.named_scope("sum_chips"):
-        mine = call(bind(add_chips), vmem(keep, got), [(C * 3 * s.eight, W)] * s.chips)
+        *mine, shares[2] = call(
+            bind(add_chips),
+            vmem(keep, got),
+            [(C * 3 * s.eight, W)] * s.chips,
+            passed=(shares[2],),
+        )
         mine = [mine[0]] + [exchange(mine[m], 2 * m, R) for m in range(1, s.chips)]
+    with jax.named_scope("sum_shares"):
+        mask = 1
+        while mask < C:
+            arrived.append(flip(shares[mask], mask, C))
+            mask *= 2
     with jax.named_scope("sum_cols"):
         scr = [pltpu.VMEM((C * 3 * s.eight, W), f32)]
         cols = call(bind(add_cols), vmem(*mine), [(3 * s.eight, W)] * C, scr)
         cols = [cols[0]] + [flip(cols[m], m, C) for m in range(1, C)]
+    with jax.named_scope("rows_out"):
+        parent_rows, child_rows = call(
+            bind(rows_out),
+            smem(parent_blocks, parent_sizes, child_sizes) + vmem(th, tl, *arrived),
+            [(s.RC * s.share, W)] * 2,
+        )
     with jax.named_scope("spread"):
-        half //= 2
-        done, stay, leave = call(
-            bind(add_all),
-            vmem(*cols, stay, got_rows),
-            [(3 * s.eight, W)] + [(half, 2 * W)] * 2,
-        )
-        got_rows = flip(leave, 2, C)
-        mask = 4
-        while mask < C:
-            half //= 2
-            stay, leave = call(bind(halve), vmem(stay, got_rows), [(half, 2 * W)] * 2)
-            got_rows = flip(leave, mask, C)
-            mask *= 2
+        done, parent_rows, child_rows = call(
+            bind(add_all), vmem(*cols), [(3 * s.eight, W)], passed=(parent_rows, child_rows)
+        )
         parts = {0: done}
         for mask in range(2, R, 2):
             parts[mask] = exchange(done, mask, R)
         for mask in range(0, R, 2):
             parts[mask + 1] = exchange(parts[mask], 1, R)
-    with jax.named_scope("rows_out"):
-        parent_rows, child_rows = call(
-            bind(rows_out),
-            smem(parent_blocks, parent_sizes, child_sizes) + vmem(th, tl, stay, got_rows),
-            [(s.RC * s.share, W)] * 2,
-        )
     with jax.named_scope("finish"):
-        parent_diag, child_upper, child_diag, parent_rows, child_rows = call(
+        parent_diag, child_upper, child_diag = call(
             bind(finish),
             vmem(parent_diagonal, child_diagonal, base, *[parts[m] for m in range(R)]),
             [(ws, W)] * 3,
-            passed=(parent_rows, child_rows),
         )
     shape = (s.RC, 1, s.share, W)
     return (
@@ -648,10 +635,9 @@
         and cols & (cols - 1) == 0
         and rows % cols == 0
         and cols > 2
+        and s.Q == 2
         and width == 2 * s.B
-        and s.payload % cols == 0
-        and s.chunk % 16 == 0
-        and s.piece % s.chunk == 0
+        and s.ws % 16 == 0
         and s.share % 16 == 0
         and s.ws % rows == 0
         and s.eight % 8 == 0

time: 76.2 us -> 72.5 us (0.951)
  starting transfers between devices: 34.7 us -> 28.4 us
  waiting for transfers between devices: 27.7 us -> 31.5 us
  Pallas kernels: 10.4 us -> 9.29 us
    ppermute x8 -> x9, waiting for transfers between devices: 6.92 us -> 14.6 us  [flip(): return lax.ppermute(value, 'col', [(i, i ^ mask) for i in range(col_total)])]
    ppermute x4 -> x1, starting transfers between devices: 9.07 us -> 1.6 us  [fast_body(): own = lax.ppermute(sent, ('row', 'col'), swap_perm(s))]
    ppermute x4 -> x1, waiting for transfers between devices: 5.42 us -> 0.01 us  [fast_body(): own = lax.ppermute(sent, ('row', 'col'), swap_perm(s))]
    ppermute x8 -> x9, starting transfers between devices: 12.5 us -> 15.6 us  [flip(): return lax.ppermute(value, 'col', [(i, i ^ mask) for i in range(col_total)])]
    ppermute x19 -> x18, starting transfers between devices: 13 us -> 11.2 us  [exchange(): return lax.ppermute(value, 'row', [(i, i ^ mask) for i in range(row_total)])]
    ppermute x19 -> x18, waiting for transfers between devices: 15.4 us -> 16.9 us  [exchange(): return lax.ppermute(value, 'row', [(i, i ^ mask) for i in range(row_total)])]
    pallas_call x11 -> x12, Pallas kernels: 10.4 us -> 9.29 us  [call(): pl.pallas_call(kernel, out_shape=shapes, in_specs=[pl.BlockSpec(memory_sp...]
  transfers between devices with their start and end apart: 31 -> 28, of which waited for: 13 -> 16; matrix products, arithmetic and copies ran while one was open for 0% -> 0% of each run, Pallas kernels for 5% -> 9%
where the time goes in v4:
time: 72.5 us; the launch traced here: 72.3 us
  waiting for transfers between devices  31.5 us (43%)
  starting transfers between devices  28.4 us (39%)
  Pallas kernels  9.29 us (13%)
  local copies, waits for them, and re-layouts  2.27 us (3%)
  between operations  0.79 us (1%)
    ppermute x18, waiting for transfers between devices, exchange(): return lax.ppermute(value, 'row', [(i, i ^ mask) for i in range(row_total)])  16.9 us
    ppermute x9, starting transfers between devices, flip(): return lax.ppermute(value, 'col', [(i, i ^ mask) for i in range(col_total)])  15.6 us
    ppermute x9, waiting for transfers between devices, flip(): return lax.ppermute(value, 'col', [(i, i ^ mask) for i in range(col_total)])  14.6 us
    ppermute x18, starting transfers between devices, exchange(): return lax.ppermute(value, 'row', [(i, i ^ mask) for i in range(row_total)])  11.2 us
    pallas_call x12, Pallas kernels, call(): pl.pallas_call(kernel, out_shape=shapes, in_specs=[pl.BlockSpec(memory_sp...  9.29 us
    unnamed x16, local copies, waits for them, and re-layouts  2.27 us
    ppermute x1, starting transfers between devices, fast_body(): own = lax.ppermute(sent, ('row', 'col'), swap_perm(s))  1.6 us
  transfers between devices with their start and end apart: 28, of which 16 were waited for; matrix products, arithmetic and copies ran while one was open for 0% of the time, Pallas kernels for 9%

profile of v4, /device:TPU:0, one launch (start us, length us, event | category | flops | bytes accessed | tf_op | source)
XLA Modules:
  0.0 72.3 jit_solution(17045017625765424231)
XLA Ops:
  0.6 1.8 %pack.1 = (f32[456,128]{1,0:T(8,128)}, f32[384,128]{1,0:T(8,128)}) custom-call(s32[3]{0:T(128)} %blocks.3, s32[3]{0:T(128)} %psize.1, s32[3]{0:T(128)} %csize.1, f32[3,64,128]{2,1,0:T(8,128)} %bitcast.12, f32[3,64,128]{2,1,0:T(8,128)} %bitcast.13, f32[64,256]{1,0:T(8,128)} %refs_5_.1), custom_call_target="tpu_custom_call" | custom-call | bytes 692260 | tf_op jit(solution)/shard_map/pack/pallas_call | solution.py:42
  2.5 1.6 %collective-permute-start = (f32[456,128]{1,0:T(8,128)}, f32[456,128]{1,0:T(8,128)S(1)}, u32[]{:S(2)}, u32[]{:S(2)}) collective-permute-start(f32[456,128]{1,0:T(8,128)} %get-tuple-element.49), channel_id=1, source_target_pairs={{0,0},{1,4},{2,8},{3,12},{4,1},{5,5},{6,9},{7,13},{8,2},{9,6},{10,... | collective-permute-start | bytes 700424 | tf_op jit(solution)/shard_map/swap/ppermute | solution.py:353
  4.1 3.4 %collective-permute-start.1 = (f32[384,128]{1,0:T(8,128)}, f32[384,128]{1,0:T(8,128)S(1)}, u32[]{:S(2)}, u32[]{:S(2)}) collective-permute-start(f32[384,128]{1,0:T(8,128)} %get-tuple-element.48.refs_0_), channel_id=1, source_target_pairs={{0,1},{1,0},{2,3},{3,2},{4,5},{5,4},{6,7},{7,6},{8,9},{9,8},{10,11... | collective-permute-start | bytes 589832 | tf_op jit(solution)/shard_map/owned/ppermute | solution.py:80
  7.5 1.6 %copy-done = f32[4,1,128,8,1,128]{5,4,3,2,1,0:T(1,128)S(1)} copy-done((f32[4,1,128,8,1,128]{5,4,3,2,1,0:T(1,128)S(1)}, f32[4,1,128,8,1,128]{5,4,3,2,1,0:T(1,128)}, u32[]{:S(2)}) %copy-start) | copy-done | bytes 2097176
  9.1 0.7 copy-done.3
  9.7 1.2 %split_live.1 = (bf16[384,1024]{1,0:T(8,128)(2,1)S(1)}, bf16[384,1024]{1,0:T(8,128)(2,1)S(1)}) custom-call(f32[4096,128]{1,0:T(8,128)S(1)} %bitcast.9, s32[3]{0:T(128)S(1)} %copy-done.3), custom_call_target="tpu_custom_call" | custom-call | bytes 3670028 | tf_op jit(solution)/shard_map/split_live/pallas_call | solution.py:42
  10.9 9.5 %collective-permute-done.1.refs_1_ = f32[384,128]{1,0:T(8,128)S(1)} collective-permute-done((f32[384,128]{1,0:T(8,128)}, f32[384,128]{1,0:T(8,128)S(1)}, u32[]{:S(2)}, u32[]{:S(2)}) %collective-permute-start.1) | collective-permute-done | bytes 196640 | tf_op jit(solution)/shard_map/owned/ppermute | solution.py:80
  20.4 3.0 %collective-permute-start.9 = (f32[456,128]{1,0:T(8,128)S(1)}, f32[456,128]{1,0:T(8,128)S(1)}, u32[]{:S(2)}, u32[]{:S(2)}) collective-permute-start(f32[456,128]{1,0:T(8,128)S(1)} %get-tuple-element.55.refs_0_), channel_id=1, source_target_pairs={{0,24},{4,28},{8,16},{12,20},{16,8},{20,12},{24,0},{28,4},{1,25},{... | collective-permute-start | bytes 700424 | tf_op jit(solution)/shard_map/panels/ppermute | solution.py:76
  23.4 0.0 collective-permute-start.5
  23.4 0.5 collective-permute-start.7
  23.9 0.7 collective-permute-start.2
  24.6 0.2 collective-permute-start.4
  24.8 5.1 %collective-permute-done.9.refs_6_ = f32[456,128]{1,0:T(8,128)S(1)} collective-permute-done((f32[456,128]{1,0:T(8,128)S(1)}, f32[456,128]{1,0:T(8,128)S(1)}, u32[]{:S(2)}, u32[]{:S(2)}) %collective-permute-start.9) | collective-permute-done | bytes 233504 | tf_op jit(solution)/shard_map/panels/ppermute | solution.py:76
  30.0 1.8 %collective-permute-done.5.refs_2_ = f32[456,128]{1,0:T(8,128)S(1)} collective-permute-done((f32[456,128]{1,0:T(8,128)S(1)}, f32[456,128]{1,0:T(8,128)S(1)}, u32[]{:S(2)}, u32[]{:S(2)}) %collective-permute-start.5) | collective-permute-done | bytes 233504 | tf_op jit(solution)/shard_map/panels/ppermute | solution.py:76
  31.8 0.7 collective-permute-done.7.refs_4_
  32.5 1.9 %collective-permute-done.2.refs_2_ = f32[384,128]{1,0:T(8,128)S(1)} collective-permute-done((f32[384,128]{1,0:T(8,128)S(1)}, f32[384,128]{1,0:T(8,128)S(1)}, u32[]{:S(2)}, u32[]{:S(2)}) %collective-permute-start.2) | collective-permute-done | bytes 196640 | tf_op jit(solution)/shard_map/owned/ppermute | solution.py:80
  34.4 0.2 collective-permute-start.3
  34.6 2.2 %shares_of.1 = (f32[96,512]{1,0:T(8,128)S(1)}, f32[96,512]{1,0:T(8,128)S(1)}, f32[96,512]{1,0:T(8,128)S(1)}, f32[96,512]{1,0:T(8,128)S(1)}, bf16[384,512]{1,0:T(...) custom-call(f32[64,256]{1,0:T(8,128)S(1)} %copy-done.1, ...), custom_call_target="tpu_custom_call" | custom-call | bytes 5931008 | tf_op jit(solution)/shard_map/shares_of/pallas_call | solution.py:42
  36.8 1.9 %collective-permute-start.12 = (f32[96,512]{1,0:T(8,128)S(1)}, f32[96,512]{1,0:T(8,128)S(1)}, u32[]{:S(2)}, u32[]{:S(2)}) collective-permute-start(f32[96,512]{1,0:T(8,128)S(1)} %get-tuple-element.70), channel_id=1, source_target_pairs={{0,1},{1,0},{2,3},{3,2},{4,5},{5,4},{6,7},{7,6},{8,9},{9,8},{10,11... | collective-permute-start | bytes 589832 | tf_op jit(solution)/shard_map/sum_shares/ppermute | solution.py:80
  38.8 1.7 %collective-permute-done.3.refs_3_ = f32[384,128]{1,0:T(8,128)S(1)} collective-permute-done((f32[384,128]{1,0:T(8,128)S(1)}, f32[384,128]{1,0:T(8,128)S(1)}, u32[]{:S(2)}, u32[]{:S(2)}) %collective-permute-start.3) | collective-permute-done | bytes 196640 | tf_op jit(solution)/shard_map/owned/ppermute | solution.py:80
  40.5 0.1 products.2
  40.6 1.6 %products.3 = (f32[384,256]{1,0:T(8,128)S(1)}, f32[384,256]{1,0:T(8,128)S(1)}) custom-call(bf16[384,512]{1,0:T(8,128)(2,1)S(1)} %get-tuple-element.58.gh, bf16[384,512]{1,0:T(8,128)(2,1)S(1)} %get-tuple-element.59.gl, bf16[256,256]{1,0:T(8,128)(2,1)S(1)} %get-tuple-element.60.th, bf16[256,256]{1,0:T(8,128)(2,1)S(1)} %get-tuple-element.61.tl, ...), custom_call_target="tpu_custom_call" | custom-call | bytes 3145728 | tf_op jit(solution)/shard_map/products/pallas_call | solution.py:42
  42.2 0.1 collective-permute-start.11
  42.3 1.9 %collective-permute-start.19 = (f32[96,512]{1,0:T(8,128)S(1)}, f32[96,512]{1,0:T(8,128)S(1)}, u32[]{:S(2)}, u32[]{:S(2)}) collective-permute-start(f32[96,512]{1,0:T(8,128)S(1)} %get-tuple-element.80), channel_id=1, source_target_pairs={{0,1},{1,0},{2,3},{3,2},{4,5},{5,4},{6,7},{7,6},{8,9},{9,8},{10,11... | collective-permute-start | bytes 589832 | tf_op jit(solution)/shard_map/sum_shares/ppermute | solution.py:80
  44.2 0.2 collective-permute-done.12.refs_1_
  44.4 0.0 copy-start.2
  44.4 0.1 sum_chips.1
  44.5 3.0 %collective-permute-start.20 = (f32[96,512]{1,0:T(8,128)S(1)}, f32[96,512]{1,0:T(8,128)S(1)}, u32[]{:S(2)}, u32[]{:S(2)}) collective-permute-start(f32[96,512]{1,0:T(8,128)S(1)} %get-tuple-element.81), channel_id=1, source_target_pairs={{0,2},{1,3},{2,0},{3,1},{4,6},{5,7},{6,4},{7,5},{8,10},{9,11},{10,... | collective-permute-start | bytes 589832 | tf_op jit(solution)/shard_map/sum_shares/ppermute | solution.py:80
  47.5 2.2 %collective-permute-start.13 = (f32[96,256]{1,0:T(8,128)S(1)}, f32[96,256]{1,0:T(8,128)S(1)}, u32[]{:S(2)}, u32[]{:S(2)}) collective-permute-start(f32[96,256]{1,0:T(8,128)S(1)} %get-tuple-element.72), channel_id=1, source_target_pairs={{0,8},{4,12},{8,0},{12,4},{16,24},{20,28},{24,16},{28,20},{1,9},{5... | collective-permute-start | bytes 294920 | tf_op jit(solution)/shard_map/sum_chips/ppermute | solution.py:76
  49.7 1.5 %collective-permute-start.14 = (f32[96,256]{1,0:T(8,128)S(1)}, f32[96,256]{1,0:T(8,128)S(1)}, u32[]{:S(2)}, u32[]{:S(2)}) collective-permute-start(f32[96,256]{1,0:T(8,128)S(1)} %get-tuple-element.73), channel_id=1, source_target_pairs={{0,16},{4,20},{8,24},{12,28},{16,0},{20,4},{24,8},{28,12},{1,17},{... | collective-permute-start | bytes 294920 | tf_op jit(solution)/shard_map/sum_chips/ppermute | solution.py:76
  51.2 1.5 %collective-permute-done.13.refs_1_ = f32[96,256]{1,0:T(8,128)S(1)} collective-permute-done((f32[96,256]{1,0:T(8,128)S(1)}, f32[96,256]{1,0:T(8,128)S(1)}, u32[]{:S(2)}, u32[]{:S(2)}) %collective-permute-start.13) | collective-permute-done | bytes 98336 | tf_op jit(solution)/shard_map/sum_chips/ppermute | solution.py:76
  52.7 2.6 %collective-permute-done.14.refs_2_ = f32[96,256]{1,0:T(8,128)S(1)} collective-permute-done((f32[96,256]{1,0:T(8,128)S(1)}, f32[96,256]{1,0:T(8,128)S(1)}, u32[]{:S(2)}, u32[]{:S(2)}) %collective-permute-start.14) | collective-permute-done | bytes 98336 | tf_op jit(solution)/shard_map/sum_chips/ppermute | solution.py:76
  55.3 1.4 %collective-permute-done.15.refs_3_ = f32[96,256]{1,0:T(8,128)S(1)} collective-permute-done((f32[96,256]{1,0:T(8,128)S(1)}, f32[96,256]{1,0:T(8,128)S(1)}, u32[]{:S(2)}, u32[]{:S(2)}) %collective-permute-start.15) | collective-permute-done | bytes 98336 | tf_op jit(solution)/shard_map/sum_chips/ppermute | solution.py:76
  56.7 1.6 %collective-permute-start.16 = (f32[24,256]{1,0:T(8,128)S(1)}, f32[24,256]{1,0:T(8,128)S(1)}, u32[]{:S(2)}, u32[]{:S(2)}) collective-permute-start(f32[24,256]{1,0:T(8,128)S(1)} %get-tuple-element.76), channel_id=1, source_target_pairs={{0,1},{1,0},{2,3},{3,2},{4,5},{5,4},{6,7},{7,6},{8,9},{9,8},{10,11... | collective-permute-start | bytes 73736 | tf_op jit(solution)/shard_map/sum_cols/ppermute | solution.py:80
  58.3 0.1 collective-permute-start.17
  58.4 2.8 %collective-permute-start.18 = (f32[24,256]{1,0:T(8,128)S(1)}, f32[24,256]{1,0:T(8,128)S(1)}, u32[]{:S(2)}, u32[]{:S(2)}) collective-permute-start(f32[24,256]{1,0:T(8,128)S(1)} %get-tuple-element.78), channel_id=1, source_target_pairs={{0,3},{1,2},{2,1},{3,0},{4,7},{5,6},{6,5},{7,4},{8,11},{9,10},{10,... | collective-permute-start | bytes 73736 | tf_op jit(solution)/shard_map/sum_cols/ppermute | solution.py:80
  61.2 1.5 %rows_out.1 = (f32[128,256]{1,0:T(8,128)}, f32[128,256]{1,0:T(8,128)}) custom-call(s32[3]{0:T(128)S(1)} %copy-done.4, s32[3]{0:T(128)S(1)} %copy-done.5, s32[3]{0:T(128)S(1)} %copy-done.6, bf16[256,256]{1,0:T(8,128)(2,1)S(1)} %get-tuple-element.60.th, bf16[256,256]{1,0:T(8,128)(2,1)S(1)} %get-tuple-element.61.tl, f32[96,512]{1,0:T(8,128)S(1)} %get-tuple-element.79.refs_0_, ...), custom_call_target="tpu_custom_call" | custom-call | bytes 1114148 | tf_op jit(solution)/shard_map/rows_out/pallas_call | solution.py:42
  62.7 0.5 collective-permute-done.17.refs_2_
  63.2 0.8 %collective-permute-done.18.refs_3_ = f32[24,256]{1,0:T(8,128)S(1)} collective-permute-done((f32[24,256]{1,0:T(8,128)S(1)}, f32[24,256]{1,0:T(8,128)S(1)}, u32[]{:S(2)}, u32[]{:S(2)}) %collective-permute-start.18) | collective-permute-done | bytes 24608 | tf_op jit(solution)/shard_map/sum_cols/ppermute | solution.py:80
  64.1 0.9 %collective-permute-start.22 = (f32[24,256]{1,0:T(8,128)S(1)}, f32[24,256]{1,0:T(8,128)S(1)}, u32[]{:S(2)}, u32[]{:S(2)}) collective-permute-start(f32[24,256]{1,0:T(8,128)S(1)} %get-tuple-element.86.refs_0_), channel_id=1, source_target_pairs={{0,8},{4,12},{8,0},{12,4},{16,24},{20,28},{24,16},{28,20},{1,9},{5... | collective-permute-start | bytes 73736 | tf_op jit(solution)/shard_map/spread/ppermute | solution.py:76
  65.0 0.6 collective-permute-start.24
  65.6 2.0 %collective-permute-start.26 = (f32[24,256]{1,0:T(8,128)S(1)}, f32[24,256]{1,0:T(8,128)S(1)}, u32[]{:S(2)}, u32[]{:S(2)}) collective-permute-start(f32[24,256]{1,0:T(8,128)S(1)} %get-tuple-element.86.refs_0_), channel_id=1, source_target_pairs={{0,24},{4,28},{8,16},{12,20},{16,8},{20,12},{24,0},{28,4},{1,25},{... | collective-permute-start | bytes 73736 | tf_op jit(solution)/shard_map/spread/ppermute | solution.py:76
  67.6 0.3 collective-permute-done.22.refs_2_
  68.0 0.2 collective-permute-start.23
  68.1 0.7 collective-permute-done.24.refs_4_
  68.8 1.5 %collective-permute-done.26.refs_6_ = f32[24,256]{1,0:T(8,128)S(1)} collective-permute-done((f32[24,256]{1,0:T(8,128)S(1)}, f32[24,256]{1,0:T(8,128)S(1)}, u32[]{:S(2)}, u32[]{:S(2)}) %collective-permute-start.26) | collective-permute-done | bytes 24608 | tf_op jit(solution)/shard_map/spread/ppermute | solution.py:76
  70.4 1.2 %collective-permute-done.27.refs_7_ = f32[24,256]{1,0:T(8,128)S(1)} collective-permute-done((f32[24,256]{1,0:T(8,128)S(1)}, f32[24,256]{1,0:T(8,128)S(1)}, u32[]{:S(2)}, u32[]{:S(2)}) %collective-permute-start.27) | collective-permute-done | bytes 24608 | tf_op jit(solution)/shard_map/spread/ppermute | solution.py:76
  71.6 0.7 finish.1
  (36 shorter events, 0.1 us)
Async XLA Ops:
  0.6 34.0 %copy-start.1 = (f32[64,256]{1,0:T(8,128)S(1)}, f32[64,256]{1,0:T(8,128)}, u32[]{:S(2)}) copy-start(f32[64,256]{1,0:T(8,128)} %pd.3) | copy-start | bytes 196612
  2.5 17.9 %collective-permute-start = (f32[456,128]{1,0:T(8,128)}, f32[456,128]{1,0:T(8,128)S(1)}, u32[]{:S(2)}, u32[]{:S(2)}) collective-permute-start(f32[456,128]{1,0:T(8,128)} %get-tuple-element.49), channel_id=1, source_target_pairs={{0,0},{1,4},{2,8},{3,12},{4,1},{5,5},{6,9},{7,13},{8,2},{9,6},{10,... | collective-permute-start | bytes 700424 | tf_op jit(solution)/shard_map/swap/ppermute | solution.py:353
  4.1 16.3 %collective-permute-start.1 = (f32[384,128]{1,0:T(8,128)}, f32[384,128]{1,0:T(8,128)S(1)}, u32[]{:S(2)}, u32[]{:S(2)}) collective-permute-start(f32[384,128]{1,0:T(8,128)} %get-tuple-element.48.refs_0_), channel_id=1, source_target_pairs={{0,1},{1,0},{2,3},{3,2},{4,5},{5,4},{6,7},{7,6},{8,9},{9,8},{10,11... | collective-permute-start | bytes 589832 | tf_op jit(solution)/shard_map/owned/ppermute | solution.py:80
  7.5 1.6 %copy-start = (f32[4,1,128,8,1,128]{5,4,3,2,1,0:T(1,128)S(1)}, f32[4,1,128,8,1,128]{5,4,3,2,1,0:T(1,128)}, u32[]{:S(2)}) copy-start(f32[4,1,128,8,1,128]{5,4,3,2,1,0:T(1,128)} %param.10) | copy-start | bytes 6291460
  9.1 0.7 copy-start.3
  9.7 14.2 %copy-start.7 = (f32[384,128]{1,0:T(8,128)S(1)}, f32[384,128]{1,0:T(8,128)}, u32[]{:S(2)}) copy-start(f32[384,128]{1,0:T(8,128)} %get-tuple-element.48.refs_0_) | copy-start | bytes 589828
  20.4 9.5 %collective-permute-start.9 = (f32[456,128]{1,0:T(8,128)S(1)}, f32[456,128]{1,0:T(8,128)S(1)}, u32[]{:S(2)}, u32[]{:S(2)}) collective-permute-start(f32[456,128]{1,0:T(8,128)S(1)} %get-tuple-element.55.refs_0_), channel_id=1, source_target_pairs={{0,24},{4,28},{8,16},{12,20},{16,8},{20,12},{24,0},{28,4},{1,25},{... | collective-permute-start | bytes 700424 | tf_op jit(solution)/shard_map/panels/ppermute | solution.py:76
  23.4 8.4 %collective-permute-start.5 = (f32[456,128]{1,0:T(8,128)S(1)}, f32[456,128]{1,0:T(8,128)S(1)}, u32[]{:S(2)}, u32[]{:S(2)}) collective-permute-start(f32[456,128]{1,0:T(8,128)S(1)} %get-tuple-element.55.refs_0_), channel_id=1, source_target_pairs={{0,8},{4,12},{8,0},{12,4},{16,24},{20,28},{24,16},{28,20},{1,9},{5... | collective-permute-start | bytes 700424 | tf_op jit(solution)/shard_map/panels/ppermute | solution.py:76
  23.4 9.1 %collective-permute-start.7 = (f32[456,128]{1,0:T(8,128)S(1)}, f32[456,128]{1,0:T(8,128)S(1)}, u32[]{:S(2)}, u32[]{:S(2)}) collective-permute-start(f32[456,128]{1,0:T(8,128)S(1)} %get-tuple-element.55.refs_0_), channel_id=1, source_target_pairs={{0,16},{4,20},{8,24},{12,28},{16,0},{20,4},{24,8},{28,12},{1,17},{... | collective-permute-start | bytes 700424 | tf_op jit(solution)/shard_map/panels/ppermute | solution.py:76
  23.9 10.4 %collective-permute-start.2 = (f32[384,128]{1,0:T(8,128)S(1)}, f32[384,128]{1,0:T(8,128)S(1)}, u32[]{:S(2)}, u32[]{:S(2)}) collective-permute-start(f32[384,128]{1,0:T(8,128)S(1)} %copy-done.7), channel_id=1, source_target_pairs={{0,2},{1,3},{2,0},{3,1},{4,6},{5,7},{6,4},{7,5},{8,10},{9,11},{10,... | collective-permute-start | bytes 589832 | tf_op jit(solution)/shard_map/owned/ppermute | solution.py:80
  24.6 10.0 %collective-permute-start.4 = (f32[456,128]{1,0:T(8,128)S(1)}, f32[456,128]{1,0:T(8,128)S(1)}, u32[]{:S(2)}, u32[]{:S(2)}) collective-permute-start(f32[456,128]{1,0:T(8,128)S(1)} %get-tuple-element.55.refs_0_), channel_id=1, source_target_pairs={{0,4},{4,0},{8,12},{12,8},{16,20},{20,16},{24,28},{28,24},{1,5},{5... | collective-permute-start | bytes 700424 | tf_op jit(solution)/shard_map/panels/ppermute | solution.py:76
  30.0 4.6 %collective-permute-start.10 = (f32[456,128]{1,0:T(8,128)S(1)}, f32[456,128]{1,0:T(8,128)S(1)}, u32[]{:S(2)}, u32[]{:S(2)}) collective-permute-start(f32[456,128]{1,0:T(8,128)S(1)} %collective-permute-done.9.refs_6_), channel_id=1, source_target_pairs={{0,4},{4,0},{8,12},{12,8},{16,20},{20,16},{24,28},{28,24},{1,5},{5... | collective-permute-start | bytes 700424 | tf_op jit(solution)/shard_map/panels/ppermute | solution.py:76
  31.8 2.8 %collective-permute-start.6 = (f32[456,128]{1,0:T(8,128)S(1)}, f32[456,128]{1,0:T(8,128)S(1)}, u32[]{:S(2)}, u32[]{:S(2)}) collective-permute-start(f32[456,128]{1,0:T(8,128)S(1)} %collective-permute-done.5.refs_2_), channel_id=1, source_target_pairs={{0,4},{4,0},{8,12},{12,8},{16,20},{20,16},{24,28},{28,24},{1,5},{5... | collective-permute-start | bytes 700424 | tf_op jit(solution)/shard_map/panels/ppermute | solution.py:76
  32.5 2.1 %collective-permute-start.8 = (f32[456,128]{1,0:T(8,128)S(1)}, f32[456,128]{1,0:T(8,128)S(1)}, u32[]{:S(2)}, u32[]{:S(2)}) collective-permute-start(f32[456,128]{1,0:T(8,128)S(1)} %collective-permute-done.7.refs_4_), channel_id=1, source_target_pairs={{0,4},{4,0},{8,12},{12,8},{16,20},{20,16},{24,28},{28,24},{1,5},{5... | collective-permute-start | bytes 700424 | tf_op jit(solution)/shard_map/panels/ppermute | solution.py:76
  34.4 6.1 %collective-permute-start.3 = (f32[384,128]{1,0:T(8,128)S(1)}, f32[384,128]{1,0:T(8,128)S(1)}, u32[]{:S(2)}, u32[]{:S(2)}) collective-permute-start(f32[384,128]{1,0:T(8,128)S(1)} %collective-permute-done.2.refs_2_), channel_id=1, source_target_pairs={{0,1},{1,0},{2,3},{3,2},{4,5},{5,4},{6,7},{7,6},{8,9},{9,8},{10,11... | collective-permute-start | bytes 589832 | tf_op jit(solution)/shard_map/owned/ppermute | solution.py:80
  36.8 7.5 %collective-permute-start.12 = (f32[96,512]{1,0:T(8,128)S(1)}, f32[96,512]{1,0:T(8,128)S(1)}, u32[]{:S(2)}, u32[]{:S(2)}) collective-permute-start(f32[96,512]{1,0:T(8,128)S(1)} %get-tuple-element.70), channel_id=1, source_target_pairs={{0,1},{1,0},{2,3},{3,2},{4,5},{5,4},{6,7},{7,6},{8,9},{9,8},{10,11... | collective-permute-start | bytes 589832 | tf_op jit(solution)/shard_map/sum_shares/ppermute | solution.py:80
  42.2 2.2 %collective-permute-start.11 = (f32[384,256]{1,0:T(8,128)S(1)}, f32[384,256]{1,0:T(8,128)S(1)}, u32[]{:S(2)}, u32[]{:S(2)}) collective-permute-start(f32[384,256]{1,0:T(8,128)S(1)} %get-tuple-element.68), channel_id=1, source_target_pairs={{0,4},{4,0},{8,12},{12,8},{16,20},{20,16},{24,28},{28,24},{1,5},{5... | collective-permute-start | bytes 1179656 | tf_op jit(solution)/shard_map/sum_core/ppermute | solution.py:76
  42.3 18.9 %collective-permute-start.19 = (f32[96,512]{1,0:T(8,128)S(1)}, f32[96,512]{1,0:T(8,128)S(1)}, u32[]{:S(2)}, u32[]{:S(2)}) collective-permute-start(f32[96,512]{1,0:T(8,128)S(1)} %get-tuple-element.80), channel_id=1, source_target_pairs={{0,1},{1,0},{2,3},{3,2},{4,5},{5,4},{6,7},{7,6},{8,9},{9,8},{10,11... | collective-permute-start | bytes 589832 | tf_op jit(solution)/shard_map/sum_shares/ppermute | solution.py:80
  44.3 16.8 %copy-start.4 = (s32[3]{0:T(128)S(1)}, s32[3]{0:T(128)}, u32[]{:S(2)}) copy-start(s32[3]{0:T(128)} %blocks.3) | copy-start | bytes 40
  44.3 16.8 %copy-start.5 = (s32[3]{0:T(128)S(1)}, s32[3]{0:T(128)}, u32[]{:S(2)}) copy-start(s32[3]{0:T(128)} %psize.1) | copy-start | bytes 40
  44.3 16.9 %copy-start.6 = (s32[3]{0:T(128)S(1)}, s32[3]{0:T(128)}, u32[]{:S(2)}) copy-start(s32[3]{0:T(128)} %csize.1) | copy-start | bytes 40
  44.4 27.2 %copy-start.2 = (f32[64,256]{1,0:T(8,128)S(1)}, f32[64,256]{1,0:T(8,128)}, u32[]{:S(2)}) copy-start(f32[64,256]{1,0:T(8,128)} %cd.1) | copy-start | bytes 196612
  44.5 16.7 %collective-permute-start.20 = (f32[96,512]{1,0:T(8,128)S(1)}, f32[96,512]{1,0:T(8,128)S(1)}, u32[]{:S(2)}, u32[]{:S(2)}) collective-permute-start(f32[96,512]{1,0:T(8,128)S(1)} %get-tuple-element.81), channel_id=1, source_target_pairs={{0,2},{1,3},{2,0},{3,1},{4,6},{5,7},{6,4},{7,5},{8,10},{9,11},{10,... | collective-permute-start | bytes 589832 | tf_op jit(solution)/shard_map/sum_shares/ppermute | solution.py:80
  47.5 5.2 %collective-permute-start.13 = (f32[96,256]{1,0:T(8,128)S(1)}, f32[96,256]{1,0:T(8,128)S(1)}, u32[]{:S(2)}, u32[]{:S(2)}) collective-permute-start(f32[96,256]{1,0:T(8,128)S(1)} %get-tuple-element.72), channel_id=1, source_target_pairs={{0,8},{4,12},{8,0},{12,4},{16,24},{20,28},{24,16},{28,20},{1,9},{5... | collective-permute-start | bytes 294920 | tf_op jit(solution)/shard_map/sum_chips/ppermute | solution.py:76
  49.7 5.7 %collective-permute-start.14 = (f32[96,256]{1,0:T(8,128)S(1)}, f32[96,256]{1,0:T(8,128)S(1)}, u32[]{:S(2)}, u32[]{:S(2)}) collective-permute-start(f32[96,256]{1,0:T(8,128)S(1)} %get-tuple-element.73), channel_id=1, source_target_pairs={{0,16},{4,20},{8,24},{12,28},{16,0},{20,4},{24,8},{28,12},{1,17},{... | collective-permute-start | bytes 294920 | tf_op jit(solution)/shard_map/sum_chips/ppermute | solution.py:76
  51.2 5.5 %collective-permute-start.15 = (f32[96,256]{1,0:T(8,128)S(1)}, f32[96,256]{1,0:T(8,128)S(1)}, u32[]{:S(2)}, u32[]{:S(2)}) collective-permute-start(f32[96,256]{1,0:T(8,128)S(1)} %get-tuple-element.74), channel_id=1, source_target_pairs={{0,24},{4,28},{8,16},{12,20},{16,8},{20,12},{24,0},{28,4},{1,25},{... | collective-permute-start | bytes 294920 | tf_op jit(solution)/shard_map/sum_chips/ppermute | solution.py:76
  56.7 6.0 %collective-permute-start.16 = (f32[24,256]{1,0:T(8,128)S(1)}, f32[24,256]{1,0:T(8,128)S(1)}, u32[]{:S(2)}, u32[]{:S(2)}) collective-permute-start(f32[24,256]{1,0:T(8,128)S(1)} %get-tuple-element.76), channel_id=1, source_target_pairs={{0,1},{1,0},{2,3},{3,2},{4,5},{5,4},{6,7},{7,6},{8,9},{9,8},{10,11... | collective-permute-start | bytes 73736 | tf_op jit(solution)/shard_map/sum_cols/ppermute | solution.py:80
  58.3 4.9 %collective-permute-start.17 = (f32[24,256]{1,0:T(8,128)S(1)}, f32[24,256]{1,0:T(8,128)S(1)}, u32[]{:S(2)}, u32[]{:S(2)}) collective-permute-start(f32[24,256]{1,0:T(8,128)S(1)} %get-tuple-element.77), channel_id=1, source_target_pairs={{0,2},{1,3},{2,0},{3,1},{4,6},{5,7},{6,4},{7,5},{8,10},{9,11},{10,... | collective-permute-start | bytes 73736 | tf_op jit(solution)/shard_map/sum_cols/ppermute | solution.py:80
  58.4 5.6 %collective-permute-start.18 = (f32[24,256]{1,0:T(8,128)S(1)}, f32[24,256]{1,0:T(8,128)S(1)}, u32[]{:S(2)}, u32[]{:S(2)}) collective-permute-start(f32[24,256]{1,0:T(8,128)S(1)} %get-tuple-element.78), channel_id=1, source_target_pairs={{0,3},{1,2},{2,1},{3,0},{4,7},{5,6},{6,5},{7,4},{8,11},{9,10},{10,... | collective-permute-start | bytes 73736 | tf_op jit(solution)/shard_map/sum_cols/ppermute | solution.py:80
  64.1 3.9 %collective-permute-start.22 = (f32[24,256]{1,0:T(8,128)S(1)}, f32[24,256]{1,0:T(8,128)S(1)}, u32[]{:S(2)}, u32[]{:S(2)}) collective-permute-start(f32[24,256]{1,0:T(8,128)S(1)} %get-tuple-element.86.refs_0_), channel_id=1, source_target_pairs={{0,8},{4,12},{8,0},{12,4},{16,24},{20,28},{24,16},{28,20},{1,9},{5... | collective-permute-start | bytes 73736 | tf_op jit(solution)/shard_map/spread/ppermute | solution.py:76
  65.0 3.8 %collective-permute-start.24 = (f32[24,256]{1,0:T(8,128)S(1)}, f32[24,256]{1,0:T(8,128)S(1)}, u32[]{:S(2)}, u32[]{:S(2)}) collective-permute-start(f32[24,256]{1,0:T(8,128)S(1)} %get-tuple-element.86.refs_0_), channel_id=1, source_target_pairs={{0,16},{4,20},{8,24},{12,28},{16,0},{20,4},{24,8},{28,12},{1,17},{... | collective-permute-start | bytes 73736 | tf_op jit(solution)/shard_map/spread/ppermute | solution.py:76
  65.6 4.7 %collective-permute-start.26 = (f32[24,256]{1,0:T(8,128)S(1)}, f32[24,256]{1,0:T(8,128)S(1)}, u32[]{:S(2)}, u32[]{:S(2)}) collective-permute-start(f32[24,256]{1,0:T(8,128)S(1)} %get-tuple-element.86.refs_0_), channel_id=1, source_target_pairs={{0,24},{4,28},{8,16},{12,20},{16,8},{20,12},{24,0},{28,4},{1,25},{... | collective-permute-start | bytes 73736 | tf_op jit(solution)/shard_map/spread/ppermute | solution.py:76
  67.6 2.8 %collective-permute-start.21 = (f32[24,256]{1,0:T(8,128)S(1)}, f32[24,256]{1,0:T(8,128)S(1)}, u32[]{:S(2)}, u32[]{:S(2)}) collective-permute-start(f32[24,256]{1,0:T(8,128)S(1)} %get-tuple-element.86.refs_0_), channel_id=1, source_target_pairs={{0,4},{4,0},{8,12},{12,8},{16,20},{20,16},{24,28},{28,24},{1,5},{5... | collective-permute-start | bytes 73736 | tf_op jit(solution)/shard_map/spread/ppermute | solution.py:76
  68.0 2.4 %collective-permute-start.23 = (f32[24,256]{1,0:T(8,128)S(1)}, f32[24,256]{1,0:T(8,128)S(1)}, u32[]{:S(2)}, u32[]{:S(2)}) collective-permute-start(f32[24,256]{1,0:T(8,128)S(1)} %collective-permute-done.22.refs_2_), channel_id=1, source_target_pairs={{0,4},{4,0},{8,12},{12,8},{16,20},{20,16},{24,28},{28,24},{1,5},{5... | collective-permute-start | bytes 73736 | tf_op jit(solution)/shard_map/spread/ppermute | solution.py:76
  68.8 1.6 %collective-permute-start.25 = (f32[24,256]{1,0:T(8,128)S(1)}, f32[24,256]{1,0:T(8,128)S(1)}, u32[]{:S(2)}, u32[]{:S(2)}) collective-permute-start(f32[24,256]{1,0:T(8,128)S(1)} %collective-permute-done.24.refs_4_), channel_id=1, source_target_pairs={{0,4},{4,0},{8,12},{12,8},{16,20},{20,16},{24,28},{28,24},{1,5},{5... | collective-permute-start | bytes 73736 | tf_op jit(solution)/shard_map/spread/ppermute | solution.py:76
  70.4 1.2 %collective-permute-start.27 = (f32[24,256]{1,0:T(8,128)S(1)}, f32[24,256]{1,0:T(8,128)S(1)}, u32[]{:S(2)}, u32[]{:S(2)}) collective-permute-start(f32[24,256]{1,0:T(8,128)S(1)} %collective-permute-done.26.refs_6_), channel_id=1, source_target_pairs={{0,4},{4,0},{8,12},{12,8},{16,20},{20,16},{24,28},{28,24},{1,5},{5... | collective-permute-start | bytes 73736 | tf_op jit(solution)/shard_map/spread/ppermute | solution.py:76

commit v5 on v4

--- a/solution.py
+++ b/solution.py
@@ -59,8 +59,8 @@
     return [(pltpu.SMEM, a) for a in arrays]
 
 
-def hbm(*arrays):
-    return [(pltpu.HBM, a) for a in arrays]
+def anywhere(*arrays):
+    return [(pl.ANY, a) for a in arrays]
 
 
 def fetch(sources, targets, sems):
@@ -74,6 +74,10 @@
 
 def exchange(value, mask, row_total):
     return lax.ppermute(value, "row", [(i, i ^ mask) for i in range(row_total)])
+
+
+def shift(value, step, col_total):
+    return lax.ppermute(value, "col", [(i, (i + step) % col_total) for i in range(col_total)])
 
 
 def flip(value, mask, col_total):
@@ -94,29 +98,65 @@
         self.eight = self.ws // rows
         self.live = self.slots * self.B
         self.parts = self.W // self.B
-        self.block = self.payload + self.ws + 8
+        self.part = self.payload // 2
+        self.block = self.part + self.ws // 2 + 8
 
 
 def pack(s, *refs):
-    sources, (sent, mine, *targets, sems) = refs[:6], refs[6:]
+    sources, (kept, sent, mine, parents, children, *targets, sems) = refs[:6], refs[6:]
     for copy in fetch(sources, targets, sems):
         copy.wait()
     blocks, psize, csize, parent, child, top = targets
+    row = lax.axis_index("row")
+    side = lax.div(lax.rem(row, s.C), s.C // 2)
     lane = lax.broadcasted_iota(jnp.int32, (s.ws, s.B), 1)
     for slot in range(s.slots):
         base = slot * 2 * s.ws
-        for which, panel, sizes in ((0, parent, psize), (1, child, csize)):
+        for which, panel, sizes, half in ((0, parent, psize, parents), (1, child, csize, children)):
             live = jnp.where(lane < sizes[slot], panel[slot], 0.0)
-            rows = slice(base + which * s.ws, base + (which + 1) * s.ws)
-            mine[rows, :] = live
-            sent[rows, :] = live
-    half = lax.div(lax.axis_index("row"), s.C) * s.B
-    sent[s.payload : s.payload + s.ws, :] = top[:, pl.ds(pl.multiple_of(half, s.B), s.B)]
+            mine[base + which * s.ws : base + (which + 1) * s.ws, :] = live
+            half[slot * s.ws : (slot + 1) * s.ws, :] = live
+    columns = pl.ds(pl.multiple_of(lax.div(row, s.C) * s.B, s.B), s.B)
     row8 = lax.broadcasted_iota(jnp.int32, (8, s.B), 0)
     ids = jnp.zeros((8, s.B), f32)
     for slot in range(s.slots):
         ids = jnp.where(row8 == slot, blocks[slot].astype(f32), ids)
-    sent[s.payload + s.ws :, :] = ids
+    quarter = s.ws // 2
+    for out, at in ((kept, side), (sent, 1 - side)):
+
+        @pl.when(at == 0)
+        def _():
+            out[: s.part, :] = parents[...]
+
+        @pl.when(at == 1)
+        def _():
+            out[: s.part, :] = children[...]
+
+        rows = pl.ds(pl.multiple_of(at * quarter, quarter), quarter)
+        out[s.part : s.part + quarter, :] = top[rows, columns]
+        out[s.part + quarter :, :] = ids
+
+
+def route(s, kept, got, first, second, sems):
+    side = lax.div(lax.rem(lax.axis_index("row"), s.C), s.C // 2)
+    high = lax.div(lax.axis_index("col"), s.C // 2)
+    own = high == side
+
+    @pl.when(own)
+    def _():
+        for copy in fetch((kept, got), (first, second), sems):
+            copy.wait()
+
+    @pl.when(jnp.logical_not(own))
+    def _():
+        for copy in fetch((got, kept), (first, second), sems):
+            copy.wait()
+
+
+def join(s, first, second, *refs):
+    out = refs[-1 - (len(refs) - 1) // 2]
+    out[: s.block, :] = first[...]
+    out[s.block :, :] = second[...]
 
 
 def order(s, *refs):
@@ -152,7 +192,7 @@
     places = []
     for owner in range(s.Q):
         for slot in range(s.slots):
-            at = s.payload + s.ws + slot
+            at = s.block - 8 + slot
             number = jnp.max(panels[owner * s.C][at : at + 1, :]).astype(jnp.int32)
             places.append(jnp.where(number < 0, s.CC, lax.div(jnp.maximum(number, 0), s.C)))
     for m in range(s.CC):
@@ -165,19 +205,25 @@
             xh[m] = jnp.zeros((2 * s.W, s.B), bf16)
             xl[m] = jnp.zeros((2 * s.W, s.B), bf16)
 
+    high, quarter = lax.div(col, s.C // 2), s.ws // 2
     for mask in range(s.R):
         sender = jnp.bitwise_xor(row, mask)
-        first = pl.multiple_of(lax.rem(sender, s.C) * s.ws, s.ws)
-        for slot in range(s.slots):
-            place = places[mask // s.C * s.slots + slot]
-            for which in range(2):
-                start = (slot * 2 + which) * s.ws
-                high, low = split(panels[mask][start : start + s.ws, :])
-                rows = pl.ds(pl.multiple_of(which * s.W + first, s.ws), s.ws)
-                xh[place, rows, :] = high
-                xl[place, rows, :] = low
-        half = pl.multiple_of(lax.div(sender, s.C) * s.B, s.B)
-        top[pl.ds(first, s.ws), pl.ds(half, s.B)] = panels[mask][s.payload : s.payload + s.ws, :]
+        owner, inside = lax.div(sender, s.C), lax.rem(sender, s.C)
+        side, low = lax.div(inside, s.C // 2), lax.rem(inside, s.C // 2)
+        lanes = pl.ds(pl.multiple_of(owner * s.B, s.B), s.B)
+        for turn in range(2):
+            source = jnp.bitwise_xor(high, turn) * (s.C // 2) + low
+            begin = turn * s.block
+            rows = pl.ds(pl.multiple_of(side * s.W + source * s.ws, s.ws), s.ws)
+            for slot in range(s.slots):
+                place = places[mask // s.C * s.slots + slot]
+                start = begin + slot * s.ws
+                up, down = split(panels[mask][start : start + s.ws, :])
+                xh[place, rows, :] = up
+                xl[place, rows, :] = down
+            start = begin + s.part
+            rows = pl.ds(pl.multiple_of(source * s.ws + side * quarter, quarter), quarter)
+            top[rows, lanes] = panels[mask][start : start + quarter, :]
     right = tuple(jnp.concatenate([x[i] for i in range(s.CC)], axis=1) for x in (xh, xl))
     total[...] = dot3((sh[...], sl[...]), right, NT)
     gh[...], gl[...] = split(total[...])
@@ -247,9 +293,9 @@
     for term in terms[1:]:
         value = value + term[...]
     total[...] = value
-    for mask in range(s.C):
-        rows = pl.ds(pl.multiple_of(jnp.bitwise_xor(col, mask) * size, size), size)
-        outs[mask][...] = total[rows, :]
+    for step in range(s.C):
+        rows = pl.ds(pl.multiple_of(lax.rem(col + step, s.C) * size, size), size)
+        outs[step][...] = total[rows, :]
 
 
 def plus(s, *refs):
@@ -259,7 +305,7 @@
 
 
 def add_all(s, *refs):
-    terms, out = refs[: s.C], refs[s.C + 2]
+    terms, out = refs[:-1], refs[-1]
     value = terms[0][...]
     for term in terms[1:]:
         value = value + term[...]
@@ -303,13 +349,15 @@
             child[rows, :] = z[slot * s.share : (slot + 1) * s.share, :]
 
 
-def swap_perm(s):
-    return [
-        ((q * s.C + a) * s.C + c, (q * s.C + c) * s.C + a)
-        for q in range(s.Q)
-        for a in range(s.C)
-        for c in range(s.C)
-    ]
+def column_perm(s, turn):
+    half, pairs = s.C // 2, []
+    for q in range(s.Q):
+        for at in range(s.C):
+            for c in range(s.C):
+                to = (turn ^ c // half) * half + at % half
+                row = q * s.C + at // half * half + c % half
+                pairs.append(((q * s.C + at) * s.C + c, row * s.C + to))
+    return pairs
 
 
 def fast_body(
@@ -333,9 +381,9 @@
     numbers = pltpu.SMEM((s.slots,), jnp.int32)
     by_slot = (s.slots, ws, B)
     with jax.named_scope("pack"):
-        sent, mine = call(
+        kept, sent, mine, parents, children = call(
             bind(pack),
-            hbm(
+            anywhere(
                 parent_blocks,
                 parent_sizes,
                 child_sizes,
@@ -343,31 +391,45 @@
                 jnp.transpose(child_panel, (1, 0, 2)),
                 child_top,
             ),
-            [(s.block, B), (s.payload, B)],
+            [(s.block, B)] * 2 + [(s.payload, B)] + [(s.part, B)] * 2,
             [numbers] * 3
             + [pltpu.VMEM(by_slot, f32)] * 2
             + [pltpu.VMEM((ws, W), f32), pltpu.SemaphoreType.DMA((6,))],
             limit=None,
         )
-    with jax.named_scope("swap"):
-        own = lax.ppermute(sent, ("row", "col"), swap_perm(s))
+    with jax.named_scope("to_column"):
+        got = exchange(sent, C // 2, R)
+        pieces = call(
+            bind(route),
+            anywhere(kept, got),
+            [(s.block, B)] * 2,
+            [pltpu.SemaphoreType.DMA((2,))],
+        )
+        pieces = [
+            lax.ppermute(pieces[turn], ("row", "col"), column_perm(s, turn)) for turn in range(2)
+        ]
     with jax.named_scope("split_live"):
         sh, sl = call(
             bind(split_live),
-            hbm(cached, parent_blocks),
+            anywhere(cached, parent_blocks),
             [((live, s.CC * B), bf16)] * 2,
             [pltpu.VMEM((s.slots * B * s.CC, B), f32), numbers]
             + [pltpu.SemaphoreType.DMA((1 + s.slots,))],
         )
     with jax.named_scope("owned"):
-        owned = {0: mine, 1: flip(mine, 1, C)}
-        mask = C // 2
+        near = flip(mine, 1, C)
+        held, mask = {0: mine}, C // 2
         while mask > 1:
-            owned.update({m ^ mask: flip(owned[m], mask, C) for m in owned if m != 1})
+            held.update({m ^ mask: flip(held[m], mask, C) for m in list(held)})
             mask //= 2
-        owned.update({m ^ 1: flip(owned[m], 1, C) for m in list(owned) if m > 1})
-    with jax.named_scope("order"):
-        own, owned[1], sh, sl = call(bind(order), (), (), passed=(own, owned[1], sh, sl))
+        owned = {0: mine, 1: near}
+        for m in range(2, C, 2):
+            (owned[m],) = call(bind(order), (), (), passed=(held[m],), ahead=8e9)
+            owned[m + 1] = flip(owned[m], 1, C)
+    with jax.named_scope("join"):
+        own, owned[1], sh, sl = call(
+            bind(join), vmem(*pieces), [(2 * s.block, B)], passed=(owned[1], sh, sl)
+        )
     with jax.named_scope("panels"):
         panels = {0: own}
         for mask in range(2, R, 2):
@@ -427,6 +489,7 @@
             passed=(shares[2],),
         )
         mine = [mine[0]] + [exchange(mine[m], 2 * m, R) for m in range(1, s.chips)]
+
     with jax.named_scope("sum_shares"):
         mask = 1
         while mask < C:
@@ -435,7 +498,12 @@
     with jax.named_scope("sum_cols"):
         scr = [pltpu.VMEM((C * 3 * s.eight, W), f32)]
         cols = call(bind(add_cols), vmem(*mine), [(3 * s.eight, W)] * C, scr)
-        cols = [cols[0]] + [flip(cols[m], m, C) for m in range(1, C)]
+        cols = [cols[0]] + [shift(cols[k], k, C) for k in range(1, C)]
+    with jax.named_scope("spread"):
+        (done,) = call(bind(add_all), vmem(*cols), [(3 * s.eight, W)])
+        parts = {0: done}
+        for mask in range(2, R, 2):
+            parts[mask] = exchange(done, mask, R)
     with jax.named_scope("rows_out"):
         parent_rows, child_rows = call(
             bind(rows_out),
@@ -443,12 +511,9 @@
             [(s.RC * s.share, W)] * 2,
         )
     with jax.named_scope("spread"):
-        done, parent_rows, child_rows = call(
-            bind(add_all), vmem(*cols), [(3 * s.eight, W)], passed=(parent_rows, child_rows)
-        )
-        parts = {0: done}
-        for mask in range(2, R, 2):
-            parts[mask] = exchange(done, mask, R)
+        parts[R - 2], parent_rows, child_rows = call(
+            bind(order), (), (), passed=(parts[R - 2], parent_rows, child_rows)
+        )
         for mask in range(0, R, 2):
             parts[mask + 1] = exchange(parts[mask], 1, R)
     with jax.named_scope("finish"):

time: 72.5 us -> 70.5 us (0.972)
  waiting for transfers between devices: 31.5 us -> 19.5 us
  starting transfers between devices: 28.4 us -> 37.1 us
  local copies, waits for them, and re-layouts: 2.27 us -> 3.17 us
    ppermute x9 -> x6, waiting for transfers between devices: 14.6 us -> 4.59 us  [flip(): return lax.ppermute(value, 'col', [(i, i ^ mask) for i in range(col_total)])]
    ppermute x18 -> x19, starting transfers between devices: 11.2 us -> 18.9 us  [exchange(): return lax.ppermute(value, 'row', [(i, i ^ mask) for i in range(row_total)])]
    ppermute x1 -> x5, starting transfers between devices: 1.6 us -> 7.45 us  [the longest x3 3.88 us: shift(): lax.ppermute(value, 'col', [(i, (i + step) % col_total) for i in range(co...]
    ppermute x9 -> x6, starting transfers between devices: 15.6 us -> 10.7 us  [flip(): return lax.ppermute(value, 'col', [(i, i ^ mask) for i in range(col_total)])]
    ppermute x18 -> x19, waiting for transfers between devices: 16.9 us -> 12.5 us  [exchange(): return lax.ppermute(value, 'row', [(i, i ^ mask) for i in range(row_total)])]
    ppermute x1 -> x5, waiting for transfers between devices: 0.01 us -> 2.47 us  [the longest x3 2.36 us: shift(): lax.ppermute(value, 'col', [(i, (i + step) % col_total) for i in range(co...]
    unnamed x16 -> x18, local copies, waits for them, and re-layouts: 2.27 us -> 3.17 us
    pallas_call x12 -> x15, Pallas kernels: 9.29 us -> 9.68 us  [call(): pl.pallas_call(kernel, out_shape=shapes, in_specs=[pl.BlockSpec(memory_sp...]
  transfers between devices with their start and end apart: 28 -> 30, of which waited for: 16 -> 15; matrix products, arithmetic and copies ran while one was open for 0% -> 0% of each run, Pallas kernels for 9% -> 10%
where the time goes in v5:
time: 70.5 us; the launch traced here: 70.3 us
  starting transfers between devices  37.1 us (53%)
  waiting for transfers between devices  19.5 us (28%)
  Pallas kernels  9.68 us (14%)
  local copies, waits for them, and re-layouts  3.17 us (4%)
  between operations  0.81 us (1%)
    ppermute x19, starting transfers between devices, exchange(): return lax.ppermute(value, 'row', [(i, i ^ mask) for i in range(row_total)])  18.9 us
    ppermute x19, waiting for transfers between devices, exchange(): return lax.ppermute(value, 'row', [(i, i ^ mask) for i in range(row_total)])  12.5 us
    ppermute x6, starting transfers between devices, flip(): return lax.ppermute(value, 'col', [(i, i ^ mask) for i in range(col_total)])  10.7 us
    pallas_call x15, Pallas kernels, call(): pl.pallas_call(kernel, out_shape=shapes, in_specs=[pl.BlockSpec(memory_sp...  9.68 us
    ppermute x6, waiting for transfers between devices, flip(): return lax.ppermute(value, 'col', [(i, i ^ mask) for i in range(col_total)])  4.59 us
    ppermute x3, starting transfers between devices, shift(): lax.ppermute(value, 'col', [(i, (i + step) % col_total) for i in range(co...  3.88 us
    ppermute x2, starting transfers between devices, fast_body(): lax.ppermute(pieces[turn], ('row', 'col'), column_perm(s, turn))  3.57 us
    unnamed x18, local copies, waits for them, and re-layouts  3.17 us
  transfers between devices with their start and end apart: 30, of which 15 were waited for; matrix products, arithmetic and copies ran while one was open for 0% of the time, Pallas kernels for 10%

profile of v5, /device:TPU:0, one launch (start us, length us, event | category | flops | bytes accessed | tf_op | source)
XLA Modules:
  0.0 70.3 jit_solution(17030601642119224801)
XLA Ops:
  0.6 1.9 %pack.1 = (f32[232,128]{1,0:T(8,128)}, f32[232,128]{1,0:T(8,128)}, f32[384,128]{1,0:T(8,128)}, f32[192,128]{1,0:T(8,128)}, f32[192,128]{1,0:T(8,128)}) custom-call(s32[3]{0:T(128)} %blocks.3, s32[3]{0:T(128)} %psize.1, s32[3]{0:T(128)} %csize.1, f32[3,64,128]{2,1,0:T(8,128)} %bitcast.12, f32[3,64,128]{2,1,0:T(8,128)} %bitcast.13, f32[64,256]{1,0:T(8,128)} %refs_5_.1), custom_call_target="tpu_custom_call" | custom-call | bytes 892964 | tf_op jit(solution)/shard_map/pack/pallas_call | solution.py:42
  2.5 3.0 %collective-permute-start = (f32[232,128]{1,0:T(8,128)}, f32[232,128]{1,0:T(8,128)S(1)}, u32[]{:S(2)}, u32[]{:S(2)}) collective-permute-start(f32[232,128]{1,0:T(8,128)} %get-tuple-element.53), channel_id=1, source_target_pairs={{0,8},{4,12},{8,0},{12,4},{16,24},{20,28},{24,16},{28,20},{1,9},{5... | collective-permute-start | bytes 356360 | tf_op jit(solution)/shard_map/to_column/ppermute | solution.py:76
  5.5 1.6 %collective-permute-start.3 = (f32[384,128]{1,0:T(8,128)}, f32[384,128]{1,0:T(8,128)S(1)}, u32[]{:S(2)}, u32[]{:S(2)}) collective-permute-start(f32[384,128]{1,0:T(8,128)} %get-tuple-element.51.refs_0_), channel_id=1, source_target_pairs={{0,1},{1,0},{2,3},{3,2},{4,5},{5,4},{6,7},{7,6},{8,9},{9,8},{10,11... | collective-permute-start | bytes 589832 | tf_op jit(solution)/shard_map/owned/ppermute | solution.py:84
  7.1 1.9 %collective-permute-done.got = f32[232,128]{1,0:T(8,128)S(1)} collective-permute-done((f32[232,128]{1,0:T(8,128)}, f32[232,128]{1,0:T(8,128)S(1)}, u32[]{:S(2)}, u32[]{:S(2)}) %collective-permute-start) | collective-permute-done | bytes 118816 | tf_op jit(solution)/shard_map/to_column/ppermute | solution.py:76
  9.0 0.9 %copy-done.2 = f32[232,128]{1,0:T(8,128)S(1)} copy-done((f32[232,128]{1,0:T(8,128)S(1)}, f32[232,128]{1,0:T(8,128)}, u32[]{:S(2)}) %copy-start.2) | copy-done | bytes 118808
  9.9 0.3 to_column.1
  10.2 0.7 collective-permute-start.1
  10.8 2.9 %collective-permute-start.2 = (f32[232,128]{1,0:T(8,128)S(1)}, f32[232,128]{1,0:T(8,128)S(1)}, u32[]{:S(2)}, u32[]{:S(2)}) collective-permute-start(f32[232,128]{1,0:T(8,128)S(1)} %get-tuple-element.55), channel_id=1, source_target_pairs={{0,2},{1,6},{2,0},{3,4},{4,3},{5,7},{6,1},{7,5},{8,10},{9,14},{10,... | collective-permute-start | bytes 356360 | tf_op jit(solution)/shard_map/to_column/ppermute | solution.py:409
  13.8 1.6 %copy-done = f32[4,1,128,8,1,128]{5,4,3,2,1,0:T(1,128)S(1)} copy-done((f32[4,1,128,8,1,128]{5,4,3,2,1,0:T(1,128)S(1)}, f32[4,1,128,8,1,128]{5,4,3,2,1,0:T(1,128)}, u32[]{:S(2)}) %copy-start) | copy-done | bytes 2097176
  15.3 0.7 copy-done.4
  16.0 1.2 %split_live.1 = (bf16[384,1024]{1,0:T(8,128)(2,1)S(1)}, bf16[384,1024]{1,0:T(8,128)(2,1)S(1)}) custom-call(f32[4096,128]{1,0:T(8,128)S(1)} %bitcast.9, s32[3]{0:T(128)S(1)} %copy-done.4), custom_call_target="tpu_custom_call" | custom-call | bytes 3670028 | tf_op jit(solution)/shard_map/split_live/pallas_call | solution.py:42
  17.3 1.6 %collective-permute-start.9 = (f32[464,128]{1,0:T(8,128)S(1)}, f32[464,128]{1,0:T(8,128)S(1)}, u32[]{:S(2)}, u32[]{:S(2)}) collective-permute-start(f32[464,128]{1,0:T(8,128)S(1)} %get-tuple-element.61.refs_0_), channel_id=1, source_target_pairs={{0,16},{4,20},{8,24},{12,28},{16,0},{20,4},{24,8},{28,12},{1,17},{... | collective-permute-start | bytes 712712 | tf_op jit(solution)/shard_map/panels/ppermute | solution.py:76
  18.9 1.4 %collective-permute-start.11 = (f32[464,128]{1,0:T(8,128)S(1)}, f32[464,128]{1,0:T(8,128)S(1)}, u32[]{:S(2)}, u32[]{:S(2)}) collective-permute-start(f32[464,128]{1,0:T(8,128)S(1)} %get-tuple-element.61.refs_0_), channel_id=1, source_target_pairs={{0,24},{4,28},{8,16},{12,20},{16,8},{20,12},{24,0},{28,4},{1,25},{... | collective-permute-start | bytes 712712 | tf_op jit(solution)/shard_map/panels/ppermute | solution.py:76
  20.3 0.5 collective-permute-start.7
  20.9 3.5 %collective-permute-start.4 = (f32[384,128]{1,0:T(8,128)S(1)}, f32[384,128]{1,0:T(8,128)S(1)}, u32[]{:S(2)}, u32[]{:S(2)}) collective-permute-start(f32[384,128]{1,0:T(8,128)S(1)} %copy-done.8), channel_id=1, source_target_pairs={{0,2},{1,3},{2,0},{3,1},{4,6},{5,7},{6,4},{7,5},{8,10},{9,11},{10,... | collective-permute-start | bytes 589832 | tf_op jit(solution)/shard_map/owned/ppermute | solution.py:84
  24.4 0.7 %collective-permute-start.6 = (f32[464,128]{1,0:T(8,128)S(1)}, f32[464,128]{1,0:T(8,128)S(1)}, u32[]{:S(2)}, u32[]{:S(2)}) collective-permute-start(f32[464,128]{1,0:T(8,128)S(1)} %get-tuple-element.61.refs_0_), channel_id=1, source_target_pairs={{0,4},{4,0},{8,12},{12,8},{16,20},{20,16},{24,28},{28,24},{1,5},{5... | collective-permute-start | bytes 712712 | tf_op jit(solution)/shard_map/panels/ppermute | solution.py:76
  25.1 3.4 %collective-permute-done.9.refs_4_ = f32[464,128]{1,0:T(8,128)S(1)} collective-permute-done((f32[464,128]{1,0:T(8,128)S(1)}, f32[464,128]{1,0:T(8,128)S(1)}, u32[]{:S(2)}, u32[]{:S(2)}) %collective-permute-start.9) | collective-permute-done | bytes 237600 | tf_op jit(solution)/shard_map/panels/ppermute | solution.py:76
  28.5 2.8 %collective-permute-start.10 = (f32[464,128]{1,0:T(8,128)S(1)}, f32[464,128]{1,0:T(8,128)S(1)}, u32[]{:S(2)}, u32[]{:S(2)}) collective-permute-start(f32[464,128]{1,0:T(8,128)S(1)} %collective-permute-done.9.refs_4_), channel_id=1, source_target_pairs={{0,4},{4,0},{8,12},{12,8},{16,20},{20,16},{24,28},{28,24},{1,5},{5... | collective-permute-start | bytes 712712 | tf_op jit(solution)/shard_map/panels/ppermute | solution.py:76
  31.3 1.2 %collective-permute-start.8 = (f32[464,128]{1,0:T(8,128)S(1)}, f32[464,128]{1,0:T(8,128)S(1)}, u32[]{:S(2)}, u32[]{:S(2)}) collective-permute-start(f32[464,128]{1,0:T(8,128)S(1)} %collective-permute-done.7.refs_2_), channel_id=1, source_target_pairs={{0,4},{4,0},{8,12},{12,8},{16,20},{20,16},{24,28},{28,24},{1,5},{5... | collective-permute-start | bytes 712712 | tf_op jit(solution)/shard_map/panels/ppermute | solution.py:76
  32.5 0.8 %collective-permute-start.5 = (f32[384,128]{1,0:T(8,128)S(1)}, f32[384,128]{1,0:T(8,128)S(1)}, u32[]{:S(2)}, u32[]{:S(2)}) collective-permute-start(f32[384,128]{1,0:T(8,128)S(1)} %owned.1.refs_2_), channel_id=1, source_target_pairs={{0,1},{1,0},{2,3},{3,2},{4,5},{5,4},{6,7},{7,6},{8,9},{9,8},{10,11... | collective-permute-start | bytes 589832 | tf_op jit(solution)/shard_map/owned/ppermute | solution.py:84
  33.2 0.4 collective-permute-done.8.refs_3_
  33.6 2.3 %shares_of.1 = (f32[96,512]{1,0:T(8,128)S(1)}, f32[96,512]{1,0:T(8,128)S(1)}, f32[96,512]{1,0:T(8,128)S(1)}, f32[96,512]{1,0:T(8,128)S(1)}, bf16[384,512]{1,0:T(...) custom-call(f32[64,256]{1,0:T(8,128)S(1)} %copy-done.1, ...), custom_call_target="tpu_custom_call" | custom-call | bytes 5963776 | tf_op jit(solution)/shard_map/shares_of/pallas_call | solution.py:42
  35.9 1.1 %collective-permute-start.14 = (f32[96,512]{1,0:T(8,128)S(1)}, f32[96,512]{1,0:T(8,128)S(1)}, u32[]{:S(2)}, u32[]{:S(2)}) collective-permute-start(f32[96,512]{1,0:T(8,128)S(1)} %get-tuple-element.76), channel_id=1, source_target_pairs={{0,1},{1,0},{2,3},{3,2},{4,5},{5,4},{6,7},{7,6},{8,9},{9,8},{10,11... | collective-permute-start | bytes 589832 | tf_op jit(solution)/shard_map/sum_shares/ppermute | solution.py:84
  37.0 2.8 %collective-permute-done.5.refs_3_ = f32[384,128]{1,0:T(8,128)S(1)} collective-permute-done((f32[384,128]{1,0:T(8,128)S(1)}, f32[384,128]{1,0:T(8,128)S(1)}, u32[]{:S(2)}, u32[]{:S(2)}) %collective-permute-start.5) | collective-permute-done | bytes 196640 | tf_op jit(solution)/shard_map/owned/ppermute | solution.py:84
  39.9 1.6 %products.3 = (f32[384,256]{1,0:T(8,128)S(1)}, f32[384,256]{1,0:T(8,128)S(1)}) custom-call(bf16[384,512]{1,0:T(8,128)(2,1)S(1)} %get-tuple-element.64.gh, bf16[384,512]{1,0:T(8,128)(2,1)S(1)} %get-tuple-element.65.gl, bf16[256,256]{1,0:T(8,128)(2,1)S(1)} %get-tuple-element.66.th, bf16[256,256]{1,0:T(8,128)(2,1)S(1)} %get-tuple-element.67.tl, ...), custom_call_target="tpu_custom_call" | custom-call | bytes 3145728 | tf_op jit(solution)/shard_map/products/pallas_call | solution.py:42
  41.6 0.2 collective-permute-start.22
  41.8 1.8 %collective-permute-done.14.refs_1_ = f32[96,512]{1,0:T(8,128)S(1)} collective-permute-done((f32[96,512]{1,0:T(8,128)S(1)}, f32[96,512]{1,0:T(8,128)S(1)}, u32[]{:S(2)}, u32[]{:S(2)}) %collective-permute-start.14) | collective-permute-done | bytes 196640 | tf_op jit(solution)/shard_map/sum_shares/ppermute | solution.py:84
  43.7 3.6 %collective-permute-start.23 = (f32[96,512]{1,0:T(8,128)S(1)}, f32[96,512]{1,0:T(8,128)S(1)}, u32[]{:S(2)}, u32[]{:S(2)}) collective-permute-start(f32[96,512]{1,0:T(8,128)S(1)} %get-tuple-element.87), channel_id=1, source_target_pairs={{0,2},{1,3},{2,0},{3,1},{4,6},{5,7},{6,4},{7,5},{8,10},{9,11},{10,... | collective-permute-start | bytes 589832 | tf_op jit(solution)/shard_map/sum_shares/ppermute | solution.py:84
  47.3 1.5 %collective-permute-start.15 = (f32[96,256]{1,0:T(8,128)S(1)}, f32[96,256]{1,0:T(8,128)S(1)}, u32[]{:S(2)}, u32[]{:S(2)}) collective-permute-start(f32[96,256]{1,0:T(8,128)S(1)} %get-tuple-element.78), channel_id=1, source_target_pairs={{0,8},{4,12},{8,0},{12,4},{16,24},{20,28},{24,16},{28,20},{1,9},{5... | collective-permute-start | bytes 294920 | tf_op jit(solution)/shard_map/sum_chips/ppermute | solution.py:76
  48.8 1.5 %collective-permute-start.16 = (f32[96,256]{1,0:T(8,128)S(1)}, f32[96,256]{1,0:T(8,128)S(1)}, u32[]{:S(2)}, u32[]{:S(2)}) collective-permute-start(f32[96,256]{1,0:T(8,128)S(1)} %get-tuple-element.79), channel_id=1, source_target_pairs={{0,16},{4,20},{8,24},{12,28},{16,0},{20,4},{24,8},{28,12},{1,17},{... | collective-permute-start | bytes 294920 | tf_op jit(solution)/shard_map/sum_chips/ppermute | solution.py:76
  50.3 0.5 collective-permute-start.17
  50.8 1.2 %collective-permute-done.15.refs_1_ = f32[96,256]{1,0:T(8,128)S(1)} collective-permute-done((f32[96,256]{1,0:T(8,128)S(1)}, f32[96,256]{1,0:T(8,128)S(1)}, u32[]{:S(2)}, u32[]{:S(2)}) %collective-permute-start.15) | collective-permute-done | bytes 98336 | tf_op jit(solution)/shard_map/sum_chips/ppermute | solution.py:76
  52.0 2.4 %collective-permute-done.16.refs_2_ = f32[96,256]{1,0:T(8,128)S(1)} collective-permute-done((f32[96,256]{1,0:T(8,128)S(1)}, f32[96,256]{1,0:T(8,128)S(1)}, u32[]{:S(2)}, u32[]{:S(2)}) %collective-permute-start.16) | collective-permute-done | bytes 98336 | tf_op jit(solution)/shard_map/sum_chips/ppermute | solution.py:76
  54.5 1.4 %collective-permute-done.17.refs_3_ = f32[96,256]{1,0:T(8,128)S(1)} collective-permute-done((f32[96,256]{1,0:T(8,128)S(1)}, f32[96,256]{1,0:T(8,128)S(1)}, u32[]{:S(2)}, u32[]{:S(2)}) %collective-permute-start.17) | collective-permute-done | bytes 98336 | tf_op jit(solution)/shard_map/sum_chips/ppermute | solution.py:76
  55.8 0.3 collective-permute-start.18
  56.3 3.5 %collective-permute-start.20 = (f32[24,256]{1,0:T(8,128)S(1)}, f32[24,256]{1,0:T(8,128)S(1)}, u32[]{:S(2)}, u32[]{:S(2)}) collective-permute-start(f32[24,256]{1,0:T(8,128)S(1)} %get-tuple-element.84), channel_id=1, source_target_pairs={{0,3},{1,0},{2,1},{3,2},{4,7},{5,4},{6,5},{7,6},{8,11},{9,8},{10,9... | collective-permute-start | bytes 73736 | tf_op jit(solution)/shard_map/sum_cols/ppermute | solution.py:80
  59.7 1.8 %collective-permute-done.18.refs_1_ = f32[24,256]{1,0:T(8,128)S(1)} collective-permute-done((f32[24,256]{1,0:T(8,128)S(1)}, f32[24,256]{1,0:T(8,128)S(1)}, u32[]{:S(2)}, u32[]{:S(2)}) %collective-permute-start.18) | collective-permute-done | bytes 24608 | tf_op jit(solution)/shard_map/sum_cols/ppermute | solution.py:80
  61.5 0.6 collective-permute-done.20.refs_3_
  62.1 0.7 %collective-permute-start.25 = (f32[24,256]{1,0:T(8,128)S(1)}, f32[24,256]{1,0:T(8,128)S(1)}, u32[]{:S(2)}, u32[]{:S(2)}) collective-permute-start(f32[24,256]{1,0:T(8,128)S(1)} %spread.2.refs_0_), channel_id=1, source_target_pairs={{0,8},{4,12},{8,0},{12,4},{16,24},{20,28},{24,16},{28,20},{1,9},{5... | collective-permute-start | bytes 73736 | tf_op jit(solution)/shard_map/spread/ppermute | solution.py:76
  62.8 0.8 %collective-permute-start.27 = (f32[24,256]{1,0:T(8,128)S(1)}, f32[24,256]{1,0:T(8,128)S(1)}, u32[]{:S(2)}, u32[]{:S(2)}) collective-permute-start(f32[24,256]{1,0:T(8,128)S(1)} %spread.2.refs_0_), channel_id=1, source_target_pairs={{0,16},{4,20},{8,24},{12,28},{16,0},{20,4},{24,8},{28,12},{1,17},{... | collective-permute-start | bytes 73736 | tf_op jit(solution)/shard_map/spread/ppermute | solution.py:76
  63.6 2.0 %collective-permute-start.21 = (f32[24,256]{1,0:T(8,128)S(1)}, f32[24,256]{1,0:T(8,128)S(1)}, u32[]{:S(2)}, u32[]{:S(2)}) collective-permute-start(f32[24,256]{1,0:T(8,128)S(1)} %spread.2.refs_0_), channel_id=1, source_target_pairs={{0,24},{4,28},{8,16},{12,20},{16,8},{20,12},{24,0},{28,4},{1,25},{... | collective-permute-start | bytes 73736 | tf_op jit(solution)/shard_map/spread/ppermute | solution.py:76
  65.7 0.3 collective-permute-done.25.refs_2_
  66.0 0.2 collective-permute-start.26
  66.2 0.5 collective-permute-done.27.refs_4_
  66.7 1.5 %rows_out.1 = (f32[128,256]{1,0:T(8,128)}, f32[128,256]{1,0:T(8,128)}) custom-call(s32[3]{0:T(128)S(1)} %copy-done.5, s32[3]{0:T(128)S(1)} %copy-done.6, s32[3]{0:T(128)S(1)} %copy-done.7, bf16[256,256]{1,0:T(8,128)(2,1)S(1)} %get-tuple-element.66.th, bf16[256,256]{1,0:T(8,128)(2,1)S(1)} %get-tuple-element.67.tl, f32[96,512]{1,0:T(8,128)S(1)} %get-tuple-element.85.refs_0_, ...), custom_call_target="tpu_custom_call" | custom-call | bytes 1114148 | tf_op jit(solution)/shard_map/rows_out/pallas_call | solution.py:42
  68.4 0.3 collective-permute-start.29
  68.7 0.9 %collective-permute-done.29.refs_7_ = f32[24,256]{1,0:T(8,128)S(1)} collective-permute-done((f32[24,256]{1,0:T(8,128)S(1)}, f32[24,256]{1,0:T(8,128)S(1)}, u32[]{:S(2)}, u32[]{:S(2)}) %collective-permute-start.29) | collective-permute-done | bytes 24608 | tf_op jit(solution)/shard_map/spread/ppermute | solution.py:76
  69.6 0.7 %finish.1 = (f32[64,256]{1,0:T(8,128)}, f32[64,256]{1,0:T(8,128)}, f32[64,256]{1,0:T(8,128)}) custom-call(f32[64,256]{1,0:T(8,128)S(1)} %copy-done.1, f32[64,256]{1,0:T(8,128)S(1)} %copy-done.3, f32[64,256]{1,0:T(8,128)S(1)} %get-tuple-element.91.base, f32[24,256]{1,0:T(8,128)S(1)} %spread.2.refs_0_, f32[24,256]{1,0:T(8,128)S(1)} %collective-permute-done.24.refs_1_, ...), custom_call_target="tpu_custom_call" | custom-call | bytes 589824 | tf_op jit(solution)/shard_map/finish/pallas_call | solution.py:42
  (45 shorter events, 0.8 us)
Async XLA Ops:
  2.5 6.4 %collective-permute-start = (f32[232,128]{1,0:T(8,128)}, f32[232,128]{1,0:T(8,128)S(1)}, u32[]{:S(2)}, u32[]{:S(2)}) collective-permute-start(f32[232,128]{1,0:T(8,128)} %get-tuple-element.53), channel_id=1, source_target_pairs={{0,8},{4,12},{8,0},{12,4},{16,24},{20,28},{24,16},{28,20},{1,9},{5... | collective-permute-start | bytes 356360 | tf_op jit(solution)/shard_map/to_column/ppermute | solution.py:76
  5.5 11.7 %collective-permute-start.3 = (f32[384,128]{1,0:T(8,128)}, f32[384,128]{1,0:T(8,128)S(1)}, u32[]{:S(2)}, u32[]{:S(2)}) collective-permute-start(f32[384,128]{1,0:T(8,128)} %get-tuple-element.51.refs_0_), channel_id=1, source_target_pairs={{0,1},{1,0},{2,3},{3,2},{4,5},{5,4},{6,7},{7,6},{8,9},{9,8},{10,11... | collective-permute-start | bytes 589832 | tf_op jit(solution)/shard_map/owned/ppermute | solution.py:84
  9.0 0.9 %copy-start.2 = (f32[232,128]{1,0:T(8,128)S(1)}, f32[232,128]{1,0:T(8,128)}, u32[]{:S(2)}) copy-start(f32[232,128]{1,0:T(8,128)} %get-tuple-element.52.kept) | copy-start | bytes 356356
  9.9 11.0 %copy-start.8 = (f32[384,128]{1,0:T(8,128)S(1)}, f32[384,128]{1,0:T(8,128)}, u32[]{:S(2)}) copy-start(f32[384,128]{1,0:T(8,128)} %get-tuple-element.51.refs_0_) | copy-start | bytes 589828
  10.2 7.0 %collective-permute-start.1 = (f32[232,128]{1,0:T(8,128)S(1)}, f32[232,128]{1,0:T(8,128)S(1)}, u32[]{:S(2)}, u32[]{:S(2)}) collective-permute-start(f32[232,128]{1,0:T(8,128)S(1)} %get-tuple-element.54), channel_id=1, source_target_pairs={{0,0},{1,4},{2,2},{3,6},{4,1},{5,5},{6,3},{7,7},{8,8},{9,12},{10,1... | collective-permute-start | bytes 356360 | tf_op jit(solution)/shard_map/to_column/ppermute | solution.py:409
  10.8 6.4 %collective-permute-start.2 = (f32[232,128]{1,0:T(8,128)S(1)}, f32[232,128]{1,0:T(8,128)S(1)}, u32[]{:S(2)}, u32[]{:S(2)}) collective-permute-start(f32[232,128]{1,0:T(8,128)S(1)} %get-tuple-element.55), channel_id=1, source_target_pairs={{0,2},{1,6},{2,0},{3,4},{4,3},{5,7},{6,1},{7,5},{8,10},{9,14},{10,... | collective-permute-start | bytes 356360 | tf_op jit(solution)/shard_map/to_column/ppermute | solution.py:409
  13.7 1.6 %copy-start = (f32[4,1,128,8,1,128]{5,4,3,2,1,0:T(1,128)S(1)}, f32[4,1,128,8,1,128]{5,4,3,2,1,0:T(1,128)}, u32[]{:S(2)}) copy-start(f32[4,1,128,8,1,128]{5,4,3,2,1,0:T(1,128)} %param.10) | copy-start | bytes 6291460
  15.3 0.7 copy-start.4
  17.3 16.3 %copy-start.1 = (f32[64,256]{1,0:T(8,128)S(1)}, f32[64,256]{1,0:T(8,128)}, u32[]{:S(2)}) copy-start(f32[64,256]{1,0:T(8,128)} %pd.3) | copy-start | bytes 196612
  17.3 11.1 %collective-permute-start.9 = (f32[464,128]{1,0:T(8,128)S(1)}, f32[464,128]{1,0:T(8,128)S(1)}, u32[]{:S(2)}, u32[]{:S(2)}) collective-permute-start(f32[464,128]{1,0:T(8,128)S(1)} %get-tuple-element.61.refs_0_), channel_id=1, source_target_pairs={{0,16},{4,20},{8,24},{12,28},{16,0},{20,4},{24,8},{28,12},{1,17},{... | collective-permute-start | bytes 712712 | tf_op jit(solution)/shard_map/panels/ppermute | solution.py:76
  18.9 12.3 %collective-permute-start.11 = (f32[464,128]{1,0:T(8,128)S(1)}, f32[464,128]{1,0:T(8,128)S(1)}, u32[]{:S(2)}, u32[]{:S(2)}) collective-permute-start(f32[464,128]{1,0:T(8,128)S(1)} %get-tuple-element.61.refs_0_), channel_id=1, source_target_pairs={{0,24},{4,28},{8,16},{12,20},{16,8},{20,12},{24,0},{28,4},{1,25},{... | collective-permute-start | bytes 712712 | tf_op jit(solution)/shard_map/panels/ppermute | solution.py:76
  20.3 10.9 %collective-permute-start.7 = (f32[464,128]{1,0:T(8,128)S(1)}, f32[464,128]{1,0:T(8,128)S(1)}, u32[]{:S(2)}, u32[]{:S(2)}) collective-permute-start(f32[464,128]{1,0:T(8,128)S(1)} %get-tuple-element.61.refs_0_), channel_id=1, source_target_pairs={{0,8},{4,12},{8,0},{12,4},{16,24},{20,28},{24,16},{28,20},{1,9},{5... | collective-permute-start | bytes 712712 | tf_op jit(solution)/shard_map/panels/ppermute | solution.py:76
  20.9 11.6 %collective-permute-start.4 = (f32[384,128]{1,0:T(8,128)S(1)}, f32[384,128]{1,0:T(8,128)S(1)}, u32[]{:S(2)}, u32[]{:S(2)}) collective-permute-start(f32[384,128]{1,0:T(8,128)S(1)} %copy-done.8), channel_id=1, source_target_pairs={{0,2},{1,3},{2,0},{3,1},{4,6},{5,7},{6,4},{7,5},{8,10},{9,11},{10,... | collective-permute-start | bytes 589832 | tf_op jit(solution)/shard_map/owned/ppermute | solution.py:84
  24.4 8.9 %collective-permute-start.6 = (f32[464,128]{1,0:T(8,128)S(1)}, f32[464,128]{1,0:T(8,128)S(1)}, u32[]{:S(2)}, u32[]{:S(2)}) collective-permute-start(f32[464,128]{1,0:T(8,128)S(1)} %get-tuple-element.61.refs_0_), channel_id=1, source_target_pairs={{0,4},{4,0},{8,12},{12,8},{16,20},{20,16},{24,28},{28,24},{1,5},{5... | collective-permute-start | bytes 712712 | tf_op jit(solution)/shard_map/panels/ppermute | solution.py:76
  28.5 4.8 %collective-permute-start.10 = (f32[464,128]{1,0:T(8,128)S(1)}, f32[464,128]{1,0:T(8,128)S(1)}, u32[]{:S(2)}, u32[]{:S(2)}) collective-permute-start(f32[464,128]{1,0:T(8,128)S(1)} %collective-permute-done.9.refs_4_), channel_id=1, source_target_pairs={{0,4},{4,0},{8,12},{12,8},{16,20},{20,16},{24,28},{28,24},{1,5},{5... | collective-permute-start | bytes 712712 | tf_op jit(solution)/shard_map/panels/ppermute | solution.py:76
  31.3 2.0 %collective-permute-start.12 = (f32[464,128]{1,0:T(8,128)S(1)}, f32[464,128]{1,0:T(8,128)S(1)}, u32[]{:S(2)}, u32[]{:S(2)}) collective-permute-start(f32[464,128]{1,0:T(8,128)S(1)} %collective-permute-done.11.refs_6_), channel_id=1, source_target_pairs={{0,4},{4,0},{8,12},{12,8},{16,20},{20,16},{24,28},{28,24},{1,5},{5... | collective-permute-start | bytes 712712 | tf_op jit(solution)/shard_map/panels/ppermute | solution.py:76
  31.3 2.3 %collective-permute-start.8 = (f32[464,128]{1,0:T(8,128)S(1)}, f32[464,128]{1,0:T(8,128)S(1)}, u32[]{:S(2)}, u32[]{:S(2)}) collective-permute-start(f32[464,128]{1,0:T(8,128)S(1)} %collective-permute-done.7.refs_2_), channel_id=1, source_target_pairs={{0,4},{4,0},{8,12},{12,8},{16,20},{20,16},{24,28},{28,24},{1,5},{5... | collective-permute-start | bytes 712712 | tf_op jit(solution)/shard_map/panels/ppermute | solution.py:76
  32.5 7.3 %collective-permute-start.5 = (f32[384,128]{1,0:T(8,128)S(1)}, f32[384,128]{1,0:T(8,128)S(1)}, u32[]{:S(2)}, u32[]{:S(2)}) collective-permute-start(f32[384,128]{1,0:T(8,128)S(1)} %owned.1.refs_2_), channel_id=1, source_target_pairs={{0,1},{1,0},{2,3},{3,2},{4,5},{5,4},{6,7},{7,6},{8,9},{9,8},{10,11... | collective-permute-start | bytes 589832 | tf_op jit(solution)/shard_map/owned/ppermute | solution.py:84
  35.9 7.7 %collective-permute-start.14 = (f32[96,512]{1,0:T(8,128)S(1)}, f32[96,512]{1,0:T(8,128)S(1)}, u32[]{:S(2)}, u32[]{:S(2)}) collective-permute-start(f32[96,512]{1,0:T(8,128)S(1)} %get-tuple-element.76), channel_id=1, source_target_pairs={{0,1},{1,0},{2,3},{3,2},{4,5},{5,4},{6,7},{7,6},{8,9},{9,8},{10,11... | collective-permute-start | bytes 589832 | tf_op jit(solution)/shard_map/sum_shares/ppermute | solution.py:84
  41.5 2.1 %collective-permute-start.13 = (f32[384,256]{1,0:T(8,128)S(1)}, f32[384,256]{1,0:T(8,128)S(1)}, u32[]{:S(2)}, u32[]{:S(2)}) collective-permute-start(f32[384,256]{1,0:T(8,128)S(1)} %get-tuple-element.74), channel_id=1, source_target_pairs={{0,4},{4,0},{8,12},{12,8},{16,20},{20,16},{24,28},{28,24},{1,5},{5... | collective-permute-start | bytes 1179656 | tf_op jit(solution)/shard_map/sum_core/ppermute | solution.py:76
  41.6 24.1 %collective-permute-start.22 = (f32[96,512]{1,0:T(8,128)S(1)}, f32[96,512]{1,0:T(8,128)S(1)}, u32[]{:S(2)}, u32[]{:S(2)}) collective-permute-start(f32[96,512]{1,0:T(8,128)S(1)} %get-tuple-element.86), channel_id=1, source_target_pairs={{0,1},{1,0},{2,3},{3,2},{4,5},{5,4},{6,7},{7,6},{8,9},{9,8},{10,11... | collective-permute-start | bytes 589832 | tf_op jit(solution)/shard_map/sum_shares/ppermute | solution.py:84
  43.6 23.1 %copy-start.5 = (s32[3]{0:T(128)S(1)}, s32[3]{0:T(128)}, u32[]{:S(2)}) copy-start(s32[3]{0:T(128)} %blocks.3) | copy-start | bytes 40
  43.6 23.1 %copy-start.6 = (s32[3]{0:T(128)S(1)}, s32[3]{0:T(128)}, u32[]{:S(2)}) copy-start(s32[3]{0:T(128)} %psize.1) | copy-start | bytes 40
  43.6 23.1 %copy-start.7 = (s32[3]{0:T(128)S(1)}, s32[3]{0:T(128)}, u32[]{:S(2)}) copy-start(s32[3]{0:T(128)} %csize.1) | copy-start | bytes 40
  43.6 26.0 %copy-start.3 = (f32[64,256]{1,0:T(8,128)S(1)}, f32[64,256]{1,0:T(8,128)}, u32[]{:S(2)}) copy-start(f32[64,256]{1,0:T(8,128)} %cd.1) | copy-start | bytes 196612
  43.7 23.0 %collective-permute-start.23 = (f32[96,512]{1,0:T(8,128)S(1)}, f32[96,512]{1,0:T(8,128)S(1)}, u32[]{:S(2)}, u32[]{:S(2)}) collective-permute-start(f32[96,512]{1,0:T(8,128)S(1)} %get-tuple-element.87), channel_id=1, source_target_pairs={{0,2},{1,3},{2,0},{3,1},{4,6},{5,7},{6,4},{7,5},{8,10},{9,11},{10,... | collective-permute-start | bytes 589832 | tf_op jit(solution)/shard_map/sum_shares/ppermute | solution.py:84
  47.3 4.7 %collective-permute-start.15 = (f32[96,256]{1,0:T(8,128)S(1)}, f32[96,256]{1,0:T(8,128)S(1)}, u32[]{:S(2)}, u32[]{:S(2)}) collective-permute-start(f32[96,256]{1,0:T(8,128)S(1)} %get-tuple-element.78), channel_id=1, source_target_pairs={{0,8},{4,12},{8,0},{12,4},{16,24},{20,28},{24,16},{28,20},{1,9},{5... | collective-permute-start | bytes 294920 | tf_op jit(solution)/shard_map/sum_chips/ppermute | solution.py:76
  48.8 5.7 %collective-permute-start.16 = (f32[96,256]{1,0:T(8,128)S(1)}, f32[96,256]{1,0:T(8,128)S(1)}, u32[]{:S(2)}, u32[]{:S(2)}) collective-permute-start(f32[96,256]{1,0:T(8,128)S(1)} %get-tuple-element.79), channel_id=1, source_target_pairs={{0,16},{4,20},{8,24},{12,28},{16,0},{20,4},{24,8},{28,12},{1,17},{... | collective-permute-start | bytes 294920 | tf_op jit(solution)/shard_map/sum_chips/ppermute | solution.py:76
  50.3 5.5 %collective-permute-start.17 = (f32[96,256]{1,0:T(8,128)S(1)}, f32[96,256]{1,0:T(8,128)S(1)}, u32[]{:S(2)}, u32[]{:S(2)}) collective-permute-start(f32[96,256]{1,0:T(8,128)S(1)} %get-tuple-element.80), channel_id=1, source_target_pairs={{0,24},{4,28},{8,16},{12,20},{16,8},{20,12},{24,0},{28,4},{1,25},{... | collective-permute-start | bytes 294920 | tf_op jit(solution)/shard_map/sum_chips/ppermute | solution.py:76
  55.8 5.7 %collective-permute-start.18 = (f32[24,256]{1,0:T(8,128)S(1)}, f32[24,256]{1,0:T(8,128)S(1)}, u32[]{:S(2)}, u32[]{:S(2)}) collective-permute-start(f32[24,256]{1,0:T(8,128)S(1)} %get-tuple-element.82), channel_id=1, source_target_pairs={{0,1},{1,2},{2,3},{3,0},{4,5},{5,6},{6,7},{7,4},{8,9},{9,10},{10,1... | collective-permute-start | bytes 73736 | tf_op jit(solution)/shard_map/sum_cols/ppermute | solution.py:80
  56.2 5.3 %collective-permute-start.19 = (f32[24,256]{1,0:T(8,128)S(1)}, f32[24,256]{1,0:T(8,128)S(1)}, u32[]{:S(2)}, u32[]{:S(2)}) collective-permute-start(f32[24,256]{1,0:T(8,128)S(1)} %get-tuple-element.83), channel_id=1, source_target_pairs={{0,2},{1,3},{2,0},{3,1},{4,6},{5,7},{6,4},{7,5},{8,10},{9,11},{10,... | collective-permute-start | bytes 73736 | tf_op jit(solution)/shard_map/sum_cols/ppermute | solution.py:80
  56.3 5.8 %collective-permute-start.20 = (f32[24,256]{1,0:T(8,128)S(1)}, f32[24,256]{1,0:T(8,128)S(1)}, u32[]{:S(2)}, u32[]{:S(2)}) collective-permute-start(f32[24,256]{1,0:T(8,128)S(1)} %get-tuple-element.84), channel_id=1, source_target_pairs={{0,3},{1,0},{2,1},{3,2},{4,7},{5,4},{6,5},{7,6},{8,11},{9,8},{10,9... | collective-permute-start | bytes 73736 | tf_op jit(solution)/shard_map/sum_cols/ppermute | solution.py:80
  62.1 3.9 %collective-permute-start.25 = (f32[24,256]{1,0:T(8,128)S(1)}, f32[24,256]{1,0:T(8,128)S(1)}, u32[]{:S(2)}, u32[]{:S(2)}) collective-permute-start(f32[24,256]{1,0:T(8,128)S(1)} %spread.2.refs_0_), channel_id=1, source_target_pairs={{0,8},{4,12},{8,0},{12,4},{16,24},{20,28},{24,16},{28,20},{1,9},{5... | collective-permute-start | bytes 73736 | tf_op jit(solution)/shard_map/spread/ppermute | solution.py:76
  62.8 3.8 %collective-permute-start.27 = (f32[24,256]{1,0:T(8,128)S(1)}, f32[24,256]{1,0:T(8,128)S(1)}, u32[]{:S(2)}, u32[]{:S(2)}) collective-permute-start(f32[24,256]{1,0:T(8,128)S(1)} %spread.2.refs_0_), channel_id=1, source_target_pairs={{0,16},{4,20},{8,24},{12,28},{16,0},{20,4},{24,8},{28,12},{1,17},{... | collective-permute-start | bytes 73736 | tf_op jit(solution)/shard_map/spread/ppermute | solution.py:76
  63.6 4.7 %collective-permute-start.21 = (f32[24,256]{1,0:T(8,128)S(1)}, f32[24,256]{1,0:T(8,128)S(1)}, u32[]{:S(2)}, u32[]{:S(2)}) collective-permute-start(f32[24,256]{1,0:T(8,128)S(1)} %spread.2.refs_0_), channel_id=1, source_target_pairs={{0,24},{4,28},{8,16},{12,20},{16,8},{20,12},{24,0},{28,4},{1,25},{... | collective-permute-start | bytes 73736 | tf_op jit(solution)/shard_map/spread/ppermute | solution.py:76
  65.7 3.0 %collective-permute-start.24 = (f32[24,256]{1,0:T(8,128)S(1)}, f32[24,256]{1,0:T(8,128)S(1)}, u32[]{:S(2)}, u32[]{:S(2)}) collective-permute-start(f32[24,256]{1,0:T(8,128)S(1)} %spread.2.refs_0_), channel_id=1, source_target_pairs={{0,4},{4,0},{8,12},{12,8},{16,20},{20,16},{24,28},{28,24},{1,5},{5... | collective-permute-start | bytes 73736 | tf_op jit(solution)/shard_map/spread/ppermute | solution.py:76
  66.0 2.7 %collective-permute-start.26 = (f32[24,256]{1,0:T(8,128)S(1)}, f32[24,256]{1,0:T(8,128)S(1)}, u32[]{:S(2)}, u32[]{:S(2)}) collective-permute-start(f32[24,256]{1,0:T(8,128)S(1)} %collective-permute-done.25.refs_2_), channel_id=1, source_target_pairs={{0,4},{4,0},{8,12},{12,8},{16,20},{20,16},{24,28},{28,24},{1,5},{5... | collective-permute-start | bytes 73736 | tf_op jit(solution)/shard_map/spread/ppermute | solution.py:76
  66.6 2.0 %collective-permute-start.28 = (f32[24,256]{1,0:T(8,128)S(1)}, f32[24,256]{1,0:T(8,128)S(1)}, u32[]{:S(2)}, u32[]{:S(2)}) collective-permute-start(f32[24,256]{1,0:T(8,128)S(1)} %collective-permute-done.27.refs_4_), channel_id=1, source_target_pairs={{0,4},{4,0},{8,12},{12,8},{16,20},{20,16},{24,28},{28,24},{1,5},{5... | collective-permute-start | bytes 73736 | tf_op jit(solution)/shard_map/spread/ppermute | solution.py:76
  68.4 1.2 %collective-permute-start.29 = (f32[24,256]{1,0:T(8,128)S(1)}, f32[24,256]{1,0:T(8,128)S(1)}, u32[]{:S(2)}, u32[]{:S(2)}) collective-permute-start(f32[24,256]{1,0:T(8,128)S(1)} %get-tuple-element.92.refs_6_), channel_id=1, source_target_pairs={{0,4},{4,0},{8,12},{12,8},{16,20},{20,16},{24,28},{28,24},{1,5},{5... | collective-permute-start | bytes 73736 | tf_op jit(solution)/shard_map/spread/ppermute | solution.py:76

commit v6 on v5

--- a/solution.py
+++ b/solution.py
@@ -135,6 +135,11 @@
         rows = pl.ds(pl.multiple_of(at * quarter, quarter), quarter)
         out[s.part : s.part + quarter, :] = top[rows, columns]
         out[s.part + quarter :, :] = ids
+
+
+def keep(s, source, target, sems):
+    for copy in fetch((source,), (target,), sems):
+        copy.wait()
 
 
 def route(s, kept, got, first, second, sems):
@@ -399,6 +404,9 @@
         )
     with jax.named_scope("to_column"):
         got = exchange(sent, C // 2, R)
+        (kept,) = call(
+            bind(keep), anywhere(kept), [(s.block, B)], [pltpu.SemaphoreType.DMA((1,))]
+        )
         pieces = call(
             bind(route),
             anywhere(kept, got),
@@ -457,7 +465,7 @@
             ahead=3e9,
             passed=(gh, gl),
         )
-        keep, send = call(
+        stays, send = call(
             bind(products),
             vmem(gh, gl, th, tl, ih, il, extra, lh, ll),
             [(3 * W // 2, W)] * 2,
@@ -484,7 +492,7 @@
     with jax.named_scope("sum_chips"):
         *mine, shares[2] = call(
             bind(add_chips),
-            vmem(keep, got),
+            vmem(stays, got),
             [(C * 3 * s.eight, W)] * s.chips,
             passed=(shares[2],),
         )

time: 70.5 us -> 69.5 us (0.986)
  starting transfers between devices: 37.1 us -> 35 us
  waiting for transfers between devices: 19.5 us -> 20.5 us
    ppermute x6, starting transfers between devices: 10.7 us -> 9.64 us  [flip(): return lax.ppermute(value, 'col', [(i, i ^ mask) for i in range(col_total)])]
    ppermute x19, starting transfers between devices: 18.9 us -> 17.9 us  [exchange(): return lax.ppermute(value, 'row', [(i, i ^ mask) for i in range(row_total)])]
    pallas_call x15 -> x16, Pallas kernels: 9.68 us -> 9.84 us  [call(): pl.pallas_call(kernel, out_shape=shapes, in_specs=[pl.BlockSpec(memory_sp...]
  transfers between devices with their start and end apart: 30 -> 30, of which waited for: 15 -> 16; matrix products, arithmetic and copies ran while one was open for 0% -> 0% of each run, Pallas kernels for 10% -> 10%
where the time goes in v6:
time: 69.5 us; the launch traced here: 69.3 us
  starting transfers between devices  35 us (50%)
  waiting for transfers between devices  20.5 us (29%)
  Pallas kernels  9.84 us (14%)
  local copies, waits for them, and re-layouts  3.17 us (5%)
  between operations  0.82 us (1%)
    ppermute x19, starting transfers between devices, exchange(): return lax.ppermute(value, 'row', [(i, i ^ mask) for i in range(row_total)])  17.9 us
    ppermute x19, waiting for transfers between devices, exchange(): return lax.ppermute(value, 'row', [(i, i ^ mask) for i in range(row_total)])  13.1 us
    pallas_call x16, Pallas kernels, call(): pl.pallas_call(kernel, out_shape=shapes, in_specs=[pl.BlockSpec(memory_sp...  9.84 us
    ppermute x6, starting transfers between devices, flip(): return lax.ppermute(value, 'col', [(i, i ^ mask) for i in range(col_total)])  9.64 us
    ppermute x6, waiting for transfers between devices, flip(): return lax.ppermute(value, 'col', [(i, i ^ mask) for i in range(col_total)])  4.56 us
    ppermute x3, starting transfers between devices, shift(): lax.ppermute(value, 'col', [(i, (i + step) % col_total) for i in range(co...  3.88 us
    ppermute x2, starting transfers between devices, fast_body(): lax.ppermute(pieces[turn], ('row', 'col'), column_perm(s, turn))  3.57 us
    unnamed x18, local copies, waits for them, and re-layouts  3.17 us
  transfers between devices with their start and end apart: 30, of which 16 were waited for; matrix products, arithmetic and copies ran while one was open for 0% of the time, Pallas kernels for 10%

profile of v6, /device:TPU:0, one launch (start us, length us, event | category | flops | bytes accessed | tf_op | source)
XLA Modules:
  0.0 69.3 jit_solution(6019417008445486572)
XLA Ops:
  0.6 1.9 %pack.1 = (f32[232,128]{1,0:T(8,128)}, f32[232,128]{1,0:T(8,128)}, f32[384,128]{1,0:T(8,128)}, f32[192,128]{1,0:T(8,128)}, f32[192,128]{1,0:T(8,128)}) custom-call(s32[3]{0:T(128)} %blocks.3, s32[3]{0:T(128)} %psize.1, s32[3]{0:T(128)} %csize.1, f32[3,64,128]{2,1,0:T(8,128)} %bitcast.12, f32[3,64,128]{2,1,0:T(8,128)} %bitcast.13, f32[64,256]{1,0:T(8,128)} %refs_5_.1), custom_call_target="tpu_custom_call" | custom-call | bytes 892964 | tf_op jit(solution)/shard_map/pack/pallas_call | solution.py:42
  2.5 3.0 %collective-permute-start = (f32[232,128]{1,0:T(8,128)}, f32[232,128]{1,0:T(8,128)S(1)}, u32[]{:S(2)}, u32[]{:S(2)}) collective-permute-start(f32[232,128]{1,0:T(8,128)} %get-tuple-element.53), channel_id=1, source_target_pairs={{0,8},{4,12},{8,0},{12,4},{16,24},{20,28},{24,16},{28,20},{1,9},{5... | collective-permute-start | bytes 356360 | tf_op jit(solution)/shard_map/to_column/ppermute | solution.py:76
  5.5 1.6 %collective-permute-start.3 = (f32[384,128]{1,0:T(8,128)}, f32[384,128]{1,0:T(8,128)S(1)}, u32[]{:S(2)}, u32[]{:S(2)}) collective-permute-start(f32[384,128]{1,0:T(8,128)} %get-tuple-element.51.refs_0_), channel_id=1, source_target_pairs={{0,1},{1,0},{2,3},{3,2},{4,5},{5,4},{6,7},{7,6},{8,9},{9,8},{10,11... | collective-permute-start | bytes 589832 | tf_op jit(solution)/shard_map/owned/ppermute | solution.py:84
  7.1 0.9 %copy-done.2 = f32[232,128]{1,0:T(8,128)S(1)} copy-done((f32[232,128]{1,0:T(8,128)S(1)}, f32[232,128]{1,0:T(8,128)}, u32[]{:S(2)}) %copy-start.2) | copy-done | bytes 118808
  8.1 0.8 %collective-permute-done.got = f32[232,128]{1,0:T(8,128)S(1)} collective-permute-done((f32[232,128]{1,0:T(8,128)}, f32[232,128]{1,0:T(8,128)S(1)}, u32[]{:S(2)}, u32[]{:S(2)}) %collective-permute-start) | collective-permute-done | bytes 118816 | tf_op jit(solution)/shard_map/to_column/ppermute | solution.py:76
  9.0 0.3 to_column.3
  9.3 0.7 collective-permute-start.1
  9.9 2.9 %collective-permute-start.2 = (f32[232,128]{1,0:T(8,128)S(1)}, f32[232,128]{1,0:T(8,128)S(1)}, u32[]{:S(2)}, u32[]{:S(2)}) collective-permute-start(f32[232,128]{1,0:T(8,128)S(1)} %get-tuple-element.55), channel_id=1, source_target_pairs={{0,2},{1,6},{2,0},{3,4},{4,3},{5,7},{6,1},{7,5},{8,10},{9,14},{10,... | collective-permute-start | bytes 356360 | tf_op jit(solution)/shard_map/to_column/ppermute | solution.py:417
  12.9 1.6 %copy-done = f32[4,1,128,8,1,128]{5,4,3,2,1,0:T(1,128)S(1)} copy-done((f32[4,1,128,8,1,128]{5,4,3,2,1,0:T(1,128)S(1)}, f32[4,1,128,8,1,128]{5,4,3,2,1,0:T(1,128)}, u32[]{:S(2)}) %copy-start) | copy-done | bytes 2097176
  14.4 0.7 copy-done.4
  15.1 1.2 %split_live.1 = (bf16[384,1024]{1,0:T(8,128)(2,1)S(1)}, bf16[384,1024]{1,0:T(8,128)(2,1)S(1)}) custom-call(f32[4096,128]{1,0:T(8,128)S(1)} %bitcast.9, s32[3]{0:T(128)S(1)} %copy-done.4), custom_call_target="tpu_custom_call" | custom-call | bytes 3670028 | tf_op jit(solution)/shard_map/split_live/pallas_call | solution.py:42
  16.3 0.5 collective-permute-done.2.second
  16.8 1.6 %collective-permute-start.9 = (f32[464,128]{1,0:T(8,128)S(1)}, f32[464,128]{1,0:T(8,128)S(1)}, u32[]{:S(2)}, u32[]{:S(2)}) collective-permute-start(f32[464,128]{1,0:T(8,128)S(1)} %get-tuple-element.61.refs_0_), channel_id=1, source_target_pairs={{0,16},{4,20},{8,24},{12,28},{16,0},{20,4},{24,8},{28,12},{1,17},{... | collective-permute-start | bytes 712712 | tf_op jit(solution)/shard_map/panels/ppermute | solution.py:76
  18.4 1.1 %collective-permute-start.11 = (f32[464,128]{1,0:T(8,128)S(1)}, f32[464,128]{1,0:T(8,128)S(1)}, u32[]{:S(2)}, u32[]{:S(2)}) collective-permute-start(f32[464,128]{1,0:T(8,128)S(1)} %get-tuple-element.61.refs_0_), channel_id=1, source_target_pairs={{0,24},{4,28},{8,16},{12,20},{16,8},{20,12},{24,0},{28,4},{1,25},{... | collective-permute-start | bytes 712712 | tf_op jit(solution)/shard_map/panels/ppermute | solution.py:76
  19.4 0.9 %collective-permute-start.7 = (f32[464,128]{1,0:T(8,128)S(1)}, f32[464,128]{1,0:T(8,128)S(1)}, u32[]{:S(2)}, u32[]{:S(2)}) collective-permute-start(f32[464,128]{1,0:T(8,128)S(1)} %get-tuple-element.61.refs_0_), channel_id=1, source_target_pairs={{0,8},{4,12},{8,0},{12,4},{16,24},{20,28},{24,16},{28,20},{1,9},{5... | collective-permute-start | bytes 712712 | tf_op jit(solution)/shard_map/panels/ppermute | solution.py:76
  20.3 3.1 %collective-permute-start.4 = (f32[384,128]{1,0:T(8,128)S(1)}, f32[384,128]{1,0:T(8,128)S(1)}, u32[]{:S(2)}, u32[]{:S(2)}) collective-permute-start(f32[384,128]{1,0:T(8,128)S(1)} %copy-done.8), channel_id=1, source_target_pairs={{0,2},{1,3},{2,0},{3,1},{4,6},{5,7},{6,4},{7,5},{8,10},{9,11},{10,... | collective-permute-start | bytes 589832 | tf_op jit(solution)/shard_map/owned/ppermute | solution.py:84
  23.5 0.7 %collective-permute-start.6 = (f32[464,128]{1,0:T(8,128)S(1)}, f32[464,128]{1,0:T(8,128)S(1)}, u32[]{:S(2)}, u32[]{:S(2)}) collective-permute-start(f32[464,128]{1,0:T(8,128)S(1)} %get-tuple-element.61.refs_0_), channel_id=1, source_target_pairs={{0,4},{4,0},{8,12},{12,8},{16,20},{20,16},{24,28},{28,24},{1,5},{5... | collective-permute-start | bytes 712712 | tf_op jit(solution)/shard_map/panels/ppermute | solution.py:76
  24.2 4.6 %collective-permute-done.9.refs_4_ = f32[464,128]{1,0:T(8,128)S(1)} collective-permute-done((f32[464,128]{1,0:T(8,128)S(1)}, f32[464,128]{1,0:T(8,128)S(1)}, u32[]{:S(2)}, u32[]{:S(2)}) %collective-permute-start.9) | collective-permute-done | bytes 237600 | tf_op jit(solution)/shard_map/panels/ppermute | solution.py:76
  28.8 1.9 %collective-permute-start.10 = (f32[464,128]{1,0:T(8,128)S(1)}, f32[464,128]{1,0:T(8,128)S(1)}, u32[]{:S(2)}, u32[]{:S(2)}) collective-permute-start(f32[464,128]{1,0:T(8,128)S(1)} %collective-permute-done.9.refs_4_), channel_id=1, source_target_pairs={{0,4},{4,0},{8,12},{12,8},{16,20},{20,16},{24,28},{28,24},{1,5},{5... | collective-permute-start | bytes 712712 | tf_op jit(solution)/shard_map/panels/ppermute | solution.py:76
  30.9 1.1 %collective-permute-start.8 = (f32[464,128]{1,0:T(8,128)S(1)}, f32[464,128]{1,0:T(8,128)S(1)}, u32[]{:S(2)}, u32[]{:S(2)}) collective-permute-start(f32[464,128]{1,0:T(8,128)S(1)} %collective-permute-done.7.refs_2_), channel_id=1, source_target_pairs={{0,4},{4,0},{8,12},{12,8},{16,20},{20,16},{24,28},{28,24},{1,5},{5... | collective-permute-start | bytes 712712 | tf_op jit(solution)/shard_map/panels/ppermute | solution.py:76
  31.9 0.4 collective-permute-start.5
  32.3 0.7 %collective-permute-done.8.refs_3_ = f32[464,128]{1,0:T(8,128)S(1)} collective-permute-done((f32[464,128]{1,0:T(8,128)S(1)}, f32[464,128]{1,0:T(8,128)S(1)}, u32[]{:S(2)}, u32[]{:S(2)}) %collective-permute-start.8) | collective-permute-done | bytes 237600 | tf_op jit(solution)/shard_map/panels/ppermute | solution.py:76
  33.1 2.3 %shares_of.1 = (f32[96,512]{1,0:T(8,128)S(1)}, f32[96,512]{1,0:T(8,128)S(1)}, f32[96,512]{1,0:T(8,128)S(1)}, f32[96,512]{1,0:T(8,128)S(1)}, bf16[384,512]{1,0:T(...) custom-call(f32[64,256]{1,0:T(8,128)S(1)} %copy-done.1, ...), custom_call_target="tpu_custom_call" | custom-call | bytes 5963776 | tf_op jit(solution)/shard_map/shares_of/pallas_call | solution.py:42
  35.3 1.1 %collective-permute-start.14 = (f32[96,512]{1,0:T(8,128)S(1)}, f32[96,512]{1,0:T(8,128)S(1)}, u32[]{:S(2)}, u32[]{:S(2)}) collective-permute-start(f32[96,512]{1,0:T(8,128)S(1)} %get-tuple-element.76), channel_id=1, source_target_pairs={{0,1},{1,0},{2,3},{3,2},{4,5},{5,4},{6,7},{7,6},{8,9},{9,8},{10,11... | collective-permute-start | bytes 589832 | tf_op jit(solution)/shard_map/sum_shares/ppermute | solution.py:84
  36.4 2.7 %collective-permute-done.5.refs_3_ = f32[384,128]{1,0:T(8,128)S(1)} collective-permute-done((f32[384,128]{1,0:T(8,128)S(1)}, f32[384,128]{1,0:T(8,128)S(1)}, u32[]{:S(2)}, u32[]{:S(2)}) %collective-permute-start.5) | collective-permute-done | bytes 196640 | tf_op jit(solution)/shard_map/owned/ppermute | solution.py:84
  39.3 1.6 %products.3 = (f32[384,256]{1,0:T(8,128)S(1)}, f32[384,256]{1,0:T(8,128)S(1)}) custom-call(bf16[384,512]{1,0:T(8,128)(2,1)S(1)} %get-tuple-element.64.gh, bf16[384,512]{1,0:T(8,128)(2,1)S(1)} %get-tuple-element.65.gl, bf16[256,256]{1,0:T(8,128)(2,1)S(1)} %get-tuple-element.66.th, bf16[256,256]{1,0:T(8,128)(2,1)S(1)} %get-tuple-element.67.tl, ...), custom_call_target="tpu_custom_call" | custom-call | bytes 3145728 | tf_op jit(solution)/shard_map/products/pallas_call | solution.py:42
  41.0 0.2 collective-permute-start.22
  41.2 1.8 %collective-permute-done.14.refs_1_ = f32[96,512]{1,0:T(8,128)S(1)} collective-permute-done((f32[96,512]{1,0:T(8,128)S(1)}, f32[96,512]{1,0:T(8,128)S(1)}, u32[]{:S(2)}, u32[]{:S(2)}) %collective-permute-start.14) | collective-permute-done | bytes 196640 | tf_op jit(solution)/shard_map/sum_shares/ppermute | solution.py:84
  43.1 3.3 %collective-permute-start.23 = (f32[96,512]{1,0:T(8,128)S(1)}, f32[96,512]{1,0:T(8,128)S(1)}, u32[]{:S(2)}, u32[]{:S(2)}) collective-permute-start(f32[96,512]{1,0:T(8,128)S(1)} %get-tuple-element.87), channel_id=1, source_target_pairs={{0,2},{1,3},{2,0},{3,1},{4,6},{5,7},{6,4},{7,5},{8,10},{9,11},{10,... | collective-permute-start | bytes 589832 | tf_op jit(solution)/shard_map/sum_shares/ppermute | solution.py:84
  46.4 1.5 %collective-permute-start.15 = (f32[96,256]{1,0:T(8,128)S(1)}, f32[96,256]{1,0:T(8,128)S(1)}, u32[]{:S(2)}, u32[]{:S(2)}) collective-permute-start(f32[96,256]{1,0:T(8,128)S(1)} %get-tuple-element.78), channel_id=1, source_target_pairs={{0,8},{4,12},{8,0},{12,4},{16,24},{20,28},{24,16},{28,20},{1,9},{5... | collective-permute-start | bytes 294920 | tf_op jit(solution)/shard_map/sum_chips/ppermute | solution.py:76
  47.9 1.5 %collective-permute-start.16 = (f32[96,256]{1,0:T(8,128)S(1)}, f32[96,256]{1,0:T(8,128)S(1)}, u32[]{:S(2)}, u32[]{:S(2)}) collective-permute-start(f32[96,256]{1,0:T(8,128)S(1)} %get-tuple-element.79), channel_id=1, source_target_pairs={{0,16},{4,20},{8,24},{12,28},{16,0},{20,4},{24,8},{28,12},{1,17},{... | collective-permute-start | bytes 294920 | tf_op jit(solution)/shard_map/sum_chips/ppermute | solution.py:76
  49.4 0.5 collective-permute-start.17
  49.9 1.3 %collective-permute-done.15.refs_1_ = f32[96,256]{1,0:T(8,128)S(1)} collective-permute-done((f32[96,256]{1,0:T(8,128)S(1)}, f32[96,256]{1,0:T(8,128)S(1)}, u32[]{:S(2)}, u32[]{:S(2)}) %collective-permute-start.15) | collective-permute-done | bytes 98336 | tf_op jit(solution)/shard_map/sum_chips/ppermute | solution.py:76
  51.2 2.4 %collective-permute-done.16.refs_2_ = f32[96,256]{1,0:T(8,128)S(1)} collective-permute-done((f32[96,256]{1,0:T(8,128)S(1)}, f32[96,256]{1,0:T(8,128)S(1)}, u32[]{:S(2)}, u32[]{:S(2)}) %collective-permute-start.16) | collective-permute-done | bytes 98336 | tf_op jit(solution)/shard_map/sum_chips/ppermute | solution.py:76
  53.6 1.4 %collective-permute-done.17.refs_3_ = f32[96,256]{1,0:T(8,128)S(1)} collective-permute-done((f32[96,256]{1,0:T(8,128)S(1)}, f32[96,256]{1,0:T(8,128)S(1)}, u32[]{:S(2)}, u32[]{:S(2)}) %collective-permute-start.17) | collective-permute-done | bytes 98336 | tf_op jit(solution)/shard_map/sum_chips/ppermute | solution.py:76
  55.0 0.3 collective-permute-start.18
  55.4 3.5 %collective-permute-start.20 = (f32[24,256]{1,0:T(8,128)S(1)}, f32[24,256]{1,0:T(8,128)S(1)}, u32[]{:S(2)}, u32[]{:S(2)}) collective-permute-start(f32[24,256]{1,0:T(8,128)S(1)} %get-tuple-element.84), channel_id=1, source_target_pairs={{0,3},{1,0},{2,1},{3,2},{4,7},{5,4},{6,5},{7,6},{8,11},{9,8},{10,9... | collective-permute-start | bytes 73736 | tf_op jit(solution)/shard_map/sum_cols/ppermute | solution.py:80
  58.8 1.8 %collective-permute-done.18.refs_1_ = f32[24,256]{1,0:T(8,128)S(1)} collective-permute-done((f32[24,256]{1,0:T(8,128)S(1)}, f32[24,256]{1,0:T(8,128)S(1)}, u32[]{:S(2)}, u32[]{:S(2)}) %collective-permute-start.18) | collective-permute-done | bytes 24608 | tf_op jit(solution)/shard_map/sum_cols/ppermute | solution.py:80
  60.6 0.6 collective-permute-done.20.refs_3_
  61.2 0.7 collective-permute-start.25
  61.9 0.8 %collective-permute-start.27 = (f32[24,256]{1,0:T(8,128)S(1)}, f32[24,256]{1,0:T(8,128)S(1)}, u32[]{:S(2)}, u32[]{:S(2)}) collective-permute-start(f32[24,256]{1,0:T(8,128)S(1)} %spread.2.refs_0_), channel_id=1, source_target_pairs={{0,16},{4,20},{8,24},{12,28},{16,0},{20,4},{24,8},{28,12},{1,17},{... | collective-permute-start | bytes 73736 | tf_op jit(solution)/shard_map/spread/ppermute | solution.py:76
  62.7 2.1 %collective-permute-start.21 = (f32[24,256]{1,0:T(8,128)S(1)}, f32[24,256]{1,0:T(8,128)S(1)}, u32[]{:S(2)}, u32[]{:S(2)}) collective-permute-start(f32[24,256]{1,0:T(8,128)S(1)} %spread.2.refs_0_), channel_id=1, source_target_pairs={{0,24},{4,28},{8,16},{12,20},{16,8},{20,12},{24,0},{28,4},{1,25},{... | collective-permute-start | bytes 73736 | tf_op jit(solution)/shard_map/spread/ppermute | solution.py:76
  64.8 0.3 collective-permute-done.25.refs_2_
  65.3 0.4 collective-permute-done.27.refs_4_
  65.7 1.5 %rows_out.1 = (f32[128,256]{1,0:T(8,128)}, f32[128,256]{1,0:T(8,128)}) custom-call(s32[3]{0:T(128)S(1)} %copy-done.5, s32[3]{0:T(128)S(1)} %copy-done.6, s32[3]{0:T(128)S(1)} %copy-done.7, bf16[256,256]{1,0:T(8,128)(2,1)S(1)} %get-tuple-element.66.th, bf16[256,256]{1,0:T(8,128)(2,1)S(1)} %get-tuple-element.67.tl, f32[96,512]{1,0:T(8,128)S(1)} %get-tuple-element.85.refs_0_, ...), custom_call_target="tpu_custom_call" | custom-call | bytes 1114148 | tf_op jit(solution)/shard_map/rows_out/pallas_call | solution.py:42
  67.4 0.3 collective-permute-start.29
  67.7 0.9 %collective-permute-done.29.refs_7_ = f32[24,256]{1,0:T(8,128)S(1)} collective-permute-done((f32[24,256]{1,0:T(8,128)S(1)}, f32[24,256]{1,0:T(8,128)S(1)}, u32[]{:S(2)}, u32[]{:S(2)}) %collective-permute-start.29) | collective-permute-done | bytes 24608 | tf_op jit(solution)/shard_map/spread/ppermute | solution.py:76
  68.6 0.7 %finish.1 = (f32[64,256]{1,0:T(8,128)}, f32[64,256]{1,0:T(8,128)}, f32[64,256]{1,0:T(8,128)}) custom-call(f32[64,256]{1,0:T(8,128)S(1)} %copy-done.1, f32[64,256]{1,0:T(8,128)S(1)} %copy-done.3, f32[64,256]{1,0:T(8,128)S(1)} %get-tuple-element.91.base, f32[24,256]{1,0:T(8,128)S(1)} %spread.2.refs_0_, f32[24,256]{1,0:T(8,128)S(1)} %collective-permute-done.24.refs_1_, ...), custom_call_target="tpu_custom_call" | custom-call | bytes 589824 | tf_op jit(solution)/shard_map/finish/pallas_call | solution.py:42
  (46 shorter events, 1.1 us)
Async XLA Ops:
  2.5 6.4 %collective-permute-start = (f32[232,128]{1,0:T(8,128)}, f32[232,128]{1,0:T(8,128)S(1)}, u32[]{:S(2)}, u32[]{:S(2)}) collective-permute-start(f32[232,128]{1,0:T(8,128)} %get-tuple-element.53), channel_id=1, source_target_pairs={{0,8},{4,12},{8,0},{12,4},{16,24},{20,28},{24,16},{28,20},{1,9},{5... | collective-permute-start | bytes 356360 | tf_op jit(solution)/shard_map/to_column/ppermute | solution.py:76
  5.5 10.8 %collective-permute-start.3 = (f32[384,128]{1,0:T(8,128)}, f32[384,128]{1,0:T(8,128)S(1)}, u32[]{:S(2)}, u32[]{:S(2)}) collective-permute-start(f32[384,128]{1,0:T(8,128)} %get-tuple-element.51.refs_0_), channel_id=1, source_target_pairs={{0,1},{1,0},{2,3},{3,2},{4,5},{5,4},{6,7},{7,6},{8,9},{9,8},{10,11... | collective-permute-start | bytes 589832 | tf_op jit(solution)/shard_map/owned/ppermute | solution.py:84
  7.1 0.9 %copy-start.2 = (f32[232,128]{1,0:T(8,128)S(1)}, f32[232,128]{1,0:T(8,128)}, u32[]{:S(2)}) copy-start(f32[232,128]{1,0:T(8,128)} %get-tuple-element.52.source) | copy-start | bytes 356356
  9.0 11.4 %copy-start.8 = (f32[384,128]{1,0:T(8,128)S(1)}, f32[384,128]{1,0:T(8,128)}, u32[]{:S(2)}) copy-start(f32[384,128]{1,0:T(8,128)} %get-tuple-element.51.refs_0_) | copy-start | bytes 589828
  9.3 7.0 %collective-permute-start.1 = (f32[232,128]{1,0:T(8,128)S(1)}, f32[232,128]{1,0:T(8,128)S(1)}, u32[]{:S(2)}, u32[]{:S(2)}) collective-permute-start(f32[232,128]{1,0:T(8,128)S(1)} %get-tuple-element.54), channel_id=1, source_target_pairs={{0,0},{1,4},{2,2},{3,6},{4,1},{5,5},{6,3},{7,7},{8,8},{9,12},{10,1... | collective-permute-start | bytes 356360 | tf_op jit(solution)/shard_map/to_column/ppermute | solution.py:417
  9.9 6.8 %collective-permute-start.2 = (f32[232,128]{1,0:T(8,128)S(1)}, f32[232,128]{1,0:T(8,128)S(1)}, u32[]{:S(2)}, u32[]{:S(2)}) collective-permute-start(f32[232,128]{1,0:T(8,128)S(1)} %get-tuple-element.55), channel_id=1, source_target_pairs={{0,2},{1,6},{2,0},{3,4},{4,3},{5,7},{6,1},{7,5},{8,10},{9,14},{10,... | collective-permute-start | bytes 356360 | tf_op jit(solution)/shard_map/to_column/ppermute | solution.py:417
  12.9 1.6 %copy-start = (f32[4,1,128,8,1,128]{5,4,3,2,1,0:T(1,128)S(1)}, f32[4,1,128,8,1,128]{5,4,3,2,1,0:T(1,128)}, u32[]{:S(2)}) copy-start(f32[4,1,128,8,1,128]{5,4,3,2,1,0:T(1,128)} %param.10) | copy-start | bytes 6291460
  14.4 0.7 copy-start.4
  16.8 16.3 %copy-start.1 = (f32[64,256]{1,0:T(8,128)S(1)}, f32[64,256]{1,0:T(8,128)}, u32[]{:S(2)}) copy-start(f32[64,256]{1,0:T(8,128)} %pd.3) | copy-start | bytes 196612
  16.8 12.0 %collective-permute-start.9 = (f32[464,128]{1,0:T(8,128)S(1)}, f32[464,128]{1,0:T(8,128)S(1)}, u32[]{:S(2)}, u32[]{:S(2)}) collective-permute-start(f32[464,128]{1,0:T(8,128)S(1)} %get-tuple-element.61.refs_0_), channel_id=1, source_target_pairs={{0,16},{4,20},{8,24},{12,28},{16,0},{20,4},{24,8},{28,12},{1,17},{... | collective-permute-start | bytes 712712 | tf_op jit(solution)/shard_map/panels/ppermute | solution.py:76
  18.4 12.3 %collective-permute-start.11 = (f32[464,128]{1,0:T(8,128)S(1)}, f32[464,128]{1,0:T(8,128)S(1)}, u32[]{:S(2)}, u32[]{:S(2)}) collective-permute-start(f32[464,128]{1,0:T(8,128)S(1)} %get-tuple-element.61.refs_0_), channel_id=1, source_target_pairs={{0,24},{4,28},{8,16},{12,20},{16,8},{20,12},{24,0},{28,4},{1,25},{... | collective-permute-start | bytes 712712 | tf_op jit(solution)/shard_map/panels/ppermute | solution.py:76
  19.4 11.4 %collective-permute-start.7 = (f32[464,128]{1,0:T(8,128)S(1)}, f32[464,128]{1,0:T(8,128)S(1)}, u32[]{:S(2)}, u32[]{:S(2)}) collective-permute-start(f32[464,128]{1,0:T(8,128)S(1)} %get-tuple-element.61.refs_0_), channel_id=1, source_target_pairs={{0,8},{4,12},{8,0},{12,4},{16,24},{20,28},{24,16},{28,20},{1,9},{5... | collective-permute-start | bytes 712712 | tf_op jit(solution)/shard_map/panels/ppermute | solution.py:76
  20.3 11.6 %collective-permute-start.4 = (f32[384,128]{1,0:T(8,128)S(1)}, f32[384,128]{1,0:T(8,128)S(1)}, u32[]{:S(2)}, u32[]{:S(2)}) collective-permute-start(f32[384,128]{1,0:T(8,128)S(1)} %copy-done.8), channel_id=1, source_target_pairs={{0,2},{1,3},{2,0},{3,1},{4,6},{5,7},{6,4},{7,5},{8,10},{9,11},{10,... | collective-permute-start | bytes 589832 | tf_op jit(solution)/shard_map/owned/ppermute | solution.py:84
  23.5 8.9 %collective-permute-start.6 = (f32[464,128]{1,0:T(8,128)S(1)}, f32[464,128]{1,0:T(8,128)S(1)}, u32[]{:S(2)}, u32[]{:S(2)}) collective-permute-start(f32[464,128]{1,0:T(8,128)S(1)} %get-tuple-element.61.refs_0_), channel_id=1, source_target_pairs={{0,4},{4,0},{8,12},{12,8},{16,20},{20,16},{24,28},{28,24},{1,5},{5... | collective-permute-start | bytes 712712 | tf_op jit(solution)/shard_map/panels/ppermute | solution.py:76
  28.8 3.6 %collective-permute-start.10 = (f32[464,128]{1,0:T(8,128)S(1)}, f32[464,128]{1,0:T(8,128)S(1)}, u32[]{:S(2)}, u32[]{:S(2)}) collective-permute-start(f32[464,128]{1,0:T(8,128)S(1)} %collective-permute-done.9.refs_4_), channel_id=1, source_target_pairs={{0,4},{4,0},{8,12},{12,8},{16,20},{20,16},{24,28},{28,24},{1,5},{5... | collective-permute-start | bytes 712712 | tf_op jit(solution)/shard_map/panels/ppermute | solution.py:76
  30.7 1.6 %collective-permute-start.12 = (f32[464,128]{1,0:T(8,128)S(1)}, f32[464,128]{1,0:T(8,128)S(1)}, u32[]{:S(2)}, u32[]{:S(2)}) collective-permute-start(f32[464,128]{1,0:T(8,128)S(1)} %collective-permute-done.11.refs_6_), channel_id=1, source_target_pairs={{0,4},{4,0},{8,12},{12,8},{16,20},{20,16},{24,28},{28,24},{1,5},{5... | collective-permute-start | bytes 712712 | tf_op jit(solution)/shard_map/panels/ppermute | solution.py:76
  30.9 2.2 %collective-permute-start.8 = (f32[464,128]{1,0:T(8,128)S(1)}, f32[464,128]{1,0:T(8,128)S(1)}, u32[]{:S(2)}, u32[]{:S(2)}) collective-permute-start(f32[464,128]{1,0:T(8,128)S(1)} %collective-permute-done.7.refs_2_), channel_id=1, source_target_pairs={{0,4},{4,0},{8,12},{12,8},{16,20},{20,16},{24,28},{28,24},{1,5},{5... | collective-permute-start | bytes 712712 | tf_op jit(solution)/shard_map/panels/ppermute | solution.py:76
  31.9 7.2 %collective-permute-start.5 = (f32[384,128]{1,0:T(8,128)S(1)}, f32[384,128]{1,0:T(8,128)S(1)}, u32[]{:S(2)}, u32[]{:S(2)}) collective-permute-start(f32[384,128]{1,0:T(8,128)S(1)} %owned.1.refs_2_), channel_id=1, source_target_pairs={{0,1},{1,0},{2,3},{3,2},{4,5},{5,4},{6,7},{7,6},{8,9},{9,8},{10,11... | collective-permute-start | bytes 589832 | tf_op jit(solution)/shard_map/owned/ppermute | solution.py:84
  35.3 7.7 %collective-permute-start.14 = (f32[96,512]{1,0:T(8,128)S(1)}, f32[96,512]{1,0:T(8,128)S(1)}, u32[]{:S(2)}, u32[]{:S(2)}) collective-permute-start(f32[96,512]{1,0:T(8,128)S(1)} %get-tuple-element.76), channel_id=1, source_target_pairs={{0,1},{1,0},{2,3},{3,2},{4,5},{5,4},{6,7},{7,6},{8,9},{9,8},{10,11... | collective-permute-start | bytes 589832 | tf_op jit(solution)/shard_map/sum_shares/ppermute | solution.py:84
  40.9 2.2 %collective-permute-start.13 = (f32[384,256]{1,0:T(8,128)S(1)}, f32[384,256]{1,0:T(8,128)S(1)}, u32[]{:S(2)}, u32[]{:S(2)}) collective-permute-start(f32[384,256]{1,0:T(8,128)S(1)} %get-tuple-element.74), channel_id=1, source_target_pairs={{0,4},{4,0},{8,12},{12,8},{16,20},{20,16},{24,28},{28,24},{1,5},{5... | collective-permute-start | bytes 1179656 | tf_op jit(solution)/shard_map/sum_core/ppermute | solution.py:76
  41.0 23.8 %collective-permute-start.22 = (f32[96,512]{1,0:T(8,128)S(1)}, f32[96,512]{1,0:T(8,128)S(1)}, u32[]{:S(2)}, u32[]{:S(2)}) collective-permute-start(f32[96,512]{1,0:T(8,128)S(1)} %get-tuple-element.86), channel_id=1, source_target_pairs={{0,1},{1,0},{2,3},{3,2},{4,5},{5,4},{6,7},{7,6},{8,9},{9,8},{10,11... | collective-permute-start | bytes 589832 | tf_op jit(solution)/shard_map/sum_shares/ppermute | solution.py:84
  43.0 22.7 %copy-start.5 = (s32[3]{0:T(128)S(1)}, s32[3]{0:T(128)}, u32[]{:S(2)}) copy-start(s32[3]{0:T(128)} %blocks.3) | copy-start | bytes 40
  43.0 22.7 %copy-start.6 = (s32[3]{0:T(128)S(1)}, s32[3]{0:T(128)}, u32[]{:S(2)}) copy-start(s32[3]{0:T(128)} %psize.1) | copy-start | bytes 40
  43.0 22.7 %copy-start.7 = (s32[3]{0:T(128)S(1)}, s32[3]{0:T(128)}, u32[]{:S(2)}) copy-start(s32[3]{0:T(128)} %csize.1) | copy-start | bytes 40
  43.1 25.6 %copy-start.3 = (f32[64,256]{1,0:T(8,128)S(1)}, f32[64,256]{1,0:T(8,128)}, u32[]{:S(2)}) copy-start(f32[64,256]{1,0:T(8,128)} %cd.1) | copy-start | bytes 196612
  43.1 22.6 %collective-permute-start.23 = (f32[96,512]{1,0:T(8,128)S(1)}, f32[96,512]{1,0:T(8,128)S(1)}, u32[]{:S(2)}, u32[]{:S(2)}) collective-permute-start(f32[96,512]{1,0:T(8,128)S(1)} %get-tuple-element.87), channel_id=1, source_target_pairs={{0,2},{1,3},{2,0},{3,1},{4,6},{5,7},{6,4},{7,5},{8,10},{9,11},{10,... | collective-permute-start | bytes 589832 | tf_op jit(solution)/shard_map/sum_shares/ppermute | solution.py:84
  46.4 4.8 %collective-permute-start.15 = (f32[96,256]{1,0:T(8,128)S(1)}, f32[96,256]{1,0:T(8,128)S(1)}, u32[]{:S(2)}, u32[]{:S(2)}) collective-permute-start(f32[96,256]{1,0:T(8,128)S(1)} %get-tuple-element.78), channel_id=1, source_target_pairs={{0,8},{4,12},{8,0},{12,4},{16,24},{20,28},{24,16},{28,20},{1,9},{5... | collective-permute-start | bytes 294920 | tf_op jit(solution)/shard_map/sum_chips/ppermute | solution.py:76
  47.9 5.7 %collective-permute-start.16 = (f32[96,256]{1,0:T(8,128)S(1)}, f32[96,256]{1,0:T(8,128)S(1)}, u32[]{:S(2)}, u32[]{:S(2)}) collective-permute-start(f32[96,256]{1,0:T(8,128)S(1)} %get-tuple-element.79), channel_id=1, source_target_pairs={{0,16},{4,20},{8,24},{12,28},{16,0},{20,4},{24,8},{28,12},{1,17},{... | collective-permute-start | bytes 294920 | tf_op jit(solution)/shard_map/sum_chips/ppermute | solution.py:76
  49.4 5.5 %collective-permute-start.17 = (f32[96,256]{1,0:T(8,128)S(1)}, f32[96,256]{1,0:T(8,128)S(1)}, u32[]{:S(2)}, u32[]{:S(2)}) collective-permute-start(f32[96,256]{1,0:T(8,128)S(1)} %get-tuple-element.80), channel_id=1, source_target_pairs={{0,24},{4,28},{8,16},{12,20},{16,8},{20,12},{24,0},{28,4},{1,25},{... | collective-permute-start | bytes 294920 | tf_op jit(solution)/shard_map/sum_chips/ppermute | solution.py:76
  55.0 5.7 %collective-permute-start.18 = (f32[24,256]{1,0:T(8,128)S(1)}, f32[24,256]{1,0:T(8,128)S(1)}, u32[]{:S(2)}, u32[]{:S(2)}) collective-permute-start(f32[24,256]{1,0:T(8,128)S(1)} %get-tuple-element.82), channel_id=1, source_target_pairs={{0,1},{1,2},{2,3},{3,0},{4,5},{5,6},{6,7},{7,4},{8,9},{9,10},{10,1... | collective-permute-start | bytes 73736 | tf_op jit(solution)/shard_map/sum_cols/ppermute | solution.py:80
  55.3 5.3 %collective-permute-start.19 = (f32[24,256]{1,0:T(8,128)S(1)}, f32[24,256]{1,0:T(8,128)S(1)}, u32[]{:S(2)}, u32[]{:S(2)}) collective-permute-start(f32[24,256]{1,0:T(8,128)S(1)} %get-tuple-element.83), channel_id=1, source_target_pairs={{0,2},{1,3},{2,0},{3,1},{4,6},{5,7},{6,4},{7,5},{8,10},{9,11},{10,... | collective-permute-start | bytes 73736 | tf_op jit(solution)/shard_map/sum_cols/ppermute | solution.py:80
  55.4 5.8 %collective-permute-start.20 = (f32[24,256]{1,0:T(8,128)S(1)}, f32[24,256]{1,0:T(8,128)S(1)}, u32[]{:S(2)}, u32[]{:S(2)}) collective-permute-start(f32[24,256]{1,0:T(8,128)S(1)} %get-tuple-element.84), channel_id=1, source_target_pairs={{0,3},{1,0},{2,1},{3,2},{4,7},{5,4},{6,5},{7,6},{8,11},{9,8},{10,9... | collective-permute-start | bytes 73736 | tf_op jit(solution)/shard_map/sum_cols/ppermute | solution.py:80
  61.2 3.9 %collective-permute-start.25 = (f32[24,256]{1,0:T(8,128)S(1)}, f32[24,256]{1,0:T(8,128)S(1)}, u32[]{:S(2)}, u32[]{:S(2)}) collective-permute-start(f32[24,256]{1,0:T(8,128)S(1)} %spread.2.refs_0_), channel_id=1, source_target_pairs={{0,8},{4,12},{8,0},{12,4},{16,24},{20,28},{24,16},{28,20},{1,9},{5... | collective-permute-start | bytes 73736 | tf_op jit(solution)/shard_map/spread/ppermute | solution.py:76
  61.9 3.8 %collective-permute-start.27 = (f32[24,256]{1,0:T(8,128)S(1)}, f32[24,256]{1,0:T(8,128)S(1)}, u32[]{:S(2)}, u32[]{:S(2)}) collective-permute-start(f32[24,256]{1,0:T(8,128)S(1)} %spread.2.refs_0_), channel_id=1, source_target_pairs={{0,16},{4,20},{8,24},{12,28},{16,0},{20,4},{24,8},{28,12},{1,17},{... | collective-permute-start | bytes 73736 | tf_op jit(solution)/shard_map/spread/ppermute | solution.py:76
  62.7 4.7 %collective-permute-start.21 = (f32[24,256]{1,0:T(8,128)S(1)}, f32[24,256]{1,0:T(8,128)S(1)}, u32[]{:S(2)}, u32[]{:S(2)}) collective-permute-start(f32[24,256]{1,0:T(8,128)S(1)} %spread.2.refs_0_), channel_id=1, source_target_pairs={{0,24},{4,28},{8,16},{12,20},{16,8},{20,12},{24,0},{28,4},{1,25},{... | collective-permute-start | bytes 73736 | tf_op jit(solution)/shard_map/spread/ppermute | solution.py:76
  64.8 3.0 %collective-permute-start.24 = (f32[24,256]{1,0:T(8,128)S(1)}, f32[24,256]{1,0:T(8,128)S(1)}, u32[]{:S(2)}, u32[]{:S(2)}) collective-permute-start(f32[24,256]{1,0:T(8,128)S(1)} %spread.2.refs_0_), channel_id=1, source_target_pairs={{0,4},{4,0},{8,12},{12,8},{16,20},{20,16},{24,28},{28,24},{1,5},{5... | collective-permute-start | bytes 73736 | tf_op jit(solution)/shard_map/spread/ppermute | solution.py:76
  65.1 2.6 %collective-permute-start.26 = (f32[24,256]{1,0:T(8,128)S(1)}, f32[24,256]{1,0:T(8,128)S(1)}, u32[]{:S(2)}, u32[]{:S(2)}) collective-permute-start(f32[24,256]{1,0:T(8,128)S(1)} %collective-permute-done.25.refs_2_), channel_id=1, source_target_pairs={{0,4},{4,0},{8,12},{12,8},{16,20},{20,16},{24,28},{28,24},{1,5},{5... | collective-permute-start | bytes 73736 | tf_op jit(solution)/shard_map/spread/ppermute | solution.py:76
  65.7 2.0 %collective-permute-start.28 = (f32[24,256]{1,0:T(8,128)S(1)}, f32[24,256]{1,0:T(8,128)S(1)}, u32[]{:S(2)}, u32[]{:S(2)}) collective-permute-start(f32[24,256]{1,0:T(8,128)S(1)} %collective-permute-done.27.refs_4_), channel_id=1, source_target_pairs={{0,4},{4,0},{8,12},{12,8},{16,20},{20,16},{24,28},{28,24},{1,5},{5... | collective-permute-start | bytes 73736 | tf_op jit(solution)/shard_map/spread/ppermute | solution.py:76
  67.4 1.2 %collective-permute-start.29 = (f32[24,256]{1,0:T(8,128)S(1)}, f32[24,256]{1,0:T(8,128)S(1)}, u32[]{:S(2)}, u32[]{:S(2)}) collective-permute-start(f32[24,256]{1,0:T(8,128)S(1)} %get-tuple-element.92.refs_6_), channel_id=1, source_target_pairs={{0,4},{4,0},{8,12},{12,8},{16,20},{20,16},{24,28},{28,24},{1,5},{5... | collective-permute-start | bytes 73736 | tf_op jit(solution)/shard_map/spread/ppermute | solution.py:76

commit v7 on v6

--- a/solution.py
+++ b/solution.py
@@ -103,7 +103,7 @@
 
 
 def pack(s, *refs):
-    sources, (kept, sent, mine, parents, children, *targets, sems) = refs[:6], refs[6:]
+    sources, (kept, sent, mine, *targets, sems) = refs[:6], refs[6:]
     for copy in fetch(sources, targets, sems):
         copy.wait()
     blocks, psize, csize, parent, child, top = targets
@@ -112,10 +112,9 @@
     lane = lax.broadcasted_iota(jnp.int32, (s.ws, s.B), 1)
     for slot in range(s.slots):
         base = slot * 2 * s.ws
-        for which, panel, sizes, half in ((0, parent, psize, parents), (1, child, csize, children)):
+        for which, panel, sizes in ((0, parent, psize), (1, child, csize)):
             live = jnp.where(lane < sizes[slot], panel[slot], 0.0)
             mine[base + which * s.ws : base + (which + 1) * s.ws, :] = live
-            half[slot * s.ws : (slot + 1) * s.ws, :] = live
     columns = pl.ds(pl.multiple_of(lax.div(row, s.C) * s.B, s.B), s.B)
     row8 = lax.broadcasted_iota(jnp.int32, (8, s.B), 0)
     ids = jnp.zeros((8, s.B), f32)
@@ -123,15 +122,9 @@
         ids = jnp.where(row8 == slot, blocks[slot].astype(f32), ids)
     quarter = s.ws // 2
     for out, at in ((kept, side), (sent, 1 - side)):
-
-        @pl.when(at == 0)
-        def _():
-            out[: s.part, :] = parents[...]
-
-        @pl.when(at == 1)
-        def _():
-            out[: s.part, :] = children[...]
-
+        for slot in range(s.slots):
+            rows = pl.ds(pl.multiple_of((slot * 2 + at) * s.ws, s.ws), s.ws)
+            out[slot * s.ws : (slot + 1) * s.ws, :] = mine[rows, :]
         rows = pl.ds(pl.multiple_of(at * quarter, quarter), quarter)
         out[s.part : s.part + quarter, :] = top[rows, columns]
         out[s.part + quarter :, :] = ids
@@ -168,7 +161,7 @@
     pass
 
 
-def split_live(s, cached, blocks, high, low, held, numbers, sems):
+def split_live(s, cached, blocks, after, high, low, held, numbers, sems):
     copy = pltpu.make_async_copy(blocks, numbers, sems.at[0])
     copy.start()
     copy.wait()
@@ -386,7 +379,7 @@
     numbers = pltpu.SMEM((s.slots,), jnp.int32)
     by_slot = (s.slots, ws, B)
     with jax.named_scope("pack"):
-        kept, sent, mine, parents, children = call(
+        kept, sent, mine = call(
             bind(pack),
             anywhere(
                 parent_blocks,
@@ -396,7 +389,7 @@
                 jnp.transpose(child_panel, (1, 0, 2)),
                 child_top,
             ),
-            [(s.block, B)] * 2 + [(s.payload, B)] + [(s.part, B)] * 2,
+            [(s.block, B)] * 2 + [(s.payload, B)],
             [numbers] * 3
             + [pltpu.VMEM(by_slot, f32)] * 2
             + [pltpu.VMEM((ws, W), f32), pltpu.SemaphoreType.DMA((6,))],
@@ -416,14 +409,6 @@
         pieces = [
             lax.ppermute(pieces[turn], ("row", "col"), column_perm(s, turn)) for turn in range(2)
         ]
-    with jax.named_scope("split_live"):
-        sh, sl = call(
-            bind(split_live),
-            anywhere(cached, parent_blocks),
-            [((live, s.CC * B), bf16)] * 2,
-            [pltpu.VMEM((s.slots * B * s.CC, B), f32), numbers]
-            + [pltpu.SemaphoreType.DMA((1 + s.slots,))],
-        )
     with jax.named_scope("owned"):
         near = flip(mine, 1, C)
         held, mask = {0: mine}, C // 2
@@ -435,13 +420,20 @@
             (owned[m],) = call(bind(order), (), (), passed=(held[m],), ahead=8e9)
             owned[m + 1] = flip(owned[m], 1, C)
     with jax.named_scope("join"):
-        own, owned[1], sh, sl = call(
-            bind(join), vmem(*pieces), [(2 * s.block, B)], passed=(owned[1], sh, sl)
+        own, owned[1] = call(bind(join), vmem(*pieces), [(2 * s.block, B)], passed=(owned[1],))
+    with jax.named_scope("split_live"):
+        sh, sl = call(
+            bind(split_live),
+            anywhere(cached, parent_blocks, own),
+            [((live, s.CC * B), bf16)] * 2,
+            [pltpu.VMEM((s.slots * B * s.CC, B), f32), numbers]
+            + [pltpu.SemaphoreType.DMA((1 + s.slots,))],
         )
     with jax.named_scope("panels"):
         panels = {0: own}
         for mask in range(2, R, 2):
             panels[mask] = exchange(own, mask, R)
+        panels[C], sh, sl = call(bind(order), (), (), passed=(panels[C], sh, sl))
         for mask in range(0, R, 2):
             panels[mask + 1] = exchange(panels[mask], 1, R)
     with jax.named_scope("shares_of"):

time: 69.5 us -> 69.4 us (level)
    ppermute x19, waiting for transfers between devices: 13.1 us -> 9.44 us  [exchange(): return lax.ppermute(value, 'row', [(i, i ^ mask) for i in range(row_total)])]
    ppermute x2, waiting for transfers between devices: 0.47 us -> 3.92 us  [fast_body(): lax.ppermute(pieces[turn], ('row', 'col'), column_perm(s, turn))]
    pallas_call x16 -> x17, Pallas kernels: 9.84 us -> 9.77 us  [call(): pl.pallas_call(kernel, out_shape=shapes, in_specs=[pl.BlockSpec(memory_sp...]
where the time goes in v7:
time: 69.4 us; the launch traced here: 69.2 us
  starting transfers between devices  35.2 us (51%)
  waiting for transfers between devices  20.3 us (29%)
  Pallas kernels  9.77 us (14%)
  local copies, waits for them, and re-layouts  3.17 us (5%)
  between operations  0.79 us (1%)
    ppermute x19, starting transfers between devices, exchange(): return lax.ppermute(value, 'row', [(i, i ^ mask) for i in range(row_total)])  17.9 us
    ppermute x6, starting transfers between devices, flip(): return lax.ppermute(value, 'col', [(i, i ^ mask) for i in range(col_total)])  9.88 us
    pallas_call x17, Pallas kernels, call(): pl.pallas_call(kernel, out_shape=shapes, in_specs=[pl.BlockSpec(memory_sp...  9.77 us
    ppermute x19, waiting for transfers between devices, exchange(): return lax.ppermute(value, 'row', [(i, i ^ mask) for i in range(row_total)])  9.44 us
    ppermute x6, waiting for transfers between devices, flip(): return lax.ppermute(value, 'col', [(i, i ^ mask) for i in range(col_total)])  4.54 us
    ppermute x2, waiting for transfers between devices, fast_body(): lax.ppermute(pieces[turn], ('row', 'col'), column_perm(s, turn))  3.92 us
    ppermute x3, starting transfers between devices, shift(): lax.ppermute(value, 'col', [(i, (i + step) % col_total) for i in range(co...  3.88 us
    ppermute x2, starting transfers between devices, fast_body(): lax.ppermute(pieces[turn], ('row', 'col'), column_perm(s, turn))  3.57 us
  transfers between devices with their start and end apart: 30, of which 16 were waited for; matrix products, arithmetic and copies ran while one was open for 0% of the time, Pallas kernels for 10%

profile of v7, /device:TPU:0, one launch (start us, length us, event | category | flops | bytes accessed | tf_op | source)
XLA Modules:
  0.0 69.2 jit_solution(17630812784406077372)
XLA Ops:
  0.6 1.8 %pack.1 = (f32[232,128]{1,0:T(8,128)}, f32[232,128]{1,0:T(8,128)}, f32[384,128]{1,0:T(8,128)}) custom-call(s32[3]{0:T(128)} %blocks.3, s32[3]{0:T(128)} %psize.1, s32[3]{0:T(128)} %csize.1, f32[3,64,128]{2,1,0:T(8,128)} %bitcast.12, f32[3,64,128]{2,1,0:T(8,128)} %bitcast.13, f32[64,256]{1,0:T(8,128)} %refs_5_.1), custom_call_target="tpu_custom_call" | custom-call | bytes 696356 | tf_op jit(solution)/shard_map/pack/pallas_call | solution.py:42
  2.4 3.0 %collective-permute-start = (f32[232,128]{1,0:T(8,128)}, f32[232,128]{1,0:T(8,128)S(1)}, u32[]{:S(2)}, u32[]{:S(2)}) collective-permute-start(f32[232,128]{1,0:T(8,128)} %get-tuple-element.54), channel_id=1, source_target_pairs={{0,8},{4,12},{8,0},{12,4},{16,24},{20,28},{24,16},{28,20},{1,9},{5... | collective-permute-start | bytes 356360 | tf_op jit(solution)/shard_map/to_column/ppermute | solution.py:76
  5.4 1.6 %collective-permute-start.3 = (f32[384,128]{1,0:T(8,128)}, f32[384,128]{1,0:T(8,128)S(1)}, u32[]{:S(2)}, u32[]{:S(2)}) collective-permute-start(f32[384,128]{1,0:T(8,128)} %get-tuple-element.52.refs_0_), channel_id=1, source_target_pairs={{0,1},{1,0},{2,3},{3,2},{4,5},{5,4},{6,7},{7,6},{8,9},{9,8},{10,11... | collective-permute-start | bytes 589832 | tf_op jit(solution)/shard_map/owned/ppermute | solution.py:84
  7.0 0.9 %copy-done.2 = f32[232,128]{1,0:T(8,128)S(1)} copy-done((f32[232,128]{1,0:T(8,128)S(1)}, f32[232,128]{1,0:T(8,128)}, u32[]{:S(2)}) %copy-start.2) | copy-done | bytes 118808
  8.0 0.8 %collective-permute-done.got = f32[232,128]{1,0:T(8,128)S(1)} collective-permute-done((f32[232,128]{1,0:T(8,128)}, f32[232,128]{1,0:T(8,128)S(1)}, u32[]{:S(2)}, u32[]{:S(2)}) %collective-permute-start) | collective-permute-done | bytes 118816 | tf_op jit(solution)/shard_map/to_column/ppermute | solution.py:76
  8.9 0.3 to_column.3
  9.2 0.7 collective-permute-start.1
  9.8 2.9 %collective-permute-start.2 = (f32[232,128]{1,0:T(8,128)S(1)}, f32[232,128]{1,0:T(8,128)S(1)}, u32[]{:S(2)}, u32[]{:S(2)}) collective-permute-start(f32[232,128]{1,0:T(8,128)S(1)} %get-tuple-element.56), channel_id=1, source_target_pairs={{0,2},{1,6},{2,0},{3,4},{4,3},{5,7},{6,1},{7,5},{8,10},{9,14},{10,... | collective-permute-start | bytes 356360 | tf_op jit(solution)/shard_map/to_column/ppermute | solution.py:410
  12.8 3.9 %collective-permute-done.2.second = f32[232,128]{1,0:T(8,128)S(1)} collective-permute-done((f32[232,128]{1,0:T(8,128)S(1)}, f32[232,128]{1,0:T(8,128)S(1)}, u32[]{:S(2)}, u32[]{:S(2)}) %collective-permute-start.2) | collective-permute-done | bytes 118816 | tf_op jit(solution)/shard_map/to_column/ppermute | solution.py:410
  16.7 1.6 %collective-permute-start.6 = (f32[464,128]{1,0:T(8,128)S(1)}, f32[464,128]{1,0:T(8,128)S(1)}, u32[]{:S(2)}, u32[]{:S(2)}) collective-permute-start(f32[464,128]{1,0:T(8,128)S(1)} %get-tuple-element.58.after.refs_0_), channel_id=1, source_target_pairs={{0,16},{4,20},{8,24},{12,28},{16,0},{20,4},{24,8},{28,12},{1,17},{... | collective-permute-start | bytes 712712 | tf_op jit(solution)/shard_map/panels/ppermute | solution.py:76
  18.3 1.1 %collective-permute-start.11 = (f32[464,128]{1,0:T(8,128)S(1)}, f32[464,128]{1,0:T(8,128)S(1)}, u32[]{:S(2)}, u32[]{:S(2)}) collective-permute-start(f32[464,128]{1,0:T(8,128)S(1)} %get-tuple-element.58.after.refs_0_), channel_id=1, source_target_pairs={{0,24},{4,28},{8,16},{12,20},{16,8},{20,12},{24,0},{28,4},{1,25},{... | collective-permute-start | bytes 712712 | tf_op jit(solution)/shard_map/panels/ppermute | solution.py:76
  19.3 0.9 %collective-permute-start.8 = (f32[464,128]{1,0:T(8,128)S(1)}, f32[464,128]{1,0:T(8,128)S(1)}, u32[]{:S(2)}, u32[]{:S(2)}) collective-permute-start(f32[464,128]{1,0:T(8,128)S(1)} %get-tuple-element.58.after.refs_0_), channel_id=1, source_target_pairs={{0,8},{4,12},{8,0},{12,4},{16,24},{20,28},{24,16},{28,20},{1,9},{5... | collective-permute-start | bytes 712712 | tf_op jit(solution)/shard_map/panels/ppermute | solution.py:76
  20.2 3.1 %collective-permute-start.4 = (f32[384,128]{1,0:T(8,128)}, f32[384,128]{1,0:T(8,128)S(1)}, u32[]{:S(2)}, u32[]{:S(2)}) collective-permute-start(f32[384,128]{1,0:T(8,128)} %get-tuple-element.52.refs_0_), channel_id=1, source_target_pairs={{0,2},{1,3},{2,0},{3,1},{4,6},{5,7},{6,4},{7,5},{8,10},{9,11},{10,... | collective-permute-start | bytes 589832 | tf_op jit(solution)/shard_map/owned/ppermute | solution.py:84
  23.3 0.7 %collective-permute-start.7 = (f32[464,128]{1,0:T(8,128)S(1)}, f32[464,128]{1,0:T(8,128)S(1)}, u32[]{:S(2)}, u32[]{:S(2)}) collective-permute-start(f32[464,128]{1,0:T(8,128)S(1)} %get-tuple-element.58.after.refs_0_), channel_id=1, source_target_pairs={{0,4},{4,0},{8,12},{12,8},{16,20},{20,16},{24,28},{28,24},{1,5},{5... | collective-permute-start | bytes 712712 | tf_op jit(solution)/shard_map/panels/ppermute | solution.py:76
  24.1 1.6 %copy-done = f32[4,1,128,8,1,128]{5,4,3,2,1,0:T(1,128)S(1)} copy-done((f32[4,1,128,8,1,128]{5,4,3,2,1,0:T(1,128)S(1)}, f32[4,1,128,8,1,128]{5,4,3,2,1,0:T(1,128)}, u32[]{:S(2)}) %copy-start) | copy-done | bytes 2097176
  25.7 0.7 copy-done.4
  26.3 1.2 %split_live.1 = (bf16[384,1024]{1,0:T(8,128)(2,1)S(1)}, bf16[384,1024]{1,0:T(8,128)(2,1)S(1)}) custom-call(f32[4096,128]{1,0:T(8,128)S(1)} %bitcast.9, s32[3]{0:T(128)S(1)} %copy-done.4, f32[464,128]{1,0:T(8,128)S(1)} %get-tuple-element.58.after.refs_0_), custom_call_target="tpu_custom_call" | custom-call | bytes 3907596 | tf_op jit(solution)/shard_map/split_live/pallas_call | solution.py:42
  27.5 1.2 %collective-permute-done.6.refs_0_ = f32[464,128]{1,0:T(8,128)S(1)} collective-permute-done((f32[464,128]{1,0:T(8,128)S(1)}, f32[464,128]{1,0:T(8,128)S(1)}, u32[]{:S(2)}, u32[]{:S(2)}) %collective-permute-start.6) | collective-permute-done | bytes 237600 | tf_op jit(solution)/shard_map/panels/ppermute | solution.py:76
  28.7 1.9 %collective-permute-start.10 = (f32[464,128]{1,0:T(8,128)S(1)}, f32[464,128]{1,0:T(8,128)S(1)}, u32[]{:S(2)}, u32[]{:S(2)}) collective-permute-start(f32[464,128]{1,0:T(8,128)S(1)} %get-tuple-element.63.refs_4_), channel_id=1, source_target_pairs={{0,4},{4,0},{8,12},{12,8},{16,20},{20,16},{24,28},{28,24},{1,5},{5... | collective-permute-start | bytes 712712 | tf_op jit(solution)/shard_map/panels/ppermute | solution.py:76
  30.8 1.0 %collective-permute-start.9 = (f32[464,128]{1,0:T(8,128)S(1)}, f32[464,128]{1,0:T(8,128)S(1)}, u32[]{:S(2)}, u32[]{:S(2)}) collective-permute-start(f32[464,128]{1,0:T(8,128)S(1)} %collective-permute-done.8.refs_2_), channel_id=1, source_target_pairs={{0,4},{4,0},{8,12},{12,8},{16,20},{20,16},{24,28},{28,24},{1,5},{5... | collective-permute-start | bytes 712712 | tf_op jit(solution)/shard_map/panels/ppermute | solution.py:76
  31.8 0.7 collective-permute-start.5
  32.5 0.4 collective-permute-done.9.refs_3_
  33.0 2.3 %shares_of.1 = (f32[96,512]{1,0:T(8,128)S(1)}, f32[96,512]{1,0:T(8,128)S(1)}, f32[96,512]{1,0:T(8,128)S(1)}, f32[96,512]{1,0:T(8,128)S(1)}, bf16[384,512]{1,0:T(...) custom-call(f32[64,256]{1,0:T(8,128)S(1)} %copy-done.1, ...), custom_call_target="tpu_custom_call" | custom-call | bytes 5963776 | tf_op jit(solution)/shard_map/shares_of/pallas_call | solution.py:42
  35.3 1.0 %collective-permute-start.14 = (f32[96,512]{1,0:T(8,128)S(1)}, f32[96,512]{1,0:T(8,128)S(1)}, u32[]{:S(2)}, u32[]{:S(2)}) collective-permute-start(f32[96,512]{1,0:T(8,128)S(1)} %get-tuple-element.78), channel_id=1, source_target_pairs={{0,1},{1,0},{2,3},{3,2},{4,5},{5,4},{6,7},{7,6},{8,9},{9,8},{10,11... | collective-permute-start | bytes 589832 | tf_op jit(solution)/shard_map/sum_shares/ppermute | solution.py:84
  36.3 2.7 %collective-permute-done.5.refs_3_ = f32[384,128]{1,0:T(8,128)S(1)} collective-permute-done((f32[384,128]{1,0:T(8,128)S(1)}, f32[384,128]{1,0:T(8,128)S(1)}, u32[]{:S(2)}, u32[]{:S(2)}) %collective-permute-start.5) | collective-permute-done | bytes 196640 | tf_op jit(solution)/shard_map/owned/ppermute | solution.py:84
  39.2 1.6 %products.3 = (f32[384,256]{1,0:T(8,128)S(1)}, f32[384,256]{1,0:T(8,128)S(1)}) custom-call(bf16[384,512]{1,0:T(8,128)(2,1)S(1)} %get-tuple-element.66.gh, bf16[384,512]{1,0:T(8,128)(2,1)S(1)} %get-tuple-element.67.gl, bf16[256,256]{1,0:T(8,128)(2,1)S(1)} %get-tuple-element.68.th, bf16[256,256]{1,0:T(8,128)(2,1)S(1)} %get-tuple-element.69.tl, ...), custom_call_target="tpu_custom_call" | custom-call | bytes 3145728 | tf_op jit(solution)/shard_map/products/pallas_call | solution.py:42
  40.9 0.2 collective-permute-start.22
  41.1 1.8 %collective-permute-done.14.refs_1_ = f32[96,512]{1,0:T(8,128)S(1)} collective-permute-done((f32[96,512]{1,0:T(8,128)S(1)}, f32[96,512]{1,0:T(8,128)S(1)}, u32[]{:S(2)}, u32[]{:S(2)}) %collective-permute-start.14) | collective-permute-done | bytes 196640 | tf_op jit(solution)/shard_map/sum_shares/ppermute | solution.py:84
  43.1 3.2 %collective-permute-start.23 = (f32[96,512]{1,0:T(8,128)S(1)}, f32[96,512]{1,0:T(8,128)S(1)}, u32[]{:S(2)}, u32[]{:S(2)}) collective-permute-start(f32[96,512]{1,0:T(8,128)S(1)} %get-tuple-element.89), channel_id=1, source_target_pairs={{0,2},{1,3},{2,0},{3,1},{4,6},{5,7},{6,4},{7,5},{8,10},{9,11},{10,... | collective-permute-start | bytes 589832 | tf_op jit(solution)/shard_map/sum_shares/ppermute | solution.py:84
  46.3 1.5 %collective-permute-start.15 = (f32[96,256]{1,0:T(8,128)S(1)}, f32[96,256]{1,0:T(8,128)S(1)}, u32[]{:S(2)}, u32[]{:S(2)}) collective-permute-start(f32[96,256]{1,0:T(8,128)S(1)} %get-tuple-element.80), channel_id=1, source_target_pairs={{0,8},{4,12},{8,0},{12,4},{16,24},{20,28},{24,16},{28,20},{1,9},{5... | collective-permute-start | bytes 294920 | tf_op jit(solution)/shard_map/sum_chips/ppermute | solution.py:76
  47.8 1.5 %collective-permute-start.16 = (f32[96,256]{1,0:T(8,128)S(1)}, f32[96,256]{1,0:T(8,128)S(1)}, u32[]{:S(2)}, u32[]{:S(2)}) collective-permute-start(f32[96,256]{1,0:T(8,128)S(1)} %get-tuple-element.81), channel_id=1, source_target_pairs={{0,16},{4,20},{8,24},{12,28},{16,0},{20,4},{24,8},{28,12},{1,17},{... | collective-permute-start | bytes 294920 | tf_op jit(solution)/shard_map/sum_chips/ppermute | solution.py:76
  49.3 0.5 collective-permute-start.17
  49.8 1.2 %collective-permute-done.15.refs_1_ = f32[96,256]{1,0:T(8,128)S(1)} collective-permute-done((f32[96,256]{1,0:T(8,128)S(1)}, f32[96,256]{1,0:T(8,128)S(1)}, u32[]{:S(2)}, u32[]{:S(2)}) %collective-permute-start.15) | collective-permute-done | bytes 98336 | tf_op jit(solution)/shard_map/sum_chips/ppermute | solution.py:76
  51.0 2.4 %collective-permute-done.16.refs_2_ = f32[96,256]{1,0:T(8,128)S(1)} collective-permute-done((f32[96,256]{1,0:T(8,128)S(1)}, f32[96,256]{1,0:T(8,128)S(1)}, u32[]{:S(2)}, u32[]{:S(2)}) %collective-permute-start.16) | collective-permute-done | bytes 98336 | tf_op jit(solution)/shard_map/sum_chips/ppermute | solution.py:76
  53.5 1.4 %collective-permute-done.17.refs_3_ = f32[96,256]{1,0:T(8,128)S(1)} collective-permute-done((f32[96,256]{1,0:T(8,128)S(1)}, f32[96,256]{1,0:T(8,128)S(1)}, u32[]{:S(2)}, u32[]{:S(2)}) %collective-permute-start.17) | collective-permute-done | bytes 98336 | tf_op jit(solution)/shard_map/sum_chips/ppermute | solution.py:76
  54.8 0.3 collective-permute-start.18
  55.3 3.5 %collective-permute-start.20 = (f32[24,256]{1,0:T(8,128)S(1)}, f32[24,256]{1,0:T(8,128)S(1)}, u32[]{:S(2)}, u32[]{:S(2)}) collective-permute-start(f32[24,256]{1,0:T(8,128)S(1)} %get-tuple-element.86), channel_id=1, source_target_pairs={{0,3},{1,0},{2,1},{3,2},{4,7},{5,4},{6,5},{7,6},{8,11},{9,8},{10,9... | collective-permute-start | bytes 73736 | tf_op jit(solution)/shard_map/sum_cols/ppermute | solution.py:80
  58.7 1.8 %collective-permute-done.18.refs_1_ = f32[24,256]{1,0:T(8,128)S(1)} collective-permute-done((f32[24,256]{1,0:T(8,128)S(1)}, f32[24,256]{1,0:T(8,128)S(1)}, u32[]{:S(2)}, u32[]{:S(2)}) %collective-permute-start.18) | collective-permute-done | bytes 24608 | tf_op jit(solution)/shard_map/sum_cols/ppermute | solution.py:80
  60.5 0.6 collective-permute-done.20.refs_3_
  61.1 0.7 collective-permute-start.25
  61.8 0.8 %collective-permute-start.27 = (f32[24,256]{1,0:T(8,128)S(1)}, f32[24,256]{1,0:T(8,128)S(1)}, u32[]{:S(2)}, u32[]{:S(2)}) collective-permute-start(f32[24,256]{1,0:T(8,128)S(1)} %spread.2.refs_0_), channel_id=1, source_target_pairs={{0,16},{4,20},{8,24},{12,28},{16,0},{20,4},{24,8},{28,12},{1,17},{... | collective-permute-start | bytes 73736 | tf_op jit(solution)/shard_map/spread/ppermute | solution.py:76
  62.6 2.1 %collective-permute-start.21 = (f32[24,256]{1,0:T(8,128)S(1)}, f32[24,256]{1,0:T(8,128)S(1)}, u32[]{:S(2)}, u32[]{:S(2)}) collective-permute-start(f32[24,256]{1,0:T(8,128)S(1)} %spread.2.refs_0_), channel_id=1, source_target_pairs={{0,24},{4,28},{8,16},{12,20},{16,8},{20,12},{24,0},{28,4},{1,25},{... | collective-permute-start | bytes 73736 | tf_op jit(solution)/shard_map/spread/ppermute | solution.py:76
  64.7 0.3 collective-permute-done.25.refs_2_
  65.2 0.4 collective-permute-done.27.refs_4_
  65.6 1.5 %rows_out.1 = (f32[128,256]{1,0:T(8,128)}, f32[128,256]{1,0:T(8,128)}) custom-call(s32[3]{0:T(128)S(1)} %copy-done.5, s32[3]{0:T(128)S(1)} %copy-done.6, s32[3]{0:T(128)S(1)} %copy-done.7, bf16[256,256]{1,0:T(8,128)(2,1)S(1)} %get-tuple-element.68.th, bf16[256,256]{1,0:T(8,128)(2,1)S(1)} %get-tuple-element.69.tl, f32[96,512]{1,0:T(8,128)S(1)} %get-tuple-element.87.refs_0_, ...), custom_call_target="tpu_custom_call" | custom-call | bytes 1114148 | tf_op jit(solution)/shard_map/rows_out/pallas_call | solution.py:42
  67.3 0.3 collective-permute-start.29
  67.6 0.9 %collective-permute-done.29.refs_7_ = f32[24,256]{1,0:T(8,128)S(1)} collective-permute-done((f32[24,256]{1,0:T(8,128)S(1)}, f32[24,256]{1,0:T(8,128)S(1)}, u32[]{:S(2)}, u32[]{:S(2)}) %collective-permute-start.29) | collective-permute-done | bytes 24608 | tf_op jit(solution)/shard_map/spread/ppermute | solution.py:76
  68.5 0.7 %finish.1 = (f32[64,256]{1,0:T(8,128)}, f32[64,256]{1,0:T(8,128)}, f32[64,256]{1,0:T(8,128)}) custom-call(f32[64,256]{1,0:T(8,128)S(1)} %copy-done.1, f32[64,256]{1,0:T(8,128)S(1)} %copy-done.3, f32[64,256]{1,0:T(8,128)S(1)} %get-tuple-element.93.base, f32[24,256]{1,0:T(8,128)S(1)} %spread.2.refs_0_, f32[24,256]{1,0:T(8,128)S(1)} %collective-permute-done.24.refs_1_, ...), custom_call_target="tpu_custom_call" | custom-call | bytes 589824 | tf_op jit(solution)/shard_map/finish/pallas_call | solution.py:42
  (47 shorter events, 1.1 us)
Async XLA Ops:
  2.4 6.4 %collective-permute-start = (f32[232,128]{1,0:T(8,128)}, f32[232,128]{1,0:T(8,128)S(1)}, u32[]{:S(2)}, u32[]{:S(2)}) collective-permute-start(f32[232,128]{1,0:T(8,128)} %get-tuple-element.54), channel_id=1, source_target_pairs={{0,8},{4,12},{8,0},{12,4},{16,24},{20,28},{24,16},{28,20},{1,9},{5... | collective-permute-start | bytes 356360 | tf_op jit(solution)/shard_map/to_column/ppermute | solution.py:76
  5.4 7.3 %collective-permute-start.3 = (f32[384,128]{1,0:T(8,128)}, f32[384,128]{1,0:T(8,128)S(1)}, u32[]{:S(2)}, u32[]{:S(2)}) collective-permute-start(f32[384,128]{1,0:T(8,128)} %get-tuple-element.52.refs_0_), channel_id=1, source_target_pairs={{0,1},{1,0},{2,3},{3,2},{4,5},{5,4},{6,7},{7,6},{8,9},{9,8},{10,11... | collective-permute-start | bytes 589832 | tf_op jit(solution)/shard_map/owned/ppermute | solution.py:84
  7.0 0.9 %copy-start.2 = (f32[232,128]{1,0:T(8,128)S(1)}, f32[232,128]{1,0:T(8,128)}, u32[]{:S(2)}) copy-start(f32[232,128]{1,0:T(8,128)} %get-tuple-element.53.source) | copy-start | bytes 356356
  9.2 3.6 %collective-permute-start.1 = (f32[232,128]{1,0:T(8,128)S(1)}, f32[232,128]{1,0:T(8,128)S(1)}, u32[]{:S(2)}, u32[]{:S(2)}) collective-permute-start(f32[232,128]{1,0:T(8,128)S(1)} %get-tuple-element.55), channel_id=1, source_target_pairs={{0,0},{1,4},{2,2},{3,6},{4,1},{5,5},{6,3},{7,7},{8,8},{9,12},{10,1... | collective-permute-start | bytes 356360 | tf_op jit(solution)/shard_map/to_column/ppermute | solution.py:410
  9.8 6.8 %collective-permute-start.2 = (f32[232,128]{1,0:T(8,128)S(1)}, f32[232,128]{1,0:T(8,128)S(1)}, u32[]{:S(2)}, u32[]{:S(2)}) collective-permute-start(f32[232,128]{1,0:T(8,128)S(1)} %get-tuple-element.56), channel_id=1, source_target_pairs={{0,2},{1,6},{2,0},{3,4},{4,3},{5,7},{6,1},{7,5},{8,10},{9,14},{10,... | collective-permute-start | bytes 356360 | tf_op jit(solution)/shard_map/to_column/ppermute | solution.py:410
  16.7 12.0 %collective-permute-start.6 = (f32[464,128]{1,0:T(8,128)S(1)}, f32[464,128]{1,0:T(8,128)S(1)}, u32[]{:S(2)}, u32[]{:S(2)}) collective-permute-start(f32[464,128]{1,0:T(8,128)S(1)} %get-tuple-element.58.after.refs_0_), channel_id=1, source_target_pairs={{0,16},{4,20},{8,24},{12,28},{16,0},{20,4},{24,8},{28,12},{1,17},{... | collective-permute-start | bytes 712712 | tf_op jit(solution)/shard_map/panels/ppermute | solution.py:76
  18.3 12.3 %collective-permute-start.11 = (f32[464,128]{1,0:T(8,128)S(1)}, f32[464,128]{1,0:T(8,128)S(1)}, u32[]{:S(2)}, u32[]{:S(2)}) collective-permute-start(f32[464,128]{1,0:T(8,128)S(1)} %get-tuple-element.58.after.refs_0_), channel_id=1, source_target_pairs={{0,24},{4,28},{8,16},{12,20},{16,8},{20,12},{24,0},{28,4},{1,25},{... | collective-permute-start | bytes 712712 | tf_op jit(solution)/shard_map/panels/ppermute | solution.py:76
  19.3 11.4 %collective-permute-start.8 = (f32[464,128]{1,0:T(8,128)S(1)}, f32[464,128]{1,0:T(8,128)S(1)}, u32[]{:S(2)}, u32[]{:S(2)}) collective-permute-start(f32[464,128]{1,0:T(8,128)S(1)} %get-tuple-element.58.after.refs_0_), channel_id=1, source_target_pairs={{0,8},{4,12},{8,0},{12,4},{16,24},{20,28},{24,16},{28,20},{1,9},{5... | collective-permute-start | bytes 712712 | tf_op jit(solution)/shard_map/panels/ppermute | solution.py:76
  20.2 11.6 %collective-permute-start.4 = (f32[384,128]{1,0:T(8,128)}, f32[384,128]{1,0:T(8,128)S(1)}, u32[]{:S(2)}, u32[]{:S(2)}) collective-permute-start(f32[384,128]{1,0:T(8,128)} %get-tuple-element.52.refs_0_), channel_id=1, source_target_pairs={{0,2},{1,3},{2,0},{3,1},{4,6},{5,7},{6,4},{7,5},{8,10},{9,11},{10,... | collective-permute-start | bytes 589832 | tf_op jit(solution)/shard_map/owned/ppermute | solution.py:84
  23.3 9.2 %collective-permute-start.7 = (f32[464,128]{1,0:T(8,128)S(1)}, f32[464,128]{1,0:T(8,128)S(1)}, u32[]{:S(2)}, u32[]{:S(2)}) collective-permute-start(f32[464,128]{1,0:T(8,128)S(1)} %get-tuple-element.58.after.refs_0_), channel_id=1, source_target_pairs={{0,4},{4,0},{8,12},{12,8},{16,20},{20,16},{24,28},{28,24},{1,5},{5... | collective-permute-start | bytes 712712 | tf_op jit(solution)/shard_map/panels/ppermute | solution.py:76
  24.1 1.6 %copy-start = (f32[4,1,128,8,1,128]{5,4,3,2,1,0:T(1,128)S(1)}, f32[4,1,128,8,1,128]{5,4,3,2,1,0:T(1,128)}, u32[]{:S(2)}) copy-start(f32[4,1,128,8,1,128]{5,4,3,2,1,0:T(1,128)} %param.10) | copy-start | bytes 6291460
  25.7 0.7 copy-start.4
  28.7 4.2 %copy-start.1 = (f32[64,256]{1,0:T(8,128)S(1)}, f32[64,256]{1,0:T(8,128)}, u32[]{:S(2)}) copy-start(f32[64,256]{1,0:T(8,128)} %pd.3) | copy-start | bytes 196612
  28.7 3.8 %collective-permute-start.10 = (f32[464,128]{1,0:T(8,128)S(1)}, f32[464,128]{1,0:T(8,128)S(1)}, u32[]{:S(2)}, u32[]{:S(2)}) collective-permute-start(f32[464,128]{1,0:T(8,128)S(1)} %get-tuple-element.63.refs_4_), channel_id=1, source_target_pairs={{0,4},{4,0},{8,12},{12,8},{16,20},{20,16},{24,28},{28,24},{1,5},{5... | collective-permute-start | bytes 712712 | tf_op jit(solution)/shard_map/panels/ppermute | solution.py:76
  30.6 1.9 %collective-permute-start.12 = (f32[464,128]{1,0:T(8,128)S(1)}, f32[464,128]{1,0:T(8,128)S(1)}, u32[]{:S(2)}, u32[]{:S(2)}) collective-permute-start(f32[464,128]{1,0:T(8,128)S(1)} %collective-permute-done.11.refs_6_), channel_id=1, source_target_pairs={{0,4},{4,0},{8,12},{12,8},{16,20},{20,16},{24,28},{28,24},{1,5},{5... | collective-permute-start | bytes 712712 | tf_op jit(solution)/shard_map/panels/ppermute | solution.py:76
  30.8 2.2 %collective-permute-start.9 = (f32[464,128]{1,0:T(8,128)S(1)}, f32[464,128]{1,0:T(8,128)S(1)}, u32[]{:S(2)}, u32[]{:S(2)}) collective-permute-start(f32[464,128]{1,0:T(8,128)S(1)} %collective-permute-done.8.refs_2_), channel_id=1, source_target_pairs={{0,4},{4,0},{8,12},{12,8},{16,20},{20,16},{24,28},{28,24},{1,5},{5... | collective-permute-start | bytes 712712 | tf_op jit(solution)/shard_map/panels/ppermute | solution.py:76
  31.8 7.2 %copy-start.8 = (f32[384,128]{1,0:T(8,128)S(1)}, f32[384,128]{1,0:T(8,128)}, u32[]{:S(2)}) copy-start(f32[384,128]{1,0:T(8,128)} %get-tuple-element.52.refs_0_) | copy-start | bytes 589828
  31.8 7.2 %collective-permute-start.5 = (f32[384,128]{1,0:T(8,128)S(1)}, f32[384,128]{1,0:T(8,128)S(1)}, u32[]{:S(2)}, u32[]{:S(2)}) collective-permute-start(f32[384,128]{1,0:T(8,128)S(1)} %owned.1.refs_2_), channel_id=1, source_target_pairs={{0,1},{1,0},{2,3},{3,2},{4,5},{5,4},{6,7},{7,6},{8,9},{9,8},{10,11... | collective-permute-start | bytes 589832 | tf_op jit(solution)/shard_map/owned/ppermute | solution.py:84
  35.3 7.7 %collective-permute-start.14 = (f32[96,512]{1,0:T(8,128)S(1)}, f32[96,512]{1,0:T(8,128)S(1)}, u32[]{:S(2)}, u32[]{:S(2)}) collective-permute-start(f32[96,512]{1,0:T(8,128)S(1)} %get-tuple-element.78), channel_id=1, source_target_pairs={{0,1},{1,0},{2,3},{3,2},{4,5},{5,4},{6,7},{7,6},{8,9},{9,8},{10,11... | collective-permute-start | bytes 589832 | tf_op jit(solution)/shard_map/sum_shares/ppermute | solution.py:84
  40.8 2.2 %collective-permute-start.13 = (f32[384,256]{1,0:T(8,128)S(1)}, f32[384,256]{1,0:T(8,128)S(1)}, u32[]{:S(2)}, u32[]{:S(2)}) collective-permute-start(f32[384,256]{1,0:T(8,128)S(1)} %get-tuple-element.76), channel_id=1, source_target_pairs={{0,4},{4,0},{8,12},{12,8},{16,20},{20,16},{24,28},{28,24},{1,5},{5... | collective-permute-start | bytes 1179656 | tf_op jit(solution)/shard_map/sum_core/ppermute | solution.py:76
  40.9 23.8 %collective-permute-start.22 = (f32[96,512]{1,0:T(8,128)S(1)}, f32[96,512]{1,0:T(8,128)S(1)}, u32[]{:S(2)}, u32[]{:S(2)}) collective-permute-start(f32[96,512]{1,0:T(8,128)S(1)} %get-tuple-element.88), channel_id=1, source_target_pairs={{0,1},{1,0},{2,3},{3,2},{4,5},{5,4},{6,7},{7,6},{8,9},{9,8},{10,11... | collective-permute-start | bytes 589832 | tf_op jit(solution)/shard_map/sum_shares/ppermute | solution.py:84
  42.9 22.7 %copy-start.5 = (s32[3]{0:T(128)S(1)}, s32[3]{0:T(128)}, u32[]{:S(2)}) copy-start(s32[3]{0:T(128)} %blocks.3) | copy-start | bytes 40
  42.9 22.7 %copy-start.6 = (s32[3]{0:T(128)S(1)}, s32[3]{0:T(128)}, u32[]{:S(2)}) copy-start(s32[3]{0:T(128)} %psize.1) | copy-start | bytes 40
  42.9 22.7 %copy-start.7 = (s32[3]{0:T(128)S(1)}, s32[3]{0:T(128)}, u32[]{:S(2)}) copy-start(s32[3]{0:T(128)} %csize.1) | copy-start | bytes 40
  43.0 25.6 %copy-start.3 = (f32[64,256]{1,0:T(8,128)S(1)}, f32[64,256]{1,0:T(8,128)}, u32[]{:S(2)}) copy-start(f32[64,256]{1,0:T(8,128)} %cd.1) | copy-start | bytes 196612
  43.1 22.6 %collective-permute-start.23 = (f32[96,512]{1,0:T(8,128)S(1)}, f32[96,512]{1,0:T(8,128)S(1)}, u32[]{:S(2)}, u32[]{:S(2)}) collective-permute-start(f32[96,512]{1,0:T(8,128)S(1)} %get-tuple-element.89), channel_id=1, source_target_pairs={{0,2},{1,3},{2,0},{3,1},{4,6},{5,7},{6,4},{7,5},{8,10},{9,11},{10,... | collective-permute-start | bytes 589832 | tf_op jit(solution)/shard_map/sum_shares/ppermute | solution.py:84
  46.3 4.7 %collective-permute-start.15 = (f32[96,256]{1,0:T(8,128)S(1)}, f32[96,256]{1,0:T(8,128)S(1)}, u32[]{:S(2)}, u32[]{:S(2)}) collective-permute-start(f32[96,256]{1,0:T(8,128)S(1)} %get-tuple-element.80), channel_id=1, source_target_pairs={{0,8},{4,12},{8,0},{12,4},{16,24},{20,28},{24,16},{28,20},{1,9},{5... | collective-permute-start | bytes 294920 | tf_op jit(solution)/shard_map/sum_chips/ppermute | solution.py:76
  47.8 5.7 %collective-permute-start.16 = (f32[96,256]{1,0:T(8,128)S(1)}, f32[96,256]{1,0:T(8,128)S(1)}, u32[]{:S(2)}, u32[]{:S(2)}) collective-permute-start(f32[96,256]{1,0:T(8,128)S(1)} %get-tuple-element.81), channel_id=1, source_target_pairs={{0,16},{4,20},{8,24},{12,28},{16,0},{20,4},{24,8},{28,12},{1,17},{... | collective-permute-start | bytes 294920 | tf_op jit(solution)/shard_map/sum_chips/ppermute | solution.py:76
  49.3 5.5 %collective-permute-start.17 = (f32[96,256]{1,0:T(8,128)S(1)}, f32[96,256]{1,0:T(8,128)S(1)}, u32[]{:S(2)}, u32[]{:S(2)}) collective-permute-start(f32[96,256]{1,0:T(8,128)S(1)} %get-tuple-element.82), channel_id=1, source_target_pairs={{0,24},{4,28},{8,16},{12,20},{16,8},{20,12},{24,0},{28,4},{1,25},{... | collective-permute-start | bytes 294920 | tf_op jit(solution)/shard_map/sum_chips/ppermute | solution.py:76
  54.8 5.7 %collective-permute-start.18 = (f32[24,256]{1,0:T(8,128)S(1)}, f32[24,256]{1,0:T(8,128)S(1)}, u32[]{:S(2)}, u32[]{:S(2)}) collective-permute-start(f32[24,256]{1,0:T(8,128)S(1)} %get-tuple-element.84), channel_id=1, source_target_pairs={{0,1},{1,2},{2,3},{3,0},{4,5},{5,6},{6,7},{7,4},{8,9},{9,10},{10,1... | collective-permute-start | bytes 73736 | tf_op jit(solution)/shard_map/sum_cols/ppermute | solution.py:80
  55.2 5.3 %collective-permute-start.19 = (f32[24,256]{1,0:T(8,128)S(1)}, f32[24,256]{1,0:T(8,128)S(1)}, u32[]{:S(2)}, u32[]{:S(2)}) collective-permute-start(f32[24,256]{1,0:T(8,128)S(1)} %get-tuple-element.85), channel_id=1, source_target_pairs={{0,2},{1,3},{2,0},{3,1},{4,6},{5,7},{6,4},{7,5},{8,10},{9,11},{10,... | collective-permute-start | bytes 73736 | tf_op jit(solution)/shard_map/sum_cols/ppermute | solution.py:80
  55.3 5.8 %collective-permute-start.20 = (f32[24,256]{1,0:T(8,128)S(1)}, f32[24,256]{1,0:T(8,128)S(1)}, u32[]{:S(2)}, u32[]{:S(2)}) collective-permute-start(f32[24,256]{1,0:T(8,128)S(1)} %get-tuple-element.86), channel_id=1, source_target_pairs={{0,3},{1,0},{2,1},{3,2},{4,7},{5,4},{6,5},{7,6},{8,11},{9,8},{10,9... | collective-permute-start | bytes 73736 | tf_op jit(solution)/shard_map/sum_cols/ppermute | solution.py:80
  61.1 3.9 %collective-permute-start.25 = (f32[24,256]{1,0:T(8,128)S(1)}, f32[24,256]{1,0:T(8,128)S(1)}, u32[]{:S(2)}, u32[]{:S(2)}) collective-permute-start(f32[24,256]{1,0:T(8,128)S(1)} %spread.2.refs_0_), channel_id=1, source_target_pairs={{0,8},{4,12},{8,0},{12,4},{16,24},{20,28},{24,16},{28,20},{1,9},{5... | collective-permute-start | bytes 73736 | tf_op jit(solution)/shard_map/spread/ppermute | solution.py:76
  61.8 3.8 %collective-permute-start.27 = (f32[24,256]{1,0:T(8,128)S(1)}, f32[24,256]{1,0:T(8,128)S(1)}, u32[]{:S(2)}, u32[]{:S(2)}) collective-permute-start(f32[24,256]{1,0:T(8,128)S(1)} %spread.2.refs_0_), channel_id=1, source_target_pairs={{0,16},{4,20},{8,24},{12,28},{16,0},{20,4},{24,8},{28,12},{1,17},{... | collective-permute-start | bytes 73736 | tf_op jit(solution)/shard_map/spread/ppermute | solution.py:76
  62.6 4.7 %collective-permute-start.21 = (f32[24,256]{1,0:T(8,128)S(1)}, f32[24,256]{1,0:T(8,128)S(1)}, u32[]{:S(2)}, u32[]{:S(2)}) collective-permute-start(f32[24,256]{1,0:T(8,128)S(1)} %spread.2.refs_0_), channel_id=1, source_target_pairs={{0,24},{4,28},{8,16},{12,20},{16,8},{20,12},{24,0},{28,4},{1,25},{... | collective-permute-start | bytes 73736 | tf_op jit(solution)/shard_map/spread/ppermute | solution.py:76
  64.7 3.0 %collective-permute-start.24 = (f32[24,256]{1,0:T(8,128)S(1)}, f32[24,256]{1,0:T(8,128)S(1)}, u32[]{:S(2)}, u32[]{:S(2)}) collective-permute-start(f32[24,256]{1,0:T(8,128)S(1)} %spread.2.refs_0_), channel_id=1, source_target_pairs={{0,4},{4,0},{8,12},{12,8},{16,20},{20,16},{24,28},{28,24},{1,5},{5... | collective-permute-start | bytes 73736 | tf_op jit(solution)/shard_map/spread/ppermute | solution.py:76
  65.0 2.6 %collective-permute-start.26 = (f32[24,256]{1,0:T(8,128)S(1)}, f32[24,256]{1,0:T(8,128)S(1)}, u32[]{:S(2)}, u32[]{:S(2)}) collective-permute-start(f32[24,256]{1,0:T(8,128)S(1)} %collective-permute-done.25.refs_2_), channel_id=1, source_target_pairs={{0,4},{4,0},{8,12},{12,8},{16,20},{20,16},{24,28},{28,24},{1,5},{5... | collective-permute-start | bytes 73736 | tf_op jit(solution)/shard_map/spread/ppermute | solution.py:76
  65.6 2.0 %collective-permute-start.28 = (f32[24,256]{1,0:T(8,128)S(1)}, f32[24,256]{1,0:T(8,128)S(1)}, u32[]{:S(2)}, u32[]{:S(2)}) collective-permute-start(f32[24,256]{1,0:T(8,128)S(1)} %collective-permute-done.27.refs_4_), channel_id=1, source_target_pairs={{0,4},{4,0},{8,12},{12,8},{16,20},{20,16},{24,28},{28,24},{1,5},{5... | collective-permute-start | bytes 73736 | tf_op jit(solution)/shard_map/spread/ppermute | solution.py:76
  67.3 1.2 %collective-permute-start.29 = (f32[24,256]{1,0:T(8,128)S(1)}, f32[24,256]{1,0:T(8,128)S(1)}, u32[]{:S(2)}, u32[]{:S(2)}) collective-permute-start(f32[24,256]{1,0:T(8,128)S(1)} %get-tuple-element.94.refs_6_), channel_id=1, source_target_pairs={{0,4},{4,0},{8,12},{12,8},{16,20},{20,16},{24,28},{28,24},{1,5},{5... | collective-permute-start | bytes 73736 | tf_op jit(solution)/shard_map/spread/ppermute | solution.py:76

commit v8 on v7

--- a/solution.py
+++ b/solution.py
@@ -303,7 +303,7 @@
 
 
 def add_all(s, *refs):
-    terms, out = refs[:-1], refs[-1]
+    terms, out = refs[: s.C], refs[s.C + 2]
     value = terms[0][...]
     for term in terms[1:]:
         value = value + term[...]
@@ -488,7 +488,7 @@
             [(C * 3 * s.eight, W)] * s.chips,
             passed=(shares[2],),
         )
-        mine = [mine[0]] + [exchange(mine[m], 2 * m, R) for m in range(1, s.chips)]
+        mine = [mine[0]] + [exchange(mine[m], 2 * m, R) for m in range(s.chips - 1, 0, -1)]
 
     with jax.named_scope("sum_shares"):
         mask = 1
@@ -499,11 +499,6 @@
         scr = [pltpu.VMEM((C * 3 * s.eight, W), f32)]
         cols = call(bind(add_cols), vmem(*mine), [(3 * s.eight, W)] * C, scr)
         cols = [cols[0]] + [shift(cols[k], k, C) for k in range(1, C)]
-    with jax.named_scope("spread"):
-        (done,) = call(bind(add_all), vmem(*cols), [(3 * s.eight, W)])
-        parts = {0: done}
-        for mask in range(2, R, 2):
-            parts[mask] = exchange(done, mask, R)
     with jax.named_scope("rows_out"):
         parent_rows, child_rows = call(
             bind(rows_out),
@@ -511,9 +506,13 @@
             [(s.RC * s.share, W)] * 2,
         )
     with jax.named_scope("spread"):
-        parts[R - 2], parent_rows, child_rows = call(
-            bind(order), (), (), passed=(parts[R - 2], parent_rows, child_rows)
-        )
+        done, parent_rows, child_rows = call(
+            bind(add_all), vmem(*cols), [(3 * s.eight, W)], passed=(parent_rows, child_rows)
+        )
+        parts = {0: done}
+        for mask in range(R - 2, 0, -2):
+            parts[mask] = exchange(done, mask, R)
+    with jax.named_scope("spread"):
         for mask in range(0, R, 2):
             parts[mask + 1] = exchange(parts[mask], 1, R)
     with jax.named_scope("finish"):

time: 69.4 us -> 69.2 us (level)
    ppermute x19, waiting for transfers between devices: 9.44 us -> 11 us  [exchange(): return lax.ppermute(value, 'row', [(i, i ^ mask) for i in range(row_total)])]
    ppermute x3, waiting for transfers between devices: 2.36 us -> 0.83 us  [shift(): lax.ppermute(value, 'col', [(i, (i + step) % col_total) for i in range(co...]
    pallas_call x17 -> x16, Pallas kernels: 9.77 us -> 9.74 us  [call(): pl.pallas_call(kernel, out_shape=shapes, in_specs=[pl.BlockSpec(memory_sp...]
where the time goes in v8:
time: 69.2 us; the launch traced here: 69 us
  starting transfers between devices  34.9 us (50%)
  waiting for transfers between devices  20.3 us (29%)
  Pallas kernels  9.74 us (14%)
  local copies, waits for them, and re-layouts  3.17 us (5%)
  between operations  0.8 us (1%)
    ppermute x19, starting transfers between devices, exchange(): return lax.ppermute(value, 'row', [(i, i ^ mask) for i in range(row_total)])  17.6 us
    ppermute x19, waiting for transfers between devices, exchange(): return lax.ppermute(value, 'row', [(i, i ^ mask) for i in range(row_total)])  11 us
    ppermute x6, starting transfers between devices, flip(): return lax.ppermute(value, 'col', [(i, i ^ mask) for i in range(col_total)])  9.88 us
    pallas_call x16, Pallas kernels, call(): pl.pallas_call(kernel, out_shape=shapes, in_specs=[pl.BlockSpec(memory_sp...  9.74 us
    ppermute x6, waiting for transfers between devices, flip(): return lax.ppermute(value, 'col', [(i, i ^ mask) for i in range(col_total)])  4.58 us
    ppermute x2, waiting for transfers between devices, fast_body(): lax.ppermute(pieces[turn], ('row', 'col'), column_perm(s, turn))  3.92 us
    ppermute x3, starting transfers between devices, shift(): lax.ppermute(value, 'col', [(i, (i + step) % col_total) for i in range(co...  3.88 us
    ppermute x2, starting transfers between devices, fast_body(): lax.ppermute(pieces[turn], ('row', 'col'), column_perm(s, turn))  3.57 us
  transfers between devices with their start and end apart: 30, of which 16 were waited for; matrix products, arithmetic and copies ran while one was open for 0% of the time, Pallas kernels for 10%

profile of v8, /device:TPU:0, one launch (start us, length us, event | category | flops | bytes accessed | tf_op | source)
XLA Modules:
  0.0 69.0 jit_solution(7207248145931409421)
XLA Ops:
  0.6 1.8 %pack.1 = (f32[232,128]{1,0:T(8,128)}, f32[232,128]{1,0:T(8,128)}, f32[384,128]{1,0:T(8,128)}) custom-call(s32[3]{0:T(128)} %blocks.3, s32[3]{0:T(128)} %psize.1, s32[3]{0:T(128)} %csize.1, f32[3,64,128]{2,1,0:T(8,128)} %bitcast.12, f32[3,64,128]{2,1,0:T(8,128)} %bitcast.13, f32[64,256]{1,0:T(8,128)} %refs_5_.1), custom_call_target="tpu_custom_call" | custom-call | bytes 696356 | tf_op jit(solution)/shard_map/pack/pallas_call | solution.py:42
  2.4 3.0 %collective-permute-start = (f32[232,128]{1,0:T(8,128)}, f32[232,128]{1,0:T(8,128)S(1)}, u32[]{:S(2)}, u32[]{:S(2)}) collective-permute-start(f32[232,128]{1,0:T(8,128)} %get-tuple-element.54), channel_id=1, source_target_pairs={{0,8},{4,12},{8,0},{12,4},{16,24},{20,28},{24,16},{28,20},{1,9},{5... | collective-permute-start | bytes 356360 | tf_op jit(solution)/shard_map/to_column/ppermute | solution.py:76
  5.4 1.6 %collective-permute-start.3 = (f32[384,128]{1,0:T(8,128)}, f32[384,128]{1,0:T(8,128)S(1)}, u32[]{:S(2)}, u32[]{:S(2)}) collective-permute-start(f32[384,128]{1,0:T(8,128)} %get-tuple-element.52.refs_0_), channel_id=1, source_target_pairs={{0,1},{1,0},{2,3},{3,2},{4,5},{5,4},{6,7},{7,6},{8,9},{9,8},{10,11... | collective-permute-start | bytes 589832 | tf_op jit(solution)/shard_map/owned/ppermute | solution.py:84
  7.0 0.9 %copy-done.2 = f32[232,128]{1,0:T(8,128)S(1)} copy-done((f32[232,128]{1,0:T(8,128)S(1)}, f32[232,128]{1,0:T(8,128)}, u32[]{:S(2)}) %copy-start.2) | copy-done | bytes 118808
  8.0 0.8 %collective-permute-done.got = f32[232,128]{1,0:T(8,128)S(1)} collective-permute-done((f32[232,128]{1,0:T(8,128)}, f32[232,128]{1,0:T(8,128)S(1)}, u32[]{:S(2)}, u32[]{:S(2)}) %collective-permute-start) | collective-permute-done | bytes 118816 | tf_op jit(solution)/shard_map/to_column/ppermute | solution.py:76
  8.9 0.3 to_column.3
  9.2 0.7 collective-permute-start.1
  9.8 2.9 %collective-permute-start.2 = (f32[232,128]{1,0:T(8,128)S(1)}, f32[232,128]{1,0:T(8,128)S(1)}, u32[]{:S(2)}, u32[]{:S(2)}) collective-permute-start(f32[232,128]{1,0:T(8,128)S(1)} %get-tuple-element.56), channel_id=1, source_target_pairs={{0,2},{1,6},{2,0},{3,4},{4,3},{5,7},{6,1},{7,5},{8,10},{9,14},{10,... | collective-permute-start | bytes 356360 | tf_op jit(solution)/shard_map/to_column/ppermute | solution.py:410
  12.8 3.9 %collective-permute-done.2.second = f32[232,128]{1,0:T(8,128)S(1)} collective-permute-done((f32[232,128]{1,0:T(8,128)S(1)}, f32[232,128]{1,0:T(8,128)S(1)}, u32[]{:S(2)}, u32[]{:S(2)}) %collective-permute-start.2) | collective-permute-done | bytes 118816 | tf_op jit(solution)/shard_map/to_column/ppermute | solution.py:410
  16.7 1.6 %collective-permute-start.6 = (f32[464,128]{1,0:T(8,128)S(1)}, f32[464,128]{1,0:T(8,128)S(1)}, u32[]{:S(2)}, u32[]{:S(2)}) collective-permute-start(f32[464,128]{1,0:T(8,128)S(1)} %get-tuple-element.58.after.refs_0_), channel_id=1, source_target_pairs={{0,16},{4,20},{8,24},{12,28},{16,0},{20,4},{24,8},{28,12},{1,17},{... | collective-permute-start | bytes 712712 | tf_op jit(solution)/shard_map/panels/ppermute | solution.py:76
  18.3 1.1 %collective-permute-start.11 = (f32[464,128]{1,0:T(8,128)S(1)}, f32[464,128]{1,0:T(8,128)S(1)}, u32[]{:S(2)}, u32[]{:S(2)}) collective-permute-start(f32[464,128]{1,0:T(8,128)S(1)} %get-tuple-element.58.after.refs_0_), channel_id=1, source_target_pairs={{0,24},{4,28},{8,16},{12,20},{16,8},{20,12},{24,0},{28,4},{1,25},{... | collective-permute-start | bytes 712712 | tf_op jit(solution)/shard_map/panels/ppermute | solution.py:76
  19.3 0.9 %collective-permute-start.8 = (f32[464,128]{1,0:T(8,128)S(1)}, f32[464,128]{1,0:T(8,128)S(1)}, u32[]{:S(2)}, u32[]{:S(2)}) collective-permute-start(f32[464,128]{1,0:T(8,128)S(1)} %get-tuple-element.58.after.refs_0_), channel_id=1, source_target_pairs={{0,8},{4,12},{8,0},{12,4},{16,24},{20,28},{24,16},{28,20},{1,9},{5... | collective-permute-start | bytes 712712 | tf_op jit(solution)/shard_map/panels/ppermute | solution.py:76
  20.2 3.1 %collective-permute-start.4 = (f32[384,128]{1,0:T(8,128)}, f32[384,128]{1,0:T(8,128)S(1)}, u32[]{:S(2)}, u32[]{:S(2)}) collective-permute-start(f32[384,128]{1,0:T(8,128)} %get-tuple-element.52.refs_0_), channel_id=1, source_target_pairs={{0,2},{1,3},{2,0},{3,1},{4,6},{5,7},{6,4},{7,5},{8,10},{9,11},{10,... | collective-permute-start | bytes 589832 | tf_op jit(solution)/shard_map/owned/ppermute | solution.py:84
  23.3 0.7 %collective-permute-start.7 = (f32[464,128]{1,0:T(8,128)S(1)}, f32[464,128]{1,0:T(8,128)S(1)}, u32[]{:S(2)}, u32[]{:S(2)}) collective-permute-start(f32[464,128]{1,0:T(8,128)S(1)} %get-tuple-element.58.after.refs_0_), channel_id=1, source_target_pairs={{0,4},{4,0},{8,12},{12,8},{16,20},{20,16},{24,28},{28,24},{1,5},{5... | collective-permute-start | bytes 712712 | tf_op jit(solution)/shard_map/panels/ppermute | solution.py:76
  24.1 1.6 %copy-done = f32[4,1,128,8,1,128]{5,4,3,2,1,0:T(1,128)S(1)} copy-done((f32[4,1,128,8,1,128]{5,4,3,2,1,0:T(1,128)S(1)}, f32[4,1,128,8,1,128]{5,4,3,2,1,0:T(1,128)}, u32[]{:S(2)}) %copy-start) | copy-done | bytes 2097176
  25.7 0.7 copy-done.4
  26.3 1.2 %split_live.1 = (bf16[384,1024]{1,0:T(8,128)(2,1)S(1)}, bf16[384,1024]{1,0:T(8,128)(2,1)S(1)}) custom-call(f32[4096,128]{1,0:T(8,128)S(1)} %bitcast.9, s32[3]{0:T(128)S(1)} %copy-done.4, f32[464,128]{1,0:T(8,128)S(1)} %get-tuple-element.58.after.refs_0_), custom_call_target="tpu_custom_call" | custom-call | bytes 3907596 | tf_op jit(solution)/shard_map/split_live/pallas_call | solution.py:42
  27.5 1.2 %collective-permute-done.6.refs_0_ = f32[464,128]{1,0:T(8,128)S(1)} collective-permute-done((f32[464,128]{1,0:T(8,128)S(1)}, f32[464,128]{1,0:T(8,128)S(1)}, u32[]{:S(2)}, u32[]{:S(2)}) %collective-permute-start.6) | collective-permute-done | bytes 237600 | tf_op jit(solution)/shard_map/panels/ppermute | solution.py:76
  28.7 1.9 %collective-permute-start.10 = (f32[464,128]{1,0:T(8,128)S(1)}, f32[464,128]{1,0:T(8,128)S(1)}, u32[]{:S(2)}, u32[]{:S(2)}) collective-permute-start(f32[464,128]{1,0:T(8,128)S(1)} %get-tuple-element.63.refs_4_), channel_id=1, source_target_pairs={{0,4},{4,0},{8,12},{12,8},{16,20},{20,16},{24,28},{28,24},{1,5},{5... | collective-permute-start | bytes 712712 | tf_op jit(solution)/shard_map/panels/ppermute | solution.py:76
  30.8 1.0 %collective-permute-start.9 = (f32[464,128]{1,0:T(8,128)S(1)}, f32[464,128]{1,0:T(8,128)S(1)}, u32[]{:S(2)}, u32[]{:S(2)}) collective-permute-start(f32[464,128]{1,0:T(8,128)S(1)} %collective-permute-done.8.refs_2_), channel_id=1, source_target_pairs={{0,4},{4,0},{8,12},{12,8},{16,20},{20,16},{24,28},{28,24},{1,5},{5... | collective-permute-start | bytes 712712 | tf_op jit(solution)/shard_map/panels/ppermute | solution.py:76
  31.8 0.7 %collective-permute-start.5 = (f32[384,128]{1,0:T(8,128)S(1)}, f32[384,128]{1,0:T(8,128)S(1)}, u32[]{:S(2)}, u32[]{:S(2)}) collective-permute-start(f32[384,128]{1,0:T(8,128)S(1)} %owned.1.refs_2_), channel_id=1, source_target_pairs={{0,1},{1,0},{2,3},{3,2},{4,5},{5,4},{6,7},{7,6},{8,9},{9,8},{10,11... | collective-permute-start | bytes 589832 | tf_op jit(solution)/shard_map/owned/ppermute | solution.py:84
  32.5 0.4 collective-permute-done.9.refs_3_
  33.0 2.3 %shares_of.1 = (f32[96,512]{1,0:T(8,128)S(1)}, f32[96,512]{1,0:T(8,128)S(1)}, f32[96,512]{1,0:T(8,128)S(1)}, f32[96,512]{1,0:T(8,128)S(1)}, bf16[384,512]{1,0:T(...) custom-call(f32[64,256]{1,0:T(8,128)S(1)} %copy-done.1, ...), custom_call_target="tpu_custom_call" | custom-call | bytes 5963776 | tf_op jit(solution)/shard_map/shares_of/pallas_call | solution.py:42
  35.2 1.1 %collective-permute-start.14 = (f32[96,512]{1,0:T(8,128)S(1)}, f32[96,512]{1,0:T(8,128)S(1)}, u32[]{:S(2)}, u32[]{:S(2)}) collective-permute-start(f32[96,512]{1,0:T(8,128)S(1)} %get-tuple-element.78), channel_id=1, source_target_pairs={{0,1},{1,0},{2,3},{3,2},{4,5},{5,4},{6,7},{7,6},{8,9},{9,8},{10,11... | collective-permute-start | bytes 589832 | tf_op jit(solution)/shard_map/sum_shares/ppermute | solution.py:84
  36.4 2.7 %collective-permute-done.5.refs_3_ = f32[384,128]{1,0:T(8,128)S(1)} collective-permute-done((f32[384,128]{1,0:T(8,128)S(1)}, f32[384,128]{1,0:T(8,128)S(1)}, u32[]{:S(2)}, u32[]{:S(2)}) %collective-permute-start.5) | collective-permute-done | bytes 196640 | tf_op jit(solution)/shard_map/owned/ppermute | solution.py:84
  39.2 1.6 %products.3 = (f32[384,256]{1,0:T(8,128)S(1)}, f32[384,256]{1,0:T(8,128)S(1)}) custom-call(bf16[384,512]{1,0:T(8,128)(2,1)S(1)} %get-tuple-element.66.gh, bf16[384,512]{1,0:T(8,128)(2,1)S(1)} %get-tuple-element.67.gl, bf16[256,256]{1,0:T(8,128)(2,1)S(1)} %get-tuple-element.68.th, bf16[256,256]{1,0:T(8,128)(2,1)S(1)} %get-tuple-element.69.tl, ...), custom_call_target="tpu_custom_call" | custom-call | bytes 3145728 | tf_op jit(solution)/shard_map/products/pallas_call | solution.py:42
  40.9 0.2 collective-permute-start.21
  41.1 1.8 %collective-permute-done.14.refs_1_ = f32[96,512]{1,0:T(8,128)S(1)} collective-permute-done((f32[96,512]{1,0:T(8,128)S(1)}, f32[96,512]{1,0:T(8,128)S(1)}, u32[]{:S(2)}, u32[]{:S(2)}) %collective-permute-start.14) | collective-permute-done | bytes 196640 | tf_op jit(solution)/shard_map/sum_shares/ppermute | solution.py:84
  43.1 3.2 %collective-permute-start.22 = (f32[96,512]{1,0:T(8,128)S(1)}, f32[96,512]{1,0:T(8,128)S(1)}, u32[]{:S(2)}, u32[]{:S(2)}) collective-permute-start(f32[96,512]{1,0:T(8,128)S(1)} %get-tuple-element.89), channel_id=1, source_target_pairs={{0,2},{1,3},{2,0},{3,1},{4,6},{5,7},{6,4},{7,5},{8,10},{9,11},{10,... | collective-permute-start | bytes 589832 | tf_op jit(solution)/shard_map/sum_shares/ppermute | solution.py:84
  46.3 2.4 %collective-permute-start.15 = (f32[96,256]{1,0:T(8,128)S(1)}, f32[96,256]{1,0:T(8,128)S(1)}, u32[]{:S(2)}, u32[]{:S(2)}) collective-permute-start(f32[96,256]{1,0:T(8,128)S(1)} %get-tuple-element.80), channel_id=1, source_target_pairs={{0,24},{4,28},{8,16},{12,20},{16,8},{20,12},{24,0},{28,4},{1,25},{... | collective-permute-start | bytes 294920 | tf_op jit(solution)/shard_map/sum_chips/ppermute | solution.py:76
  48.7 0.5 collective-permute-start.16
  49.2 0.5 collective-permute-start.17
  49.8 2.2 %collective-permute-done.15.refs_1_ = f32[96,256]{1,0:T(8,128)S(1)} collective-permute-done((f32[96,256]{1,0:T(8,128)S(1)}, f32[96,256]{1,0:T(8,128)S(1)}, u32[]{:S(2)}, u32[]{:S(2)}) %collective-permute-start.15) | collective-permute-done | bytes 98336 | tf_op jit(solution)/shard_map/sum_chips/ppermute | solution.py:76
  51.9 1.8 %collective-permute-done.16.refs_2_ = f32[96,256]{1,0:T(8,128)S(1)} collective-permute-done((f32[96,256]{1,0:T(8,128)S(1)}, f32[96,256]{1,0:T(8,128)S(1)}, u32[]{:S(2)}, u32[]{:S(2)}) %collective-permute-start.16) | collective-permute-done | bytes 98336 | tf_op jit(solution)/shard_map/sum_chips/ppermute | solution.py:76
  53.7 0.2 collective-permute-done.17.refs_3_
  53.9 0.4 collective-permute-start.18
  54.5 3.4 %collective-permute-start.20 = (f32[24,256]{1,0:T(8,128)S(1)}, f32[24,256]{1,0:T(8,128)S(1)}, u32[]{:S(2)}, u32[]{:S(2)}) collective-permute-start(f32[24,256]{1,0:T(8,128)S(1)} %get-tuple-element.86), channel_id=1, source_target_pairs={{0,3},{1,0},{2,1},{3,2},{4,7},{5,4},{6,5},{7,6},{8,11},{9,8},{10,9... | collective-permute-start | bytes 73736 | tf_op jit(solution)/shard_map/sum_cols/ppermute | solution.py:80
  57.9 1.5 %rows_out.1 = (f32[128,256]{1,0:T(8,128)}, f32[128,256]{1,0:T(8,128)}) custom-call(s32[3]{0:T(128)S(1)} %copy-done.5, s32[3]{0:T(128)S(1)} %copy-done.6, s32[3]{0:T(128)S(1)} %copy-done.7, bf16[256,256]{1,0:T(8,128)(2,1)S(1)} %get-tuple-element.68.th, bf16[256,256]{1,0:T(8,128)(2,1)S(1)} %get-tuple-element.69.tl, f32[96,512]{1,0:T(8,128)S(1)} %get-tuple-element.87.refs_0_, ...), custom_call_target="tpu_custom_call" | custom-call | bytes 1114148 | tf_op jit(solution)/shard_map/rows_out/pallas_call | solution.py:42
  59.4 0.3 collective-permute-done.18.refs_1_
  59.6 0.6 collective-permute-done.20.refs_3_
  60.2 1.2 %collective-permute-start.24 = (f32[24,256]{1,0:T(8,128)S(1)}, f32[24,256]{1,0:T(8,128)S(1)}, u32[]{:S(2)}, u32[]{:S(2)}) collective-permute-start(f32[24,256]{1,0:T(8,128)S(1)} %get-tuple-element.94.refs_0_), channel_id=1, source_target_pairs={{0,8},{4,12},{8,0},{12,4},{16,24},{20,28},{24,16},{28,20},{1,9},{5... | collective-permute-start | bytes 73736 | tf_op jit(solution)/shard_map/spread/ppermute | solution.py:76
  61.4 0.9 %collective-permute-start.26 = (f32[24,256]{1,0:T(8,128)S(1)}, f32[24,256]{1,0:T(8,128)S(1)}, u32[]{:S(2)}, u32[]{:S(2)}) collective-permute-start(f32[24,256]{1,0:T(8,128)S(1)} %get-tuple-element.94.refs_0_), channel_id=1, source_target_pairs={{0,16},{4,20},{8,24},{12,28},{16,0},{20,4},{24,8},{28,12},{1,17},{... | collective-permute-start | bytes 73736 | tf_op jit(solution)/shard_map/spread/ppermute | solution.py:76
  62.3 1.4 %collective-permute-start.28 = (f32[24,256]{1,0:T(8,128)S(1)}, f32[24,256]{1,0:T(8,128)S(1)}, u32[]{:S(2)}, u32[]{:S(2)}) collective-permute-start(f32[24,256]{1,0:T(8,128)S(1)} %get-tuple-element.94.refs_0_), channel_id=1, source_target_pairs={{0,24},{4,28},{8,16},{12,20},{16,8},{20,12},{24,0},{28,4},{1,25},{... | collective-permute-start | bytes 73736 | tf_op jit(solution)/shard_map/spread/ppermute | solution.py:76
  63.8 0.3 collective-permute-done.24.refs_2_
  64.3 1.0 %collective-permute-done.26.refs_4_ = f32[24,256]{1,0:T(8,128)S(1)} collective-permute-done((f32[24,256]{1,0:T(8,128)S(1)}, f32[24,256]{1,0:T(8,128)S(1)}, u32[]{:S(2)}, u32[]{:S(2)}) %collective-permute-start.26) | collective-permute-done | bytes 24608 | tf_op jit(solution)/shard_map/spread/ppermute | solution.py:76
  65.3 1.8 %collective-permute-done.28.refs_6_ = f32[24,256]{1,0:T(8,128)S(1)} collective-permute-done((f32[24,256]{1,0:T(8,128)S(1)}, f32[24,256]{1,0:T(8,128)S(1)}, u32[]{:S(2)}, u32[]{:S(2)}) %collective-permute-start.28) | collective-permute-done | bytes 24608 | tf_op jit(solution)/shard_map/spread/ppermute | solution.py:76
  67.1 1.2 %collective-permute-done.29.refs_7_ = f32[24,256]{1,0:T(8,128)S(1)} collective-permute-done((f32[24,256]{1,0:T(8,128)S(1)}, f32[24,256]{1,0:T(8,128)S(1)}, u32[]{:S(2)}, u32[]{:S(2)}) %collective-permute-start.29) | collective-permute-done | bytes 24608 | tf_op jit(solution)/shard_map/spread/ppermute | solution.py:76
  68.2 0.7 %finish.1 = (f32[64,256]{1,0:T(8,128)}, f32[64,256]{1,0:T(8,128)}, f32[64,256]{1,0:T(8,128)}) custom-call(f32[64,256]{1,0:T(8,128)S(1)} %copy-done.1, f32[64,256]{1,0:T(8,128)S(1)} %copy-done.3, f32[64,256]{1,0:T(8,128)S(1)} %get-tuple-element.93.base, f32[24,256]{1,0:T(8,128)S(1)} %get-tuple-element.94.refs_0_, ...), custom_call_target="tpu_custom_call" | custom-call | bytes 589824 | tf_op jit(solution)/shard_map/finish/pallas_call | solution.py:42
  (46 shorter events, 1.0 us)
Async XLA Ops:
  2.4 6.4 %collective-permute-start = (f32[232,128]{1,0:T(8,128)}, f32[232,128]{1,0:T(8,128)S(1)}, u32[]{:S(2)}, u32[]{:S(2)}) collective-permute-start(f32[232,128]{1,0:T(8,128)} %get-tuple-element.54), channel_id=1, source_target_pairs={{0,8},{4,12},{8,0},{12,4},{16,24},{20,28},{24,16},{28,20},{1,9},{5... | collective-permute-start | bytes 356360 | tf_op jit(solution)/shard_map/to_column/ppermute | solution.py:76
  5.4 7.3 %collective-permute-start.3 = (f32[384,128]{1,0:T(8,128)}, f32[384,128]{1,0:T(8,128)S(1)}, u32[]{:S(2)}, u32[]{:S(2)}) collective-permute-start(f32[384,128]{1,0:T(8,128)} %get-tuple-element.52.refs_0_), channel_id=1, source_target_pairs={{0,1},{1,0},{2,3},{3,2},{4,5},{5,4},{6,7},{7,6},{8,9},{9,8},{10,11... | collective-permute-start | bytes 589832 | tf_op jit(solution)/shard_map/owned/ppermute | solution.py:84
  7.0 0.9 %copy-start.2 = (f32[232,128]{1,0:T(8,128)S(1)}, f32[232,128]{1,0:T(8,128)}, u32[]{:S(2)}) copy-start(f32[232,128]{1,0:T(8,128)} %get-tuple-element.53.source) | copy-start | bytes 356356
  9.2 3.6 %collective-permute-start.1 = (f32[232,128]{1,0:T(8,128)S(1)}, f32[232,128]{1,0:T(8,128)S(1)}, u32[]{:S(2)}, u32[]{:S(2)}) collective-permute-start(f32[232,128]{1,0:T(8,128)S(1)} %get-tuple-element.55), channel_id=1, source_target_pairs={{0,0},{1,4},{2,2},{3,6},{4,1},{5,5},{6,3},{7,7},{8,8},{9,12},{10,1... | collective-permute-start | bytes 356360 | tf_op jit(solution)/shard_map/to_column/ppermute | solution.py:410
  9.8 6.8 %collective-permute-start.2 = (f32[232,128]{1,0:T(8,128)S(1)}, f32[232,128]{1,0:T(8,128)S(1)}, u32[]{:S(2)}, u32[]{:S(2)}) collective-permute-start(f32[232,128]{1,0:T(8,128)S(1)} %get-tuple-element.56), channel_id=1, source_target_pairs={{0,2},{1,6},{2,0},{3,4},{4,3},{5,7},{6,1},{7,5},{8,10},{9,14},{10,... | collective-permute-start | bytes 356360 | tf_op jit(solution)/shard_map/to_column/ppermute | solution.py:410
  16.7 12.0 %collective-permute-start.6 = (f32[464,128]{1,0:T(8,128)S(1)}, f32[464,128]{1,0:T(8,128)S(1)}, u32[]{:S(2)}, u32[]{:S(2)}) collective-permute-start(f32[464,128]{1,0:T(8,128)S(1)} %get-tuple-element.58.after.refs_0_), channel_id=1, source_target_pairs={{0,16},{4,20},{8,24},{12,28},{16,0},{20,4},{24,8},{28,12},{1,17},{... | collective-permute-start | bytes 712712 | tf_op jit(solution)/shard_map/panels/ppermute | solution.py:76
  18.3 12.3 %collective-permute-start.11 = (f32[464,128]{1,0:T(8,128)S(1)}, f32[464,128]{1,0:T(8,128)S(1)}, u32[]{:S(2)}, u32[]{:S(2)}) collective-permute-start(f32[464,128]{1,0:T(8,128)S(1)} %get-tuple-element.58.after.refs_0_), channel_id=1, source_target_pairs={{0,24},{4,28},{8,16},{12,20},{16,8},{20,12},{24,0},{28,4},{1,25},{... | collective-permute-start | bytes 712712 | tf_op jit(solution)/shard_map/panels/ppermute | solution.py:76
  19.3 11.4 %collective-permute-start.8 = (f32[464,128]{1,0:T(8,128)S(1)}, f32[464,128]{1,0:T(8,128)S(1)}, u32[]{:S(2)}, u32[]{:S(2)}) collective-permute-start(f32[464,128]{1,0:T(8,128)S(1)} %get-tuple-element.58.after.refs_0_), channel_id=1, source_target_pairs={{0,8},{4,12},{8,0},{12,4},{16,24},{20,28},{24,16},{28,20},{1,9},{5... | collective-permute-start | bytes 712712 | tf_op jit(solution)/shard_map/panels/ppermute | solution.py:76
  20.2 11.6 %collective-permute-start.4 = (f32[384,128]{1,0:T(8,128)}, f32[384,128]{1,0:T(8,128)S(1)}, u32[]{:S(2)}, u32[]{:S(2)}) collective-permute-start(f32[384,128]{1,0:T(8,128)} %get-tuple-element.52.refs_0_), channel_id=1, source_target_pairs={{0,2},{1,3},{2,0},{3,1},{4,6},{5,7},{6,4},{7,5},{8,10},{9,11},{10,... | collective-permute-start | bytes 589832 | tf_op jit(solution)/shard_map/owned/ppermute | solution.py:84
  23.3 9.2 %collective-permute-start.7 = (f32[464,128]{1,0:T(8,128)S(1)}, f32[464,128]{1,0:T(8,128)S(1)}, u32[]{:S(2)}, u32[]{:S(2)}) collective-permute-start(f32[464,128]{1,0:T(8,128)S(1)} %get-tuple-element.58.after.refs_0_), channel_id=1, source_target_pairs={{0,4},{4,0},{8,12},{12,8},{16,20},{20,16},{24,28},{28,24},{1,5},{5... | collective-permute-start | bytes 712712 | tf_op jit(solution)/shard_map/panels/ppermute | solution.py:76
  24.1 1.6 %copy-start = (f32[4,1,128,8,1,128]{5,4,3,2,1,0:T(1,128)S(1)}, f32[4,1,128,8,1,128]{5,4,3,2,1,0:T(1,128)}, u32[]{:S(2)}) copy-start(f32[4,1,128,8,1,128]{5,4,3,2,1,0:T(1,128)} %param.10) | copy-start | bytes 6291460
  25.7 0.7 copy-start.4
  28.7 4.2 %copy-start.1 = (f32[64,256]{1,0:T(8,128)S(1)}, f32[64,256]{1,0:T(8,128)}, u32[]{:S(2)}) copy-start(f32[64,256]{1,0:T(8,128)} %pd.3) | copy-start | bytes 196612
  28.7 3.8 %collective-permute-start.10 = (f32[464,128]{1,0:T(8,128)S(1)}, f32[464,128]{1,0:T(8,128)S(1)}, u32[]{:S(2)}, u32[]{:S(2)}) collective-permute-start(f32[464,128]{1,0:T(8,128)S(1)} %get-tuple-element.63.refs_4_), channel_id=1, source_target_pairs={{0,4},{4,0},{8,12},{12,8},{16,20},{20,16},{24,28},{28,24},{1,5},{5... | collective-permute-start | bytes 712712 | tf_op jit(solution)/shard_map/panels/ppermute | solution.py:76
  30.6 1.9 %collective-permute-start.12 = (f32[464,128]{1,0:T(8,128)S(1)}, f32[464,128]{1,0:T(8,128)S(1)}, u32[]{:S(2)}, u32[]{:S(2)}) collective-permute-start(f32[464,128]{1,0:T(8,128)S(1)} %collective-permute-done.11.refs_6_), channel_id=1, source_target_pairs={{0,4},{4,0},{8,12},{12,8},{16,20},{20,16},{24,28},{28,24},{1,5},{5... | collective-permute-start | bytes 712712 | tf_op jit(solution)/shard_map/panels/ppermute | solution.py:76
  30.8 2.2 %collective-permute-start.9 = (f32[464,128]{1,0:T(8,128)S(1)}, f32[464,128]{1,0:T(8,128)S(1)}, u32[]{:S(2)}, u32[]{:S(2)}) collective-permute-start(f32[464,128]{1,0:T(8,128)S(1)} %collective-permute-done.8.refs_2_), channel_id=1, source_target_pairs={{0,4},{4,0},{8,12},{12,8},{16,20},{20,16},{24,28},{28,24},{1,5},{5... | collective-permute-start | bytes 712712 | tf_op jit(solution)/shard_map/panels/ppermute | solution.py:76
  31.8 7.3 %copy-start.8 = (f32[384,128]{1,0:T(8,128)S(1)}, f32[384,128]{1,0:T(8,128)}, u32[]{:S(2)}) copy-start(f32[384,128]{1,0:T(8,128)} %get-tuple-element.52.refs_0_) | copy-start | bytes 589828
  31.8 7.2 %collective-permute-start.5 = (f32[384,128]{1,0:T(8,128)S(1)}, f32[384,128]{1,0:T(8,128)S(1)}, u32[]{:S(2)}, u32[]{:S(2)}) collective-permute-start(f32[384,128]{1,0:T(8,128)S(1)} %owned.1.refs_2_), channel_id=1, source_target_pairs={{0,1},{1,0},{2,3},{3,2},{4,5},{5,4},{6,7},{7,6},{8,9},{9,8},{10,11... | collective-permute-start | bytes 589832 | tf_op jit(solution)/shard_map/owned/ppermute | solution.py:84
  35.2 7.7 %collective-permute-start.14 = (f32[96,512]{1,0:T(8,128)S(1)}, f32[96,512]{1,0:T(8,128)S(1)}, u32[]{:S(2)}, u32[]{:S(2)}) collective-permute-start(f32[96,512]{1,0:T(8,128)S(1)} %get-tuple-element.78), channel_id=1, source_target_pairs={{0,1},{1,0},{2,3},{3,2},{4,5},{5,4},{6,7},{7,6},{8,9},{9,8},{10,11... | collective-permute-start | bytes 589832 | tf_op jit(solution)/shard_map/sum_shares/ppermute | solution.py:84
  40.8 2.1 %collective-permute-start.13 = (f32[384,256]{1,0:T(8,128)S(1)}, f32[384,256]{1,0:T(8,128)S(1)}, u32[]{:S(2)}, u32[]{:S(2)}) collective-permute-start(f32[384,256]{1,0:T(8,128)S(1)} %get-tuple-element.76), channel_id=1, source_target_pairs={{0,4},{4,0},{8,12},{12,8},{16,20},{20,16},{24,28},{28,24},{1,5},{5... | collective-permute-start | bytes 1179656 | tf_op jit(solution)/shard_map/sum_core/ppermute | solution.py:76
  40.9 16.9 %collective-permute-start.21 = (f32[96,512]{1,0:T(8,128)S(1)}, f32[96,512]{1,0:T(8,128)S(1)}, u32[]{:S(2)}, u32[]{:S(2)}) collective-permute-start(f32[96,512]{1,0:T(8,128)S(1)} %get-tuple-element.88), channel_id=1, source_target_pairs={{0,1},{1,0},{2,3},{3,2},{4,5},{5,4},{6,7},{7,6},{8,9},{9,8},{10,11... | collective-permute-start | bytes 589832 | tf_op jit(solution)/shard_map/sum_shares/ppermute | solution.py:84
  42.9 14.9 %copy-start.5 = (s32[3]{0:T(128)S(1)}, s32[3]{0:T(128)}, u32[]{:S(2)}) copy-start(s32[3]{0:T(128)} %blocks.3) | copy-start | bytes 40
  42.9 14.9 %copy-start.6 = (s32[3]{0:T(128)S(1)}, s32[3]{0:T(128)}, u32[]{:S(2)}) copy-start(s32[3]{0:T(128)} %psize.1) | copy-start | bytes 40
  42.9 14.9 %copy-start.7 = (s32[3]{0:T(128)S(1)}, s32[3]{0:T(128)}, u32[]{:S(2)}) copy-start(s32[3]{0:T(128)} %csize.1) | copy-start | bytes 40
  43.0 25.3 %copy-start.3 = (f32[64,256]{1,0:T(8,128)S(1)}, f32[64,256]{1,0:T(8,128)}, u32[]{:S(2)}) copy-start(f32[64,256]{1,0:T(8,128)} %cd.1) | copy-start | bytes 196612
  43.1 14.8 %collective-permute-start.22 = (f32[96,512]{1,0:T(8,128)S(1)}, f32[96,512]{1,0:T(8,128)S(1)}, u32[]{:S(2)}, u32[]{:S(2)}) collective-permute-start(f32[96,512]{1,0:T(8,128)S(1)} %get-tuple-element.89), channel_id=1, source_target_pairs={{0,2},{1,3},{2,0},{3,1},{4,6},{5,7},{6,4},{7,5},{8,10},{9,11},{10,... | collective-permute-start | bytes 589832 | tf_op jit(solution)/shard_map/sum_shares/ppermute | solution.py:84
  46.3 5.6 %collective-permute-start.15 = (f32[96,256]{1,0:T(8,128)S(1)}, f32[96,256]{1,0:T(8,128)S(1)}, u32[]{:S(2)}, u32[]{:S(2)}) collective-permute-start(f32[96,256]{1,0:T(8,128)S(1)} %get-tuple-element.80), channel_id=1, source_target_pairs={{0,24},{4,28},{8,16},{12,20},{16,8},{20,12},{24,0},{28,4},{1,25},{... | collective-permute-start | bytes 294920 | tf_op jit(solution)/shard_map/sum_chips/ppermute | solution.py:76
  48.7 5.0 %collective-permute-start.16 = (f32[96,256]{1,0:T(8,128)S(1)}, f32[96,256]{1,0:T(8,128)S(1)}, u32[]{:S(2)}, u32[]{:S(2)}) collective-permute-start(f32[96,256]{1,0:T(8,128)S(1)} %get-tuple-element.81), channel_id=1, source_target_pairs={{0,16},{4,20},{8,24},{12,28},{16,0},{20,4},{24,8},{28,12},{1,17},{... | collective-permute-start | bytes 294920 | tf_op jit(solution)/shard_map/sum_chips/ppermute | solution.py:76
  49.2 4.7 %collective-permute-start.17 = (f32[96,256]{1,0:T(8,128)S(1)}, f32[96,256]{1,0:T(8,128)S(1)}, u32[]{:S(2)}, u32[]{:S(2)}) collective-permute-start(f32[96,256]{1,0:T(8,128)S(1)} %get-tuple-element.82), channel_id=1, source_target_pairs={{0,8},{4,12},{8,0},{12,4},{16,24},{20,28},{24,16},{28,20},{1,9},{5... | collective-permute-start | bytes 294920 | tf_op jit(solution)/shard_map/sum_chips/ppermute | solution.py:76
  53.9 5.7 %collective-permute-start.18 = (f32[24,256]{1,0:T(8,128)S(1)}, f32[24,256]{1,0:T(8,128)S(1)}, u32[]{:S(2)}, u32[]{:S(2)}) collective-permute-start(f32[24,256]{1,0:T(8,128)S(1)} %get-tuple-element.84), channel_id=1, source_target_pairs={{0,1},{1,2},{2,3},{3,0},{4,5},{5,6},{6,7},{7,4},{8,9},{9,10},{10,1... | collective-permute-start | bytes 73736 | tf_op jit(solution)/shard_map/sum_cols/ppermute | solution.py:80
  54.3 5.3 %collective-permute-start.19 = (f32[24,256]{1,0:T(8,128)S(1)}, f32[24,256]{1,0:T(8,128)S(1)}, u32[]{:S(2)}, u32[]{:S(2)}) collective-permute-start(f32[24,256]{1,0:T(8,128)S(1)} %get-tuple-element.85), channel_id=1, source_target_pairs={{0,2},{1,3},{2,0},{3,1},{4,6},{5,7},{6,4},{7,5},{8,10},{9,11},{10,... | collective-permute-start | bytes 73736 | tf_op jit(solution)/shard_map/sum_cols/ppermute | solution.py:80
  54.5 5.7 %collective-permute-start.20 = (f32[24,256]{1,0:T(8,128)S(1)}, f32[24,256]{1,0:T(8,128)S(1)}, u32[]{:S(2)}, u32[]{:S(2)}) collective-permute-start(f32[24,256]{1,0:T(8,128)S(1)} %get-tuple-element.86), channel_id=1, source_target_pairs={{0,3},{1,0},{2,1},{3,2},{4,7},{5,4},{6,5},{7,6},{8,11},{9,8},{10,9... | collective-permute-start | bytes 73736 | tf_op jit(solution)/shard_map/sum_cols/ppermute | solution.py:80
  60.2 3.9 %collective-permute-start.24 = (f32[24,256]{1,0:T(8,128)S(1)}, f32[24,256]{1,0:T(8,128)S(1)}, u32[]{:S(2)}, u32[]{:S(2)}) collective-permute-start(f32[24,256]{1,0:T(8,128)S(1)} %get-tuple-element.94.refs_0_), channel_id=1, source_target_pairs={{0,8},{4,12},{8,0},{12,4},{16,24},{20,28},{24,16},{28,20},{1,9},{5... | collective-permute-start | bytes 73736 | tf_op jit(solution)/shard_map/spread/ppermute | solution.py:76
  61.4 3.8 %collective-permute-start.26 = (f32[24,256]{1,0:T(8,128)S(1)}, f32[24,256]{1,0:T(8,128)S(1)}, u32[]{:S(2)}, u32[]{:S(2)}) collective-permute-start(f32[24,256]{1,0:T(8,128)S(1)} %get-tuple-element.94.refs_0_), channel_id=1, source_target_pairs={{0,16},{4,20},{8,24},{12,28},{16,0},{20,4},{24,8},{28,12},{1,17},{... | collective-permute-start | bytes 73736 | tf_op jit(solution)/shard_map/spread/ppermute | solution.py:76
  62.3 4.7 %collective-permute-start.28 = (f32[24,256]{1,0:T(8,128)S(1)}, f32[24,256]{1,0:T(8,128)S(1)}, u32[]{:S(2)}, u32[]{:S(2)}) collective-permute-start(f32[24,256]{1,0:T(8,128)S(1)} %get-tuple-element.94.refs_0_), channel_id=1, source_target_pairs={{0,24},{4,28},{8,16},{12,20},{16,8},{20,12},{24,0},{28,4},{1,25},{... | collective-permute-start | bytes 73736 | tf_op jit(solution)/shard_map/spread/ppermute | solution.py:76
  63.8 3.3 %collective-permute-start.23 = (f32[24,256]{1,0:T(8,128)S(1)}, f32[24,256]{1,0:T(8,128)S(1)}, u32[]{:S(2)}, u32[]{:S(2)}) collective-permute-start(f32[24,256]{1,0:T(8,128)S(1)} %get-tuple-element.94.refs_0_), channel_id=1, source_target_pairs={{0,4},{4,0},{8,12},{12,8},{16,20},{20,16},{24,28},{28,24},{1,5},{5... | collective-permute-start | bytes 73736 | tf_op jit(solution)/shard_map/spread/ppermute | solution.py:76
  64.1 3.0 %collective-permute-start.25 = (f32[24,256]{1,0:T(8,128)S(1)}, f32[24,256]{1,0:T(8,128)S(1)}, u32[]{:S(2)}, u32[]{:S(2)}) collective-permute-start(f32[24,256]{1,0:T(8,128)S(1)} %collective-permute-done.24.refs_2_), channel_id=1, source_target_pairs={{0,4},{4,0},{8,12},{12,8},{16,20},{20,16},{24,28},{28,24},{1,5},{5... | collective-permute-start | bytes 73736 | tf_op jit(solution)/shard_map/spread/ppermute | solution.py:76
  65.3 1.8 %collective-permute-start.27 = (f32[24,256]{1,0:T(8,128)S(1)}, f32[24,256]{1,0:T(8,128)S(1)}, u32[]{:S(2)}, u32[]{:S(2)}) collective-permute-start(f32[24,256]{1,0:T(8,128)S(1)} %collective-permute-done.26.refs_4_), channel_id=1, source_target_pairs={{0,4},{4,0},{8,12},{12,8},{16,20},{20,16},{24,28},{28,24},{1,5},{5... | collective-permute-start | bytes 73736 | tf_op jit(solution)/shard_map/spread/ppermute | solution.py:76
  67.0 1.2 %collective-permute-start.29 = (f32[24,256]{1,0:T(8,128)S(1)}, f32[24,256]{1,0:T(8,128)S(1)}, u32[]{:S(2)}, u32[]{:S(2)}) collective-permute-start(f32[24,256]{1,0:T(8,128)S(1)} %collective-permute-done.28.refs_6_), channel_id=1, source_target_pairs={{0,4},{4,0},{8,12},{12,8},{16,20},{20,16},{24,28},{28,24},{1,5},{5... | collective-permute-start | bytes 73736 | tf_op jit(solution)/shard_map/spread/ppermute | solution.py:76

commit v9 on v8

--- a/solution.py
+++ b/solution.py
@@ -182,10 +182,10 @@
             low[rows, m * s.B : (m + 1) * s.B] = l
 
 
-def shares_of(s, pd, sh, sl, *refs):
+def shares_of(s, sh, sl, *refs):
     panels, refs = refs[: s.R], refs[s.R :]
     shares, refs = refs[: s.C], refs[s.C :]
-    gh, gl, th, tl, ih, il, base, extra, xh, xl, total, top = refs
+    gh, gl, top, xh, xl, total = refs
     row, col = lax.axis_index("row"), lax.axis_index("col")
     places = []
     for owner in range(s.Q):
@@ -231,6 +231,10 @@
             start = pl.multiple_of(slot * s.B + target * s.share, s.share)
             rows = slice(slot * s.share, (slot + 1) * s.share)
             shares[mask][rows, :] = total[pl.ds(start, s.share), :]
+
+
+def tops(s, pd, top, th, tl, ih, il, base, extra):
+    col = lax.axis_index("col")
     th[...], tl[...] = split(top[...])
     ih[...], il[...] = split(top[...].T)
     lead = dot3(split(pd[...]), (th[...], tl[...]), NN)
@@ -438,16 +442,20 @@
             panels[mask + 1] = exchange(panels[mask], 1, R)
     with jax.named_scope("shares_of"):
         pair = lambda rows, cols: [((rows, cols), bf16)] * 2
-        *shares, gh, gl, th, tl, ih, il, base, extra = call(
+        *shares, gh, gl, top = call(
             bind(shares_of),
-            vmem(parent_diagonal, sh, sl, *[panels[m] for m in range(R)]),
+            vmem(sh, sl, *[panels[m] for m in range(R)]),
             [(s.slots * s.share, 2 * W)] * C
             + pair(live, 2 * W)
-            + pair(W, W)
-            + pair(W, W)
-            + [(ws, W), (W, W)],
+            + [(W, W)],
             [pltpu.VMEM((s.CC + 1, 2 * W, B), bf16)] * 2
-            + [pltpu.VMEM((live, 2 * W), f32), pltpu.VMEM((W, W), f32)],
+            + [pltpu.VMEM((live, 2 * W), f32)],
+        )
+    with jax.named_scope("tops"):
+        th, tl, ih, il, base, extra = call(
+            bind(tops),
+            vmem(parent_diagonal, top),
+            pair(W, W) + pair(W, W) + [(ws, W), (W, W)],
         )
     with jax.named_scope("products"):
         lh, ll, gh, gl = call(

time: 69.2 us -> 69.4 us (level)
    pallas_call x16 -> x17, Pallas kernels: 9.74 us -> 9.92 us  [call(): pl.pallas_call(kernel, out_shape=shapes, in_specs=[pl.BlockSpec(memory_sp...]
  transfers between devices with their start and end apart: 30 -> 30, of which waited for: 16 -> 16; matrix products, arithmetic and copies ran while one was open for 0% -> 0% of each run, Pallas kernels for 10% -> 11%
where the time goes in v9:
time: 69.4 us; the launch traced here: 69.2 us
  starting transfers between devices  35 us (50%)
  waiting for transfers between devices  20.2 us (29%)
  Pallas kernels  9.92 us (14%)
  local copies, waits for them, and re-layouts  3.17 us (5%)
  between operations  0.81 us (1%)
    ppermute x19, starting transfers between devices, exchange(): return lax.ppermute(value, 'row', [(i, i ^ mask) for i in range(row_total)])  17.6 us
    ppermute x19, waiting for transfers between devices, exchange(): return lax.ppermute(value, 'row', [(i, i ^ mask) for i in range(row_total)])  11.1 us
    ppermute x6, starting transfers between devices, flip(): return lax.ppermute(value, 'col', [(i, i ^ mask) for i in range(col_total)])  9.99 us
    pallas_call x17, Pallas kernels, call(): pl.pallas_call(kernel, out_shape=shapes, in_specs=[pl.BlockSpec(memory_sp...  9.92 us
    ppermute x6, waiting for transfers between devices, flip(): return lax.ppermute(value, 'col', [(i, i ^ mask) for i in range(col_total)])  4.35 us
    ppermute x2, waiting for transfers between devices, fast_body(): lax.ppermute(pieces[turn], ('row', 'col'), column_perm(s, turn))  3.92 us
    ppermute x3, starting transfers between devices, shift(): lax.ppermute(value, 'col', [(i, (i + step) % col_total) for i in range(co...  3.88 us
    ppermute x2, starting transfers between devices, fast_body(): lax.ppermute(pieces[turn], ('row', 'col'), column_perm(s, turn))  3.57 us
  transfers between devices with their start and end apart: 30, of which 16 were waited for; matrix products, arithmetic and copies ran while one was open for 0% of the time, Pallas kernels for 11%

profile of v9, /device:TPU:0, one launch (start us, length us, event | category | flops | bytes accessed | tf_op | source)
XLA Modules:
  0.0 69.2 jit_solution(8078292592551398739)
XLA Ops:
  0.6 1.8 %pack.1 = (f32[232,128]{1,0:T(8,128)}, f32[232,128]{1,0:T(8,128)}, f32[384,128]{1,0:T(8,128)}) custom-call(s32[3]{0:T(128)} %blocks.3, s32[3]{0:T(128)} %psize.1, s32[3]{0:T(128)} %csize.1, f32[3,64,128]{2,1,0:T(8,128)} %bitcast.12, f32[3,64,128]{2,1,0:T(8,128)} %bitcast.13, f32[64,256]{1,0:T(8,128)} %refs_5_.1), custom_call_target="tpu_custom_call" | custom-call | bytes 696356 | tf_op jit(solution)/shard_map/pack/pallas_call | solution.py:42
  2.4 3.0 %collective-permute-start = (f32[232,128]{1,0:T(8,128)}, f32[232,128]{1,0:T(8,128)S(1)}, u32[]{:S(2)}, u32[]{:S(2)}) collective-permute-start(f32[232,128]{1,0:T(8,128)} %get-tuple-element.55), channel_id=1, source_target_pairs={{0,8},{4,12},{8,0},{12,4},{16,24},{20,28},{24,16},{28,20},{1,9},{5... | collective-permute-start | bytes 356360 | tf_op jit(solution)/shard_map/to_column/ppermute | solution.py:76
  5.4 1.6 %collective-permute-start.3 = (f32[384,128]{1,0:T(8,128)}, f32[384,128]{1,0:T(8,128)S(1)}, u32[]{:S(2)}, u32[]{:S(2)}) collective-permute-start(f32[384,128]{1,0:T(8,128)} %get-tuple-element.53.refs_0_), channel_id=1, source_target_pairs={{0,1},{1,0},{2,3},{3,2},{4,5},{5,4},{6,7},{7,6},{8,9},{9,8},{10,11... | collective-permute-start | bytes 589832 | tf_op jit(solution)/shard_map/owned/ppermute | solution.py:84
  7.0 0.9 %copy-done.2 = f32[232,128]{1,0:T(8,128)S(1)} copy-done((f32[232,128]{1,0:T(8,128)S(1)}, f32[232,128]{1,0:T(8,128)}, u32[]{:S(2)}) %copy-start.2) | copy-done | bytes 118808
  8.0 0.8 %collective-permute-done.got = f32[232,128]{1,0:T(8,128)S(1)} collective-permute-done((f32[232,128]{1,0:T(8,128)}, f32[232,128]{1,0:T(8,128)S(1)}, u32[]{:S(2)}, u32[]{:S(2)}) %collective-permute-start) | collective-permute-done | bytes 118816 | tf_op jit(solution)/shard_map/to_column/ppermute | solution.py:76
  8.9 0.3 to_column.3
  9.2 0.7 collective-permute-start.1
  9.8 2.9 %collective-permute-start.2 = (f32[232,128]{1,0:T(8,128)S(1)}, f32[232,128]{1,0:T(8,128)S(1)}, u32[]{:S(2)}, u32[]{:S(2)}) collective-permute-start(f32[232,128]{1,0:T(8,128)S(1)} %get-tuple-element.57), channel_id=1, source_target_pairs={{0,2},{1,6},{2,0},{3,4},{4,3},{5,7},{6,1},{7,5},{8,10},{9,14},{10,... | collective-permute-start | bytes 356360 | tf_op jit(solution)/shard_map/to_column/ppermute | solution.py:414
  12.8 3.9 %collective-permute-done.2.second = f32[232,128]{1,0:T(8,128)S(1)} collective-permute-done((f32[232,128]{1,0:T(8,128)S(1)}, f32[232,128]{1,0:T(8,128)S(1)}, u32[]{:S(2)}, u32[]{:S(2)}) %collective-permute-start.2) | collective-permute-done | bytes 118816 | tf_op jit(solution)/shard_map/to_column/ppermute | solution.py:414
  16.7 1.6 %collective-permute-start.6 = (f32[464,128]{1,0:T(8,128)S(1)}, f32[464,128]{1,0:T(8,128)S(1)}, u32[]{:S(2)}, u32[]{:S(2)}) collective-permute-start(f32[464,128]{1,0:T(8,128)S(1)} %get-tuple-element.59.after.refs_0_), channel_id=1, source_target_pairs={{0,16},{4,20},{8,24},{12,28},{16,0},{20,4},{24,8},{28,12},{1,17},{... | collective-permute-start | bytes 712712 | tf_op jit(solution)/shard_map/panels/ppermute | solution.py:76
  18.3 1.1 %collective-permute-start.11 = (f32[464,128]{1,0:T(8,128)S(1)}, f32[464,128]{1,0:T(8,128)S(1)}, u32[]{:S(2)}, u32[]{:S(2)}) collective-permute-start(f32[464,128]{1,0:T(8,128)S(1)} %get-tuple-element.59.after.refs_0_), channel_id=1, source_target_pairs={{0,24},{4,28},{8,16},{12,20},{16,8},{20,12},{24,0},{28,4},{1,25},{... | collective-permute-start | bytes 712712 | tf_op jit(solution)/shard_map/panels/ppermute | solution.py:76
  19.3 0.9 %collective-permute-start.8 = (f32[464,128]{1,0:T(8,128)S(1)}, f32[464,128]{1,0:T(8,128)S(1)}, u32[]{:S(2)}, u32[]{:S(2)}) collective-permute-start(f32[464,128]{1,0:T(8,128)S(1)} %get-tuple-element.59.after.refs_0_), channel_id=1, source_target_pairs={{0,8},{4,12},{8,0},{12,4},{16,24},{20,28},{24,16},{28,20},{1,9},{5... | collective-permute-start | bytes 712712 | tf_op jit(solution)/shard_map/panels/ppermute | solution.py:76
  20.2 3.1 %collective-permute-start.4 = (f32[384,128]{1,0:T(8,128)}, f32[384,128]{1,0:T(8,128)S(1)}, u32[]{:S(2)}, u32[]{:S(2)}) collective-permute-start(f32[384,128]{1,0:T(8,128)} %get-tuple-element.53.refs_0_), channel_id=1, source_target_pairs={{0,2},{1,3},{2,0},{3,1},{4,6},{5,7},{6,4},{7,5},{8,10},{9,11},{10,... | collective-permute-start | bytes 589832 | tf_op jit(solution)/shard_map/owned/ppermute | solution.py:84
  23.3 0.7 %collective-permute-start.7 = (f32[464,128]{1,0:T(8,128)S(1)}, f32[464,128]{1,0:T(8,128)S(1)}, u32[]{:S(2)}, u32[]{:S(2)}) collective-permute-start(f32[464,128]{1,0:T(8,128)S(1)} %get-tuple-element.59.after.refs_0_), channel_id=1, source_target_pairs={{0,4},{4,0},{8,12},{12,8},{16,20},{20,16},{24,28},{28,24},{1,5},{5... | collective-permute-start | bytes 712712 | tf_op jit(solution)/shard_map/panels/ppermute | solution.py:76
  24.1 1.6 %copy-done = f32[4,1,128,8,1,128]{5,4,3,2,1,0:T(1,128)S(1)} copy-done((f32[4,1,128,8,1,128]{5,4,3,2,1,0:T(1,128)S(1)}, f32[4,1,128,8,1,128]{5,4,3,2,1,0:T(1,128)}, u32[]{:S(2)}) %copy-start) | copy-done | bytes 2097176
  25.7 0.7 copy-done.4
  26.3 1.2 %split_live.1 = (bf16[384,1024]{1,0:T(8,128)(2,1)S(1)}, bf16[384,1024]{1,0:T(8,128)(2,1)S(1)}) custom-call(f32[4096,128]{1,0:T(8,128)S(1)} %bitcast.9, s32[3]{0:T(128)S(1)} %copy-done.4, f32[464,128]{1,0:T(8,128)S(1)} %get-tuple-element.59.after.refs_0_), custom_call_target="tpu_custom_call" | custom-call | bytes 3907596 | tf_op jit(solution)/shard_map/split_live/pallas_call | solution.py:42
  27.5 1.2 %collective-permute-done.6.refs_0_ = f32[464,128]{1,0:T(8,128)S(1)} collective-permute-done((f32[464,128]{1,0:T(8,128)S(1)}, f32[464,128]{1,0:T(8,128)S(1)}, u32[]{:S(2)}, u32[]{:S(2)}) %collective-permute-start.6) | collective-permute-done | bytes 237600 | tf_op jit(solution)/shard_map/panels/ppermute | solution.py:76
  28.7 1.9 %collective-permute-start.10 = (f32[464,128]{1,0:T(8,128)S(1)}, f32[464,128]{1,0:T(8,128)S(1)}, u32[]{:S(2)}, u32[]{:S(2)}) collective-permute-start(f32[464,128]{1,0:T(8,128)S(1)} %get-tuple-element.64.refs_4_), channel_id=1, source_target_pairs={{0,4},{4,0},{8,12},{12,8},{16,20},{20,16},{24,28},{28,24},{1,5},{5... | collective-permute-start | bytes 712712 | tf_op jit(solution)/shard_map/panels/ppermute | solution.py:76
  30.8 1.0 %collective-permute-start.9 = (f32[464,128]{1,0:T(8,128)S(1)}, f32[464,128]{1,0:T(8,128)S(1)}, u32[]{:S(2)}, u32[]{:S(2)}) collective-permute-start(f32[464,128]{1,0:T(8,128)S(1)} %collective-permute-done.8.refs_2_), channel_id=1, source_target_pairs={{0,4},{4,0},{8,12},{12,8},{16,20},{20,16},{24,28},{28,24},{1,5},{5... | collective-permute-start | bytes 712712 | tf_op jit(solution)/shard_map/panels/ppermute | solution.py:76
  31.8 0.7 collective-permute-start.5
  32.5 0.4 collective-permute-done.9.refs_3_
  33.0 2.0 %shares_of.1 = (f32[96,512]{1,0:T(8,128)S(1)}, f32[96,512]{1,0:T(8,128)S(1)}, f32[96,512]{1,0:T(8,128)S(1)}, f32[96,512]{1,0:T(8,128)S(1)}, bf16[384,512]{1,0:T(...) custom-call(bf16[384,1024]{1,0:T(8,128)(2,1)S(1)} %get-tuple-element.62.sh, ...), custom_call_target="tpu_custom_call" | custom-call | bytes 5308416 | tf_op jit(solution)/shard_map/shares_of/pallas_call | solution.py:42
  35.0 1.1 %collective-permute-start.14 = (f32[96,512]{1,0:T(8,128)S(1)}, f32[96,512]{1,0:T(8,128)S(1)}, u32[]{:S(2)}, u32[]{:S(2)}) collective-permute-start(f32[96,512]{1,0:T(8,128)S(1)} %get-tuple-element.80), channel_id=1, source_target_pairs={{0,1},{1,0},{2,3},{3,2},{4,5},{5,4},{6,7},{7,6},{8,9},{9,8},{10,11... | collective-permute-start | bytes 589832 | tf_op jit(solution)/shard_map/sum_shares/ppermute | solution.py:84
  36.1 0.4 tops.1
  36.6 2.8 %collective-permute-done.5.refs_3_ = f32[384,128]{1,0:T(8,128)S(1)} collective-permute-done((f32[384,128]{1,0:T(8,128)S(1)}, f32[384,128]{1,0:T(8,128)S(1)}, u32[]{:S(2)}, u32[]{:S(2)}) %collective-permute-start.5) | collective-permute-done | bytes 196640 | tf_op jit(solution)/shard_map/owned/ppermute | solution.py:84
  39.5 1.6 %products.3 = (f32[384,256]{1,0:T(8,128)S(1)}, f32[384,256]{1,0:T(8,128)S(1)}) custom-call(bf16[384,512]{1,0:T(8,128)(2,1)S(1)} %get-tuple-element.67.gh, bf16[384,512]{1,0:T(8,128)(2,1)S(1)} %get-tuple-element.68.gl, bf16[256,256]{1,0:T(8,128)(2,1)S(1)} %get-tuple-element.70.th, bf16[256,256]{1,0:T(8,128)(2,1)S(1)} %get-tuple-element.71.tl, ...), custom_call_target="tpu_custom_call" | custom-call | bytes 3145728 | tf_op jit(solution)/shard_map/products/pallas_call | solution.py:42
  41.4 1.5 %collective-permute-done.14.refs_1_ = f32[96,512]{1,0:T(8,128)S(1)} collective-permute-done((f32[96,512]{1,0:T(8,128)S(1)}, f32[96,512]{1,0:T(8,128)S(1)}, u32[]{:S(2)}, u32[]{:S(2)}) %collective-permute-start.14) | collective-permute-done | bytes 196640 | tf_op jit(solution)/shard_map/sum_shares/ppermute | solution.py:84
  43.1 3.3 %collective-permute-start.22 = (f32[96,512]{1,0:T(8,128)S(1)}, f32[96,512]{1,0:T(8,128)S(1)}, u32[]{:S(2)}, u32[]{:S(2)}) collective-permute-start(f32[96,512]{1,0:T(8,128)S(1)} %get-tuple-element.91), channel_id=1, source_target_pairs={{0,2},{1,3},{2,0},{3,1},{4,6},{5,7},{6,4},{7,5},{8,10},{9,11},{10,... | collective-permute-start | bytes 589832 | tf_op jit(solution)/shard_map/sum_shares/ppermute | solution.py:84
  46.4 2.4 %collective-permute-start.15 = (f32[96,256]{1,0:T(8,128)S(1)}, f32[96,256]{1,0:T(8,128)S(1)}, u32[]{:S(2)}, u32[]{:S(2)}) collective-permute-start(f32[96,256]{1,0:T(8,128)S(1)} %get-tuple-element.82), channel_id=1, source_target_pairs={{0,24},{4,28},{8,16},{12,20},{16,8},{20,12},{24,0},{28,4},{1,25},{... | collective-permute-start | bytes 294920 | tf_op jit(solution)/shard_map/sum_chips/ppermute | solution.py:76
  48.8 0.5 collective-permute-start.16
  49.3 0.5 collective-permute-start.17
  49.8 2.1 %collective-permute-done.15.refs_1_ = f32[96,256]{1,0:T(8,128)S(1)} collective-permute-done((f32[96,256]{1,0:T(8,128)S(1)}, f32[96,256]{1,0:T(8,128)S(1)}, u32[]{:S(2)}, u32[]{:S(2)}) %collective-permute-start.15) | collective-permute-done | bytes 98336 | tf_op jit(solution)/shard_map/sum_chips/ppermute | solution.py:76
  52.0 2.0 %collective-permute-done.16.refs_2_ = f32[96,256]{1,0:T(8,128)S(1)} collective-permute-done((f32[96,256]{1,0:T(8,128)S(1)}, f32[96,256]{1,0:T(8,128)S(1)}, u32[]{:S(2)}, u32[]{:S(2)}) %collective-permute-start.16) | collective-permute-done | bytes 98336 | tf_op jit(solution)/shard_map/sum_chips/ppermute | solution.py:76
  54.1 0.5 collective-permute-start.18
  54.5 0.3 collective-permute-start.19
  54.8 3.1 %collective-permute-start.20 = (f32[24,256]{1,0:T(8,128)S(1)}, f32[24,256]{1,0:T(8,128)S(1)}, u32[]{:S(2)}, u32[]{:S(2)}) collective-permute-start(f32[24,256]{1,0:T(8,128)S(1)} %get-tuple-element.88), channel_id=1, source_target_pairs={{0,3},{1,0},{2,1},{3,2},{4,7},{5,4},{6,5},{7,6},{8,11},{9,8},{10,9... | collective-permute-start | bytes 73736 | tf_op jit(solution)/shard_map/sum_cols/ppermute | solution.py:80
  58.0 1.5 %rows_out.1 = (f32[128,256]{1,0:T(8,128)}, f32[128,256]{1,0:T(8,128)}) custom-call(s32[3]{0:T(128)S(1)} %copy-done.5, s32[3]{0:T(128)S(1)} %copy-done.6, s32[3]{0:T(128)S(1)} %copy-done.7, bf16[256,256]{1,0:T(8,128)(2,1)S(1)} %get-tuple-element.70.th, bf16[256,256]{1,0:T(8,128)(2,1)S(1)} %get-tuple-element.71.tl, f32[96,512]{1,0:T(8,128)S(1)} %get-tuple-element.89.refs_0_, ...), custom_call_target="tpu_custom_call" | custom-call | bytes 1114148 | tf_op jit(solution)/shard_map/rows_out/pallas_call | solution.py:42
  59.5 0.3 collective-permute-done.18.refs_1_
  59.8 0.5 collective-permute-done.20.refs_3_
  60.3 1.5 %collective-permute-start.24 = (f32[24,256]{1,0:T(8,128)S(1)}, f32[24,256]{1,0:T(8,128)S(1)}, u32[]{:S(2)}, u32[]{:S(2)}) collective-permute-start(f32[24,256]{1,0:T(8,128)S(1)} %get-tuple-element.96.refs_0_), channel_id=1, source_target_pairs={{0,8},{4,12},{8,0},{12,4},{16,24},{20,28},{24,16},{28,20},{1,9},{5... | collective-permute-start | bytes 73736 | tf_op jit(solution)/shard_map/spread/ppermute | solution.py:76
  61.8 0.7 %collective-permute-start.26 = (f32[24,256]{1,0:T(8,128)S(1)}, f32[24,256]{1,0:T(8,128)S(1)}, u32[]{:S(2)}, u32[]{:S(2)}) collective-permute-start(f32[24,256]{1,0:T(8,128)S(1)} %get-tuple-element.96.refs_0_), channel_id=1, source_target_pairs={{0,16},{4,20},{8,24},{12,28},{16,0},{20,4},{24,8},{28,12},{1,17},{... | collective-permute-start | bytes 73736 | tf_op jit(solution)/shard_map/spread/ppermute | solution.py:76
  62.5 1.4 %collective-permute-start.28 = (f32[24,256]{1,0:T(8,128)S(1)}, f32[24,256]{1,0:T(8,128)S(1)}, u32[]{:S(2)}, u32[]{:S(2)}) collective-permute-start(f32[24,256]{1,0:T(8,128)S(1)} %get-tuple-element.96.refs_0_), channel_id=1, source_target_pairs={{0,24},{4,28},{8,16},{12,20},{16,8},{20,12},{24,0},{28,4},{1,25},{... | collective-permute-start | bytes 73736 | tf_op jit(solution)/shard_map/spread/ppermute | solution.py:76
  63.9 0.3 collective-permute-done.24.refs_2_
  64.4 1.2 %collective-permute-done.26.refs_4_ = f32[24,256]{1,0:T(8,128)S(1)} collective-permute-done((f32[24,256]{1,0:T(8,128)S(1)}, f32[24,256]{1,0:T(8,128)S(1)}, u32[]{:S(2)}, u32[]{:S(2)}) %collective-permute-start.26) | collective-permute-done | bytes 24608 | tf_op jit(solution)/shard_map/spread/ppermute | solution.py:76
  65.6 1.6 %collective-permute-done.28.refs_6_ = f32[24,256]{1,0:T(8,128)S(1)} collective-permute-done((f32[24,256]{1,0:T(8,128)S(1)}, f32[24,256]{1,0:T(8,128)S(1)}, u32[]{:S(2)}, u32[]{:S(2)}) %collective-permute-start.28) | collective-permute-done | bytes 24608 | tf_op jit(solution)/shard_map/spread/ppermute | solution.py:76
  67.3 1.2 %collective-permute-done.29.refs_7_ = f32[24,256]{1,0:T(8,128)S(1)} collective-permute-done((f32[24,256]{1,0:T(8,128)S(1)}, f32[24,256]{1,0:T(8,128)S(1)}, u32[]{:S(2)}, u32[]{:S(2)}) %collective-permute-start.29) | collective-permute-done | bytes 24608 | tf_op jit(solution)/shard_map/spread/ppermute | solution.py:76
  68.4 0.7 %finish.1 = (f32[64,256]{1,0:T(8,128)}, f32[64,256]{1,0:T(8,128)}, f32[64,256]{1,0:T(8,128)}) custom-call(f32[64,256]{1,0:T(8,128)S(1)} %copy-done.1, f32[64,256]{1,0:T(8,128)S(1)} %copy-done.3, f32[64,256]{1,0:T(8,128)S(1)} %get-tuple-element.95.base, f32[24,256]{1,0:T(8,128)S(1)} %get-tuple-element.96.refs_0_, ...), custom_call_target="tpu_custom_call" | custom-call | bytes 589824 | tf_op jit(solution)/shard_map/finish/pallas_call | solution.py:42
  (47 shorter events, 1.1 us)
Async XLA Ops:
  2.4 6.4 %collective-permute-start = (f32[232,128]{1,0:T(8,128)}, f32[232,128]{1,0:T(8,128)S(1)}, u32[]{:S(2)}, u32[]{:S(2)}) collective-permute-start(f32[232,128]{1,0:T(8,128)} %get-tuple-element.55), channel_id=1, source_target_pairs={{0,8},{4,12},{8,0},{12,4},{16,24},{20,28},{24,16},{28,20},{1,9},{5... | collective-permute-start | bytes 356360 | tf_op jit(solution)/shard_map/to_column/ppermute | solution.py:76
  5.4 7.3 %collective-permute-start.3 = (f32[384,128]{1,0:T(8,128)}, f32[384,128]{1,0:T(8,128)S(1)}, u32[]{:S(2)}, u32[]{:S(2)}) collective-permute-start(f32[384,128]{1,0:T(8,128)} %get-tuple-element.53.refs_0_), channel_id=1, source_target_pairs={{0,1},{1,0},{2,3},{3,2},{4,5},{5,4},{6,7},{7,6},{8,9},{9,8},{10,11... | collective-permute-start | bytes 589832 | tf_op jit(solution)/shard_map/owned/ppermute | solution.py:84
  7.0 0.9 %copy-start.2 = (f32[232,128]{1,0:T(8,128)S(1)}, f32[232,128]{1,0:T(8,128)}, u32[]{:S(2)}) copy-start(f32[232,128]{1,0:T(8,128)} %get-tuple-element.54.source) | copy-start | bytes 356356
  9.2 3.6 %collective-permute-start.1 = (f32[232,128]{1,0:T(8,128)S(1)}, f32[232,128]{1,0:T(8,128)S(1)}, u32[]{:S(2)}, u32[]{:S(2)}) collective-permute-start(f32[232,128]{1,0:T(8,128)S(1)} %get-tuple-element.56), channel_id=1, source_target_pairs={{0,0},{1,4},{2,2},{3,6},{4,1},{5,5},{6,3},{7,7},{8,8},{9,12},{10,1... | collective-permute-start | bytes 356360 | tf_op jit(solution)/shard_map/to_column/ppermute | solution.py:414
  9.8 6.8 %collective-permute-start.2 = (f32[232,128]{1,0:T(8,128)S(1)}, f32[232,128]{1,0:T(8,128)S(1)}, u32[]{:S(2)}, u32[]{:S(2)}) collective-permute-start(f32[232,128]{1,0:T(8,128)S(1)} %get-tuple-element.57), channel_id=1, source_target_pairs={{0,2},{1,6},{2,0},{3,4},{4,3},{5,7},{6,1},{7,5},{8,10},{9,14},{10,... | collective-permute-start | bytes 356360 | tf_op jit(solution)/shard_map/to_column/ppermute | solution.py:414
  16.7 12.0 %collective-permute-start.6 = (f32[464,128]{1,0:T(8,128)S(1)}, f32[464,128]{1,0:T(8,128)S(1)}, u32[]{:S(2)}, u32[]{:S(2)}) collective-permute-start(f32[464,128]{1,0:T(8,128)S(1)} %get-tuple-element.59.after.refs_0_), channel_id=1, source_target_pairs={{0,16},{4,20},{8,24},{12,28},{16,0},{20,4},{24,8},{28,12},{1,17},{... | collective-permute-start | bytes 712712 | tf_op jit(solution)/shard_map/panels/ppermute | solution.py:76
  18.3 12.3 %collective-permute-start.11 = (f32[464,128]{1,0:T(8,128)S(1)}, f32[464,128]{1,0:T(8,128)S(1)}, u32[]{:S(2)}, u32[]{:S(2)}) collective-permute-start(f32[464,128]{1,0:T(8,128)S(1)} %get-tuple-element.59.after.refs_0_), channel_id=1, source_target_pairs={{0,24},{4,28},{8,16},{12,20},{16,8},{20,12},{24,0},{28,4},{1,25},{... | collective-permute-start | bytes 712712 | tf_op jit(solution)/shard_map/panels/ppermute | solution.py:76
  19.3 11.4 %collective-permute-start.8 = (f32[464,128]{1,0:T(8,128)S(1)}, f32[464,128]{1,0:T(8,128)S(1)}, u32[]{:S(2)}, u32[]{:S(2)}) collective-permute-start(f32[464,128]{1,0:T(8,128)S(1)} %get-tuple-element.59.after.refs_0_), channel_id=1, source_target_pairs={{0,8},{4,12},{8,0},{12,4},{16,24},{20,28},{24,16},{28,20},{1,9},{5... | collective-permute-start | bytes 712712 | tf_op jit(solution)/shard_map/panels/ppermute | solution.py:76
  20.2 11.6 %collective-permute-start.4 = (f32[384,128]{1,0:T(8,128)}, f32[384,128]{1,0:T(8,128)S(1)}, u32[]{:S(2)}, u32[]{:S(2)}) collective-permute-start(f32[384,128]{1,0:T(8,128)} %get-tuple-element.53.refs_0_), channel_id=1, source_target_pairs={{0,2},{1,3},{2,0},{3,1},{4,6},{5,7},{6,4},{7,5},{8,10},{9,11},{10,... | collective-permute-start | bytes 589832 | tf_op jit(solution)/shard_map/owned/ppermute | solution.py:84
  23.3 9.2 %collective-permute-start.7 = (f32[464,128]{1,0:T(8,128)S(1)}, f32[464,128]{1,0:T(8,128)S(1)}, u32[]{:S(2)}, u32[]{:S(2)}) collective-permute-start(f32[464,128]{1,0:T(8,128)S(1)} %get-tuple-element.59.after.refs_0_), channel_id=1, source_target_pairs={{0,4},{4,0},{8,12},{12,8},{16,20},{20,16},{24,28},{28,24},{1,5},{5... | collective-permute-start | bytes 712712 | tf_op jit(solution)/shard_map/panels/ppermute | solution.py:76
  24.1 1.6 %copy-start = (f32[4,1,128,8,1,128]{5,4,3,2,1,0:T(1,128)S(1)}, f32[4,1,128,8,1,128]{5,4,3,2,1,0:T(1,128)}, u32[]{:S(2)}) copy-start(f32[4,1,128,8,1,128]{5,4,3,2,1,0:T(1,128)} %param.10) | copy-start | bytes 6291460
  25.7 0.7 copy-start.4
  28.7 3.8 %collective-permute-start.10 = (f32[464,128]{1,0:T(8,128)S(1)}, f32[464,128]{1,0:T(8,128)S(1)}, u32[]{:S(2)}, u32[]{:S(2)}) collective-permute-start(f32[464,128]{1,0:T(8,128)S(1)} %get-tuple-element.64.refs_4_), channel_id=1, source_target_pairs={{0,4},{4,0},{8,12},{12,8},{16,20},{20,16},{24,28},{28,24},{1,5},{5... | collective-permute-start | bytes 712712 | tf_op jit(solution)/shard_map/panels/ppermute | solution.py:76
  30.6 1.9 %collective-permute-start.12 = (f32[464,128]{1,0:T(8,128)S(1)}, f32[464,128]{1,0:T(8,128)S(1)}, u32[]{:S(2)}, u32[]{:S(2)}) collective-permute-start(f32[464,128]{1,0:T(8,128)S(1)} %collective-permute-done.11.refs_6_), channel_id=1, source_target_pairs={{0,4},{4,0},{8,12},{12,8},{16,20},{20,16},{24,28},{28,24},{1,5},{5... | collective-permute-start | bytes 712712 | tf_op jit(solution)/shard_map/panels/ppermute | solution.py:76
  30.8 2.2 %collective-permute-start.9 = (f32[464,128]{1,0:T(8,128)S(1)}, f32[464,128]{1,0:T(8,128)S(1)}, u32[]{:S(2)}, u32[]{:S(2)}) collective-permute-start(f32[464,128]{1,0:T(8,128)S(1)} %collective-permute-done.8.refs_2_), channel_id=1, source_target_pairs={{0,4},{4,0},{8,12},{12,8},{16,20},{20,16},{24,28},{28,24},{1,5},{5... | collective-permute-start | bytes 712712 | tf_op jit(solution)/shard_map/panels/ppermute | solution.py:76
  31.8 4.3 %copy-start.1 = (f32[64,256]{1,0:T(8,128)S(1)}, f32[64,256]{1,0:T(8,128)}, u32[]{:S(2)}) copy-start(f32[64,256]{1,0:T(8,128)} %pd.3) | copy-start | bytes 196612
  31.8 7.5 %copy-start.8 = (f32[384,128]{1,0:T(8,128)S(1)}, f32[384,128]{1,0:T(8,128)}, u32[]{:S(2)}) copy-start(f32[384,128]{1,0:T(8,128)} %get-tuple-element.53.refs_0_) | copy-start | bytes 589828
  31.8 7.5 %collective-permute-start.5 = (f32[384,128]{1,0:T(8,128)S(1)}, f32[384,128]{1,0:T(8,128)S(1)}, u32[]{:S(2)}, u32[]{:S(2)}) collective-permute-start(f32[384,128]{1,0:T(8,128)S(1)} %owned.1.refs_2_), channel_id=1, source_target_pairs={{0,1},{1,0},{2,3},{3,2},{4,5},{5,4},{6,7},{7,6},{8,9},{9,8},{10,11... | collective-permute-start | bytes 589832 | tf_op jit(solution)/shard_map/owned/ppermute | solution.py:84
  35.0 8.0 %collective-permute-start.14 = (f32[96,512]{1,0:T(8,128)S(1)}, f32[96,512]{1,0:T(8,128)S(1)}, u32[]{:S(2)}, u32[]{:S(2)}) collective-permute-start(f32[96,512]{1,0:T(8,128)S(1)} %get-tuple-element.80), channel_id=1, source_target_pairs={{0,1},{1,0},{2,3},{3,2},{4,5},{5,4},{6,7},{7,6},{8,9},{9,8},{10,11... | collective-permute-start | bytes 589832 | tf_op jit(solution)/shard_map/sum_shares/ppermute | solution.py:84
  41.1 1.9 %collective-permute-start.13 = (f32[384,256]{1,0:T(8,128)S(1)}, f32[384,256]{1,0:T(8,128)S(1)}, u32[]{:S(2)}, u32[]{:S(2)}) collective-permute-start(f32[384,256]{1,0:T(8,128)S(1)} %get-tuple-element.78), channel_id=1, source_target_pairs={{0,4},{4,0},{8,12},{12,8},{16,20},{20,16},{24,28},{28,24},{1,5},{5... | collective-permute-start | bytes 1179656 | tf_op jit(solution)/shard_map/sum_core/ppermute | solution.py:76
  41.2 16.7 %collective-permute-start.21 = (f32[96,512]{1,0:T(8,128)S(1)}, f32[96,512]{1,0:T(8,128)S(1)}, u32[]{:S(2)}, u32[]{:S(2)}) collective-permute-start(f32[96,512]{1,0:T(8,128)S(1)} %get-tuple-element.90), channel_id=1, source_target_pairs={{0,1},{1,0},{2,3},{3,2},{4,5},{5,4},{6,7},{7,6},{8,9},{9,8},{10,11... | collective-permute-start | bytes 589832 | tf_op jit(solution)/shard_map/sum_shares/ppermute | solution.py:84
  42.9 15.0 %copy-start.5 = (s32[3]{0:T(128)S(1)}, s32[3]{0:T(128)}, u32[]{:S(2)}) copy-start(s32[3]{0:T(128)} %blocks.3) | copy-start | bytes 40
  42.9 15.0 %copy-start.6 = (s32[3]{0:T(128)S(1)}, s32[3]{0:T(128)}, u32[]{:S(2)}) copy-start(s32[3]{0:T(128)} %psize.1) | copy-start | bytes 40
  42.9 15.0 %copy-start.7 = (s32[3]{0:T(128)S(1)}, s32[3]{0:T(128)}, u32[]{:S(2)}) copy-start(s32[3]{0:T(128)} %csize.1) | copy-start | bytes 40
  43.0 25.5 %copy-start.3 = (f32[64,256]{1,0:T(8,128)S(1)}, f32[64,256]{1,0:T(8,128)}, u32[]{:S(2)}) copy-start(f32[64,256]{1,0:T(8,128)} %cd.1) | copy-start | bytes 196612
  43.1 14.9 %collective-permute-start.22 = (f32[96,512]{1,0:T(8,128)S(1)}, f32[96,512]{1,0:T(8,128)S(1)}, u32[]{:S(2)}, u32[]{:S(2)}) collective-permute-start(f32[96,512]{1,0:T(8,128)S(1)} %get-tuple-element.91), channel_id=1, source_target_pairs={{0,2},{1,3},{2,0},{3,1},{4,6},{5,7},{6,4},{7,5},{8,10},{9,11},{10,... | collective-permute-start | bytes 589832 | tf_op jit(solution)/shard_map/sum_shares/ppermute | solution.py:84
  46.4 5.6 %collective-permute-start.15 = (f32[96,256]{1,0:T(8,128)S(1)}, f32[96,256]{1,0:T(8,128)S(1)}, u32[]{:S(2)}, u32[]{:S(2)}) collective-permute-start(f32[96,256]{1,0:T(8,128)S(1)} %get-tuple-element.82), channel_id=1, source_target_pairs={{0,24},{4,28},{8,16},{12,20},{16,8},{20,12},{24,0},{28,4},{1,25},{... | collective-permute-start | bytes 294920 | tf_op jit(solution)/shard_map/sum_chips/ppermute | solution.py:76
  48.8 5.2 %collective-permute-start.16 = (f32[96,256]{1,0:T(8,128)S(1)}, f32[96,256]{1,0:T(8,128)S(1)}, u32[]{:S(2)}, u32[]{:S(2)}) collective-permute-start(f32[96,256]{1,0:T(8,128)S(1)} %get-tuple-element.83), channel_id=1, source_target_pairs={{0,16},{4,20},{8,24},{12,28},{16,0},{20,4},{24,8},{28,12},{1,17},{... | collective-permute-start | bytes 294920 | tf_op jit(solution)/shard_map/sum_chips/ppermute | solution.py:76
  49.3 4.7 %collective-permute-start.17 = (f32[96,256]{1,0:T(8,128)S(1)}, f32[96,256]{1,0:T(8,128)S(1)}, u32[]{:S(2)}, u32[]{:S(2)}) collective-permute-start(f32[96,256]{1,0:T(8,128)S(1)} %get-tuple-element.84), channel_id=1, source_target_pairs={{0,8},{4,12},{8,0},{12,4},{16,24},{20,28},{24,16},{28,20},{1,9},{5... | collective-permute-start | bytes 294920 | tf_op jit(solution)/shard_map/sum_chips/ppermute | solution.py:76
  54.1 5.7 %collective-permute-start.18 = (f32[24,256]{1,0:T(8,128)S(1)}, f32[24,256]{1,0:T(8,128)S(1)}, u32[]{:S(2)}, u32[]{:S(2)}) collective-permute-start(f32[24,256]{1,0:T(8,128)S(1)} %get-tuple-element.86), channel_id=1, source_target_pairs={{0,1},{1,2},{2,3},{3,0},{4,5},{5,6},{6,7},{7,4},{8,9},{9,10},{10,1... | collective-permute-start | bytes 73736 | tf_op jit(solution)/shard_map/sum_cols/ppermute | solution.py:80
  54.5 5.3 %collective-permute-start.19 = (f32[24,256]{1,0:T(8,128)S(1)}, f32[24,256]{1,0:T(8,128)S(1)}, u32[]{:S(2)}, u32[]{:S(2)}) collective-permute-start(f32[24,256]{1,0:T(8,128)S(1)} %get-tuple-element.87), channel_id=1, source_target_pairs={{0,2},{1,3},{2,0},{3,1},{4,6},{5,7},{6,4},{7,5},{8,10},{9,11},{10,... | collective-permute-start | bytes 73736 | tf_op jit(solution)/shard_map/sum_cols/ppermute | solution.py:80
  54.8 5.5 %collective-permute-start.20 = (f32[24,256]{1,0:T(8,128)S(1)}, f32[24,256]{1,0:T(8,128)S(1)}, u32[]{:S(2)}, u32[]{:S(2)}) collective-permute-start(f32[24,256]{1,0:T(8,128)S(1)} %get-tuple-element.88), channel_id=1, source_target_pairs={{0,3},{1,0},{2,1},{3,2},{4,7},{5,4},{6,5},{7,6},{8,11},{9,8},{10,9... | collective-permute-start | bytes 73736 | tf_op jit(solution)/shard_map/sum_cols/ppermute | solution.py:80
  60.3 3.9 %collective-permute-start.24 = (f32[24,256]{1,0:T(8,128)S(1)}, f32[24,256]{1,0:T(8,128)S(1)}, u32[]{:S(2)}, u32[]{:S(2)}) collective-permute-start(f32[24,256]{1,0:T(8,128)S(1)} %get-tuple-element.96.refs_0_), channel_id=1, source_target_pairs={{0,8},{4,12},{8,0},{12,4},{16,24},{20,28},{24,16},{28,20},{1,9},{5... | collective-permute-start | bytes 73736 | tf_op jit(solution)/shard_map/spread/ppermute | solution.py:76
  61.8 3.8 %collective-permute-start.26 = (f32[24,256]{1,0:T(8,128)S(1)}, f32[24,256]{1,0:T(8,128)S(1)}, u32[]{:S(2)}, u32[]{:S(2)}) collective-permute-start(f32[24,256]{1,0:T(8,128)S(1)} %get-tuple-element.96.refs_0_), channel_id=1, source_target_pairs={{0,16},{4,20},{8,24},{12,28},{16,0},{20,4},{24,8},{28,12},{1,17},{... | collective-permute-start | bytes 73736 | tf_op jit(solution)/shard_map/spread/ppermute | solution.py:76
  62.5 4.7 %collective-permute-start.28 = (f32[24,256]{1,0:T(8,128)S(1)}, f32[24,256]{1,0:T(8,128)S(1)}, u32[]{:S(2)}, u32[]{:S(2)}) collective-permute-start(f32[24,256]{1,0:T(8,128)S(1)} %get-tuple-element.96.refs_0_), channel_id=1, source_target_pairs={{0,24},{4,28},{8,16},{12,20},{16,8},{20,12},{24,0},{28,4},{1,25},{... | collective-permute-start | bytes 73736 | tf_op jit(solution)/shard_map/spread/ppermute | solution.py:76
  63.9 3.4 %collective-permute-start.23 = (f32[24,256]{1,0:T(8,128)S(1)}, f32[24,256]{1,0:T(8,128)S(1)}, u32[]{:S(2)}, u32[]{:S(2)}) collective-permute-start(f32[24,256]{1,0:T(8,128)S(1)} %get-tuple-element.96.refs_0_), channel_id=1, source_target_pairs={{0,4},{4,0},{8,12},{12,8},{16,20},{20,16},{24,28},{28,24},{1,5},{5... | collective-permute-start | bytes 73736 | tf_op jit(solution)/shard_map/spread/ppermute | solution.py:76
  64.2 3.0 %collective-permute-start.25 = (f32[24,256]{1,0:T(8,128)S(1)}, f32[24,256]{1,0:T(8,128)S(1)}, u32[]{:S(2)}, u32[]{:S(2)}) collective-permute-start(f32[24,256]{1,0:T(8,128)S(1)} %collective-permute-done.24.refs_2_), channel_id=1, source_target_pairs={{0,4},{4,0},{8,12},{12,8},{16,20},{20,16},{24,28},{28,24},{1,5},{5... | collective-permute-start | bytes 73736 | tf_op jit(solution)/shard_map/spread/ppermute | solution.py:76
  65.6 1.6 %collective-permute-start.27 = (f32[24,256]{1,0:T(8,128)S(1)}, f32[24,256]{1,0:T(8,128)S(1)}, u32[]{:S(2)}, u32[]{:S(2)}) collective-permute-start(f32[24,256]{1,0:T(8,128)S(1)} %collective-permute-done.26.refs_4_), channel_id=1, source_target_pairs={{0,4},{4,0},{8,12},{12,8},{16,20},{20,16},{24,28},{28,24},{1,5},{5... | collective-permute-start | bytes 73736 | tf_op jit(solution)/shard_map/spread/ppermute | solution.py:76
  67.2 1.2 %collective-permute-start.29 = (f32[24,256]{1,0:T(8,128)S(1)}, f32[24,256]{1,0:T(8,128)S(1)}, u32[]{:S(2)}, u32[]{:S(2)}) collective-permute-start(f32[24,256]{1,0:T(8,128)S(1)} %collective-permute-done.28.refs_6_), channel_id=1, source_target_pairs={{0,4},{4,0},{8,12},{12,8},{16,20},{20,16},{24,28},{28,24},{1,5},{5... | collective-permute-start | bytes 73736 | tf_op jit(solution)/shard_map/spread/ppermute | solution.py:76
